TPU v7x, 32 devices: a whole 2x2x4 slice. The times are simulated.
32 devices in a mesh: leaf: 4 (over y, x), rows: 8 (over z, core).
Axes of the slice: x: 2, y: 2, z: 4, core: 2. Of those that a mesh axis runs over, the one named last changes fastest.
Arguments:
- leaf_rhs: float32 [8, 16, 2048], P(None, 'leaf', 'rows'), may hold values from -6 to 6
- parent_rhs: float32 [8, 4, 4096], P(None, 'leaf', 'rows'), may hold values from -6 to 6
- root_rhs: float32 [8, 4096], P(None, ('leaf', 'rows')), may hold values from -6 to 6
- leaf_inv: bfloat16 [16, 2048, 2048], P('leaf', 'rows'), as said below
- leaf_panel: bfloat16 [16, 8192, 2048], P('leaf', 'rows'), may hold values from -0.0625 to 0.0625
- leaf_rows: int32 [16, 8192], P('leaf', 'rows'), may hold values from 0 to 8191, as said below
- leaf_height: int32 [16], P('leaf'), may hold values from 2048 to 8192
- parent_inv: bfloat16 [4, 4096, 4096], P('leaf', 'rows'), as said below
- parent_panel: bfloat16 [4, 4096, 4096], P('leaf', 'rows'), may hold values from -0.046875 to 0.046875
- parent_rows: int32 [4, 4096], P('leaf', 'rows'), may hold values from 0 to 4095, as said below
- parent_height: int32 [4], P('leaf'), may hold values from 1024 to 4096
- root_inv: bfloat16 [4096, 4096], P('rows'), as said below
Outputs:
- leaf_solution: float32 [8, 16, 2048], P(None, 'leaf', 'rows')
- parent_solution: float32 [8, 4, 4096], P(None, 'leaf', 'rows')
- root_solution: float32 [8, 4096], P(None, ('leaf', 'rows'))
Inputs may be any that keep to these rules, and one draw needn't show every extreme that they name: `leaf_rows`: each leaf's first leaf_height entries are distinct and ascending; every entry is a valid ancestor index. `parent_rows`: each parent's first parent_height entries are distinct and ascending. `leaf_inv`: A dense well conditioned matrix. `parent_inv`: A dense well conditioned matrix. `root_inv`: A dense well conditioned matrix.
All inputs are finite; a program needn't handle non-finite values.
Results may differ from a plain program's by a relative error of at most 0.009.
Values may be sent and summed in bfloat16 or wider, within the bound.
No kernel may reach another device: no remote copies, remote signals or barrier semaphores. Data moves between devices by JAX's collectives and lax.ppermute only.
A program may use at most 128 MiB of HBM per device.

v0:
```python
import jax
import jax.numpy as jnp
from jax import lax
from jax.sharding import PartitionSpec as P


def shards(
    leaf_rhs,
    parent_rhs,
    root_rhs,
    leaf_inv,
    leaf_panel,
    leaf_rows,
    leaf_height,
    parent_inv,
    parent_panel,
    parent_rows,
    parent_height,
    root_inv,
):
    rcount = leaf_rhs.shape[0]
    group_leaves = leaf_rhs.shape[1]
    leaf_local = leaf_panel.shape[1]
    parent_width = parent_inv.shape[2]
    root_width = root_inv.shape[1]
    row_index = lax.axis_index("rows")
    root_cols = root_rhs.shape[1]
    flat_index = lax.axis_index("leaf") * lax.axis_size("rows") + row_index
    block = leaf_inv
    ly = jnp.einsum(
        "rln,lin->rli",
        lax.all_gather(leaf_rhs.astype(jnp.bfloat16), "rows", axis=2, tiled=True),
        block,
        preferred_element_type=jnp.float32,
    )
    lyb = ly.astype(jnp.bfloat16)
    block = leaf_panel
    lupd = jnp.einsum(
        "rln,lhn->rlh",
        lax.all_gather(lyb, "rows", axis=2, tiled=True),
        block,
        preferred_element_type=jnp.float32,
    )
    leaf_pos = row_index * leaf_local + jnp.arange(leaf_local, dtype=jnp.int32)
    leaf_mask = leaf_pos[None, :] < leaf_height[:, None]
    lupd = jnp.where(leaf_mask[None, :, :], lupd, 0.0)
    leaf_flat = leaf_rows.reshape(-1)
    local_acc = (
        jnp.zeros((rcount, parent_width + root_width), jnp.float32)
        .at[:, leaf_flat]
        .add(lupd.reshape(rcount, -1))
    )
    parent_slice = lax.psum_scatter(
        local_acc[:, :parent_width], "rows", scatter_dimension=1, tiled=True
    )
    root_from_leaves = local_acc[:, parent_width:]
    prb = (parent_rhs[:, 0, :] - parent_slice).astype(jnp.bfloat16)
    inverse_rows = parent_inv[0]
    panel_rows = parent_panel[0]
    block = inverse_rows
    py = jnp.dot(
        lax.all_gather(prb, "rows", axis=1, tiled=True), block.T, preferred_element_type=jnp.float32
    )
    pyb = py.astype(jnp.bfloat16)
    parent_local = panel_rows.shape[0]
    block = panel_rows
    pupd = jnp.dot(
        lax.all_gather(pyb, "rows", axis=1, tiled=True), block.T, preferred_element_type=jnp.float32
    )
    parent_pos = row_index * parent_local + jnp.arange(parent_local, dtype=jnp.int32)
    parent_mask = parent_pos < parent_height[0]
    pupd = jnp.where(parent_mask[None, :], pupd, 0.0)
    parent_root = jnp.zeros((rcount, root_width), jnp.float32).at[:, parent_rows[0]].add(pupd)
    leaf_share = lax.psum_scatter(
        root_from_leaves, ("leaf", "rows"), scatter_dimension=1, tiled=True
    )
    root_slice = leaf_share + lax.psum_scatter(
        parent_root, ("leaf", "rows"), scatter_dimension=1, tiled=True
    )
    rrb = (root_rhs - root_slice).astype(jnp.bfloat16)
    block = root_inv
    ry = jnp.dot(
        lax.all_gather(rrb, ("leaf", "rows"), axis=1, tiled=True),
        block.T,
        preferred_element_type=jnp.float32,
    )
    root_term = jnp.dot(ry.astype(jnp.bfloat16), root_inv, preferred_element_type=jnp.float32)
    root_full = lax.psum(root_term, "rows")
    root_solution = lax.dynamic_slice_in_dim(root_full, flat_index * root_cols, root_cols, 1)
    rxb = root_full.astype(jnp.bfloat16)
    parent_anc = rxb[:, parent_rows[0]]
    parent_anc = jnp.where(parent_mask[None, :], parent_anc, jnp.zeros_like(parent_anc))
    parent_term = jnp.dot(parent_anc, panel_rows, preferred_element_type=jnp.float32)
    parent_tail = lax.psum_scatter(parent_term, "rows", scatter_dimension=1, tiled=True)
    pvb = (py - parent_tail).astype(jnp.bfloat16)
    parent_sol_term = jnp.dot(pvb, inverse_rows, preferred_element_type=jnp.float32)
    parent_sol = lax.psum_scatter(parent_sol_term, "rows", scatter_dimension=1, tiled=True)
    parent_whole = lax.all_gather(parent_sol.astype(jnp.bfloat16), "rows", axis=1, tiled=True)
    ancestors = jnp.concatenate([parent_whole, rxb], axis=1)
    leaf_anc = ancestors[:, leaf_flat].reshape(rcount, group_leaves, leaf_local)
    leaf_anc = jnp.where(leaf_mask[None, :, :], leaf_anc, jnp.zeros_like(leaf_anc))
    leaf_term = jnp.einsum("rlh,lhc->rlc", leaf_anc, leaf_panel, preferred_element_type=jnp.float32)
    leaf_tail = lax.psum_scatter(leaf_term, "rows", scatter_dimension=2, tiled=True)
    lvb = (ly - leaf_tail).astype(jnp.bfloat16)
    leaf_sol_term = jnp.einsum("rli,lic->rlc", lvb, leaf_inv, preferred_element_type=jnp.float32)
    leaf_sol = lax.psum_scatter(leaf_sol_term, "rows", scatter_dimension=2, tiled=True)
    return (leaf_sol, parent_sol[:, None, :], root_solution)


def solution(mesh):
    return jax.shard_map(
        shards,
        mesh=mesh,
        in_specs=(
            P(None, "leaf", "rows"),
            P(None, "leaf", "rows"),
            P(None, ("leaf", "rows")),
            P("leaf", "rows", None),
            P("leaf", "rows", None),
            P("leaf", "rows"),
            P("leaf"),
            P("leaf", "rows", None),
            P("leaf", "rows", None),
            P("leaf", "rows"),
            P("leaf"),
            P("rows", None),
        ),
        out_specs=(P(None, "leaf", "rows"), P(None, "leaf", "rows"), P(None, ("leaf", "rows"))),
        check_vma=False,
    )
```

profile of v0, /device:TPU:0, one launch (start us, length us, event | category | flops | bytes accessed | tf_op | source)
XLA Modules:
  0.0 559.9 jit_solution(4094073844248728516)
XLA Ops:
  7.2 0.8 copy.44
  8.0 15.7 %all_gather.18 = bf16[8,4,2048]{2,0,1:T(8,128)(2,1)S(1)} all-gather(bf16[8,4,256]{2,0,1:T(8,128)(2,1)S(1)} %copy.44), channel_id=1, replica_groups=mesh['leaf'=4,'rows'=8] {'rows'}, dimensions={2}, use_global_device_ids=true | all-gather | bytes 147456 | tf_op jit(solution)/shard_map/all_gather | solution.py:32
  23.7 0.7 copy.42
  24.4 3.4 fusion.29
  27.8 14.0 %all_gather.19 = bf16[8,4,2048]{2,0,1:T(8,128)(2,1)S(1)} all-gather(bf16[8,4,256]{2,0,1:T(8,128)(2,1)S(1)} %get-tuple-element.14), channel_id=1, replica_groups=mesh['leaf'=4,'rows'=8] {'rows'}, dimensions={2}, use_global_device_ids=true | all-gather | bytes 147456 | tf_op jit(solution)/shard_map/all_gather | solution.py:40
  41.8 0.1 broadcast_compare_fusion
  41.9 10.2 %convolution_select_fusion = f32[4,8,1024]{2,1,0:T(8,128)S(1)} fusion(bf16[8,4,2048]{2,0,1:T(8,128)(2,1)S(1)} %all_gather.19, bf16[4,1024,2048]{2,1,0:T(8,128)(2,1)} %param.16, pred[4,1024]{1,0:T(4,128)(4,1)S(1)} %broadcast_compare_fusion), kind=kOutput, calls=%fused_computation.16 | convolution fusion | flops 134250496 | bytes 17043456 | tf_op jit(solution)/shard_map/rln,lhn->rlh/dot_general | solution.py:38
  52.1 0.6 copy.32
  52.7 24.5 %scatter_custom_fusion = f32[8,8192]{0,1:T(8,128)} fusion(s32[4096]{0:T(1024)S(1)} %bitcast.60, f32[4096,8]{1,0:T(8,128)S(1)} %copy.32, f32[]{:T(128)} %constant.13.clone.1), kind=kCustom, calls=%fused_computation.14 | custom fusion | flops 32768 | bytes 262148 | tf_op jit(solution)/shard_map/scatter-add | solution.py:51
  77.2 3.8 fusion.28
  81.0 0.0 reduce-scatter.17.cloned.1.call-start
  81.7 0.6 copy.41
  82.3 0.1 copy.31
  82.5 35.5 %reduce-scatter.7.cloned.1.call-done = f32[8,512]{0,1:T(8,128)} async-done(((f32[8,4096]{0,1:T(8,128)}), f32[8,512]{0,1:T(8,128)}) %reduce-scatter.7.cloned.1.call-update) | async-done | bytes 16400 | tf_op jit(solution)/shard_map/reduce_scatter | solution.py:53
  117.9 1.1 fusion.19
  119.1 15.8 %all_gather.20 = bf16[8,4096]{0,1:T(8,128)(2,1)S(1)} all-gather(bf16[8,512]{0,1:T(8,128)(2,1)S(1)} %fusion.19), channel_id=1, replica_groups=mesh['leaf'=4,'rows'=8] {'rows'}, dimensions={1}, use_global_device_ids=true | all-gather | bytes 73728 | tf_op jit(solution)/shard_map/all_gather | solution.py:62
  134.9 3.4 fusion.30
  138.2 14.2 %all_gather.21 = bf16[8,4096]{1,0:T(8,128)(2,1)S(1)} all-gather(bf16[8,512]{1,0:T(8,128)(2,1)S(1)} %get-tuple-element.16), channel_id=1, replica_groups=mesh['leaf'=4,'rows'=8] {'rows'}, dimensions={1}, use_global_device_ids=true | all-gather | bytes 73728 | tf_op jit(solution)/shard_map/all_gather | solution.py:68
  152.4 1.2 fusion.13
  153.6 0.1 copy.34
  153.7 2.8 scatter_custom_fusion.1
  156.5 0.6 copy.35
  157.1 0.7 add.80
  157.8 132.8 %reduce-scatter.17.cloned.1.call-done = f32[8,128]{1,0:T(8,128)} async-done(((f32[8,4096]{1,0:T(8,128)}), f32[8,128]{1,0:T(8,128)}) %reduce-scatter.17.cloned.1.call-update) | async-done | bytes 4112 | tf_op jit(solution)/shard_map/reduce_scatter | solution.py:74
  290.7 0.7 subtract_convert_fusion.4
  291.3 36.6 %all_gather.22 = bf16[8,4096]{1,0:T(8,128)(2,1)S(1)} all-gather(bf16[8,128]{1,0:T(8,128)(2,1)S(1)} %subtract_convert_fusion.4), channel_id=1, replica_groups=mesh['leaf'=4,'rows'=8] {'leaf','rows'}, dimensions={1}, use_global_device_ids=true | all-gather | bytes 67584 | tf_op jit(solution)/shard_map/all_gather | solution.py:83
  327.9 5.9 %fusion.16 = f32[8,4096]{1,0:T(8,128)} fusion(bf16[512,4096]{1,0:T(8,128)(2,1)} %param.23, bf16[8,4096]{1,0:T(8,128)(2,1)S(1)} %all_gather.22), kind=kOutput, calls=%fused_computation.21 | convolution fusion | flops 67112960 | bytes 4390912 | tf_op jit(solution)/shard_map/dot_general | solution.py:87
  333.9 52.2 %all-reduce.2.cloned.1.call-done = f32[8,4096]{1,0:T(8,128)} async-done(((f32[8,4096]{1,0:T(8,128)}), f32[8,4096]{1,0:T(8,128)}) %all-reduce.2.cloned.1.call-update) | async-done | bytes 131088 | tf_op jit(solution)/shard_map/psum | solution.py:88
  386.1 0.9 convert_element_type.36
  387.1 0.5 copy.36
  387.5 1.3 gather_fusion
  388.9 3.6 fusion
  392.6 29.3 %reduce-scatter.9.cloned.1.call-done = f32[8,512]{1,0:T(8,128)} async-done(((f32[8,4096]{1,0:T(8,128)}), f32[8,512]{1,0:T(8,128)}) %reduce-scatter.9.cloned.1.call-update) | async-done | bytes 16400 | tf_op jit(solution)/shard_map/reduce_scatter | solution.py:94
  421.8 3.5 fusion.4
  425.4 28.4 %reduce-scatter.11.cloned.1.call-done = f32[8,512]{1,0:T(8,128)} async-done(((f32[8,4096]{1,0:T(8,128)}), f32[8,512]{1,0:T(8,128)}) %reduce-scatter.11.cloned.1.call-update) | async-done | bytes 16400 | tf_op jit(solution)/shard_map/reduce_scatter | solution.py:97
  453.8 0.7 convert_element_type.38
  454.5 14.0 %all_gather.23 = bf16[8,4096]{1,0:T(8,128)(2,1)S(1)} all-gather(bf16[8,512]{1,0:T(8,128)(2,1)S(1)} %convert_element_type.38), channel_id=1, replica_groups=mesh['leaf'=4,'rows'=8] {'rows'}, dimensions={1}, use_global_device_ids=true | all-gather | bytes 73728 | tf_op jit(solution)/shard_map/all_gather | solution.py:98
  468.5 1.0 copy.37
  469.5 12.1 %gather_fusion.1 = bf16[4096,8]{1,0:T(8,128)(2,1)S(1)} fusion(bf16[8,8192]{0,1:T(8,128)(2,1)S(1)} %copy.37, s32[4096]{0:T(1024)S(1)} %broadcast_clamp_fusion), kind=kCustom, calls=%fused_computation.1 | custom fusion | bytes 147456 | tf_op jit(solution)/shard_map/gather | solution.py:100
  481.7 0.3 copy.38
  482.0 8.8 %convolution_bitcast_fusion.1 = f32[8,4,2048]{2,0,1:T(8,128)} fusion(bf16[4,1024,2048]{2,1,0:T(8,128)(2,1)} %param.16, bf16[8,4,1024]{2,0,1:T(8,128)(2,1)S(1)} %copy.38, pred[4,1024]{1,0:T(4,128)(4,1)S(1)} %broadcast_compare_fusion), kind=kOutput, calls=%fused_computation.13 | convolution fusion | flops 134250496 | bytes 17108992 | tf_op jit(solution)/shard_map/rlh,lhc->rlc/dot_general | solution.py:102
  490.8 0.0 reduce-scatter.15.cloned.1.call-start
  490.8 28.6 %reduce-scatter.13.cloned.1.call-done = f32[8,4,256]{2,0,1:T(8,128)} async-done(((f32[8,4,2048]{2,0,1:T(8,128)}), f32[8,4,256]{2,0,1:T(8,128)}) %reduce-scatter.13.cloned.1.call-update) | async-done | bytes 32784 | tf_op jit(solution)/shard_map/reduce_scatter | solution.py:103
  519.4 3.6 convolution_bitcast_fusion
  523.0 1.3 constant_dynamic-slice_fusion
  524.3 0.6 copy.40
  524.9 26.7 %reduce-scatter.15.cloned.1.call-done = f32[8,4,256]{2,0,1:T(8,128)} async-done(((f32[8,4,2048]{2,0,1:T(8,128)}), f32[8,4,256]{2,0,1:T(8,128)}) %reduce-scatter.15.cloned.1.call-update) | async-done | bytes 32784 | tf_op jit(solution)/shard_map/reduce_scatter | solution.py:106
  551.7 1.4 copy.39
  (31 shorter events, 0.4 us)
Async XLA Ops:
  7.2 34.6 %copy-start.5 = (s32[4]{0:T(128)S(1)}, s32[4]{0:T(128)}, u32[]{:S(2)}) copy-start(s32[4]{0:T(128)} %param.18) | copy-start | bytes 52
  7.2 110.8 %reduce-scatter.7.cloned.1.call-start = ((), (), s32[]{:S(2)}) async-start(), calls=%async_computation.6 | async-start | bytes 2359296 | tf_op jit(solution)/shard_map/reduce_scatter | solution.py:53
  81.0 1.3 copy-start.2
  81.0 1.5 copy-start.4
  81.0 209.6 %reduce-scatter.17.cloned.1.call-start = ((), (), s32[]{:S(2)}) async-start(), calls=%async_computation.12 | async-start | bytes 135168 | tf_op jit(solution)/shard_map/reduce_scatter | solution.py:74
  117.9 34.5 %copy-start = (bf16[1,512,4096]{2,1,0:T(8,128)(2,1)S(1)}, bf16[1,512,4096]{2,1,0:T(8,128)(2,1)}, u32[]{:S(2)}) copy-start(bf16[1,512,4096]{2,1,0:T(8,128)(2,1)} %param.20) | copy-start | bytes 12582916
  152.4 138.2 %copy-start.3 = (f32[8,128]{1,0:T(8,128)S(1)}, f32[8,128]{1,0:T(8,128)}, u32[]{:S(2)}) copy-start(f32[8,128]{1,0:T(8,128)} %param.14) | copy-start | bytes 12292
  157.8 228.4 %all-reduce.2.cloned.1.call-start = ((), (), s32[]{:S(2)}) async-start(), calls=%async_computation.7 | async-start | bytes 262144 | tf_op jit(solution)/shard_map/psum | solution.py:88
  333.8 88.0 %reduce-scatter.9.cloned.1.call-start = ((), (), s32[]{:S(2)}) async-start(), calls=%async_computation.8 | async-start | bytes 147456 | tf_op jit(solution)/shard_map/reduce_scatter | solution.py:94
  392.5 61.3 %reduce-scatter.11.cloned.1.call-start = ((), (), s32[]{:S(2)}) async-start(), calls=%async_computation.9 | async-start | bytes 147456 | tf_op jit(solution)/shard_map/reduce_scatter | solution.py:97
  425.4 94.1 %reduce-scatter.13.cloned.1.call-start = ((), (), s32[]{:S(2)}) async-start(), calls=%async_computation.10 | async-start | bytes 294912 | tf_op jit(solution)/shard_map/reduce_scatter | solution.py:103
  490.7 33.6 %copy-start.1 = (f32[8,512]{1,0:T(8,128)S(1)}, f32[8,512]{1,0:T(8,128)}, u32[]{:S(2)}) copy-start(f32[8,512]{1,0:T(8,128)} %reduce-scatter.11.cloned.1.call-done) | copy-start | bytes 49156
  490.8 60.9 %reduce-scatter.15.cloned.1.call-start = ((), (), s32[]{:S(2)}) async-start(), calls=%async_computation.11 | async-start | bytes 294912 | tf_op jit(solution)/shard_map/reduce_scatter | solution.py:106
Sparse Core Ops, SparseCore 0:
  81.2 36.7 reduce-scatter.6
  157.9 132.7 reduce-scatter.16
  334.0 52.1 all-reduce.1
  392.6 29.1 reduce-scatter.8
  425.5 28.2 reduce-scatter.10
  490.9 28.5 reduce-scatter.12
  523.1 28.4 reduce-scatter.14
where the time goes:
time: 561 us; the launch traced here: 560 us
  waiting for transfers between devices  334 us (60%)
  blocking collectives  110 us (20%)
  matrix products  43.4 us (8%)
  other arithmetic  31.5 us (6%)
  local copies, waits for them, and re-layouts  25.9 us (5%)
  between operations  14.9 us (3%)
    reduce_scatter x1, waiting for transfers between devices, shards(): lax.psum_scatter(root_from_leaves, ('leaf', 'rows'), scatter_dimension=1,...  133 us
    psum x1, waiting for transfers between devices, shards(): root_full = lax.psum(root_term, 'rows')  52.2 us
    all_gather x1, blocking collectives, shards(): lax.all_gather(rrb, ('leaf', 'rows'), axis=1, tiled=True)  36.6 us
    reduce_scatter x1, waiting for transfers between devices, shards(): lax.psum_scatter(local_acc[:, :parent_width], 'rows', scatter_dimension=1...  35.5 us
    reduce_scatter x1, waiting for transfers between devices, shards(): lax.psum_scatter(parent_term, 'rows', scatter_dimension=1, tiled=True)  29.3 us
    reduce_scatter x1, waiting for transfers between devices, shards(): lax.psum_scatter(leaf_term, 'rows', scatter_dimension=2, tiled=True)  28.6 us
    reduce_scatter x1, waiting for transfers between devices, shards(): lax.psum_scatter(parent_sol_term, 'rows', scatter_dimension=1, tiled=True)  28.4 us
    reduce_scatter x1, waiting for transfers between devices, shards(): lax.psum_scatter(leaf_sol_term, 'rows', scatter_dimension=2, tiled=True)  26.7 us
  transfers between devices with their start and end apart: 7, of which 7 were waited for; matrix products, arithmetic and copies ran while one was open for 0% of the time, Pallas kernels for 0%

commit v1 on v0

v1 whole, which is shorter than its diff:
```python
import jax
import jax.numpy as jnp
from jax import lax
from jax.sharding import PartitionSpec as P

F32 = jnp.float32
BF16 = jnp.bfloat16


def a2a_gather(x, axis):
    n = lax.axis_size(axis)
    return lax.all_to_all(jnp.broadcast_to(x[None], (n,) + x.shape), axis, 0, 0)


def a2a_reduce(x, axis):
    return lax.all_to_all(x.astype(BF16), axis, 0, 0).astype(F32).sum(0)


def shift(x, axis, k):
    n = lax.axis_size(axis)
    return lax.ppermute(x, axis, [(i, (i + k) % n) for i in range(n)])


def direct_gather(x, axis):
    n = lax.axis_size(axis)
    me = lax.axis_index(axis)
    got = [x] + [shift(x, axis, k) for k in range(1, n)]
    order = jnp.stack(got[::-1] + got[::-1])
    return lax.dynamic_slice_in_dim(order, n - 1 - me, n, 0)


def direct_reduce(x, axis):
    n = lax.axis_size(axis)
    me = lax.axis_index(axis)
    x = x.astype(BF16)
    got = []
    for k in range(n):
        part = lax.dynamic_index_in_dim(x, lax.rem(me + k, n), 0, keepdims=False)
        got.append(part if k == 0 else shift(part, axis, k))
    return sum(p.astype(F32) for p in got)


def direct_sum(x, axis):
    n = lax.axis_size(axis)
    x = x.astype(BF16)
    got = [x] + [shift(x, axis, k) for k in range(1, n)]
    return sum(p.astype(F32) for p in got)


def doubling_gather(x, axis):
    n = lax.axis_size(axis)
    me = lax.axis_index(axis)
    cur = x[None]
    step = 1
    while step < n:
        got = lax.ppermute(cur, axis, [(i, i ^ step) for i in range(n)])
        upper = (me & step) != 0
        cur = jnp.concatenate([jnp.where(upper, got, cur), jnp.where(upper, cur, got)])
        step *= 2
    return cur


def shards(
    leaf_rhs,
    parent_rhs,
    root_rhs,
    leaf_inv,
    leaf_panel,
    leaf_rows,
    leaf_height,
    parent_inv,
    parent_panel,
    parent_rows,
    parent_height,
    root_inv,
):
    n = lax.axis_size("rows")
    groups = lax.axis_size("leaf")
    rcount = leaf_rhs.shape[0]
    group_leaves = leaf_rhs.shape[1]
    leaf_local = leaf_panel.shape[1]
    parent_width = parent_inv.shape[2]
    root_width = root_inv.shape[1]
    row_index = lax.axis_index("rows")
    leaf_index = lax.axis_index("leaf")
    parent_cols = parent_width // n
    root_cols = root_rhs.shape[1]

    lb = a2a_gather(leaf_rhs.astype(BF16), "rows")
    lb = jnp.moveaxis(lb, 0, 2).reshape(rcount, group_leaves, -1)
    ly = jnp.einsum("rln,lin->rli", lb, leaf_inv, preferred_element_type=F32)
    lyb = direct_gather(ly.astype(BF16), "rows")
    lyb = jnp.moveaxis(lyb, 0, 2).reshape(rcount, group_leaves, -1)
    lupd = jnp.einsum("rln,lhn->rlh", lyb, leaf_panel, preferred_element_type=F32)
    leaf_pos = row_index * leaf_local + jnp.arange(leaf_local, dtype=jnp.int32)
    leaf_mask = leaf_pos[None, :] < leaf_height[:, None]
    lupd = jnp.where(leaf_mask[None, :, :], lupd, 0.0)
    leaf_flat = leaf_rows.reshape(-1)
    local_acc = (
        jnp.zeros((rcount, parent_width + root_width), F32)
        .at[:, leaf_flat]
        .add(lupd.reshape(rcount, -1))
    )
    pacc = a2a_reduce(
        jnp.moveaxis(local_acc[:, :parent_width].reshape(rcount, n, parent_cols), 1, 0), "rows"
    )
    root_from_leaves = local_acc[:, parent_width:]
    prb = (parent_rhs[:, 0, :] - pacc).astype(BF16)
    prb = jnp.moveaxis(doubling_gather(prb, "rows"), 0, 1).reshape(rcount, -1)
    inverse_rows = parent_inv[0]
    panel_rows = parent_panel[0]
    py = jnp.dot(prb, inverse_rows.T, preferred_element_type=F32)
    pyb = jnp.moveaxis(a2a_gather(py.astype(BF16), "rows"), 0, 1).reshape(rcount, -1)
    parent_local = panel_rows.shape[0]
    pupd = jnp.dot(pyb, panel_rows.T, preferred_element_type=F32)
    parent_pos = row_index * parent_local + jnp.arange(parent_local, dtype=jnp.int32)
    parent_mask = parent_pos < parent_height[0]
    pupd = jnp.where(parent_mask[None, :], pupd, 0.0)
    root_part = root_from_leaves.at[:, parent_rows[0]].add(pupd)
    root_part = jnp.transpose(root_part.reshape(rcount, groups, n, root_cols), (2, 0, 1, 3))
    racc = direct_sum(direct_reduce(root_part, "rows"), "leaf")
    rhs_piece = jnp.moveaxis(direct_gather(root_rhs, "leaf"), 0, 1)
    rrb = direct_gather((rhs_piece - racc).astype(BF16), "rows")
    rrb = jnp.transpose(rrb, (1, 2, 0, 3)).reshape(rcount, root_width)
    ry = jnp.dot(rrb, root_inv.T, preferred_element_type=F32)
    root_term = jnp.dot(ry.astype(BF16), root_inv, preferred_element_type=F32)
    root_term = jnp.transpose(root_term.reshape(rcount, groups, n, root_cols), (2, 0, 1, 3))
    root_piece = a2a_reduce(root_term, "rows")
    root_solution = lax.dynamic_index_in_dim(root_piece, leaf_index, 1, keepdims=False)
    rxb = doubling_gather(root_piece.astype(BF16), "rows")
    rxb = jnp.transpose(rxb, (1, 2, 0, 3)).reshape(rcount, root_width)
    parent_anc = rxb[:, parent_rows[0]]
    parent_anc = jnp.where(parent_mask[None, :], parent_anc, jnp.zeros_like(parent_anc))
    parent_term = jnp.dot(parent_anc, panel_rows, preferred_element_type=F32)
    parent_tail = direct_reduce(
        jnp.moveaxis(parent_term.reshape(rcount, n, parent_cols), 1, 0), "rows"
    )
    pvb = (py - parent_tail).astype(BF16)
    parent_sol_term = jnp.dot(pvb, inverse_rows, preferred_element_type=F32)
    parent_sol = a2a_reduce(
        jnp.moveaxis(parent_sol_term.reshape(rcount, n, parent_cols), 1, 0), "rows"
    )
    parent_whole = jnp.moveaxis(direct_gather(parent_sol.astype(BF16), "rows"), 0, 1)
    ancestors = jnp.concatenate([parent_whole.reshape(rcount, -1), rxb], axis=1)
    leaf_anc = ancestors[:, leaf_flat].reshape(rcount, group_leaves, leaf_local)
    leaf_anc = jnp.where(leaf_mask[None, :, :], leaf_anc, jnp.zeros_like(leaf_anc))
    leaf_term = jnp.einsum("rlh,lhc->rlc", leaf_anc, leaf_panel, preferred_element_type=F32)
    leaf_term = jnp.moveaxis(leaf_term.reshape(rcount, group_leaves, n, -1), 2, 0)
    leaf_tail = a2a_reduce(leaf_term, "rows")
    lvb = (ly - leaf_tail).astype(BF16)
    leaf_sol_term = jnp.einsum("rli,lic->rlc", lvb, leaf_inv, preferred_element_type=F32)
    leaf_sol_term = jnp.moveaxis(leaf_sol_term.reshape(rcount, group_leaves, n, -1), 2, 0)
    leaf_sol = direct_reduce(leaf_sol_term, "rows")
    return (leaf_sol, parent_sol[:, None, :], root_solution)


def solution(mesh):
    return jax.shard_map(
        shards,
        mesh=mesh,
        in_specs=(
            P(None, "leaf", "rows"),
            P(None, "leaf", "rows"),
            P(None, ("leaf", "rows")),
            P("leaf", "rows", None),
            P("leaf", "rows", None),
            P("leaf", "rows"),
            P("leaf"),
            P("leaf", "rows", None),
            P("leaf", "rows", None),
            P("leaf", "rows"),
            P("leaf"),
            P("rows", None),
        ),
        out_specs=(P(None, "leaf", "rows"), P(None, "leaf", "rows"), P(None, ("leaf", "rows"))),
        check_vma=False,
    )
```

time: 561 us -> 261 us (0.47)
  waiting for transfers between devices: 334 us -> 50.4 us
  blocking collectives: 110 us -> 25.8 us
  starting transfers between devices: 0.29 us -> 68.6 us
  between operations: 14.9 us -> 2.06 us
  local copies, waits for them, and re-layouts: 25.9 us -> 36.8 us
    reduce_scatter x6 -> x0, waiting for transfers between devices: 281 us -> none  [the longest x1 133 us: shards(): lax.psum_scatter(root_from_leaves, ('leaf', 'rows'), scatter_dimension=1,...]
    all_gather x6 -> x0, blocking collectives: 110 us -> none  [the longest x1 36.6 us: shards(): lax.all_gather(rrb, ('leaf', 'rows'), axis=1, tiled=True)]
    ppermute x0 -> x54, starting transfers between devices: none -> 57 us  [the longest x48 54.2 us: shift(): return lax.ppermute(x, axis, [(i, (i + k) % n) for i in range(n)])]
    psum x1 -> x0, waiting for transfers between devices: 52.2 us -> none  [shards(): root_full = lax.psum(root_term, 'rows')]
    ppermute x0 -> x54, waiting for transfers between devices: none -> 34.8 us  [the longest x48 21.7 us: shift(): return lax.ppermute(x, axis, [(i, (i + k) % n) for i in range(n)])]
    all_to_all x0 -> x3, blocking collectives: none -> 25.8 us  [a2a_reduce(): return lax.all_to_all(x.astype(BF16), axis, 0, 0).astype(F32).sum(0)]
    all_to_all x0 -> x3, waiting for transfers between devices: none -> 15.6 us  [the longest x2 9.77 us: a2a_gather(): return lax.all_to_all(jnp.broadcast_to(x[None], (n,) + x.shape), axis, 0, 0)]
    dot_general x0 -> x2, local copies, waits for them, and re-layouts: none -> 13 us  [the longest x1 6.49 us: shards(): parent_term = jnp.dot(parent_anc, panel_rows, preferred_element_type=F32)]
  transfers between devices with their start and end apart: 7 -> 57, of which waited for: 7 -> 27; matrix products, arithmetic and copies ran while one was open for 0% -> 23% of each run, Pallas kernels for 0% -> 0%
where the time goes in v1:
time: 261 us; the launch traced here: 259 us
  starting transfers between devices  68.6 us (26%)
  waiting for transfers between devices  50.4 us (19%)
  matrix products  41.3 us (16%)
  local copies, waits for them, and re-layouts  36.8 us (14%)
  other arithmetic  33.8 us (13%)
  blocking collectives  25.8 us (10%)
    ppermute x48, starting transfers between devices, shift(): return lax.ppermute(x, axis, [(i, (i + k) % n) for i in range(n)])  54.2 us
    all_to_all x3, blocking collectives, a2a_reduce(): return lax.all_to_all(x.astype(BF16), axis, 0, 0).astype(F32).sum(0)  25.8 us
    scatter-add x1, other arithmetic, shards(): local_acc = jnp.zeros((rcount, parent_width + root_width), F32).at[:, lea...  24.6 us
    ppermute x48, waiting for transfers between devices, shift(): return lax.ppermute(x, axis, [(i, (i + k) % n) for i in range(n)])  21.7 us
    ppermute x6, waiting for transfers between devices, doubling_gather(): got = lax.ppermute(cur, axis, [(i, i ^ step) for i in range(n)])  13.2 us
    gather x1, local copies, waits for them, and re-layouts, shards(): leaf_anc = ancestors[:, leaf_flat].reshape(rcount, group_leaves, leaf_local)  12.9 us
    dot_general x1, matrix products, shards(): jnp.einsum('rln,lhn->rlh', lyb, leaf_panel, preferred_element_type=F32)  10.2 us
    all_to_all x2, waiting for transfers between devices, a2a_gather(): return lax.all_to_all(jnp.broadcast_to(x[None], (n,) + x.shape), axis, 0, 0)  9.77 us
  transfers between devices with their start and end apart: 57, of which 27 were waited for; matrix products, arithmetic and copies ran while one was open for 23% of the time, Pallas kernels for 0%

profile of v1, /device:TPU:0, one launch (start us, length us, event | category | flops | bytes accessed | tf_op | source)
XLA Modules:
  0.0 258.7 jit_solution(17893289442481984184)
XLA Ops:
  0.6 3.9 %collective-permute-start.10 = (f32[8,128]{1,0:T(8,128)}, f32[8,128]{1,0:T(8,128)S(1)}, u32[]{:S(2)}, u32[]{:S(2)}) collective-permute-start(f32[8,128]{1,0:T(8,128)} %param.14), channel_id=1, source_target_pairs={{0,24},{8,0},{16,8},{24,16},{1,25},{9,1},{17,9},{25,17},{2,26},{10... | collective-permute-start | bytes 12296 | tf_op jit(solution)/shard_map/ppermute | solution.py:21
  7.1 4.9 %all-to-all-start = ((bf16[8,8,4,256]{3,1,2,0:T(8,128)(2,1)}), bf16[8,8,4,256]{3,1,2,0:T(8,128)(2,1)S(1)}, u32[]{:S(2)}, u32[]{:S(2)}) async-start(bf16[8,8,4,256]{3,1,2,0:T(8,128)(2,1)} %broadcast_in_dim.47), calls=%async_computation | async-start | bytes 262144 | tf_op jit(solution)/shard_map/all_to_all | solution.py:12
  14.9 3.9 %all-to-all-done = bf16[8,8,4,256]{3,1,2,0:T(8,128)(2,1)S(1)} async-done(((bf16[8,8,4,256]{3,1,2,0:T(8,128)(2,1)}), bf16[8,8,4,256]{3,1,2,0:T(8,128)(2,1)S(1)}, u32[]{:S(2)}, u32[]{:S(2)}) %all-to-all-start) | async-done | bytes 131104 | tf_op jit(solution)/shard_map/all_to_all | solution.py:12
  18.8 3.4 %fusion.55 = (bf16[8,4,256]{2,0,1:T(8,128)(2,1)S(1)}, f32[8,4,256]{2,0,1:T(8,128)S(1)}) fusion(bf16[4,256,2048]{2,1,0:T(8,128)(2,1)} %param.15, bf16[8,4,2048]{2,0,1:T(8,128)(2,1)S(1)} %bitcast.274), kind=kOutput, calls=%fused_computation.192 | convolution fusion | flops 33562624 | bytes 4374528 | tf_op jit(solution)/shard_map/rln,lin->rli/dot_general | solution.py:91
  25.3 1.5 collective-permute-done.1
  27.8 1.8 collective-permute-start.4
  29.6 1.9 collective-permute-done.3
  31.5 1.5 collective-permute-start.5
  33.9 3.1 %collective-permute-done.5 = bf16[8,4,256]{2,0,1:T(8,128)(2,1)S(1)} collective-permute-done((bf16[8,4,256]{2,0,1:T(8,128)(2,1)S(1)}, bf16[8,4,256]{2,0,1:T(8,128)(2,1)S(1)}, u32[]{:S(2)}, u32[]{:S(2)}) %collective-permute-start.5) | collective-permute-done | bytes 16416 | tf_op jit(solution)/shard_map/ppermute | solution.py:21
  38.1 10.2 %convolution_select_fusion = f32[4,8,1024]{2,1,0:T(8,128)S(1)} fusion(bf16[8,4,2048]{2,0,1:T(8,128)(2,1)S(1)} %bitcast.272, bf16[4,1024,2048]{2,1,0:T(8,128)(2,1)} %param.16, pred[4,1024]{1,0:T(4,128)(4,1)S(1)} %broadcast_compare_fusion), kind=kOutput, calls=%fused_computation.15 | convolution fusion | flops 134250496 | bytes 17043456 | tf_op jit(solution)/shard_map/rln,lhn->rlh/dot_general | solution.py:94
  49.0 24.6 %scatter_custom_fusion = f32[8,8192]{0,1:T(8,128)} fusion(s32[4096]{0:T(1024)S(1)} %bitcast.282, f32[4096,8]{1,0:T(8,128)S(1)} %copy.142, f32[]{:T(128)} %constant.108.clone.1), kind=kCustom, calls=%fused_computation.13 | custom fusion | flops 32768 | bytes 262148 | tf_op jit(solution)/shard_map/scatter-add | solution.py:102
  73.5 1.7 slice.16
  76.2 3.3 %all-to-all-start.1 = ((bf16[8,8,512]{2,1,0:T(8,128)(2,1)}), bf16[8,8,512]{2,1,0:T(8,128)(2,1)S(1)}, u32[]{:S(2)}, u32[]{:S(2)}) async-start(bf16[8,8,512]{2,1,0:T(8,128)(2,1)} %bitcast.18), calls=%async_computation.1 | async-start | bytes 131072 | tf_op jit(solution)/shard_map/all_to_all | solution.py:16
  79.5 5.8 %all-to-all-done.1 = bf16[8,8,512]{2,1,0:T(8,128)(2,1)S(1)} async-done(((bf16[8,8,512]{2,1,0:T(8,128)(2,1)}), bf16[8,8,512]{2,1,0:T(8,128)(2,1)S(1)}, u32[]{:S(2)}, u32[]{:S(2)}) %all-to-all-start.1) | async-done | bytes 65568 | tf_op jit(solution)/shard_map/all_to_all | solution.py:16
  87.9 3.0 %collective-permute-done.8 = bf16[2,8,512]{2,1,0:T(8,128)(2,1)S(1)} collective-permute-done((bf16[2,8,512]{2,1,0:T(8,128)(2,1)S(1)}, bf16[2,8,512]{2,1,0:T(8,128)(2,1)S(1)}, u32[]{:S(2)}, u32[]{:S(2)}) %collective-permute-start.8) | collective-permute-done | bytes 16416 | tf_op jit(solution)/shard_map/ppermute | solution.py:56
  91.5 4.7 %collective-permute-done.9 = bf16[4,8,512]{2,1,0:T(8,128)(2,1)S(1)} collective-permute-done((bf16[4,8,512]{2,1,0:T(8,128)(2,1)S(1)}, bf16[4,8,512]{2,1,0:T(8,128)(2,1)S(1)}, u32[]{:S(2)}, u32[]{:S(2)}) %collective-permute-start.9) | collective-permute-done | bytes 32800 | tf_op jit(solution)/shard_map/ppermute | solution.py:56
  96.2 3.4 %fusion.56 = (bf16[8,512]{1,0:T(8,128)(2,1)S(1)}, f32[8,512]{1,0:T(8,128)S(1)}) fusion(bf16[8,4096]{1,0:T(8,128)(2,1)S(1)} %bitcast.278, bf16[1,512,4096]{2,1,0:T(8,128)(2,1)} %param.19), kind=kOutput, calls=%fused_computation.193 | convolution fusion | flops 33558528 | bytes 4284416 | tf_op jit(solution)/shard_map/dot_general | solution.py:112
  100.2 3.3 %all-to-all-start.2 = ((bf16[8,8,512]{2,1,0:T(8,128)(2,1)}), bf16[8,8,512]{2,1,0:T(8,128)(2,1)S(1)}, u32[]{:S(2)}, u32[]{:S(2)}) async-start(bf16[8,8,512]{2,1,0:T(8,128)(2,1)} %broadcast_in_dim.80), calls=%async_computation.2 | async-start | bytes 131072 | tf_op jit(solution)/shard_map/all_to_all | solution.py:12
  103.6 5.8 %all-to-all-done.2 = bf16[8,8,512]{2,1,0:T(8,128)(2,1)S(1)} async-done(((bf16[8,8,512]{2,1,0:T(8,128)(2,1)}), bf16[8,8,512]{2,1,0:T(8,128)(2,1)S(1)}, u32[]{:S(2)}, u32[]{:S(2)}) %all-to-all-start.2) | async-done | bytes 65568 | tf_op jit(solution)/shard_map/all_to_all | solution.py:12
  109.5 3.4 %fusion.10 = f32[512,8]{0,1:T(8,128)S(1)} fusion(bf16[8,4096]{1,0:T(8,128)(2,1)S(1)} %bitcast.277, bf16[1,512,4096]{2,1,0:T(8,128)(2,1)} %param.20, pred[512]{0:T(512)(128)(4,1)S(1)} %add_compare_fusion), kind=kOutput, calls=%fused_computation.21 | convolution fusion | flops 33558528 | bytes 4276736 | tf_op jit(solution)/shard_map/dot_general | solution.py:115
  113.0 4.2 %scatter_fusion = f32[8,4096]{0,1:T(8,128)S(1)} fusion(f32[8,4096]{0,1:T(8,128)S(1)} %slice-done, s32[512]{0:T(512)S(1)} %bitcast.285, f32[512,8]{1,0:T(8,128)S(1)} %copy.147), kind=kCustom, calls=%fused_computation.3 | custom fusion | flops 4096 | bytes 51200 | tf_op jit(solution)/shard_map/scatter-add | solution.py:119
  119.3 3.2 %collective-permute-start.16 = (bf16[8,4,128]{2,0,1:T(8,128)(2,1)S(1)}, bf16[8,4,128]{2,0,1:T(8,128)(2,1)S(1)}, u32[]{:S(2)}, u32[]{:S(2)}) collective-permute-start(bf16[8,4,128]{2,0,1:T(8,128)(2,1)S(1)} %bitcast.296), channel_id=1, source_target_pairs={{0,4},{1,5},{2,6},{3,7},{4,0},{5,1},{6,2},{7,3},{8,12},{9,13},{10,... | collective-permute-start | bytes 24584 | tf_op jit(solution)/shard_map/ppermute | solution.py:21
  122.8 2.2 collective-permute-start.18
  126.9 2.4 collective-permute-start.20
  133.5 1.9 collective-permute-start.23
  135.3 1.9 collective-permute-start.24
  137.2 2.7 %collective-permute-start.26 = (bf16[8,4,128]{2,0,1:T(8,128)(2,1)S(1)}, bf16[8,4,128]{2,0,1:T(8,128)(2,1)S(1)}, u32[]{:S(2)}, u32[]{:S(2)}) collective-permute-start(bf16[8,4,128]{2,0,1:T(8,128)(2,1)S(1)} %fusion.46), channel_id=1, source_target_pairs={{0,4},{1,5},{2,6},{3,7},{4,0},{5,1},{6,2},{7,3},{8,12},{9,13},{10,... | collective-permute-start | bytes 24584 | tf_op jit(solution)/shard_map/ppermute | solution.py:21
  141.8 2.1 collective-permute-done.27
  145.6 5.3 %convolution_convert_fusion = bf16[8,4096]{1,0:T(8,128)(2,1)S(1)} fusion(bf16[512,4096]{1,0:T(8,128)(2,1)} %param.23, bf16[1,8,32,128]{3,2,1,0:T(8,128)(2,1)S(1)} %bitcast.279), kind=kOutput, calls=%fused_computation.4 | convolution fusion | flops 67145728 | bytes 4325376 | tf_op jit(solution)/shard_map/dot_general | solution.py:126
  150.9 8.4 %all_to_all.30 = bf16[8,8,4,128]{3,1,2,0:T(8,128)(2,1)S(1)} all-to-all(bf16[8,8,4,128]{3,1,2,0:T(8,128)(2,1)S(1)} %bitcast.281), channel_id=1, replica_groups=mesh['leaf'=4,'rows'=8] {'rows'}, dimensions={0} | all-to-all | bytes 131072 | tf_op jit(solution)/shard_map/all_to_all | solution.py:16
  161.3 3.0 %collective-permute-done.31 = bf16[2,8,4,128]{3,1,2,0:T(8,128)(2,1)S(1)} collective-permute-done((bf16[2,8,4,128]{3,1,2,0:T(8,128)(2,1)S(1)}, bf16[2,8,4,128]{3,1,2,0:T(8,128)(2,1)S(1)}, u32[]{:S(2)}, u32[]{:S(2)}) %collective-permute-start.31) | collective-permute-done | bytes 16416 | tf_op jit(solution)/shard_map/ppermute | solution.py:56
  164.9 6.5 %copy.176 = bf16[4096,512]{1,0:T(8,128)(2,1)} copy(bf16[4096,512]{0,1:T(8,128)(2,1)} %bitcast.260) | data formatting | bytes 8388608 | tf_op jit(solution)/shard_map/dot_general | solution.py:134
  173.3 3.5 %convolution_convert_fusion.4 = bf16[8,8,512]{2,0,1:T(8,128)(2,1)S(1)} fusion(bf16[8,512,512]{2,1,0:T(8,128)(2,1)} %bitcast.263, bf16[512,8]{1,0:T(8,128)(2,1)S(1)} %gather_fusion, pred[512]{0:T(512)(128)(4,1)S(1)} %add_compare_fusion), kind=kOutput, calls=%fused_computation.17 | convolution fusion | flops 33591296 | bytes 4268544 | tf_op jit(solution)/shard_map/dot_general | solution.py:134
  177.9 2.2 collective-permute-start.35
  180.0 1.6 collective-permute-start.36
  182.5 2.2 collective-permute-start.38
  186.1 6.5 %copy.177 = bf16[4096,512]{1,0:T(8,128)(2,1)} copy(bf16[4096,512]{0,1:T(8,128)(2,1)} %bitcast.261) | data formatting | bytes 8388608 | tf_op jit(solution)/shard_map/dot_general | solution.py:139
  192.6 3.4 %fusion.6 = bf16[8,8,512]{2,1,0:T(8,128)(2,1)S(1)} fusion(bf16[8,512,512]{2,1,0:T(8,128)(2,1)} %bitcast.262, f32[8,512]{1,0:T(8,128)S(1)} %get-tuple-element.41, bf16[8,512]{1,0:T(8,128)(2,1)S(1)} %collective-permute-done.39, bf16[8,512]{1,0:T(8,128)(2,1)S(1)} %collective-permute-done.38, bf16[8,512]{1,0:T(8,128)(2,1)S(1)} %collective-permute-done.37, ...), kind=kOutput, calls=%fused_computation.18 | convolution fusion | flops 33656832 | bytes 4341764 | tf_op jit(solution)/shard_map/dot_general | solution.py:139
  196.0 8.3 %all_to_all.31 = bf16[8,8,512]{2,1,0:T(8,128)(2,1)S(1)} all-to-all(bf16[8,8,512]{2,1,0:T(8,128)(2,1)S(1)} %fusion.6), channel_id=1, replica_groups=mesh['leaf'=4,'rows'=8] {'rows'}, dimensions={0} | all-to-all | bytes 131072 | tf_op jit(solution)/shard_map/all_to_all | solution.py:16
  206.4 1.6 collective-permute-start.43
  208.6 1.7 collective-permute-start.45
  212.0 2.0 collective-permute-done.45
  215.8 1.8 pad_maximum_fusion
  217.5 12.9 %gather_fusion.1 = bf16[4096,8]{1,0:T(8,128)(2,1)S(1)} fusion(bf16[8,8192]{0,1:T(8,128)(2,1)} %pad_maximum_fusion, s32[4096]{0:T(1024)S(1)} %broadcast_clamp_fusion), kind=kCustom, calls=%fused_computation.1 | custom fusion | bytes 147456 | tf_op jit(solution)/shard_map/gather | solution.py:145
  230.7 8.2 %convolution_convert_fusion.2 = bf16[4,8,2048]{2,1,0:T(8,128)(2,1)S(1)} fusion(bf16[4,1024,2048]{2,1,0:T(8,128)(2,1)} %param.16, bf16[8,4,1024]{2,0,1:T(8,128)(2,1)S(1)} %copy.164, pred[4,1024]{1,0:T(4,128)(4,1)S(1)} %broadcast_compare_fusion), kind=kOutput, calls=%fused_computation.10 | convolution fusion | flops 134316032 | bytes 16977920 | tf_op jit(solution)/shard_map/rlh,lhc->rlc/dot_general | solution.py:147
  238.9 9.2 %all_to_all.32 = bf16[8,8,4,256]{3,1,2,0:T(8,128)(2,1)S(1)} all-to-all(bf16[8,8,4,256]{3,1,2,0:T(8,128)(2,1)S(1)} %bitcast.276), channel_id=1, replica_groups=mesh['leaf'=4,'rows'=8] {'rows'}, dimensions={0} | all-to-all | bytes 262144 | tf_op jit(solution)/shard_map/all_to_all | solution.py:16
  251.0 2.8 %collective-permute-start.50 = (bf16[8,4,256]{2,1,0:T(4,128)(2,1)S(1)}, bf16[8,4,256]{2,1,0:T(4,128)(2,1)S(1)}, u32[]{:S(2)}, u32[]{:S(2)}) collective-permute-start(bf16[8,4,256]{2,1,0:T(4,128)(2,1)S(1)} %bitcast.291), channel_id=1, source_target_pairs={{0,4},{1,5},{2,6},{3,7},{4,0},{5,1},{6,2},{7,3},{8,12},{9,13},{10,... | collective-permute-start | bytes 49160 | tf_op jit(solution)/shard_map/ppermute | solution.py:21
  253.9 2.1 collective-permute-start.52
  (223 shorter events, 47.8 us)
Async XLA Ops:
  0.6 78.9 %collective-permute-start.10 = (f32[8,128]{1,0:T(8,128)}, f32[8,128]{1,0:T(8,128)S(1)}, u32[]{:S(2)}, u32[]{:S(2)}) collective-permute-start(f32[8,128]{1,0:T(8,128)} %param.14), channel_id=1, source_target_pairs={{0,24},{8,0},{16,8},{24,16},{1,25},{9,1},{17,9},{25,17},{2,26},{10... | collective-permute-start | bytes 12296 | tf_op jit(solution)/shard_map/ppermute | solution.py:21
  4.6 81.0 %collective-permute-start.11 = (f32[8,128]{1,0:T(8,128)}, f32[8,128]{1,0:T(8,128)S(1)}, u32[]{:S(2)}, u32[]{:S(2)}) collective-permute-start(f32[8,128]{1,0:T(8,128)} %param.14), channel_id=1, source_target_pairs={{0,16},{8,24},{16,0},{24,8},{1,17},{9,25},{17,1},{25,9},{2,18},{10... | collective-permute-start | bytes 12296 | tf_op jit(solution)/shard_map/ppermute | solution.py:21
  5.1 82.9 %collective-permute-start.12 = (f32[8,128]{1,0:T(8,128)}, f32[8,128]{1,0:T(8,128)S(1)}, u32[]{:S(2)}, u32[]{:S(2)}) collective-permute-start(f32[8,128]{1,0:T(8,128)} %param.14), channel_id=1, source_target_pairs={{0,8},{8,16},{16,24},{24,0},{1,9},{9,17},{17,25},{25,1},{2,10},{10... | collective-permute-start | bytes 12296 | tf_op jit(solution)/shard_map/ppermute | solution.py:21
  7.1 11.7 %all-to-all-start = ((bf16[8,8,4,256]{3,1,2,0:T(8,128)(2,1)}), bf16[8,8,4,256]{3,1,2,0:T(8,128)(2,1)S(1)}, u32[]{:S(2)}, u32[]{:S(2)}) async-start(bf16[8,8,4,256]{3,1,2,0:T(8,128)(2,1)} %broadcast_in_dim.47), calls=%async_computation | async-start | bytes 262144 | tf_op jit(solution)/shard_map/all_to_all | solution.py:12
  23.1 3.8 %collective-permute-start.1 = (bf16[8,4,256]{2,0,1:T(8,128)(2,1)S(1)}, bf16[8,4,256]{2,0,1:T(8,128)(2,1)S(1)}, u32[]{:S(2)}, u32[]{:S(2)}) collective-permute-start(bf16[8,4,256]{2,0,1:T(8,128)(2,1)S(1)} %get-tuple-element.38), channel_id=1, source_target_pairs={{0,6},{1,7},{2,0},{3,1},{4,2},{5,3},{6,4},{7,5},{8,14},{9,15},{10,... | collective-permute-start | bytes 49160 | tf_op jit(solution)/shard_map/ppermute | solution.py:21
  26.9 4.6 %collective-permute-start.3 = (bf16[8,4,256]{2,0,1:T(8,128)(2,1)S(1)}, bf16[8,4,256]{2,0,1:T(8,128)(2,1)S(1)}, u32[]{:S(2)}, u32[]{:S(2)}) collective-permute-start(bf16[8,4,256]{2,0,1:T(8,128)(2,1)S(1)} %get-tuple-element.38), channel_id=1, source_target_pairs={{0,4},{1,5},{2,6},{3,7},{4,0},{5,1},{6,2},{7,3},{8,12},{9,13},{10,... | collective-permute-start | bytes 49160 | tf_op jit(solution)/shard_map/ppermute | solution.py:21
  27.8 5.2 %collective-permute-start.4 = (bf16[8,4,256]{2,0,1:T(8,128)(2,1)S(1)}, bf16[8,4,256]{2,0,1:T(8,128)(2,1)S(1)}, u32[]{:S(2)}, u32[]{:S(2)}) collective-permute-start(bf16[8,4,256]{2,0,1:T(8,128)(2,1)S(1)} %get-tuple-element.38), channel_id=1, source_target_pairs={{0,3},{1,4},{2,5},{3,6},{4,7},{5,0},{6,1},{7,2},{8,11},{9,12},{10,... | collective-permute-start | bytes 49160 | tf_op jit(solution)/shard_map/ppermute | solution.py:21
  31.5 5.5 %collective-permute-start.5 = (bf16[8,4,256]{2,0,1:T(8,128)(2,1)S(1)}, bf16[8,4,256]{2,0,1:T(8,128)(2,1)S(1)}, u32[]{:S(2)}, u32[]{:S(2)}) collective-permute-start(bf16[8,4,256]{2,0,1:T(8,128)(2,1)S(1)} %get-tuple-element.38), channel_id=1, source_target_pairs={{0,2},{1,3},{2,4},{3,5},{4,6},{5,7},{6,0},{7,1},{8,10},{9,11},{10,... | collective-permute-start | bytes 49160 | tf_op jit(solution)/shard_map/ppermute | solution.py:21
  33.0 5.0 %collective-permute-start.6 = (bf16[8,4,256]{2,0,1:T(8,128)(2,1)S(1)}, bf16[8,4,256]{2,0,1:T(8,128)(2,1)S(1)}, u32[]{:S(2)}, u32[]{:S(2)}) collective-permute-start(bf16[8,4,256]{2,0,1:T(8,128)(2,1)S(1)} %get-tuple-element.38), channel_id=1, source_target_pairs={{0,1},{1,2},{2,3},{3,4},{4,5},{5,6},{6,7},{7,0},{8,9},{9,10},{10,1... | collective-permute-start | bytes 49160 | tf_op jit(solution)/shard_map/ppermute | solution.py:21
  76.2 9.2 %all-to-all-start.1 = ((bf16[8,8,512]{2,1,0:T(8,128)(2,1)}), bf16[8,8,512]{2,1,0:T(8,128)(2,1)S(1)}, u32[]{:S(2)}, u32[]{:S(2)}) async-start(bf16[8,8,512]{2,1,0:T(8,128)(2,1)} %bitcast.18), calls=%async_computation.1 | async-start | bytes 131072 | tf_op jit(solution)/shard_map/all_to_all | solution.py:16
  87.2 3.8 %collective-permute-start.8 = (bf16[2,8,512]{2,1,0:T(8,128)(2,1)S(1)}, bf16[2,8,512]{2,1,0:T(8,128)(2,1)S(1)}, u32[]{:S(2)}, u32[]{:S(2)}) collective-permute-start(bf16[2,8,512]{2,1,0:T(8,128)(2,1)S(1)} %pad_maximum_fusion.4), channel_id=1, source_target_pairs={{0,2},{1,3},{2,0},{3,1},{4,6},{5,7},{6,4},{7,5},{8,10},{9,11},{10,... | collective-permute-start | bytes 49160 | tf_op jit(solution)/shard_map/ppermute | solution.py:56
  91.0 5.2 %collective-permute-start.9 = (bf16[4,8,512]{2,1,0:T(8,128)(2,1)S(1)}, bf16[4,8,512]{2,1,0:T(8,128)(2,1)S(1)}, u32[]{:S(2)}, u32[]{:S(2)}) collective-permute-start(bf16[4,8,512]{2,1,0:T(8,128)(2,1)S(1)} %pad_maximum_fusion.2), channel_id=1, source_target_pairs={{0,4},{1,5},{2,6},{3,7},{4,0},{5,1},{6,2},{7,3},{8,12},{9,13},{10,... | collective-permute-start | bytes 98312 | tf_op jit(solution)/shard_map/ppermute | solution.py:56
  100.2 9.2 %all-to-all-start.2 = ((bf16[8,8,512]{2,1,0:T(8,128)(2,1)}), bf16[8,8,512]{2,1,0:T(8,128)(2,1)S(1)}, u32[]{:S(2)}, u32[]{:S(2)}) async-start(bf16[8,8,512]{2,1,0:T(8,128)(2,1)} %broadcast_in_dim.80), calls=%async_computation.2 | async-start | bytes 131072 | tf_op jit(solution)/shard_map/all_to_all | solution.py:12
  117.5 5.2 %collective-permute-start.13 = (bf16[8,4,128]{2,0,1:T(8,128)(2,1)S(1)}, bf16[8,4,128]{2,0,1:T(8,128)(2,1)S(1)}, u32[]{:S(2)}, u32[]{:S(2)}) collective-permute-start(bf16[8,4,128]{2,0,1:T(8,128)(2,1)S(1)} %bitcast.301), channel_id=1, source_target_pairs={{0,1},{1,2},{2,3},{3,4},{4,5},{5,6},{6,7},{7,0},{8,9},{9,10},{10,1... | collective-permute-start | bytes 24584 | tf_op jit(solution)/shard_map/ppermute | solution.py:21
  117.7 7.3 %collective-permute-start.14 = (bf16[8,4,128]{2,0,1:T(8,128)(2,1)S(1)}, bf16[8,4,128]{2,0,1:T(8,128)(2,1)S(1)}, u32[]{:S(2)}, u32[]{:S(2)}) collective-permute-start(bf16[8,4,128]{2,0,1:T(8,128)(2,1)S(1)} %bitcast.299), channel_id=1, source_target_pairs={{0,2},{1,3},{2,4},{3,5},{4,6},{5,7},{6,0},{7,1},{8,10},{9,11},{10,... | collective-permute-start | bytes 24584 | tf_op jit(solution)/shard_map/ppermute | solution.py:21
  118.5 7.1 %collective-permute-start.15 = (bf16[8,4,128]{2,0,1:T(8,128)(2,1)S(1)}, bf16[8,4,128]{2,0,1:T(8,128)(2,1)S(1)}, u32[]{:S(2)}, u32[]{:S(2)}) collective-permute-start(bf16[8,4,128]{2,0,1:T(8,128)(2,1)S(1)} %bitcast.295), channel_id=1, source_target_pairs={{0,3},{1,4},{2,5},{3,6},{4,7},{5,0},{6,1},{7,2},{8,11},{9,12},{10,... | collective-permute-start | bytes 24584 | tf_op jit(solution)/shard_map/ppermute | solution.py:21
  119.3 6.3 %collective-permute-start.16 = (bf16[8,4,128]{2,0,1:T(8,128)(2,1)S(1)}, bf16[8,4,128]{2,0,1:T(8,128)(2,1)S(1)}, u32[]{:S(2)}, u32[]{:S(2)}) collective-permute-start(bf16[8,4,128]{2,0,1:T(8,128)(2,1)S(1)} %bitcast.296), channel_id=1, source_target_pairs={{0,4},{1,5},{2,6},{3,7},{4,0},{5,1},{6,2},{7,3},{8,12},{9,13},{10,... | collective-permute-start | bytes 24584 | tf_op jit(solution)/shard_map/ppermute | solution.py:21
  122.8 3.9 %collective-permute-start.18 = (bf16[8,4,128]{2,0,1:T(8,128)(2,1)S(1)}, bf16[8,4,128]{2,0,1:T(8,128)(2,1)S(1)}, u32[]{:S(2)}, u32[]{:S(2)}) collective-permute-start(bf16[8,4,128]{2,0,1:T(8,128)(2,1)S(1)} %bitcast.300), channel_id=1, source_target_pairs={{0,6},{1,7},{2,0},{3,1},{4,2},{5,3},{6,4},{7,5},{8,14},{9,15},{10,... | collective-permute-start | bytes 24584 | tf_op jit(solution)/shard_map/ppermute | solution.py:21
  126.9 4.6 %collective-permute-start.20 = (bf16[8,4,128]{2,0,1:T(8,128)(2,1)S(1)}, bf16[8,4,128]{2,0,1:T(8,128)(2,1)S(1)}, u32[]{:S(2)}, u32[]{:S(2)}) collective-permute-start(bf16[8,4,128]{2,0,1:T(8,128)(2,1)S(1)} %fusion.45), channel_id=1, source_target_pairs={{0,8},{8,16},{16,24},{24,0},{1,9},{9,17},{17,25},{25,1},{2,10},{10... | collective-permute-start | bytes 24584 | tf_op jit(solution)/shard_map/ppermute | solution.py:21
  129.3 3.7 %collective-permute-start.21 = (bf16[8,4,128]{2,0,1:T(8,128)(2,1)S(1)}, bf16[8,4,128]{2,0,1:T(8,128)(2,1)S(1)}, u32[]{:S(2)}, u32[]{:S(2)}) collective-permute-start(bf16[8,4,128]{2,0,1:T(8,128)(2,1)S(1)} %fusion.45), channel_id=1, source_target_pairs={{0,16},{8,24},{16,0},{24,8},{1,17},{9,25},{17,1},{25,9},{2,18},{10... | collective-permute-start | bytes 24584 | tf_op jit(solution)/shard_map/ppermute | solution.py:21
  133.5 6.4 %collective-permute-start.23 = (bf16[8,4,128]{2,0,1:T(8,128)(2,1)S(1)}, bf16[8,4,128]{2,0,1:T(8,128)(2,1)S(1)}, u32[]{:S(2)}, u32[]{:S(2)}) collective-permute-start(bf16[8,4,128]{2,0,1:T(8,128)(2,1)S(1)} %fusion.46), channel_id=1, source_target_pairs={{0,7},{1,0},{2,1},{3,2},{4,3},{5,4},{6,5},{7,6},{8,15},{9,8},{10,9... | collective-permute-start | bytes 24584 | tf_op jit(solution)/shard_map/ppermute | solution.py:21
  135.3 5.2 %collective-permute-start.24 = (bf16[8,4,128]{2,0,1:T(8,128)(2,1)S(1)}, bf16[8,4,128]{2,0,1:T(8,128)(2,1)S(1)}, u32[]{:S(2)}, u32[]{:S(2)}) collective-permute-start(bf16[8,4,128]{2,0,1:T(8,128)(2,1)S(1)} %fusion.46), channel_id=1, source_target_pairs={{0,6},{1,7},{2,0},{3,1},{4,2},{5,3},{6,4},{7,5},{8,14},{9,15},{10,... | collective-permute-start | bytes 24584 | tf_op jit(solution)/shard_map/ppermute | solution.py:21
  137.2 4.6 %collective-permute-start.26 = (bf16[8,4,128]{2,0,1:T(8,128)(2,1)S(1)}, bf16[8,4,128]{2,0,1:T(8,128)(2,1)S(1)}, u32[]{:S(2)}, u32[]{:S(2)}) collective-permute-start(bf16[8,4,128]{2,0,1:T(8,128)(2,1)S(1)} %fusion.46), channel_id=1, source_target_pairs={{0,4},{1,5},{2,6},{3,7},{4,0},{5,1},{6,2},{7,3},{8,12},{9,13},{10,... | collective-permute-start | bytes 24584 | tf_op jit(solution)/shard_map/ppermute | solution.py:21
  139.9 4.0 %collective-permute-start.27 = (bf16[8,4,128]{2,0,1:T(8,128)(2,1)S(1)}, bf16[8,4,128]{2,0,1:T(8,128)(2,1)S(1)}, u32[]{:S(2)}, u32[]{:S(2)}) collective-permute-start(bf16[8,4,128]{2,0,1:T(8,128)(2,1)S(1)} %fusion.46), channel_id=1, source_target_pairs={{0,3},{1,4},{2,5},{3,6},{4,7},{5,0},{6,1},{7,2},{8,11},{9,12},{10,... | collective-permute-start | bytes 24584 | tf_op jit(solution)/shard_map/ppermute | solution.py:21
  139.9 5.5 %collective-permute-start.28 = (bf16[8,4,128]{2,0,1:T(8,128)(2,1)S(1)}, bf16[8,4,128]{2,0,1:T(8,128)(2,1)S(1)}, u32[]{:S(2)}, u32[]{:S(2)}) collective-permute-start(bf16[8,4,128]{2,0,1:T(8,128)(2,1)S(1)} %fusion.46), channel_id=1, source_target_pairs={{0,2},{1,3},{2,4},{3,5},{4,6},{5,7},{6,0},{7,1},{8,10},{9,11},{10,... | collective-permute-start | bytes 24584 | tf_op jit(solution)/shard_map/ppermute | solution.py:21
  140.5 4.9 %collective-permute-start.29 = (bf16[8,4,128]{2,0,1:T(8,128)(2,1)S(1)}, bf16[8,4,128]{2,0,1:T(8,128)(2,1)S(1)}, u32[]{:S(2)}, u32[]{:S(2)}) collective-permute-start(bf16[8,4,128]{2,0,1:T(8,128)(2,1)S(1)} %fusion.46), channel_id=1, source_target_pairs={{0,1},{1,2},{2,3},{3,4},{4,5},{5,6},{6,7},{7,0},{8,9},{9,10},{10,1... | collective-permute-start | bytes 24584 | tf_op jit(solution)/shard_map/ppermute | solution.py:21
  160.5 3.8 %collective-permute-start.31 = (bf16[2,8,4,128]{3,1,2,0:T(8,128)(2,1)S(1)}, bf16[2,8,4,128]{3,1,2,0:T(8,128)(2,1)S(1)}, u32[]{:S(2)}, u32[]{:S(2)}) collective-permute-start(bf16[2,8,4,128]{3,1,2,0:T(8,128)(2,1)S(1)} %pad_maximum_fusion.5), channel_id=1, source_target_pairs={{0,2},{1,3},{2,0},{3,1},{4,6},{5,7},{6,4},{7,5},{8,10},{9,11},{10,... | collective-permute-start | bytes 49160 | tf_op jit(solution)/shard_map/ppermute | solution.py:56
  164.4 7.0 %collective-permute-start.32 = (bf16[4,8,4,128]{3,1,2,0:T(8,128)(2,1)S(1)}, bf16[4,8,4,128]{3,1,2,0:T(8,128)(2,1)S(1)}, u32[]{:S(2)}, u32[]{:S(2)}) collective-permute-start(bf16[4,8,4,128]{3,1,2,0:T(8,128)(2,1)S(1)} %pad_maximum_fusion.3), channel_id=1, source_target_pairs={{0,4},{1,5},{2,6},{3,7},{4,0},{5,1},{6,2},{7,3},{8,12},{9,13},{10,... | collective-permute-start | bytes 98312 | tf_op jit(solution)/shard_map/ppermute | solution.py:56
  176.8 5.7 %collective-permute-start.33 = (bf16[8,512]{1,0:T(8,128)(2,1)S(1)}, bf16[8,512]{1,0:T(8,128)(2,1)S(1)}, u32[]{:S(2)}, u32[]{:S(2)}) collective-permute-start(bf16[8,512]{1,0:T(8,128)(2,1)S(1)} %get-tuple-element.21), channel_id=1, source_target_pairs={{0,1},{1,2},{2,3},{3,4},{4,5},{5,6},{6,7},{7,0},{8,9},{9,10},{10,1... | collective-permute-start | bytes 24584 | tf_op jit(solution)/shard_map/ppermute | solution.py:21
  176.9 7.8 %collective-permute-start.34 = (bf16[8,512]{1,0:T(8,128)(2,1)S(1)}, bf16[8,512]{1,0:T(8,128)(2,1)S(1)}, u32[]{:S(2)}, u32[]{:S(2)}) collective-permute-start(bf16[8,512]{1,0:T(8,128)(2,1)S(1)} %get-tuple-element.27), channel_id=1, source_target_pairs={{0,2},{1,3},{2,4},{3,5},{4,6},{5,7},{6,0},{7,1},{8,10},{9,11},{10,... | collective-permute-start | bytes 24584 | tf_op jit(solution)/shard_map/ppermute | solution.py:21
  177.9 14.7 %collective-permute-start.35 = (bf16[8,512]{1,0:T(8,128)(2,1)S(1)}, bf16[8,512]{1,0:T(8,128)(2,1)S(1)}, u32[]{:S(2)}, u32[]{:S(2)}) collective-permute-start(bf16[8,512]{1,0:T(8,128)(2,1)S(1)} %get-tuple-element.26), channel_id=1, source_target_pairs={{0,3},{1,4},{2,5},{3,6},{4,7},{5,0},{6,1},{7,2},{8,11},{9,12},{10,... | collective-permute-start | bytes 24584 | tf_op jit(solution)/shard_map/ppermute | solution.py:21
  180.0 12.5 %collective-permute-start.36 = (bf16[8,512]{1,0:T(8,128)(2,1)S(1)}, bf16[8,512]{1,0:T(8,128)(2,1)S(1)}, u32[]{:S(2)}, u32[]{:S(2)}) collective-permute-start(bf16[8,512]{1,0:T(8,128)(2,1)S(1)} %get-tuple-element.25), channel_id=1, source_target_pairs={{0,4},{1,5},{2,6},{3,7},{4,0},{5,1},{6,2},{7,3},{8,12},{9,13},{10,... | collective-permute-start | bytes 24584 | tf_op jit(solution)/shard_map/ppermute | solution.py:21
  181.6 10.9 %collective-permute-start.37 = (bf16[8,512]{1,0:T(8,128)(2,1)S(1)}, bf16[8,512]{1,0:T(8,128)(2,1)S(1)}, u32[]{:S(2)}, u32[]{:S(2)}) collective-permute-start(bf16[8,512]{1,0:T(8,128)(2,1)S(1)} %get-tuple-element.24), channel_id=1, source_target_pairs={{0,5},{1,6},{2,7},{3,0},{4,1},{5,2},{6,3},{7,4},{8,13},{9,14},{10,... | collective-permute-start | bytes 24584 | tf_op jit(solution)/shard_map/ppermute | solution.py:21
  182.5 10.1 %collective-permute-start.38 = (bf16[8,512]{1,0:T(8,128)(2,1)S(1)}, bf16[8,512]{1,0:T(8,128)(2,1)S(1)}, u32[]{:S(2)}, u32[]{:S(2)}) collective-permute-start(bf16[8,512]{1,0:T(8,128)(2,1)S(1)} %get-tuple-element.23), channel_id=1, source_target_pairs={{0,6},{1,7},{2,0},{3,1},{4,2},{5,3},{6,4},{7,5},{8,14},{9,15},{10,... | collective-permute-start | bytes 24584 | tf_op jit(solution)/shard_map/ppermute | solution.py:21
  184.7 7.9 %collective-permute-start.39 = (bf16[8,512]{1,0:T(8,128)(2,1)S(1)}, bf16[8,512]{1,0:T(8,128)(2,1)S(1)}, u32[]{:S(2)}, u32[]{:S(2)}) collective-permute-start(bf16[8,512]{1,0:T(8,128)(2,1)S(1)} %get-tuple-element.22), channel_id=1, source_target_pairs={{0,7},{1,0},{2,1},{3,2},{4,3},{5,4},{6,5},{7,6},{8,15},{9,8},{10,9... | collective-permute-start | bytes 24584 | tf_op jit(solution)/shard_map/ppermute | solution.py:21
  204.3 4.3 %collective-permute-start.40 = (bf16[8,512]{1,0:T(8,128)(2,1)S(1)}, bf16[8,512]{1,0:T(8,128)(2,1)S(1)}, u32[]{:S(2)}, u32[]{:S(2)}) collective-permute-start(bf16[8,512]{1,0:T(8,128)(2,1)S(1)} %convert_element_type.268), channel_id=1, source_target_pairs={{0,7},{1,0},{2,1},{3,2},{4,3},{5,4},{6,5},{7,6},{8,15},{9,8},{10,9... | collective-permute-start | bytes 24584 | tf_op jit(solution)/shard_map/ppermute | solution.py:21
  204.6 5.7 %collective-permute-start.41 = (bf16[8,512]{1,0:T(8,128)(2,1)S(1)}, bf16[8,512]{1,0:T(8,128)(2,1)S(1)}, u32[]{:S(2)}, u32[]{:S(2)}) collective-permute-start(bf16[8,512]{1,0:T(8,128)(2,1)S(1)} %convert_element_type.268), channel_id=1, source_target_pairs={{0,6},{1,7},{2,0},{3,1},{4,2},{5,3},{6,4},{7,5},{8,14},{9,15},{10,... | collective-permute-start | bytes 24584 | tf_op jit(solution)/shard_map/ppermute | solution.py:21
  205.6 4.8 %collective-permute-start.42 = (bf16[8,512]{1,0:T(8,128)(2,1)S(1)}, bf16[8,512]{1,0:T(8,128)(2,1)S(1)}, u32[]{:S(2)}, u32[]{:S(2)}) collective-permute-start(bf16[8,512]{1,0:T(8,128)(2,1)S(1)} %convert_element_type.268), channel_id=1, source_target_pairs={{0,5},{1,6},{2,7},{3,0},{4,1},{5,2},{6,3},{7,4},{8,13},{9,14},{10,... | collective-permute-start | bytes 24584 | tf_op jit(solution)/shard_map/ppermute | solution.py:21
  206.4 4.5 %collective-permute-start.43 = (bf16[8,512]{1,0:T(8,128)(2,1)S(1)}, bf16[8,512]{1,0:T(8,128)(2,1)S(1)}, u32[]{:S(2)}, u32[]{:S(2)}) collective-permute-start(bf16[8,512]{1,0:T(8,128)(2,1)S(1)} %convert_element_type.268), channel_id=1, source_target_pairs={{0,4},{1,5},{2,6},{3,7},{4,0},{5,1},{6,2},{7,3},{8,12},{9,13},{10,... | collective-permute-start | bytes 24584 | tf_op jit(solution)/shard_map/ppermute | solution.py:21
  208.0 4.0 %collective-permute-start.44 = (bf16[8,512]{1,0:T(8,128)(2,1)S(1)}, bf16[8,512]{1,0:T(8,128)(2,1)S(1)}, u32[]{:S(2)}, u32[]{:S(2)}) collective-permute-start(bf16[8,512]{1,0:T(8,128)(2,1)S(1)} %convert_element_type.268), channel_id=1, source_target_pairs={{0,3},{1,4},{2,5},{3,6},{4,7},{5,0},{6,1},{7,2},{8,11},{9,12},{10,... | collective-permute-start | bytes 24584 | tf_op jit(solution)/shard_map/ppermute | solution.py:21
  208.6 5.4 %collective-permute-start.45 = (bf16[8,512]{1,0:T(8,128)(2,1)S(1)}, bf16[8,512]{1,0:T(8,128)(2,1)S(1)}, u32[]{:S(2)}, u32[]{:S(2)}) collective-permute-start(bf16[8,512]{1,0:T(8,128)(2,1)S(1)} %convert_element_type.268), channel_id=1, source_target_pairs={{0,2},{1,3},{2,4},{3,5},{4,6},{5,7},{6,0},{7,1},{8,10},{9,11},{10,... | collective-permute-start | bytes 24584 | tf_op jit(solution)/shard_map/ppermute | solution.py:21
  210.3 4.9 %collective-permute-start.46 = (bf16[8,512]{1,0:T(8,128)(2,1)S(1)}, bf16[8,512]{1,0:T(8,128)(2,1)S(1)}, u32[]{:S(2)}, u32[]{:S(2)}) collective-permute-start(bf16[8,512]{1,0:T(8,128)(2,1)S(1)} %convert_element_type.268), channel_id=1, source_target_pairs={{0,1},{1,2},{2,3},{3,4},{4,5},{5,6},{6,7},{7,0},{8,9},{9,10},{10,1... | collective-permute-start | bytes 24584 | tf_op jit(solution)/shard_map/ppermute | solution.py:21
  248.8 5.1 %collective-permute-start.47 = (bf16[8,4,256]{2,1,0:T(4,128)(2,1)S(1)}, bf16[8,4,256]{2,1,0:T(4,128)(2,1)S(1)}, u32[]{:S(2)}, u32[]{:S(2)}) collective-permute-start(bf16[8,4,256]{2,1,0:T(4,128)(2,1)S(1)} %bitcast.290), channel_id=1, source_target_pairs={{0,1},{1,2},{2,3},{3,4},{4,5},{5,6},{6,7},{7,0},{8,9},{9,10},{10,1... | collective-permute-start | bytes 49160 | tf_op jit(solution)/shard_map/ppermute | solution.py:21
  248.9 7.1 %collective-permute-start.48 = (bf16[8,4,256]{2,1,0:T(4,128)(2,1)S(1)}, bf16[8,4,256]{2,1,0:T(4,128)(2,1)S(1)}, u32[]{:S(2)}, u32[]{:S(2)}) collective-permute-start(bf16[8,4,256]{2,1,0:T(4,128)(2,1)S(1)} %bitcast.288), channel_id=1, source_target_pairs={{0,2},{1,3},{2,4},{3,5},{4,6},{5,7},{6,0},{7,1},{8,10},{9,11},{10,... | collective-permute-start | bytes 49160 | tf_op jit(solution)/shard_map/ppermute | solution.py:21
  249.9 7.9 %collective-permute-start.49 = (bf16[8,4,256]{2,1,0:T(4,128)(2,1)S(1)}, bf16[8,4,256]{2,1,0:T(4,128)(2,1)S(1)}, u32[]{:S(2)}, u32[]{:S(2)}) collective-permute-start(bf16[8,4,256]{2,1,0:T(4,128)(2,1)S(1)} %bitcast.289), channel_id=1, source_target_pairs={{0,3},{1,4},{2,5},{3,6},{4,7},{5,0},{6,1},{7,2},{8,11},{9,12},{10,... | collective-permute-start | bytes 49160 | tf_op jit(solution)/shard_map/ppermute | solution.py:21
  251.0 6.9 %collective-permute-start.50 = (bf16[8,4,256]{2,1,0:T(4,128)(2,1)S(1)}, bf16[8,4,256]{2,1,0:T(4,128)(2,1)S(1)}, u32[]{:S(2)}, u32[]{:S(2)}) collective-permute-start(bf16[8,4,256]{2,1,0:T(4,128)(2,1)S(1)} %bitcast.291), channel_id=1, source_target_pairs={{0,4},{1,5},{2,6},{3,7},{4,0},{5,1},{6,2},{7,3},{8,12},{9,13},{10,... | collective-permute-start | bytes 49160 | tf_op jit(solution)/shard_map/ppermute | solution.py:21
  253.8 4.0 %collective-permute-start.51 = (bf16[8,4,256]{2,1,0:T(4,128)(2,1)S(1)}, bf16[8,4,256]{2,1,0:T(4,128)(2,1)S(1)}, u32[]{:S(2)}, u32[]{:S(2)}) collective-permute-start(bf16[8,4,256]{2,1,0:T(4,128)(2,1)S(1)} %bitcast.292), channel_id=1, source_target_pairs={{0,5},{1,6},{2,7},{3,0},{4,1},{5,2},{6,3},{7,4},{8,13},{9,14},{10,... | collective-permute-start | bytes 49160 | tf_op jit(solution)/shard_map/ppermute | solution.py:21
  253.9 3.9 %collective-permute-start.52 = (bf16[8,4,256]{2,1,0:T(4,128)(2,1)S(1)}, bf16[8,4,256]{2,1,0:T(4,128)(2,1)S(1)}, u32[]{:S(2)}, u32[]{:S(2)}) collective-permute-start(bf16[8,4,256]{2,1,0:T(4,128)(2,1)S(1)} %bitcast.294), channel_id=1, source_target_pairs={{0,6},{1,7},{2,0},{3,1},{4,2},{5,3},{6,4},{7,5},{8,14},{9,15},{10,... | collective-permute-start | bytes 49160 | tf_op jit(solution)/shard_map/ppermute | solution.py:21
  (13 other events, 113.9 us)

commit v2 on v0

v2 whole, which is shorter than its diff:
```python
import math

import jax
import jax.numpy as jnp
from jax import lax
from jax.experimental import pallas as pl
from jax.experimental.pallas import tpu as pltpu
from jax.sharding import PartitionSpec as P

F32 = jnp.float32
BF16 = jnp.bfloat16
I32 = jnp.int32


def fetch_body(count, *refs):
    sources, targets, sems = refs[:count], refs[count + 1 : 2 * count + 1], refs[-1]
    copies = [
        pltpu.make_async_copy(s, t, sems.at[i]) for i, (s, t) in enumerate(zip(sources, targets))
    ]
    for copy in copies:
        copy.start()
    for copy in copies:
        copy.wait()


def fetch(after, *weights):
    count = len(weights)
    size = sum(math.prod(w.shape) * w.dtype.itemsize for w in weights)
    return pl.pallas_call(
        lambda *refs: fetch_body(count, *refs),
        out_shape=[pltpu.VMEM(w.shape, w.dtype) for w in weights],
        in_specs=[pl.BlockSpec(memory_space=pltpu.HBM)] * count
        + [pl.BlockSpec(memory_space=pl.ANY)],
        out_specs=[pl.BlockSpec(memory_space=pltpu.VMEM)] * count,
        scratch_shapes=[pltpu.SemaphoreType.DMA((count,))],
        cost_estimate=pl.CostEstimate(flops=0, bytes_accessed=2 * size, transcendentals=0),
        compiler_params=pltpu.CompilerParams(vmem_limit_bytes=1 << 20),
        name="fetch_weights",
    )(*weights, after)


def swap(x):
    n = lax.axis_size("rows")
    return lax.ppermute(x, "rows", [(i, i ^ 1) for i in range(n)])


def far(x, k):
    n = lax.axis_size("rows")
    return lax.ppermute(x, "rows", [(i, i ^ (2 * k)) for i in range(n)])


def chips():
    return lax.axis_size("rows") // 2


def is_odd():
    return (lax.axis_index("rows") & 1) != 0


def by_chip(x):
    chip = lax.axis_index("rows") // 2
    step = 1
    while step < x.shape[0]:
        y = x.reshape((x.shape[0] // (2 * step), 2, step) + x.shape[1:])
        y = jnp.where((chip & step) != 0, y[:, ::-1], y)
        x = y.reshape(x.shape)
        step *= 2
    return x


def join(x):
    y = swap(x)
    odd = is_odd()
    pairs = jnp.stack([jnp.where(odd, y, x), jnp.where(odd, x, y)], axis=1)
    return pairs.reshape((2 * x.shape[0],) + x.shape[1:])


def part(x):
    x = x.reshape((x.shape[0] // 2, 2) + x.shape[1:])
    odd = is_odd()
    other = jnp.where(odd, x[:, 0], x[:, 1]).astype(BF16)
    return jnp.where(odd, x[:, 1], x[:, 0]) + swap(other).astype(F32)


def gather(x):
    got = [x] + [far(x, k) for k in range(1, chips())]
    return by_chip_pairs(jnp.stack(got))


def by_chip_pairs(x):
    return join(by_chip(x))


def reduce(x):
    x = by_chip(part(x))
    return x[0] + sum(far(x[k].astype(BF16), k).astype(F32) for k in range(1, chips()))


def total(x, leaf_too=False):
    x = part(x)
    if leaf_too:
        x = leaf_total(x)
    b = x.astype(BF16)
    return x + sum(far(b, k).astype(F32) for k in range(1, chips()))


def leaf_total(x):
    n = lax.axis_size("leaf")
    b = x.astype(BF16)
    for k in range(1, n):
        x = x + lax.ppermute(b, "leaf", [(i, (i + k) % n) for i in range(n)]).astype(F32)
    return x


def pieces(x, n):
    return jnp.moveaxis(x.reshape(x.shape[:-1] + (n, x.shape[-1] // n)), -2, 0)


def whole(x):
    x = jnp.moveaxis(x, 0, -2)
    return x.reshape(x.shape[:-2] + (-1,))


def place(piece, count, index):
    at = jnp.arange(count).reshape((count,) + (1,) * piece.ndim)
    return jnp.where(at == index, piece[None], jnp.zeros_like(piece[None]))


def shards(
    leaf_rhs,
    parent_rhs,
    root_rhs,
    leaf_inv,
    leaf_panel,
    leaf_rows,
    leaf_height,
    parent_inv,
    parent_panel,
    parent_rows,
    parent_height,
    root_inv,
):
    n = lax.axis_size("rows")
    groups = lax.axis_size("leaf")
    rcount = leaf_rhs.shape[0]
    group_leaves = leaf_rhs.shape[1]
    leaf_local = leaf_panel.shape[1]
    parent_width = parent_inv.shape[2]
    root_width = root_inv.shape[1]
    row_index = lax.axis_index("rows")
    flat_index = lax.axis_index("leaf") * n + row_index
    root_cols = root_rhs.shape[1]

    lb = jnp.moveaxis(leaf_rhs.astype(BF16), 1, 0)
    leaf_inv, leaf_panel = fetch(lb, leaf_inv, leaf_panel)
    lb = whole(gather(lb))
    ly = jnp.einsum("lrn,lin->lri", lb, leaf_inv, preferred_element_type=F32)
    lyb = ly.astype(BF16)
    parent_inv, parent_panel, root_inv = fetch(lyb, parent_inv[0], parent_panel[0], root_inv)
    lyb = whole(gather(lyb))
    lupd = jnp.einsum("lrn,lhn->lrh", lyb, leaf_panel, preferred_element_type=F32)
    leaf_pos = row_index * leaf_local + jnp.arange(leaf_local, dtype=I32)
    leaf_mask = leaf_pos[None, :] < leaf_height[:, None]
    lupd = jnp.where(leaf_mask[:, None, :], lupd, 0.0)
    leaf_flat = leaf_rows.reshape(-1)
    local_acc = (
        jnp.zeros((rcount, parent_width + root_width), F32)
        .at[:, leaf_flat]
        .add(jnp.moveaxis(lupd, 0, 1).reshape(rcount, -1))
    )
    pacc = pieces(local_acc[:, :parent_width], n) - place(parent_rhs[:, 0], n, row_index)
    prb = (-total(pacc)).astype(BF16)
    py = jnp.dot(whole(join(prb)), parent_inv.T, preferred_element_type=F32)
    pyb = whole(gather(py.astype(BF16)))
    parent_local = parent_panel.shape[0]
    pupd = jnp.dot(pyb, parent_panel.T, preferred_element_type=F32)
    parent_pos = row_index * parent_local + jnp.arange(parent_local, dtype=I32)
    parent_mask = parent_pos < parent_height[0]
    pupd = jnp.where(parent_mask[None, :], pupd, 0.0)
    racc = local_acc[:, parent_width:].at[:, parent_rows[0]].add(pupd)
    racc = pieces(racc, groups * n) - place(root_rhs, groups * n, flat_index)
    racc = racc.reshape((n, groups) + racc.shape[1:])
    rrb = (-total(racc, leaf_too=True)).astype(BF16)
    rrb = whole(join(rrb).reshape((n * groups,) + rrb.shape[2:]))
    ry = jnp.dot(rrb, root_inv.T, preferred_element_type=F32)
    root_term = jnp.dot(ry.astype(BF16), root_inv, preferred_element_type=F32)
    rxb = join(total(pieces(root_term, n)).astype(BF16))
    rxb = whole(rxb)
    root_solution = lax.dynamic_slice_in_dim(rxb, flat_index * root_cols, root_cols, 1).astype(F32)
    parent_anc = rxb[:, parent_rows[0]]
    parent_anc = jnp.where(parent_mask[None, :], parent_anc, jnp.zeros_like(parent_anc))
    parent_term = jnp.dot(parent_anc, parent_panel, preferred_element_type=F32)
    pvb = (py - reduce(pieces(parent_term, n))).astype(BF16)
    parent_term = jnp.dot(pvb, parent_inv, preferred_element_type=F32)
    parent_part = total(pieces(parent_term, n))
    parent_sol = lax.dynamic_index_in_dim(parent_part, row_index // 2, 0, keepdims=False)
    parent_whole = whole(join(parent_part.astype(BF16)))
    ancestors = jnp.concatenate([parent_whole, rxb], axis=1)
    leaf_anc = ancestors[:, leaf_flat].reshape(rcount, group_leaves, leaf_local)
    leaf_anc = jnp.where(leaf_mask[None, :, :], leaf_anc, jnp.zeros_like(leaf_anc))
    leaf_term = jnp.einsum("rlh,lhc->lrc", leaf_anc, leaf_panel, preferred_element_type=F32)
    lvb = (ly - reduce(pieces(leaf_term, n))).astype(BF16)
    leaf_term = jnp.einsum("lri,lic->lrc", lvb, leaf_inv, preferred_element_type=F32)
    leaf_sol = jnp.moveaxis(reduce(pieces(leaf_term, n)), 0, 1)
    return (leaf_sol, parent_sol[:, None, :], root_solution)


def solution(mesh):
    return jax.shard_map(
        shards,
        mesh=mesh,
        in_specs=(
            P(None, "leaf", "rows"),
            P(None, "leaf", "rows"),
            P(None, ("leaf", "rows")),
            P("leaf", "rows", None),
            P("leaf", "rows", None),
            P("leaf", "rows"),
            P("leaf"),
            P("leaf", "rows", None),
            P("leaf", "rows", None),
            P("leaf", "rows"),
            P("leaf"),
            P("rows", None),
        ),
        out_specs=(P(None, "leaf", "rows"), P(None, "leaf", "rows"), P(None, ("leaf", "rows"))),
        check_vma=False,
    )
```

time: 561 us -> 226 us (0.40)
  waiting for transfers between devices: 334 us -> 49 us
  blocking collectives: 110 us -> 0 us
  starting transfers between devices: 0.29 us -> 50.9 us
  local copies, waits for them, and re-layouts: 25.9 us -> 52.5 us
  between operations: 14.9 us -> 2.11 us
  matrix products: 43.4 us -> 35.8 us
    reduce_scatter x6 -> x0, waiting for transfers between devices: 281 us -> none  [the longest x1 133 us: shards(): lax.psum_scatter(root_from_leaves, ('leaf', 'rows'), scatter_dimension=1,...]
    all_gather x6 -> x0, blocking collectives: 110 us -> none  [the longest x1 36.6 us: shards(): lax.all_gather(rrb, ('leaf', 'rows'), axis=1, tiled=True)]
    psum x1 -> x0, waiting for transfers between devices: 52.2 us -> none  [shards(): root_full = lax.psum(root_term, 'rows')]
    ppermute x0 -> x47, starting transfers between devices: none -> 50.9 us  [the longest x30 44.6 us: far(): return lax.ppermute(x, 'rows', [(i, i ^ 2 * k) for i in range(n)])]
    ppermute x0 -> x47, waiting for transfers between devices: none -> 49 us  [the longest x30 32.3 us: far(): return lax.ppermute(x, 'rows', [(i, i ^ 2 * k) for i in range(n)])]
    unnamed x18 -> x34, local copies, waits for them, and re-layouts: 4.23 us -> 29 us
    dot_general x9, matrix products: 43.4 us -> 35.8 us  [the longest x1 10.2 us: shards(): jnp.einsum('lrn,lhn->lrh', lyb, leaf_panel, preferred_element_type=F32)]
  transfers between devices with their start and end apart: 7 -> 47, of which waited for: 7 -> 33; matrix products, arithmetic and copies ran while one was open for 0% -> 1% of each run, Pallas kernels for 0% -> 1%
where the time goes in v2:
time: 226 us; the launch traced here: 225 us
  local copies, waits for them, and re-layouts  52.5 us (23%)
  starting transfers between devices  50.9 us (23%)
  waiting for transfers between devices  49 us (22%)
  matrix products  35.8 us (16%)
  other arithmetic  32.3 us (14%)
  Pallas kernels  2.31 us (1%)
    ppermute x30, starting transfers between devices, far(): return lax.ppermute(x, 'rows', [(i, i ^ 2 * k) for i in range(n)])  44.6 us
    ppermute x30, waiting for transfers between devices, far(): return lax.ppermute(x, 'rows', [(i, i ^ 2 * k) for i in range(n)])  32.3 us
    unnamed x34, local copies, waits for them, and re-layouts  29 us
    scatter-add x1, other arithmetic, shards(): local_acc = jnp.zeros((rcount, parent_width + root_width), F32).at[:, lea...  24.6 us
    ppermute x14, waiting for transfers between devices, swap(): return lax.ppermute(x, 'rows', [(i, i ^ 1) for i in range(n)])  14.2 us
    gather x1, local copies, waits for them, and re-layouts, shards(): leaf_anc = ancestors[:, leaf_flat].reshape(rcount, group_leaves, leaf_local)  12.9 us
    dot_general x1, matrix products, shards(): jnp.einsum('lrn,lhn->lrh', lyb, leaf_panel, preferred_element_type=F32)  10.2 us
    dot_general x1, matrix products, shards(): jnp.einsum('rlh,lhc->lrc', leaf_anc, leaf_panel, preferred_element_type=F32)  8.05 us
  transfers between devices with their start and end apart: 47, of which 33 were waited for; matrix products, arithmetic and copies ran while one was open for 1% of the time, Pallas kernels for 1%

profile of v2, /device:TPU:0, one launch (start us, length us, event | category | flops | bytes accessed | tf_op | source)
XLA Modules:
  0.0 225.0 jit_solution(16591478726684658729)
XLA Ops:
  1.4 3.0 %collective-permute-start = (bf16[4,8,256]{2,1,0:T(8,128)(2,1)S(1)}, bf16[4,8,256]{2,1,0:T(8,128)(2,1)S(1)}, u32[]{:S(2)}, u32[]{:S(2)}) collective-permute-start(bf16[4,8,256]{2,1,0:T(8,128)(2,1)S(1)} %bitcast.381), channel_id=1, source_target_pairs={{0,2},{1,3},{2,0},{3,1},{4,6},{5,7},{6,4},{7,5},{8,10},{9,11},{10,... | collective-permute-start | bytes 49160 | tf_op jit(solution)/shard_map/ppermute | solution.py:49
  4.4 2.6 %collective-permute-start.1 = (bf16[4,8,256]{2,1,0:T(8,128)(2,1)S(1)}, bf16[4,8,256]{2,1,0:T(8,128)(2,1)S(1)}, u32[]{:S(2)}, u32[]{:S(2)}) collective-permute-start(bf16[4,8,256]{2,1,0:T(8,128)(2,1)S(1)} %bitcast.382), channel_id=1, source_target_pairs={{0,4},{1,5},{2,6},{3,7},{4,0},{5,1},{6,2},{7,3},{8,12},{9,13},{10,... | collective-permute-start | bytes 49160 | tf_op jit(solution)/shard_map/ppermute | solution.py:49
  7.8 5.8 %copy-done.2 = bf16[4,1024,2048]{2,1,0:T(8,128)(2,1)S(1)} copy-done((bf16[4,1024,2048]{2,1,0:T(8,128)(2,1)S(1)}, bf16[4,1024,2048]{2,1,0:T(8,128)(2,1)}, u32[]{:S(2)}) %copy-start.2) | copy-done | bytes 16777240
  13.6 2.2 copy-done.10
  17.2 5.8 %copy-done = bf16[4,1024,2048]{2,1,0:T(8,128)(2,1)} copy-done((bf16[4,1024,2048]{2,1,0:T(8,128)(2,1)}, bf16[4,1024,2048]{2,1,0:T(8,128)(2,1)S(1)}, u32[]{:S(2)}) %copy-start) | copy-done | bytes 16777240
  27.1 3.5 %collective-permute-start.5 = (bf16[4,8,256]{2,1,0:T(8,128)(2,1)S(1)}, bf16[4,8,256]{2,1,0:T(8,128)(2,1)S(1)}, u32[]{:S(2)}, u32[]{:S(2)}) collective-permute-start(bf16[4,8,256]{2,1,0:T(8,128)(2,1)S(1)} %get-tuple-element.63.refs_3_), channel_id=1, source_target_pairs={{0,4},{1,5},{2,6},{3,7},{4,0},{5,1},{6,2},{7,3},{8,12},{9,13},{10,... | collective-permute-start | bytes 49160 | tf_op jit(solution)/shard_map/ppermute | solution.py:49
  30.7 1.9 collective-permute-done.5
  32.5 3.6 %collective-permute-done.6 = bf16[4,8,256]{2,1,0:T(8,128)(2,1)S(1)} collective-permute-done((bf16[4,8,256]{2,1,0:T(8,128)(2,1)S(1)}, bf16[4,8,256]{2,1,0:T(8,128)(2,1)S(1)}, u32[]{:S(2)}, u32[]{:S(2)}) %collective-permute-start.6) | collective-permute-done | bytes 16416 | tf_op jit(solution)/shard_map/ppermute | solution.py:49
  37.5 10.2 %convolution_select_fusion = f32[4,8,1024]{2,1,0:T(8,128)S(1)} fusion(bf16[4,8,2048]{2,1,0:T(8,128)(2,1)S(1)} %bitcast.405, bf16[4,1024,2048]{2,1,0:T(8,128)(2,1)} %copy-done, pred[4,1024]{1,0:T(4,128)(4,1)S(1)} %broadcast_compare_fusion), kind=kOutput, calls=%fused_computation.7 | convolution fusion | flops 134250496 | bytes 17043456 | tf_op jit(solution)/shard_map/lrn,lhn->lrh/dot_general | solution.py:161
  48.4 24.6 %scatter_custom_fusion = f32[8,8192]{0,1:T(8,128)} fusion(s32[4096]{0:T(1024)S(1)} %bitcast.429, f32[4096,8]{1,0:T(8,128)S(1)} %copy.137, f32[]{:T(128)} %constant.56.clone.1), kind=kCustom, calls=%fused_computation.5 | custom fusion | flops 32768 | bytes 262148 | tf_op jit(solution)/shard_map/scatter-add | solution.py:169
  73.0 3.8 %fusion.52 = (f32[8,4096]{0,1:T(8,128)}, f32[8,4096]{0,1:T(8,128)S(1)}) fusion(f32[8,8192]{0,1:T(8,128)} %scatter_custom_fusion), kind=kLoop, calls=%fused_computation.148 | loop fusion | bytes 524288 | tf_op jit(solution)/shard_map/slice | solution.py:171
  76.8 2.2 copy.138
  81.0 2.9 %collective-permute-start.9 = (bf16[4,8,512]{2,1,0:T(8,128)(2,1)S(1)}, bf16[4,8,512]{2,1,0:T(8,128)(2,1)S(1)}, u32[]{:S(2)}, u32[]{:S(2)}) collective-permute-start(bf16[4,8,512]{2,1,0:T(8,128)(2,1)S(1)} %fusion.46), channel_id=1, source_target_pairs={{0,2},{1,3},{2,0},{3,1},{4,6},{5,7},{6,4},{7,5},{8,10},{9,11},{10,... | collective-permute-start | bytes 98312 | tf_op jit(solution)/shard_map/ppermute | solution.py:49
  83.9 1.7 collective-permute-done.10
  86.4 2.2 copy-done.7
  88.6 2.2 copy-done.8
  90.8 2.2 copy-done.9
  93.8 2.0 copy-done.5
  95.9 1.9 copy-done.6
  97.8 2.0 copy-done.3
  103.6 1.9 collective-permute-start.15
  107.2 1.9 collective-permute-done.15
  110.4 3.4 %fusion.2 = f32[512,8]{0,1:T(8,128)S(1)} fusion(bf16[8,4096]{1,0:T(8,128)(2,1)S(1)} %bitcast.418, bf16[512,4096]{1,0:T(8,128)(2,1)} %copy-done.5, pred[512]{0:T(512)(128)(4,1)S(1)} %add_compare_fusion), kind=kOutput, calls=%fused_computation.9 | convolution fusion | flops 33558528 | bytes 4276736 | tf_op jit(solution)/shard_map/dot_general | solution.py:176
  113.9 4.2 %scatter_fusion = f32[8,4096]{0,1:T(8,128)S(1)} fusion(f32[8,4096]{0,1:T(8,128)S(1)} %get-tuple-element.33, s32[512]{0:T(512)S(1)} %bitcast.433, f32[512,8]{1,0:T(8,128)S(1)} %copy.145), kind=kCustom, calls=%fused_computation.3 | custom fusion | flops 4096 | bytes 51200 | tf_op jit(solution)/shard_map/scatter-add | solution.py:180
  127.2 2.4 %collective-permute-start.22 = (bf16[4,4,8,128]{3,2,1,0:T(8,128)(2,1)S(1)}, bf16[4,4,8,128]{3,2,1,0:T(8,128)(2,1)S(1)}, u32[]{:S(2)}, u32[]{:S(2)}) collective-permute-start(bf16[4,4,8,128]{3,2,1,0:T(8,128)(2,1)S(1)} %fusion.43), channel_id=1, source_target_pairs={{0,4},{1,5},{2,6},{3,7},{4,0},{5,1},{6,2},{7,3},{8,12},{9,13},{10,... | collective-permute-start | bytes 98312 | tf_op jit(solution)/shard_map/ppermute | solution.py:49
  129.7 2.0 collective-permute-start.23
  132.1 3.2 %collective-permute-done.23 = bf16[4,4,8,128]{3,2,1,0:T(8,128)(2,1)S(1)} collective-permute-done((bf16[4,4,8,128]{3,2,1,0:T(8,128)(2,1)S(1)}, bf16[4,4,8,128]{3,2,1,0:T(8,128)(2,1)S(1)}, u32[]{:S(2)}, u32[]{:S(2)}) %collective-permute-start.23) | collective-permute-done | bytes 32800 | tf_op jit(solution)/shard_map/ppermute | solution.py:49
  136.7 5.3 %fusion.3 = f32[8,4096]{1,0:T(8,128)S(1)} fusion(bf16[512,4096]{1,0:T(8,128)(2,1)} %copy-done.6, bf16[8,4096]{1,0:T(8,128)(2,1)S(1)} %bitcast.417), kind=kOutput, calls=%fused_computation.11 | convolution fusion | flops 67112960 | bytes 4390912 | tf_op jit(solution)/shard_map/dot_general | solution.py:186
  143.4 2.5 %collective-permute-start.27 = (bf16[4,8,512]{2,1,0:T(8,128)(2,1)S(1)}, bf16[4,8,512]{2,1,0:T(8,128)(2,1)S(1)}, u32[]{:S(2)}, u32[]{:S(2)}) collective-permute-start(bf16[4,8,512]{2,1,0:T(8,128)(2,1)S(1)} %fusion.44), channel_id=1, source_target_pairs={{0,4},{1,5},{2,6},{3,7},{4,0},{5,1},{6,2},{7,3},{8,12},{9,13},{10,... | collective-permute-start | bytes 98312 | tf_op jit(solution)/shard_map/ppermute | solution.py:49
  145.9 1.9 collective-permute-start.28
  148.9 2.7 %collective-permute-done.28 = bf16[4,8,512]{2,1,0:T(8,128)(2,1)S(1)} collective-permute-done((bf16[4,8,512]{2,1,0:T(8,128)(2,1)S(1)}, bf16[4,8,512]{2,1,0:T(8,128)(2,1)S(1)}, u32[]{:S(2)}, u32[]{:S(2)}) %collective-permute-start.28) | collective-permute-done | bytes 32800 | tf_op jit(solution)/shard_map/ppermute | solution.py:49
  154.8 3.1 %fusion.6 = f32[8,4096]{1,0:T(8,128)S(1)} fusion(bf16[512,4096]{1,0:T(8,128)(2,1)} %copy-done.5, bf16[512,8]{1,0:T(8,128)(2,1)S(1)} %gather_fusion, pred[512]{0:T(512)(128)(4,1)S(1)} %add_compare_fusion), kind=kOutput, calls=%fused_computation.24 | convolution fusion | flops 33558528 | bytes 4334080 | tf_op jit(solution)/shard_map/dot_general | solution.py:192
  159.4 2.4 %collective-permute-start.32 = (bf16[8,512]{1,0:T(8,128)(2,1)S(1)}, bf16[8,512]{1,0:T(8,128)(2,1)S(1)}, u32[]{:S(2)}, u32[]{:S(2)}) collective-permute-start(bf16[8,512]{1,0:T(8,128)(2,1)S(1)} %get-tuple-element.60), channel_id=1, source_target_pairs={{0,4},{1,5},{2,6},{3,7},{4,0},{5,1},{6,2},{7,3},{8,12},{9,13},{10,... | collective-permute-start | bytes 24584 | tf_op jit(solution)/shard_map/ppermute | solution.py:49
  161.8 1.9 collective-permute-start.33
  164.0 3.3 %collective-permute-done.33 = bf16[8,512]{1,0:T(8,128)(2,1)S(1)} collective-permute-done((bf16[8,512]{1,0:T(8,128)(2,1)S(1)}, bf16[8,512]{1,0:T(8,128)(2,1)S(1)}, u32[]{:S(2)}, u32[]{:S(2)}) %collective-permute-start.33) | collective-permute-done | bytes 8224 | tf_op jit(solution)/shard_map/ppermute | solution.py:49
  169.3 2.5 %collective-permute-start.36 = (bf16[4,8,512]{2,1,0:T(8,128)(2,1)S(1)}, bf16[4,8,512]{2,1,0:T(8,128)(2,1)S(1)}, u32[]{:S(2)}, u32[]{:S(2)}) collective-permute-start(bf16[4,8,512]{2,1,0:T(8,128)(2,1)S(1)} %fusion.45), channel_id=1, source_target_pairs={{0,4},{1,5},{2,6},{3,7},{4,0},{5,1},{6,2},{7,3},{8,12},{9,13},{10,... | collective-permute-start | bytes 98312 | tf_op jit(solution)/shard_map/ppermute | solution.py:49
  171.8 1.9 collective-permute-start.37
  174.8 2.7 %collective-permute-done.37 = bf16[4,8,512]{2,1,0:T(8,128)(2,1)S(1)} collective-permute-done((bf16[4,8,512]{2,1,0:T(8,128)(2,1)S(1)}, bf16[4,8,512]{2,1,0:T(8,128)(2,1)S(1)}, u32[]{:S(2)}, u32[]{:S(2)}) %collective-permute-start.37) | collective-permute-done | bytes 32800 | tf_op jit(solution)/shard_map/ppermute | solution.py:49
  179.3 1.8 pad_maximum_fusion
  181.1 12.9 %gather_fusion.1 = bf16[4096,8]{1,0:T(8,128)(2,1)S(1)} fusion(bf16[8,8192]{0,1:T(8,128)(2,1)} %pad_maximum_fusion, s32[4096]{0:T(1024)S(1)} %broadcast_clamp_fusion), kind=kCustom, calls=%fused_computation.1 | custom fusion | bytes 147456 | tf_op jit(solution)/shard_map/gather | solution.py:199
  194.3 8.1 %fusion.19 = f32[4,8,2048]{2,1,0:T(8,128)S(1)} fusion(bf16[4,1024,2048]{2,1,0:T(8,128)(2,1)} %copy-done, bf16[8,4,1024]{2,0,1:T(8,128)(2,1)S(1)} %copy.162, pred[4,1024]{1,0:T(4,128)(4,1)S(1)} %broadcast_compare_fusion), kind=kOutput, calls=%fused_computation.64 | convolution fusion | flops 134250496 | bytes 17108992 | tf_op jit(solution)/shard_map/rlh,lhc->lrc/dot_general | solution.py:201
  203.9 2.4 %collective-permute-start.41 = (bf16[4,8,256]{2,1,0:T(8,128)(2,1)S(1)}, bf16[4,8,256]{2,1,0:T(8,128)(2,1)S(1)}, u32[]{:S(2)}, u32[]{:S(2)}) collective-permute-start(bf16[4,8,256]{2,1,0:T(8,128)(2,1)S(1)} %get-tuple-element.47), channel_id=1, source_target_pairs={{0,4},{1,5},{2,6},{3,7},{4,0},{5,1},{6,2},{7,3},{8,12},{9,13},{10,... | collective-permute-start | bytes 49160 | tf_op jit(solution)/shard_map/ppermute | solution.py:49
  206.3 2.0 collective-permute-start.42
  208.7 3.2 %collective-permute-done.42 = bf16[4,8,256]{2,1,0:T(8,128)(2,1)S(1)} collective-permute-done((bf16[4,8,256]{2,1,0:T(8,128)(2,1)S(1)}, bf16[4,8,256]{2,1,0:T(8,128)(2,1)S(1)}, u32[]{:S(2)}, u32[]{:S(2)}) %collective-permute-start.42) | collective-permute-done | bytes 16416 | tf_op jit(solution)/shard_map/ppermute | solution.py:49
  211.9 2.8 %fusion.34 = f32[4,8,2048]{2,1,0:T(8,128)S(1)} fusion(bf16[4,256,2048]{2,1,0:T(8,128)(2,1)} %copy-done.1, f32[4,8,256]{2,1,0:T(8,128)S(1)} %get-tuple-element.64, f32[4,4,8,256]{3,2,1,0:T(8,128)S(1)} %bitcast.410, bf16[4,8,256]{2,1,0:T(8,128)(2,1)S(1)} %collective-permute-done.42, bf16[4,8,256]{2,1,0:T(8,128)(2,1)S(1)} %collective-permute-done.41, ...), kind=kOutput, calls=%fused_computation.110 | convolution fusion | flops 33619968 | bytes 4571136 | tf_op jit(solution)/shard_map/lri,lic->lrc/dot_general | solution.py:203
  216.3 2.5 %collective-permute-start.45 = (bf16[4,8,256]{2,0,1:T(4,128)(2,1)S(1)}, bf16[4,8,256]{2,0,1:T(4,128)(2,1)S(1)}, u32[]{:S(2)}, u32[]{:S(2)}) collective-permute-start(bf16[4,8,256]{2,0,1:T(4,128)(2,1)S(1)} %get-tuple-element.44), channel_id=1, source_target_pairs={{0,4},{1,5},{2,6},{3,7},{4,0},{5,1},{6,2},{7,3},{8,12},{9,13},{10,... | collective-permute-start | bytes 49160 | tf_op jit(solution)/shard_map/ppermute | solution.py:49
  218.8 1.9 collective-permute-start.46
  221.3 3.0 %collective-permute-done.46 = bf16[4,8,256]{2,0,1:T(4,128)(2,1)S(1)} collective-permute-done((bf16[4,8,256]{2,0,1:T(4,128)(2,1)S(1)}, bf16[4,8,256]{2,0,1:T(4,128)(2,1)S(1)}, u32[]{:S(2)}, u32[]{:S(2)}) %collective-permute-start.46) | collective-permute-done | bytes 16416 | tf_op jit(solution)/shard_map/ppermute | solution.py:49
  (183 shorter events, 47.2 us)
Async XLA Ops:
  1.4 21.6 %collective-permute-start = (bf16[4,8,256]{2,1,0:T(8,128)(2,1)S(1)}, bf16[4,8,256]{2,1,0:T(8,128)(2,1)S(1)}, u32[]{:S(2)}, u32[]{:S(2)}) collective-permute-start(bf16[4,8,256]{2,1,0:T(8,128)(2,1)S(1)} %bitcast.381), channel_id=1, source_target_pairs={{0,2},{1,3},{2,0},{3,1},{4,6},{5,7},{6,4},{7,5},{8,10},{9,11},{10,... | collective-permute-start | bytes 49160 | tf_op jit(solution)/shard_map/ppermute | solution.py:49
  4.4 18.6 %collective-permute-start.1 = (bf16[4,8,256]{2,1,0:T(8,128)(2,1)S(1)}, bf16[4,8,256]{2,1,0:T(8,128)(2,1)S(1)}, u32[]{:S(2)}, u32[]{:S(2)}) collective-permute-start(bf16[4,8,256]{2,1,0:T(8,128)(2,1)S(1)} %bitcast.382), channel_id=1, source_target_pairs={{0,4},{1,5},{2,6},{3,7},{4,0},{5,1},{6,2},{7,3},{8,12},{9,13},{10,... | collective-permute-start | bytes 49160 | tf_op jit(solution)/shard_map/ppermute | solution.py:49
  7.0 16.0 %collective-permute-start.2 = (bf16[4,8,256]{2,1,0:T(8,128)(2,1)S(1)}, bf16[4,8,256]{2,1,0:T(8,128)(2,1)S(1)}, u32[]{:S(2)}, u32[]{:S(2)}) collective-permute-start(bf16[4,8,256]{2,1,0:T(8,128)(2,1)S(1)} %bitcast.383), channel_id=1, source_target_pairs={{0,6},{1,7},{2,4},{3,5},{4,2},{5,3},{6,0},{7,1},{8,14},{9,15},{10,... | collective-permute-start | bytes 49160 | tf_op jit(solution)/shard_map/ppermute | solution.py:49
  23.1 1.3 collective-permute-start.3
  26.2 4.5 %collective-permute-start.4 = (bf16[4,8,256]{2,1,0:T(8,128)(2,1)S(1)}, bf16[4,8,256]{2,1,0:T(8,128)(2,1)S(1)}, u32[]{:S(2)}, u32[]{:S(2)}) collective-permute-start(bf16[4,8,256]{2,1,0:T(8,128)(2,1)S(1)} %get-tuple-element.63.refs_3_), channel_id=1, source_target_pairs={{0,2},{1,3},{2,0},{3,1},{4,6},{5,7},{6,4},{7,5},{8,10},{9,11},{10,... | collective-permute-start | bytes 49160 | tf_op jit(solution)/shard_map/ppermute | solution.py:49
  27.1 5.5 %collective-permute-start.5 = (bf16[4,8,256]{2,1,0:T(8,128)(2,1)S(1)}, bf16[4,8,256]{2,1,0:T(8,128)(2,1)S(1)}, u32[]{:S(2)}, u32[]{:S(2)}) collective-permute-start(bf16[4,8,256]{2,1,0:T(8,128)(2,1)S(1)} %get-tuple-element.63.refs_3_), channel_id=1, source_target_pairs={{0,4},{1,5},{2,6},{3,7},{4,0},{5,1},{6,2},{7,3},{8,12},{9,13},{10,... | collective-permute-start | bytes 49160 | tf_op jit(solution)/shard_map/ppermute | solution.py:49
  30.6 5.5 %collective-permute-start.6 = (bf16[4,8,256]{2,1,0:T(8,128)(2,1)S(1)}, bf16[4,8,256]{2,1,0:T(8,128)(2,1)S(1)}, u32[]{:S(2)}, u32[]{:S(2)}) collective-permute-start(bf16[4,8,256]{2,1,0:T(8,128)(2,1)S(1)} %get-tuple-element.63.refs_3_), channel_id=1, source_target_pairs={{0,6},{1,7},{2,4},{3,5},{4,2},{5,3},{6,0},{7,1},{8,14},{9,15},{10,... | collective-permute-start | bytes 49160 | tf_op jit(solution)/shard_map/ppermute | solution.py:49
  36.2 1.3 collective-permute-start.7
  79.0 1.3 collective-permute-start.8
  80.3 5.2 %collective-permute-start.10 = (bf16[4,8,512]{2,1,0:T(8,128)(2,1)S(1)}, bf16[4,8,512]{2,1,0:T(8,128)(2,1)S(1)}, u32[]{:S(2)}, u32[]{:S(2)}) collective-permute-start(bf16[4,8,512]{2,1,0:T(8,128)(2,1)S(1)} %fusion.46), channel_id=1, source_target_pairs={{0,4},{1,5},{2,6},{3,7},{4,0},{5,1},{6,2},{7,3},{8,12},{9,13},{10,... | collective-permute-start | bytes 98312 | tf_op jit(solution)/shard_map/ppermute | solution.py:49
  80.4 5.8 %collective-permute-start.11 = (bf16[4,8,512]{2,1,0:T(8,128)(2,1)S(1)}, bf16[4,8,512]{2,1,0:T(8,128)(2,1)S(1)}, u32[]{:S(2)}, u32[]{:S(2)}) collective-permute-start(bf16[4,8,512]{2,1,0:T(8,128)(2,1)S(1)} %fusion.46), channel_id=1, source_target_pairs={{0,6},{1,7},{2,4},{3,5},{4,2},{5,3},{6,0},{7,1},{8,14},{9,15},{10,... | collective-permute-start | bytes 98312 | tf_op jit(solution)/shard_map/ppermute | solution.py:49
  81.0 5.3 %collective-permute-start.9 = (bf16[4,8,512]{2,1,0:T(8,128)(2,1)S(1)}, bf16[4,8,512]{2,1,0:T(8,128)(2,1)S(1)}, u32[]{:S(2)}, u32[]{:S(2)}) collective-permute-start(bf16[4,8,512]{2,1,0:T(8,128)(2,1)S(1)} %fusion.46), channel_id=1, source_target_pairs={{0,2},{1,3},{2,0},{3,1},{4,6},{5,7},{6,4},{7,5},{8,10},{9,11},{10,... | collective-permute-start | bytes 98312 | tf_op jit(solution)/shard_map/ppermute | solution.py:49
  86.3 11.5 %collective-permute-start.12 = (bf16[4,8,512]{2,1,0:T(8,128)(2,1)S(1)}, bf16[4,8,512]{2,1,0:T(8,128)(2,1)S(1)}, u32[]{:S(2)}, u32[]{:S(2)}) collective-permute-start(bf16[4,8,512]{2,1,0:T(8,128)(2,1)S(1)} %negate_convert_fusion.1), channel_id=1, source_target_pairs={{0,1},{1,0},{2,3},{3,2},{4,5},{5,4},{6,7},{7,6},{8,9},{9,8},{10,11... | collective-permute-start | bytes 98312 | tf_op jit(solution)/shard_map/ppermute | solution.py:44
  101.1 17.7 %copy-start.12 = (f32[8,128]{1,0:T(8,128)S(1)}, f32[8,128]{1,0:T(8,128)}, u32[]{:S(2)}) copy-start(f32[8,128]{1,0:T(8,128)} %param.14) | copy-start | bytes 12292
  101.1 5.1 %collective-permute-start.13 = (bf16[8,512]{1,0:T(8,128)(2,1)S(1)}, bf16[8,512]{1,0:T(8,128)(2,1)S(1)}, u32[]{:S(2)}, u32[]{:S(2)}) collective-permute-start(bf16[8,512]{1,0:T(8,128)(2,1)S(1)} %get-tuple-element.65), channel_id=1, source_target_pairs={{0,2},{1,3},{2,0},{3,1},{4,6},{5,7},{6,4},{7,5},{8,10},{9,11},{10,... | collective-permute-start | bytes 24584 | tf_op jit(solution)/shard_map/ppermute | solution.py:49
  102.6 4.6 %collective-permute-start.14 = (bf16[8,512]{1,0:T(8,128)(2,1)S(1)}, bf16[8,512]{1,0:T(8,128)(2,1)S(1)}, u32[]{:S(2)}, u32[]{:S(2)}) collective-permute-start(bf16[8,512]{1,0:T(8,128)(2,1)S(1)} %get-tuple-element.65), channel_id=1, source_target_pairs={{0,4},{1,5},{2,6},{3,7},{4,0},{5,1},{6,2},{7,3},{8,12},{9,13},{10,... | collective-permute-start | bytes 24584 | tf_op jit(solution)/shard_map/ppermute | solution.py:49
  103.6 5.4 %collective-permute-start.15 = (bf16[8,512]{1,0:T(8,128)(2,1)S(1)}, bf16[8,512]{1,0:T(8,128)(2,1)S(1)}, u32[]{:S(2)}, u32[]{:S(2)}) collective-permute-start(bf16[8,512]{1,0:T(8,128)(2,1)S(1)} %get-tuple-element.65), channel_id=1, source_target_pairs={{0,6},{1,7},{2,4},{3,5},{4,2},{5,3},{6,0},{7,1},{8,14},{9,15},{10,... | collective-permute-start | bytes 24584 | tf_op jit(solution)/shard_map/ppermute | solution.py:49
  109.1 1.3 collective-permute-start.16
  118.9 1.3 collective-permute-start.17
  120.2 4.9 %collective-permute-start.18 = (bf16[4,4,8,128]{3,2,1,0:T(8,128)(2,1)S(1)}, bf16[4,4,8,128]{3,2,1,0:T(8,128)(2,1)S(1)}, u32[]{:S(2)}, u32[]{:S(2)}) collective-permute-start(bf16[4,4,8,128]{3,2,1,0:T(8,128)(2,1)S(1)} %get-tuple-element.30), channel_id=1, source_target_pairs={{0,8},{8,16},{16,24},{24,0},{1,9},{9,17},{17,25},{25,1},{2,10},{10... | collective-permute-start | bytes 98312 | tf_op jit(solution)/shard_map/ppermute | solution.py:111
  121.7 3.9 %collective-permute-start.19 = (bf16[4,4,8,128]{3,2,1,0:T(8,128)(2,1)S(1)}, bf16[4,4,8,128]{3,2,1,0:T(8,128)(2,1)S(1)}, u32[]{:S(2)}, u32[]{:S(2)}) collective-permute-start(bf16[4,4,8,128]{3,2,1,0:T(8,128)(2,1)S(1)} %get-tuple-element.30), channel_id=1, source_target_pairs={{0,16},{8,24},{16,0},{24,8},{1,17},{9,25},{17,1},{25,9},{2,18},{10... | collective-permute-start | bytes 98312 | tf_op jit(solution)/shard_map/ppermute | solution.py:111
  123.2 3.9 %collective-permute-start.20 = (bf16[4,4,8,128]{3,2,1,0:T(8,128)(2,1)S(1)}, bf16[4,4,8,128]{3,2,1,0:T(8,128)(2,1)S(1)}, u32[]{:S(2)}, u32[]{:S(2)}) collective-permute-start(bf16[4,4,8,128]{3,2,1,0:T(8,128)(2,1)S(1)} %get-tuple-element.30), channel_id=1, source_target_pairs={{0,24},{8,0},{16,8},{24,16},{1,25},{9,1},{17,9},{25,17},{2,26},{10... | collective-permute-start | bytes 98312 | tf_op jit(solution)/shard_map/ppermute | solution.py:111
  127.2 4.5 %collective-permute-start.21 = (bf16[4,4,8,128]{3,2,1,0:T(8,128)(2,1)S(1)}, bf16[4,4,8,128]{3,2,1,0:T(8,128)(2,1)S(1)}, u32[]{:S(2)}, u32[]{:S(2)}) collective-permute-start(bf16[4,4,8,128]{3,2,1,0:T(8,128)(2,1)S(1)} %fusion.43), channel_id=1, source_target_pairs={{0,2},{1,3},{2,0},{3,1},{4,6},{5,7},{6,4},{7,5},{8,10},{9,11},{10,... | collective-permute-start | bytes 98312 | tf_op jit(solution)/shard_map/ppermute | solution.py:49
  127.2 4.9 %collective-permute-start.22 = (bf16[4,4,8,128]{3,2,1,0:T(8,128)(2,1)S(1)}, bf16[4,4,8,128]{3,2,1,0:T(8,128)(2,1)S(1)}, u32[]{:S(2)}, u32[]{:S(2)}) collective-permute-start(bf16[4,4,8,128]{3,2,1,0:T(8,128)(2,1)S(1)} %fusion.43), channel_id=1, source_target_pairs={{0,4},{1,5},{2,6},{3,7},{4,0},{5,1},{6,2},{7,3},{8,12},{9,13},{10,... | collective-permute-start | bytes 98312 | tf_op jit(solution)/shard_map/ppermute | solution.py:49
  129.7 5.7 %collective-permute-start.23 = (bf16[4,4,8,128]{3,2,1,0:T(8,128)(2,1)S(1)}, bf16[4,4,8,128]{3,2,1,0:T(8,128)(2,1)S(1)}, u32[]{:S(2)}, u32[]{:S(2)}) collective-permute-start(bf16[4,4,8,128]{3,2,1,0:T(8,128)(2,1)S(1)} %fusion.43), channel_id=1, source_target_pairs={{0,6},{1,7},{2,4},{3,5},{4,2},{5,3},{6,0},{7,1},{8,14},{9,15},{10,... | collective-permute-start | bytes 98312 | tf_op jit(solution)/shard_map/ppermute | solution.py:49
  135.4 1.3 collective-permute-start.24
  142.0 1.3 collective-permute-start.25
  143.3 4.5 %collective-permute-start.26 = (bf16[4,8,512]{2,1,0:T(8,128)(2,1)S(1)}, bf16[4,8,512]{2,1,0:T(8,128)(2,1)S(1)}, u32[]{:S(2)}, u32[]{:S(2)}) collective-permute-start(bf16[4,8,512]{2,1,0:T(8,128)(2,1)S(1)} %fusion.44), channel_id=1, source_target_pairs={{0,2},{1,3},{2,0},{3,1},{4,6},{5,7},{6,4},{7,5},{8,10},{9,11},{10,... | collective-permute-start | bytes 98312 | tf_op jit(solution)/shard_map/ppermute | solution.py:49
  143.4 5.5 %collective-permute-start.27 = (bf16[4,8,512]{2,1,0:T(8,128)(2,1)S(1)}, bf16[4,8,512]{2,1,0:T(8,128)(2,1)S(1)}, u32[]{:S(2)}, u32[]{:S(2)}) collective-permute-start(bf16[4,8,512]{2,1,0:T(8,128)(2,1)S(1)} %fusion.44), channel_id=1, source_target_pairs={{0,4},{1,5},{2,6},{3,7},{4,0},{5,1},{6,2},{7,3},{8,12},{9,13},{10,... | collective-permute-start | bytes 98312 | tf_op jit(solution)/shard_map/ppermute | solution.py:49
  145.9 5.7 %collective-permute-start.28 = (bf16[4,8,512]{2,1,0:T(8,128)(2,1)S(1)}, bf16[4,8,512]{2,1,0:T(8,128)(2,1)S(1)}, u32[]{:S(2)}, u32[]{:S(2)}) collective-permute-start(bf16[4,8,512]{2,1,0:T(8,128)(2,1)S(1)} %fusion.44), channel_id=1, source_target_pairs={{0,6},{1,7},{2,4},{3,5},{4,2},{5,3},{6,0},{7,1},{8,14},{9,15},{10,... | collective-permute-start | bytes 98312 | tf_op jit(solution)/shard_map/ppermute | solution.py:49
  151.7 1.3 collective-permute-start.29
  157.9 1.3 collective-permute-start.30
  159.3 4.5 %collective-permute-start.31 = (bf16[8,512]{1,0:T(8,128)(2,1)S(1)}, bf16[8,512]{1,0:T(8,128)(2,1)S(1)}, u32[]{:S(2)}, u32[]{:S(2)}) collective-permute-start(bf16[8,512]{1,0:T(8,128)(2,1)S(1)} %get-tuple-element.58), channel_id=1, source_target_pairs={{0,2},{1,3},{2,0},{3,1},{4,6},{5,7},{6,4},{7,5},{8,10},{9,11},{10,... | collective-permute-start | bytes 24584 | tf_op jit(solution)/shard_map/ppermute | solution.py:49
  159.4 4.6 %collective-permute-start.32 = (bf16[8,512]{1,0:T(8,128)(2,1)S(1)}, bf16[8,512]{1,0:T(8,128)(2,1)S(1)}, u32[]{:S(2)}, u32[]{:S(2)}) collective-permute-start(bf16[8,512]{1,0:T(8,128)(2,1)S(1)} %get-tuple-element.60), channel_id=1, source_target_pairs={{0,4},{1,5},{2,6},{3,7},{4,0},{5,1},{6,2},{7,3},{8,12},{9,13},{10,... | collective-permute-start | bytes 24584 | tf_op jit(solution)/shard_map/ppermute | solution.py:49
  161.8 5.4 %collective-permute-start.33 = (bf16[8,512]{1,0:T(8,128)(2,1)S(1)}, bf16[8,512]{1,0:T(8,128)(2,1)S(1)}, u32[]{:S(2)}, u32[]{:S(2)}) collective-permute-start(bf16[8,512]{1,0:T(8,128)(2,1)S(1)} %get-tuple-element.59), channel_id=1, source_target_pairs={{0,6},{1,7},{2,4},{3,5},{4,2},{5,3},{6,0},{7,1},{8,14},{9,15},{10,... | collective-permute-start | bytes 24584 | tf_op jit(solution)/shard_map/ppermute | solution.py:49
  167.9 1.3 collective-permute-start.34
  169.2 4.5 %collective-permute-start.35 = (bf16[4,8,512]{2,1,0:T(8,128)(2,1)S(1)}, bf16[4,8,512]{2,1,0:T(8,128)(2,1)S(1)}, u32[]{:S(2)}, u32[]{:S(2)}) collective-permute-start(bf16[4,8,512]{2,1,0:T(8,128)(2,1)S(1)} %fusion.45), channel_id=1, source_target_pairs={{0,2},{1,3},{2,0},{3,1},{4,6},{5,7},{6,4},{7,5},{8,10},{9,11},{10,... | collective-permute-start | bytes 98312 | tf_op jit(solution)/shard_map/ppermute | solution.py:49
  169.3 5.5 %collective-permute-start.36 = (bf16[4,8,512]{2,1,0:T(8,128)(2,1)S(1)}, bf16[4,8,512]{2,1,0:T(8,128)(2,1)S(1)}, u32[]{:S(2)}, u32[]{:S(2)}) collective-permute-start(bf16[4,8,512]{2,1,0:T(8,128)(2,1)S(1)} %fusion.45), channel_id=1, source_target_pairs={{0,4},{1,5},{2,6},{3,7},{4,0},{5,1},{6,2},{7,3},{8,12},{9,13},{10,... | collective-permute-start | bytes 98312 | tf_op jit(solution)/shard_map/ppermute | solution.py:49
  171.8 5.7 %collective-permute-start.37 = (bf16[4,8,512]{2,1,0:T(8,128)(2,1)S(1)}, bf16[4,8,512]{2,1,0:T(8,128)(2,1)S(1)}, u32[]{:S(2)}, u32[]{:S(2)}) collective-permute-start(bf16[4,8,512]{2,1,0:T(8,128)(2,1)S(1)} %fusion.45), channel_id=1, source_target_pairs={{0,6},{1,7},{2,4},{3,5},{4,2},{5,3},{6,0},{7,1},{8,14},{9,15},{10,... | collective-permute-start | bytes 98312 | tf_op jit(solution)/shard_map/ppermute | solution.py:49
  177.5 1.3 collective-permute-start.38
  202.4 1.3 collective-permute-start.39
  203.8 4.5 %collective-permute-start.40 = (bf16[4,8,256]{2,1,0:T(8,128)(2,1)S(1)}, bf16[4,8,256]{2,1,0:T(8,128)(2,1)S(1)}, u32[]{:S(2)}, u32[]{:S(2)}) collective-permute-start(bf16[4,8,256]{2,1,0:T(8,128)(2,1)S(1)} %get-tuple-element.45), channel_id=1, source_target_pairs={{0,2},{1,3},{2,0},{3,1},{4,6},{5,7},{6,4},{7,5},{8,10},{9,11},{10,... | collective-permute-start | bytes 49160 | tf_op jit(solution)/shard_map/ppermute | solution.py:49
  203.9 4.8 %collective-permute-start.41 = (bf16[4,8,256]{2,1,0:T(8,128)(2,1)S(1)}, bf16[4,8,256]{2,1,0:T(8,128)(2,1)S(1)}, u32[]{:S(2)}, u32[]{:S(2)}) collective-permute-start(bf16[4,8,256]{2,1,0:T(8,128)(2,1)S(1)} %get-tuple-element.47), channel_id=1, source_target_pairs={{0,4},{1,5},{2,6},{3,7},{4,0},{5,1},{6,2},{7,3},{8,12},{9,13},{10,... | collective-permute-start | bytes 49160 | tf_op jit(solution)/shard_map/ppermute | solution.py:49
  206.3 5.5 %collective-permute-start.42 = (bf16[4,8,256]{2,1,0:T(8,128)(2,1)S(1)}, bf16[4,8,256]{2,1,0:T(8,128)(2,1)S(1)}, u32[]{:S(2)}, u32[]{:S(2)}) collective-permute-start(bf16[4,8,256]{2,1,0:T(8,128)(2,1)S(1)} %get-tuple-element.46), channel_id=1, source_target_pairs={{0,6},{1,7},{2,4},{3,5},{4,2},{5,3},{6,0},{7,1},{8,14},{9,15},{10,... | collective-permute-start | bytes 49160 | tf_op jit(solution)/shard_map/ppermute | solution.py:49
  214.8 1.3 collective-permute-start.43
  216.3 5.1 %collective-permute-start.44 = (bf16[4,8,256]{2,0,1:T(4,128)(2,1)S(1)}, bf16[4,8,256]{2,0,1:T(4,128)(2,1)S(1)}, u32[]{:S(2)}, u32[]{:S(2)}) collective-permute-start(bf16[4,8,256]{2,0,1:T(4,128)(2,1)S(1)} %get-tuple-element.42), channel_id=1, source_target_pairs={{0,2},{1,3},{2,0},{3,1},{4,6},{5,7},{6,4},{7,5},{8,10},{9,11},{10,... | collective-permute-start | bytes 49160 | tf_op jit(solution)/shard_map/ppermute | solution.py:49
  216.3 5.0 %collective-permute-start.45 = (bf16[4,8,256]{2,0,1:T(4,128)(2,1)S(1)}, bf16[4,8,256]{2,0,1:T(4,128)(2,1)S(1)}, u32[]{:S(2)}, u32[]{:S(2)}) collective-permute-start(bf16[4,8,256]{2,0,1:T(4,128)(2,1)S(1)} %get-tuple-element.44), channel_id=1, source_target_pairs={{0,4},{1,5},{2,6},{3,7},{4,0},{5,1},{6,2},{7,3},{8,12},{9,13},{10,... | collective-permute-start | bytes 49160 | tf_op jit(solution)/shard_map/ppermute | solution.py:49
  218.8 5.5 %collective-permute-start.46 = (bf16[4,8,256]{2,0,1:T(4,128)(2,1)S(1)}, bf16[4,8,256]{2,0,1:T(4,128)(2,1)S(1)}, u32[]{:S(2)}, u32[]{:S(2)}) collective-permute-start(bf16[4,8,256]{2,0,1:T(4,128)(2,1)S(1)} %get-tuple-element.43), channel_id=1, source_target_pairs={{0,6},{1,7},{2,4},{3,5},{4,2},{5,3},{6,0},{7,1},{8,14},{9,15},{10,... | collective-permute-start | bytes 49160 | tf_op jit(solution)/shard_map/ppermute | solution.py:49
  (14 other events, 69.4 us)

commit v3 on v0

v3 whole, which is shorter than its diff:
```python
import math

import jax
import jax.numpy as jnp
from jax import lax
from jax.experimental import pallas as pl
from jax.experimental.pallas import tpu as pltpu
from jax.sharding import PartitionSpec as P

F32 = jnp.float32
BF16 = jnp.bfloat16
I32 = jnp.int32
LANES = 128
UNROLL = 4

VMEM = pl.BlockSpec(memory_space=pltpu.VMEM)
SMEM = pl.BlockSpec(memory_space=pltpu.SMEM)


def pinned(w):
    return pltpu.with_memory_space_constraint(w, pltpu.VMEM)


def call(body, outs, ins, specs, scratch=(), flops=0, moved=0, limit=6 << 20, name=None):
    return pl.pallas_call(
        body,
        out_shape=[jax.ShapeDtypeStruct(s, d) for s, d in outs],
        in_specs=list(specs),
        out_specs=[VMEM] * len(outs),
        scratch_shapes=list(scratch),
        cost_estimate=pl.CostEstimate(flops=flops, bytes_accessed=moved, transcendentals=0),
        compiler_params=pltpu.CompilerParams(vmem_limit_bytes=limit),
        name=name,
    )(*ins)


def times_transposed(x, w):
    return lax.dot_general(x, w, (((1,), (1,)), ((), ())), preferred_element_type=F32)


def times(x, w):
    return lax.dot_general(x, w, (((1,), (0,)), ((), ())), preferred_element_type=F32)


def fetch(after, *weights):
    count = len(weights)
    size = sum(math.prod(w.shape) * w.dtype.itemsize for w in weights)

    def body(*refs):
        sources, targets, sems = refs[:count], refs[count + 1 : 2 * count + 1], refs[-1]
        copies = [
            pltpu.make_async_copy(s, t, sems.at[i])
            for i, (s, t) in enumerate(zip(sources, targets))
        ]
        for copy in copies:
            copy.start()
        for copy in copies:
            copy.wait()

    return pl.pallas_call(
        body,
        out_shape=[pltpu.VMEM(w.shape, w.dtype) for w in weights],
        in_specs=[pl.BlockSpec(memory_space=pltpu.HBM)] * count
        + [pl.BlockSpec(memory_space=pl.ANY)],
        out_specs=[VMEM] * count,
        scratch_shapes=[pltpu.SemaphoreType.DMA((count,))],
        cost_estimate=pl.CostEstimate(flops=0, bytes_accessed=2 * size, transcendentals=0),
        compiler_params=pltpu.CompilerParams(vmem_limit_bytes=1 << 20),
        name="fetch_weights",
    )(*weights, after)


def walk_plan(rows, width):
    sets, length = rows.shape
    blocks = width // LANES
    tiled = rows.reshape(sets, length // LANES, LANES)
    first = tiled[:, :, 0] // LANES
    used = tiled[:, :, 0] >= 0
    last = tiled.max(-1) // LANES
    lo = jnp.where(used, first, blocks)
    span = jnp.where(used, last - first + 1, 0)
    trips = (span.max(0) + UNROLL - 1) // UNROLL
    return jnp.concatenate([lo.reshape(-1), trips]).astype(I32)


def walk(plan_ref, sets, tiles, blocks, tile, visit, carry):
    def trip(i, carry):
        at = []
        for s in range(sets):
            lo = plan_ref[s * tiles + tile] + i * UNROLL
            at += [(s, jnp.minimum(lo + u, blocks)) for u in range(UNROLL)]
        return visit(at, carry)

    return lax.fori_loop(0, plan_ref[sets * tiles + tile], trip, carry)


def pick(x, index):
    inside = (index >= 0) & (index < LANES)
    found = jnp.take_along_axis(
        x, index & (LANES - 1), axis=1, mode="promise_in_bounds"
    )
    return jnp.where(inside, found, 0.0)


def invert(rows, plan, width):
    sets, length = rows.shape
    tiles, blocks = length // LANES, width // LANES

    def body(plan_ref, rows_ref, out_ref):
        out_ref[...] = jnp.full(out_ref.shape, -1, I32)
        for tile in range(tiles):
            cols, spots = [], lax.broadcasted_iota(I32, (LANES, LANES), 0) + (tile * LANES + 1)
            for s in range(sets):
                line = rows_ref[s : s + 1, tile * LANES : (tile + 1) * LANES]
                cols.append(jnp.transpose(jnp.broadcast_to(line, (LANES, LANES))))

            def visit(at, carry):
                lane = lax.broadcasted_iota(I32, (LANES, LANES), 1)
                got = []
                for s, block in at:
                    hit = cols[s] == lane + block * LANES
                    got.append(jnp.sum(jnp.where(hit, spots, 0), axis=0, keepdims=True))
                for (s, block), g in zip(at, got):
                    out_ref[s, block] += jnp.broadcast_to(g, out_ref.shape[2:])
                return carry

            walk(plan_ref, sets, tiles, blocks, tile, visit, 0)

    return call(
        body,
        [((sets, blocks + 1, 8, LANES), I32)],
        [plan, rows],
        [SMEM, VMEM],
        moved=16 << 20,
        limit=4 << 20,
        name="invert_rows",
    )[0]


def scatter_walk(plan_ref, inverse_ref, update_ref, acc_ref, tiles):
    sets, blocks = inverse_ref.shape[0], inverse_ref.shape[1] - 1
    for tile in range(tiles):

        def visit(at, carry):
            got = []
            for s, block in at:
                x = update_ref[s, :, tile * LANES : (tile + 1) * LANES]
                got.append(pick(x, inverse_ref[s, block] - tile * LANES))
            for (s, block), g in zip(at, got):
                acc_ref[block] += g
            return carry

        walk(plan_ref, sets, tiles, blocks, tile, visit, 0)


def gather_walk(plan_ref, rows_ref, source_ref, out_ref):
    sets, length = rows_ref.shape
    tiles, blocks = length // LANES, source_ref.shape[0] - 1
    for tile in range(tiles):
        index = [
            jnp.broadcast_to(
                rows_ref[s : s + 1, tile * LANES : (tile + 1) * LANES], (8, LANES)
            )
            for s in range(sets)
        ]

        def visit(at, carry):
            carry = list(carry)
            for s, block in at:
                carry[s] = carry[s] + pick(source_ref[block], index[s] - block * LANES)
            return tuple(carry)

        zero = tuple(jnp.zeros((8, LANES), F32) for _ in range(sets))
        found = walk(plan_ref, sets, tiles, blocks, tile, visit, zero)
        for s in range(sets):
            out_ref[s, :, tile * LANES : (tile + 1) * LANES] = found[s].astype(out_ref.dtype)


def joined(ref, *at):
    return jnp.concatenate([ref[(j,) + at] for j in range(ref.shape[0])], axis=1)


def split(value, n):
    w = value.shape[1] // n
    return [value[:, j * w : (j + 1) * w] for j in range(n)]


def unite(where_ref, own_ref, other_ref, out_ref):
    core = where_ref[0]
    chips, _, w = own_ref.shape
    for k in range(chips):
        for ref, odd in ((own_ref, core), (other_ref, 1 - core)):
            out_ref[:, pl.ds(pl.multiple_of((2 * k + odd) * w, LANES), w)] = ref[k]


def deal(where_ref, value_ref, own_ref, other_ref):
    core = where_ref[0]
    chips, _, w = own_ref.shape
    for k in range(chips):
        for ref, odd in ((own_ref, core), (other_ref, 1 - core)):
            piece = value_ref[:, pl.ds(pl.multiple_of((2 * k + odd) * w, LANES), w)]
            ref[k] = piece.astype(ref.dtype)


def all_gather(copies):
    return lax.all_to_all(copies, "rows", 0, 0)


def scatter_pieces(x):
    return lax.all_to_all(x, "rows", 0, 0)


def swap(x):
    n = lax.axis_size("rows")
    return lax.ppermute(x, "rows", [(i, i ^ 1) for i in range(n)])


def far(x, k):
    n = lax.axis_size("rows")
    return lax.ppermute(x, "rows", [(i, i ^ (2 * k)) for i in range(n)])


def chips_sum(x):
    b = x.astype(BF16)
    return x + sum(far(b, k).astype(F32) for k in range(1, lax.axis_size("rows") // 2))


def chips_sum_at_once(x):
    n = lax.axis_size("rows")
    b = jnp.broadcast_to(x.astype(BF16)[None], (n // 2,) + x.shape)
    groups = [list(range(c, n, 2)) for c in range(2)]
    got = lax.all_to_all(b, "rows", 0, 0, axis_index_groups=groups)
    return got.astype(F32).sum(0)


def leaf_sum(x):
    n = lax.axis_size("leaf")
    b = x.astype(BF16)
    for k in range(1, n):
        x = x + lax.ppermute(b, "leaf", [(i, (i + k) % n) for i in range(n)]).astype(F32)
    return x


def shards(
    leaf_rhs,
    parent_rhs,
    root_rhs,
    leaf_inv,
    leaf_panel,
    leaf_rows,
    leaf_height,
    parent_inv,
    parent_panel,
    parent_rows,
    parent_height,
    root_inv,
):
    n = lax.axis_size("rows")
    chips = n // 2
    rcount, leaves, leaf_cols = leaf_rhs.shape
    leaf_local, leaf_width = leaf_panel.shape[1:]
    parent_cols, parent_width = parent_inv.shape[1:]
    parent_local = parent_panel.shape[1]
    root_local, root_width = root_inv.shape
    root_cols = root_rhs.shape[1]
    piece = root_width // n
    tall = parent_width + root_width
    row = lax.axis_index("rows")
    flat = lax.axis_index("leaf") * n + row
    where = jnp.stack([row & 1, row // 2, row, flat]).astype(I32)
    aligned = leaf_cols % LANES == 0

    def leaf_vector(got):
        return got if aligned else jnp.moveaxis(got, 0, 2).reshape(1, leaves, rcount, leaf_width)

    def leaf_pieces(x):
        if aligned:
            return x
        return jnp.moveaxis(x[0].reshape(leaves, rcount, n, leaf_cols), 2, 0)

    cuts = n if aligned else 1
    leaf_cut = leaf_width // cuts

    leaf_pos = row * leaf_local + jnp.arange(leaf_local, dtype=I32)
    leaf_list = jnp.where(leaf_pos[None, :] < leaf_height[:, None], leaf_rows, -1)
    parent_pos = row * parent_local + jnp.arange(parent_local, dtype=I32)
    parent_list = jnp.where(parent_pos[None, :] < parent_height[:, None], parent_rows, -1)
    leaf_plan = walk_plan(leaf_list, tall)
    parent_plan = walk_plan(parent_list, root_width)
    rhs_spread = lax.dynamic_update_slice_in_dim(
        jnp.zeros((rcount, root_width), F32), root_rhs, flat * root_cols, 1
    )

    lb = jnp.moveaxis(leaf_rhs.astype(BF16), 1, 0)
    lb = all_gather(jnp.broadcast_to(lb[None], (n,) + lb.shape))
    leaf_inv, leaf_panel = fetch(where, leaf_inv, leaf_panel)
    leaf_inverse = invert(leaf_list, leaf_plan, tall)
    parent_inverse = invert(parent_list, parent_plan, root_width)

    def leaf_solve(x_ref, w_ref, y_ref, copies_ref):
        for s in range(leaves):
            y = times_transposed(joined(x_ref, s), w_ref[s])
            y_ref[s] = y
            for j in range(n):
                copies_ref[j, s] = y.astype(BF16)

    ly, lyb = call(
        leaf_solve,
        [((leaves, rcount, leaf_cols), F32), ((n, leaves, rcount, leaf_cols), BF16)],
        [leaf_vector(lb), pinned(leaf_inv)],
        [VMEM] * 2,
        name="leaf_solve",
    )
    lyb = all_gather(lyb)
    parent_inv, parent_panel, root_inv = fetch(where, parent_inv[0], parent_panel[0], root_inv)

    def leaf_update(
        where_ref, plan_ref, x_ref, w_ref, inverse_ref, rhs_ref, own_ref, other_ref, root_ref,
        update_ref, acc_ref, sum_ref,
    ):
        acc_ref[...] = jnp.zeros(acc_ref.shape, F32)
        for s in range(leaves):
            update_ref[s] = times_transposed(joined(x_ref, s), w_ref[s])
        scatter_walk(plan_ref, inverse_ref, update_ref, acc_ref, leaf_local // LANES)
        for b in range(parent_width // LANES):
            sum_ref[:, b * LANES : (b + 1) * LANES] = -acc_ref[b]
        spot = pl.ds(pl.multiple_of(where_ref[2] * parent_cols, LANES), parent_cols)
        sum_ref[:, spot] += rhs_ref[...]
        deal(where_ref, sum_ref, own_ref, other_ref)
        for b in range(root_width // LANES):
            root_ref[b] = acc_ref[parent_width // LANES + b]

    own, other, root_acc = call(
        leaf_update,
        [
            ((chips, rcount, parent_cols), F32),
            ((chips, rcount, parent_cols), BF16),
            ((root_width // LANES, rcount, LANES), F32),
        ],
        [where, leaf_plan, leaf_vector(lyb), pinned(leaf_panel), leaf_inverse, parent_rhs[:, 0]],
        [SMEM, SMEM] + [VMEM] * 4,
        scratch=[
            pltpu.VMEM((leaves, rcount, leaf_local), F32),
            pltpu.VMEM((tall // LANES + 1, rcount, LANES), F32),
            pltpu.VMEM((rcount, parent_width), F32),
        ],
        name="leaf_update",
    )
    prb = chips_sum(own + swap(other).astype(F32)).astype(BF16)

    def parent_solve(where_ref, own_ref, other_ref, w_ref, y_ref, copies_ref, x_ref):
        unite(where_ref, own_ref, other_ref, x_ref)
        y = times_transposed(x_ref[...], w_ref[...])
        y_ref[...] = y
        for j in range(n):
            copies_ref[j] = y.astype(BF16)

    py, pyb = call(
        parent_solve,
        [((rcount, parent_cols), F32), ((n, rcount, parent_cols), BF16)],
        [where, prb, swap(prb), pinned(parent_inv)],
        [SMEM] + [VMEM] * 3,
        scratch=[pltpu.VMEM((rcount, parent_width), BF16)],
        name="parent_solve",
    )
    pyb = all_gather(pyb)

    def parent_update(
        where_ref, plan_ref, x_ref, w_ref, inverse_ref, root_ref, rhs_ref, own_ref, other_ref,
        update_ref, acc_ref, sum_ref,
    ):
        for b in range(root_width // LANES):
            acc_ref[b] = root_ref[b]
        update_ref[0] = times_transposed(joined(x_ref), w_ref[...])
        scatter_walk(plan_ref, inverse_ref, update_ref, acc_ref, parent_local // LANES)
        for b in range(root_width // LANES):
            lanes = slice(b * LANES, (b + 1) * LANES)
            sum_ref[:, lanes] = rhs_ref[:, lanes] - acc_ref[b]
        deal(where_ref, sum_ref, own_ref, other_ref)

    own, other = call(
        parent_update,
        [((chips, rcount, piece), F32), ((chips, rcount, piece), BF16)],
        [where, parent_plan, pyb, pinned(parent_panel), parent_inverse, root_acc, rhs_spread],
        [SMEM, SMEM] + [VMEM] * 5,
        scratch=[
            pltpu.VMEM((1, rcount, parent_local), F32),
            pltpu.VMEM((root_width // LANES + 1, rcount, LANES), F32),
            pltpu.VMEM((rcount, root_width), F32),
        ],
        name="parent_update",
    )
    rrb = chips_sum_at_once(leaf_sum(own + swap(other).astype(F32))).astype(BF16)

    def root_solve(where_ref, own_ref, other_ref, w_ref, own_out, other_out, x_ref, sum_ref):
        unite(where_ref, own_ref, other_ref, x_ref)
        y = times_transposed(x_ref[...], w_ref[...]).astype(BF16)
        sum_ref[...] = times(y, w_ref[...])
        deal(where_ref, sum_ref, own_out, other_out)

    own, other = call(
        root_solve,
        [((chips, rcount, piece), F32), ((chips, rcount, piece), BF16)],
        [where, rrb, swap(rrb), pinned(root_inv)],
        [SMEM] + [VMEM] * 3,
        scratch=[pltpu.VMEM((rcount, root_width), BF16), pltpu.VMEM((rcount, root_width), F32)],
        name="root_solve",
    )
    rxb = chips_sum_at_once(own + swap(other).astype(F32)).astype(BF16)

    def blocks_of(source_ref, target_ref, start, width):
        for b in range(width // LANES):
            target_ref[start + b] = source_ref[:, b * LANES : (b + 1) * LANES].astype(F32)

    def parent_back(
        where_ref, plan_ref, own_ref, other_ref, rows_ref, w_ref, out_ref, whole_ref,
        x_ref, found_ref,
    ):
        unite(where_ref, own_ref, other_ref, x_ref)
        blocks_of(x_ref, whole_ref, 0, root_width)
        whole_ref[root_width // LANES] = jnp.zeros((rcount, LANES), F32)
        gather_walk(plan_ref, rows_ref, whole_ref, found_ref)
        term = times(found_ref[0], w_ref[...])
        for j, part in enumerate(split(term, n)):
            out_ref[j] = part.astype(BF16)

    term, root_whole = call(
        parent_back,
        [((n, rcount, parent_cols), BF16), ((root_width // LANES + 1, rcount, LANES), F32)],
        [where, parent_plan, rxb, swap(rxb), parent_list, pinned(parent_panel)],
        [SMEM, SMEM] + [VMEM] * 4,
        scratch=[
            pltpu.VMEM((rcount, root_width), BF16),
            pltpu.VMEM((1, rcount, parent_local), BF16),
        ],
        name="parent_back",
    )
    tail = scatter_pieces(term)

    def parent_solve_back(where_ref, tail_ref, y_ref, w_ref, own_ref, other_ref, sum_ref):
        lost = sum(tail_ref[j].astype(F32) for j in range(n))
        sum_ref[...] = times((y_ref[...] - lost).astype(BF16), w_ref[...])
        deal(where_ref, sum_ref, own_ref, other_ref)

    own, other = call(
        parent_solve_back,
        [((chips, rcount, parent_cols), F32), ((chips, rcount, parent_cols), BF16)],
        [where, tail, py, pinned(parent_inv)],
        [SMEM] + [VMEM] * 3,
        scratch=[pltpu.VMEM((rcount, parent_width), F32)],
        name="parent_solve_back",
    )
    px = chips_sum(own + swap(other).astype(F32))
    pxb = px.astype(BF16)

    def leaf_back(
        where_ref, plan_ref, px_ref, own_ref, other_ref, root_ref, rows_ref, w_ref, out_ref, sol_ref,
        x_ref, whole_ref, found_ref,
    ):
        sol_ref[...] = px_ref[where_ref[1]]
        unite(where_ref, own_ref, other_ref, x_ref)
        blocks_of(x_ref, whole_ref, 0, parent_width)
        for b in range(root_width // LANES + 1):
            whole_ref[parent_width // LANES + b] = root_ref[b]
        gather_walk(plan_ref, rows_ref, whole_ref, found_ref)
        for s in range(leaves):
            for j, part in enumerate(split(times(found_ref[s], w_ref[s]), cuts)):
                out_ref[j, s] = part.astype(BF16)

    term, parent_sol = call(
        leaf_back,
        [((cuts, leaves, rcount, leaf_cut), BF16), ((rcount, parent_cols), F32)],
        [where, leaf_plan, px, pxb, swap(pxb), root_whole, leaf_list, pinned(leaf_panel)],
        [SMEM, SMEM] + [VMEM] * 6,
        scratch=[
            pltpu.VMEM((rcount, parent_width), BF16),
            pltpu.VMEM((tall // LANES + 1, rcount, LANES), F32),
            pltpu.VMEM((leaves, rcount, leaf_local), BF16),
        ],
        name="leaf_back",
    )
    tail = scatter_pieces(leaf_pieces(term))

    def leaf_solve_back(tail_ref, y_ref, w_ref, out_ref):
        for s in range(leaves):
            lost = sum(tail_ref[j, s].astype(F32) for j in range(n))
            term = times((y_ref[s] - lost).astype(BF16), w_ref[s])
            for j, part in enumerate(split(term, cuts)):
                out_ref[j, s] = part.astype(BF16)

    term = call(
        leaf_solve_back,
        [((cuts, leaves, rcount, leaf_cut), BF16)],
        [tail, ly, pinned(leaf_inv)],
        [VMEM] * 3,
        name="leaf_solve_back",
    )[0]
    leaf_sol = scatter_pieces(leaf_pieces(term)).astype(F32).sum(0)
    root_mine = jnp.moveaxis(root_whole[:-1], 0, 1).reshape(rcount, root_width)
    root_sol = lax.dynamic_slice_in_dim(root_mine, flat * root_cols, root_cols, 1)
    return (jnp.moveaxis(leaf_sol, 0, 1), parent_sol[:, None, :], root_sol)


def solution(mesh):
    return jax.shard_map(
        shards,
        mesh=mesh,
        in_specs=(
            P(None, "leaf", "rows"),
            P(None, "leaf", "rows"),
            P(None, ("leaf", "rows")),
            P("leaf", "rows", None),
            P("leaf", "rows", None),
            P("leaf", "rows"),
            P("leaf"),
            P("leaf", "rows", None),
            P("leaf", "rows", None),
            P("leaf", "rows"),
            P("leaf"),
            P("rows", None),
        ),
        out_specs=(P(None, "leaf", "rows"), P(None, "leaf", "rows"), P(None, ("leaf", "rows"))),
        check_vma=False,
    )
```

time: 561 us -> 183 us (0.33)
  waiting for transfers between devices: 334 us -> 29.2 us
  blocking collectives: 110 us -> 36.3 us
  matrix products: 43.4 us -> 0 us
  starting transfers between devices: 0.29 us -> 33.2 us
  Pallas kernels: 0 us -> 29.2 us
  other arithmetic: 31.5 us -> 2.4 us
  local copies, waits for them, and re-layouts: 25.9 us -> 49.4 us
  between operations: 14.9 us -> 1.65 us
    reduce_scatter x6 -> x0, waiting for transfers between devices: 281 us -> none  [the longest x1 133 us: shards(): lax.psum_scatter(root_from_leaves, ('leaf', 'rows'), scatter_dimension=1,...]
    all_gather x6 -> x0, blocking collectives: 110 us -> none  [the longest x1 36.6 us: shards(): lax.all_gather(rrb, ('leaf', 'rows'), axis=1, tiled=True)]
    psum x1 -> x0, waiting for transfers between devices: 52.2 us -> none  [shards(): root_full = lax.psum(root_term, 'rows')]
    unnamed x18 -> x52, local copies, waits for them, and re-layouts: 4.23 us -> 48 us
    dot_general x9 -> x0, matrix products: 43.4 us -> none  [the longest x1 10.2 us: shards(): jnp.einsum('rln,lhn->rlh', lax.all_gather(lyb, 'rows', axis=2, tiled=True...]
    all_to_all x0 -> x4, blocking collectives: none -> 36.3 us  [the longest x2 19.1 us: scatter_pieces(): return lax.all_to_all(x, 'rows', 0, 0)]
    pallas_call x0 -> x13, Pallas kernels: none -> 29.2 us  [the longest x11 26.9 us: call(): pl.pallas_call(body, out_shape=[jax.ShapeDtypeStruct(s, d) for s, d in ou...]
    scatter-add x2 -> x0, other arithmetic: 27.3 us -> none  [the longest x1 24.5 us: shards(): local_acc = jnp.zeros((rcount, parent_width + root_width), jnp.float32).a...]
  transfers between devices with their start and end apart: 7 -> 21, of which waited for: 7 -> 16; matrix products, arithmetic and copies ran while one was open for 0% -> 2% of each run, Pallas kernels for 0% -> 3%
where the time goes in v3:
time: 183 us; the launch traced here: 181 us
  local copies, waits for them, and re-layouts  49.4 us (27%)
  blocking collectives  36.3 us (20%)
  starting transfers between devices  33.2 us (18%)
  Pallas kernels  29.2 us (16%)
  waiting for transfers between devices  29.2 us (16%)
  other arithmetic  2.4 us (1%)
    unnamed x52, local copies, waits for them, and re-layouts  48 us
    pallas_call x11, Pallas kernels, call(): pl.pallas_call(body, out_shape=[jax.ShapeDtypeStruct(s, d) for s, d in ou...  26.9 us
    all_to_all x2, blocking collectives, scatter_pieces(): return lax.all_to_all(x, 'rows', 0, 0)  19.1 us
    all_to_all x2, blocking collectives, chips_sum_at_once(): got = lax.all_to_all(b, 'rows', 0, 0, axis_index_groups=groups)  17.2 us
    all_to_all x3, starting transfers between devices, all_gather(): return lax.all_to_all(copies, 'rows', 0, 0)  15 us
    ppermute x6, starting transfers between devices, far(): return lax.ppermute(x, 'rows', [(i, i ^ 2 * k) for i in range(n)])  8.9 us
    ppermute x8, waiting for transfers between devices, swap(): return lax.ppermute(x, 'rows', [(i, i ^ 1) for i in range(n)])  8.09 us
    all_to_all x3, waiting for transfers between devices, all_gather(): return lax.all_to_all(copies, 'rows', 0, 0)  7.84 us
  transfers between devices with their start and end apart: 21, of which 16 were waited for; matrix products, arithmetic and copies ran while one was open for 2% of the time, Pallas kernels for 3%

profile of v3, /device:TPU:0, one launch (start us, length us, event | category | flops | bytes accessed | tf_op | source)
XLA Modules:
  0.0 181.4 jit_solution(14509779382191758608)
XLA Ops:
  2.1 6.3 %all-to-all-start = ((bf16[8,4,8,256]{3,2,1,0:T(8,128)(2,1)}), bf16[8,4,8,256]{3,2,1,0:T(8,128)(2,1)S(1)}, u32[]{:S(2)}, u32[]{:S(2)}) async-start(bf16[8,4,8,256]{3,2,1,0:T(8,128)(2,1)} %broadcast_in_dim.50), calls=%async_computation | async-start | bytes 262144 | tf_op jit(solution)/shard_map/all_to_all | solution.py:206
  9.7 5.8 %copy-done.3 = bf16[4,1024,2048]{2,1,0:T(8,128)(2,1)S(1)} copy-done((bf16[4,1024,2048]{2,1,0:T(8,128)(2,1)S(1)}, bf16[4,1024,2048]{2,1,0:T(8,128)(2,1)}, u32[]{:S(2)}) %copy-start.3) | copy-done | bytes 16777240
  15.4 2.2 %copy-done.17 = bf16[4,256,2048]{2,1,0:T(8,128)(2,1)S(1)} copy-done((bf16[4,256,2048]{2,1,0:T(8,128)(2,1)S(1)}, bf16[4,256,2048]{2,1,0:T(8,128)(2,1)}, u32[]{:S(2)}) %copy-start.17) | copy-done | bytes 4194328
  17.6 1.4 fetch_weights.2
  19.1 5.7 %copy-done = bf16[4,1024,2048]{2,1,0:T(8,128)(2,1)} copy-done((bf16[4,1024,2048]{2,1,0:T(8,128)(2,1)}, bf16[4,1024,2048]{2,1,0:T(8,128)(2,1)S(1)}, u32[]{:S(2)}) %copy-start) | copy-done | bytes 16777240
  24.8 2.0 %copy-done.4 = bf16[4,256,2048]{2,1,0:T(8,128)(2,1)} copy-done((bf16[4,256,2048]{2,1,0:T(8,128)(2,1)}, bf16[4,256,2048]{2,1,0:T(8,128)(2,1)S(1)}, u32[]{:S(2)}) %copy-start.4) | copy-done | bytes 4194328
  26.9 2.2 %copy-done.5 = bf16[4,256,2048]{2,1,0:T(8,128)(2,1)S(1)} copy-done((bf16[4,256,2048]{2,1,0:T(8,128)(2,1)S(1)}, bf16[4,256,2048]{2,1,0:T(8,128)(2,1)}, u32[]{:S(2)}) %copy-start.5) | copy-done | bytes 4194328
  29.0 1.9 %leaf_solve.1 = (f32[4,8,256]{2,1,0:T(8,128)S(1)}, bf16[8,4,8,256]{3,2,1,0:T(8,128)(2,1)}) custom-call(bf16[8,4,8,256]{3,2,1,0:T(8,128)(2,1)S(1)} %all-to-all-done.x_ref, bf16[4,256,2048]{2,1,0:T(8,128)(2,1)S(1)} %copy-done.5), custom_call_target="tpu_custom_call" | custom-call | tf_op jit(solution)/shard_map/leaf_solve/pallas_call | solution.py:25
  30.9 5.1 %all-to-all-start.1 = ((bf16[8,4,8,256]{3,2,1,0:T(8,128)(2,1)}), bf16[8,4,8,256]{3,2,1,0:T(8,128)(2,1)S(1)}, u32[]{:S(2)}, u32[]{:S(2)}) async-start(bf16[8,4,8,256]{3,2,1,0:T(8,128)(2,1)} %get-tuple-element.26), calls=%async_computation.1 | async-start | bytes 262144 | tf_op jit(solution)/shard_map/all_to_all | solution.py:206
  36.8 2.7 %invert_rows.2.inverse_ref = s32[4,65,8,128]{3,2,1,0:T(8,128)S(1)} custom-call(s32[40]{0:T(128)S(1)} %pad_add_fusion.1.plan_ref, s32[4,1024]{1,0:T(4,128)S(1)} %compare_select_fusion.rows_ref), custom_call_target="tpu_custom_call" | custom-call | bytes 16777216 | tf_op jit(solution)/shard_map/invert_rows/pallas_call | solution.py:25
  39.5 3.2 %all-to-all-done.1.x_ref = bf16[8,4,8,256]{3,2,1,0:T(8,128)(2,1)S(1)} async-done(((bf16[8,4,8,256]{3,2,1,0:T(8,128)(2,1)}), bf16[8,4,8,256]{3,2,1,0:T(8,128)(2,1)S(1)}, u32[]{:S(2)}, u32[]{:S(2)}) %all-to-all-start.1) | async-done | bytes 131104 | tf_op jit(solution)/shard_map/all_to_all | solution.py:206
  42.8 5.8 %copy-done.1 = bf16[4,1024,2048]{2,1,0:T(8,128)(2,1)S(1)} copy-done((bf16[4,1024,2048]{2,1,0:T(8,128)(2,1)S(1)}, bf16[4,1024,2048]{2,1,0:T(8,128)(2,1)}, u32[]{:S(2)}) %copy-start.1) | copy-done | bytes 16777240
  48.5 6.1 %leaf_update.1 = (f32[4,8,512]{2,1,0:T(8,128)S(1)}, bf16[4,8,512]{2,1,0:T(8,128)(2,1)S(1)}, f32[32,8,128]{2,1,0:T(8,128)S(1)}) custom-call(s32[4]{0:T(128)S(1)} %pad_add_fusion.refs_2_.where_ref.refs_3_, s32[40]{0:T(128)S(1)} %pad_add_fusion.1.plan_ref, bf16[8,4,8,256]{3,2,1,0:T(8,128)(2,1)S(1)} %all-to-all-done.1.x_ref, ...), custom_call_target="tpu_custom_call" | custom-call | tf_op jit(solution)/shard_map/leaf_update/pallas_call | solution.py:25
  56.9 1.2 collective-permute-start.2
  58.2 2.3 %collective-permute-start.3 = (bf16[4,8,512]{2,1,0:T(8,128)(2,1)S(1)}, bf16[4,8,512]{2,1,0:T(8,128)(2,1)S(1)}, u32[]{:S(2)}, u32[]{:S(2)}) collective-permute-start(bf16[4,8,512]{2,1,0:T(8,128)(2,1)S(1)} %fusion), channel_id=1, source_target_pairs={{0,6},{1,7},{2,4},{3,5},{4,2},{5,3},{6,0},{7,1},{8,14},{9,15},{10,... | collective-permute-start | bytes 98312 | tf_op jit(solution)/shard_map/ppermute | solution.py:220
  60.5 1.2 collective-permute-done.2
  61.8 2.1 %collective-permute-done.3 = bf16[4,8,512]{2,1,0:T(8,128)(2,1)S(1)} collective-permute-done((bf16[4,8,512]{2,1,0:T(8,128)(2,1)S(1)}, bf16[4,8,512]{2,1,0:T(8,128)(2,1)S(1)}, u32[]{:S(2)}, u32[]{:S(2)}) %collective-permute-start.3) | collective-permute-done | bytes 32800 | tf_op jit(solution)/shard_map/ppermute | solution.py:220
  64.0 2.2 %copy-done.12 = bf16[1,512,4096]{2,1,0:T(8,128)(2,1)S(1)} copy-done((bf16[1,512,4096]{2,1,0:T(8,128)(2,1)S(1)}, bf16[1,512,4096]{2,1,0:T(8,128)(2,1)}, u32[]{:S(2)}) %copy-start.12) | copy-done | bytes 4194328
  66.2 2.2 %copy-done.13 = bf16[1,512,4096]{2,1,0:T(8,128)(2,1)S(1)} copy-done((bf16[1,512,4096]{2,1,0:T(8,128)(2,1)S(1)}, bf16[1,512,4096]{2,1,0:T(8,128)(2,1)}, u32[]{:S(2)}) %copy-start.13) | copy-done | bytes 4194328
  68.4 2.2 %copy-done.14 = bf16[512,4096]{1,0:T(8,128)(2,1)S(1)} copy-done((bf16[512,4096]{1,0:T(8,128)(2,1)S(1)}, bf16[512,4096]{1,0:T(8,128)(2,1)}, u32[]{:S(2)}) %copy-start.14) | copy-done | bytes 4194328
  71.5 2.0 %copy-done.15 = bf16[512,4096]{1,0:T(8,128)(2,1)} copy-done((bf16[512,4096]{1,0:T(8,128)(2,1)}, bf16[512,4096]{1,0:T(8,128)(2,1)S(1)}, u32[]{:S(2)}) %copy-start.15) | copy-done | bytes 4194328
  73.5 2.4 %parent_solve.1 = (f32[8,512]{1,0:T(8,128)S(1)}, bf16[8,8,512]{2,1,0:T(8,128)(2,1)}) custom-call(s32[4]{0:T(128)S(1)} %pad_add_fusion.refs_2_.where_ref.refs_3_, bf16[4,8,512]{2,1,0:T(8,128)(2,1)S(1)} %add_convert_fusion.2.own_ref, bf16[4,8,512]{2,1,0:T(8,128)(2,1)S(1)} %collective-permute-done.4.other_ref, bf16[512,4096]{1,0:T(8,128)(2,1)S(1)} %get-tuple-element.30.w_ref), custom_call_target="tpu_custom_call" | custom-call | tf_op jit(solution)/shard_map/parent_solve/pallas_call | solution.py:25
  75.8 2.0 %copy-done.7 = bf16[512,4096]{1,0:T(8,128)(2,1)} copy-done((bf16[512,4096]{1,0:T(8,128)(2,1)}, bf16[512,4096]{1,0:T(8,128)(2,1)S(1)}, u32[]{:S(2)}) %copy-start.7) | copy-done | bytes 4194328
  77.8 3.6 %all-to-all-start.2 = ((bf16[8,8,512]{2,1,0:T(8,128)(2,1)}), bf16[8,8,512]{2,1,0:T(8,128)(2,1)S(1)}, u32[]{:S(2)}, u32[]{:S(2)}) async-start(bf16[8,8,512]{2,1,0:T(8,128)(2,1)} %get-tuple-element.31), calls=%async_computation.2 | async-start | bytes 131072 | tf_op jit(solution)/shard_map/all_to_all | solution.py:206
  82.8 4.6 %all-to-all-done.2.x_ref = bf16[8,8,512]{2,1,0:T(8,128)(2,1)S(1)} async-done(((bf16[8,8,512]{2,1,0:T(8,128)(2,1)}), bf16[8,8,512]{2,1,0:T(8,128)(2,1)S(1)}, u32[]{:S(2)}, u32[]{:S(2)}) %all-to-all-start.2) | async-done | bytes 65568 | tf_op jit(solution)/shard_map/all_to_all | solution.py:206
  87.4 2.2 %copy-done.10 = bf16[512,4096]{1,0:T(8,128)(2,1)S(1)} copy-done((bf16[512,4096]{1,0:T(8,128)(2,1)S(1)}, bf16[512,4096]{1,0:T(8,128)(2,1)}, u32[]{:S(2)}) %copy-start.10) | copy-done | bytes 4194328
  89.6 2.3 %parent_update.1 = (f32[4,8,512]{2,1,0:T(8,128)S(1)}, bf16[4,8,512]{2,1,0:T(8,128)(2,1)S(1)}) custom-call(s32[4]{0:T(128)S(1)} %pad_add_fusion.refs_2_.where_ref.refs_3_, s32[8]{0:T(128)S(1)} %pad_add_fusion.2.plan_ref, bf16[8,8,512]{2,1,0:T(8,128)(2,1)S(1)} %all-to-all-done.2.x_ref, bf16[512,4096]{1,0:T(8,128)(2,1)S(1)} %copy-done.10, ...), custom_call_target="tpu_custom_call" | custom-call | tf_op jit(solution)/shard_map/parent_update/pallas_call | solution.py:25
  93.1 1.6 collective-permute-start.6
  94.8 1.3 collective-permute-start.7
  96.0 2.2 %collective-permute-start.8 = (bf16[4,8,512]{2,1,0:T(8,128)(2,1)S(1)}, bf16[4,8,512]{2,1,0:T(8,128)(2,1)S(1)}, u32[]{:S(2)}, u32[]{:S(2)}) collective-permute-start(bf16[4,8,512]{2,1,0:T(8,128)(2,1)S(1)} %fusion.1), channel_id=1, source_target_pairs={{0,24},{8,0},{16,8},{24,16},{1,25},{9,1},{17,9},{25,17},{2,26},{10... | collective-permute-start | bytes 98312 | tf_op jit(solution)/shard_map/ppermute | solution.py:240
  98.7 1.3 collective-permute-done.8
  100.0 8.3 %all_to_all.40 = bf16[4,4,8,512]{3,2,1,0:T(8,128)(2,1)S(1)} all-to-all(bf16[4,4,8,512]{3,2,1,0:T(8,128)(2,1)S(1)} %broadcast_in_dim.52), channel_id=1, replica_groups={{0,2,4,6},{1,3,5,7},{8,10,12,14},{9,11,13,15},{16,18,20,22},{17,19,21,2..., dimensions={0} | all-to-all | bytes 262144 | tf_op jit(solution)/shard_map/all_to_all | solution.py:232
  109.6 2.2 %copy-done.16 = bf16[512,4096]{1,0:T(8,128)(2,1)S(1)} copy-done((bf16[512,4096]{1,0:T(8,128)(2,1)S(1)}, bf16[512,4096]{1,0:T(8,128)(2,1)}, u32[]{:S(2)}) %copy-start.16) | copy-done | bytes 4194328
  111.8 2.4 %root_solve.1 = (f32[4,8,512]{2,1,0:T(8,128)S(1)}, bf16[4,8,512]{2,1,0:T(8,128)(2,1)S(1)}) custom-call(s32[4]{0:T(128)S(1)} %pad_add_fusion.refs_2_.where_ref.refs_3_, bf16[4,8,512]{2,1,0:T(8,128)(2,1)S(1)} %reduce_sum.33.own_ref, bf16[4,8,512]{2,1,0:T(8,128)(2,1)S(1)} %collective-permute-done.9.other_ref, bf16[512,4096]{1,0:T(8,128)(2,1)S(1)} %copy-done.16), custom_call_target="tpu_custom_call" | custom-call | tf_op jit(solution)/shard_map/root_solve/pallas_call | solution.py:25
  115.5 8.9 %all_to_all.41 = bf16[4,4,8,512]{3,2,1,0:T(8,128)(2,1)S(1)} all-to-all(bf16[4,4,8,512]{3,2,1,0:T(8,128)(2,1)S(1)} %broadcast_in_dim.53), channel_id=1, replica_groups={{0,2,4,6},{1,3,5,7},{8,10,12,14},{9,11,13,15},{16,18,20,22},{17,19,21,2..., dimensions={0} | all-to-all | bytes 262144 | tf_op jit(solution)/shard_map/all_to_all | solution.py:232
  125.7 2.2 %copy-done.11 = bf16[512,4096]{1,0:T(8,128)(2,1)S(1)} copy-done((bf16[512,4096]{1,0:T(8,128)(2,1)S(1)}, bf16[512,4096]{1,0:T(8,128)(2,1)}, u32[]{:S(2)}) %copy-start.11) | copy-done | bytes 4194328
  127.9 1.7 parent_back.1
  129.6 8.3 %all_to_all.42.tail_ref = bf16[8,8,512]{2,1,0:T(8,128)(2,1)S(1)} all-to-all(bf16[8,8,512]{2,1,0:T(8,128)(2,1)S(1)} %get-tuple-element.39), channel_id=1, replica_groups=mesh['leaf'=4,'rows'=8] {'rows'}, dimensions={0} | all-to-all | bytes 131072 | tf_op jit(solution)/shard_map/all_to_all | solution.py:210
  137.9 1.2 parent_solve_back.1
  141.9 2.9 %collective-permute-start.15 = (bf16[4,8,512]{2,1,0:T(8,128)(2,1)S(1)}, bf16[4,8,512]{2,1,0:T(8,128)(2,1)S(1)}, u32[]{:S(2)}, u32[]{:S(2)}) collective-permute-start(bf16[4,8,512]{2,1,0:T(8,128)(2,1)S(1)} %fusion.2), channel_id=1, source_target_pairs={{0,6},{1,7},{2,4},{3,5},{4,2},{5,3},{6,0},{7,1},{8,14},{9,15},{10,... | collective-permute-start | bytes 98312 | tf_op jit(solution)/shard_map/ppermute | solution.py:220
  144.9 1.5 collective-permute-done.14
  146.4 1.3 collective-permute-done.15
  148.9 5.8 %copy-done.2 = bf16[4,1024,2048]{2,1,0:T(8,128)(2,1)S(1)} copy-done((bf16[4,1024,2048]{2,1,0:T(8,128)(2,1)S(1)}, bf16[4,1024,2048]{2,1,0:T(8,128)(2,1)}, u32[]{:S(2)}) %copy-start.2) | copy-done | bytes 16777240
  154.7 3.8 %leaf_back.1 = (bf16[8,4,8,256]{3,2,1,0:T(8,128)(2,1)S(1)}, f32[8,512]{1,0:T(8,128)S(1)}) custom-call(s32[4]{0:T(128)S(1)} %pad_add_fusion.refs_2_.where_ref.refs_3_, s32[40]{0:T(128)S(1)} %pad_add_fusion.1.plan_ref, f32[4,8,512]{2,1,0:T(8,128)S(1)} %get-tuple-element.57.px_ref, bf16[4,8,512]{2,1,0:T(8,128)(2,1)S(1)} %get-tuple-element.56.own_ref, ...), custom_call_target="tpu_custom_call" | custom-call | tf_op jit(solution)/shard_map/leaf_back/pallas_call | solution.py:25
  158.5 10.8 %all_to_all.43.tail_ref = bf16[8,4,8,256]{3,2,1,0:T(8,128)(2,1)S(1)} all-to-all(bf16[8,4,8,256]{3,2,1,0:T(8,128)(2,1)S(1)} %get-tuple-element.44), channel_id=1, replica_groups=mesh['leaf'=4,'rows'=8] {'rows'}, dimensions={0} | all-to-all | bytes 262144 | tf_op jit(solution)/shard_map/all_to_all | solution.py:210
  169.3 1.3 leaf_solve_back.1
  170.6 3.4 %all-to-all-start.7 = ((bf16[8,4,8,256]{3,2,1,0:T(8,128)(2,1)}), bf16[8,4,8,256]{3,2,1,0:T(8,128)(2,1)S(1)}, u32[]{:S(2)}, u32[]{:S(2)}) async-start(bf16[8,4,8,256]{3,2,1,0:T(8,128)(2,1)} %leaf_solve_back.1), calls=%async_computation.7 | async-start | bytes 262144 | tf_op jit(solution)/shard_map/all_to_all | solution.py:210
  175.2 5.5 %all-to-all-done.7 = bf16[8,4,8,256]{3,2,1,0:T(8,128)(2,1)S(1)} async-done(((bf16[8,4,8,256]{3,2,1,0:T(8,128)(2,1)}), bf16[8,4,8,256]{3,2,1,0:T(8,128)(2,1)S(1)}, u32[]{:S(2)}, u32[]{:S(2)}) %all-to-all-start.7) | async-done | bytes 131104 | tf_op jit(solution)/shard_map/all_to_all | solution.py:210
  (97 shorter events, 19.1 us)
Async XLA Ops:
  2.1 24.8 %all-to-all-start = ((bf16[8,4,8,256]{3,2,1,0:T(8,128)(2,1)}), bf16[8,4,8,256]{3,2,1,0:T(8,128)(2,1)S(1)}, u32[]{:S(2)}, u32[]{:S(2)}) async-start(bf16[8,4,8,256]{3,2,1,0:T(8,128)(2,1)} %broadcast_in_dim.50), calls=%async_computation | async-start | bytes 262144 | tf_op jit(solution)/shard_map/all_to_all | solution.py:206
  9.7 5.8 %copy-start.3 = (bf16[4,1024,2048]{2,1,0:T(8,128)(2,1)S(1)}, bf16[4,1024,2048]{2,1,0:T(8,128)(2,1)}, u32[]{:S(2)}) copy-start(bf16[4,1024,2048]{2,1,0:T(8,128)(2,1)} %refs_1_.1) | copy-start | bytes 50331652
  15.4 2.2 %copy-start.17 = (bf16[4,256,2048]{2,1,0:T(8,128)(2,1)S(1)}, bf16[4,256,2048]{2,1,0:T(8,128)(2,1)}, u32[]{:S(2)}) copy-start(bf16[4,256,2048]{2,1,0:T(8,128)(2,1)} %refs_0_.1) | copy-start | bytes 12582916
  17.6 18.4 %copy-start.19 = (f32[8,1,512]{2,1,0:T(1,128)S(1)}, f32[8,1,512]{2,1,0:T(1,128)}, u32[]{:S(2)}) copy-start(f32[8,1,512]{2,1,0:T(1,128)} %param.13) | copy-start | bytes 49156
  17.6 19.1 %copy-start.18 = (s32[4,1024]{1,0:T(4,128)S(1)}, s32[4,1024]{1,0:T(4,128)}, u32[]{:S(2)}) copy-start(s32[4,1024]{1,0:T(4,128)} %param.17) | copy-start | bytes 49156
  19.1 5.8 %copy-start = (bf16[4,1024,2048]{2,1,0:T(8,128)(2,1)}, bf16[4,1024,2048]{2,1,0:T(8,128)(2,1)S(1)}, u32[]{:S(2)}) copy-start(bf16[4,1024,2048]{2,1,0:T(8,128)(2,1)S(1)} %get-tuple-element.27.w_ref) | copy-start | bytes 50331652
  24.8 2.0 %copy-start.4 = (bf16[4,256,2048]{2,1,0:T(8,128)(2,1)}, bf16[4,256,2048]{2,1,0:T(8,128)(2,1)S(1)}, u32[]{:S(2)}) copy-start(bf16[4,256,2048]{2,1,0:T(8,128)(2,1)S(1)} %get-tuple-element.25.w_ref) | copy-start | bytes 12582916
  26.8 9.9 %copy-start.21 = (s32[4]{0:T(128)S(1)}, s32[4]{0:T(128)}, u32[]{:S(2)}) copy-start(s32[4]{0:T(128)} %param.18) | copy-start | bytes 52
  26.9 2.2 %copy-start.5 = (bf16[4,256,2048]{2,1,0:T(8,128)(2,1)S(1)}, bf16[4,256,2048]{2,1,0:T(8,128)(2,1)}, u32[]{:S(2)}) copy-start(bf16[4,256,2048]{2,1,0:T(8,128)(2,1)} %copy-done.4) | copy-start | bytes 12582916
  30.9 11.9 %all-to-all-start.1 = ((bf16[8,4,8,256]{3,2,1,0:T(8,128)(2,1)}), bf16[8,4,8,256]{3,2,1,0:T(8,128)(2,1)S(1)}, u32[]{:S(2)}, u32[]{:S(2)}) async-start(bf16[8,4,8,256]{3,2,1,0:T(8,128)(2,1)} %get-tuple-element.26), calls=%async_computation.1 | async-start | bytes 262144 | tf_op jit(solution)/shard_map/all_to_all | solution.py:206
  42.8 5.8 %copy-start.1 = (bf16[4,1024,2048]{2,1,0:T(8,128)(2,1)S(1)}, bf16[4,1024,2048]{2,1,0:T(8,128)(2,1)}, u32[]{:S(2)}) copy-start(bf16[4,1024,2048]{2,1,0:T(8,128)(2,1)} %copy-done) | copy-start | bytes 50331652
  48.5 6.2 %copy-start.22 = (s32[1,512]{1,0:T(1,128)S(1)}, s32[1,512]{1,0:T(1,128)}, u32[]{:S(2)}) copy-start(s32[1,512]{1,0:T(1,128)} %param.21) | copy-start | bytes 6148
  54.7 1.3 collective-permute-start
  56.0 4.6 %collective-permute-start.1 = (bf16[4,8,512]{2,1,0:T(8,128)(2,1)S(1)}, bf16[4,8,512]{2,1,0:T(8,128)(2,1)S(1)}, u32[]{:S(2)}, u32[]{:S(2)}) collective-permute-start(bf16[4,8,512]{2,1,0:T(8,128)(2,1)S(1)} %fusion), channel_id=1, source_target_pairs={{0,2},{1,3},{2,0},{3,1},{4,6},{5,7},{6,4},{7,5},{8,10},{9,11},{10,... | collective-permute-start | bytes 98312 | tf_op jit(solution)/shard_map/ppermute | solution.py:220
  56.9 4.8 %collective-permute-start.2 = (bf16[4,8,512]{2,1,0:T(8,128)(2,1)S(1)}, bf16[4,8,512]{2,1,0:T(8,128)(2,1)S(1)}, u32[]{:S(2)}, u32[]{:S(2)}) collective-permute-start(bf16[4,8,512]{2,1,0:T(8,128)(2,1)S(1)} %fusion), channel_id=1, source_target_pairs={{0,4},{1,5},{2,6},{3,7},{4,0},{5,1},{6,2},{7,3},{8,12},{9,13},{10,... | collective-permute-start | bytes 98312 | tf_op jit(solution)/shard_map/ppermute | solution.py:220
  58.2 5.7 %collective-permute-start.3 = (bf16[4,8,512]{2,1,0:T(8,128)(2,1)S(1)}, bf16[4,8,512]{2,1,0:T(8,128)(2,1)S(1)}, u32[]{:S(2)}, u32[]{:S(2)}) collective-permute-start(bf16[4,8,512]{2,1,0:T(8,128)(2,1)S(1)} %fusion), channel_id=1, source_target_pairs={{0,6},{1,7},{2,4},{3,5},{4,2},{5,3},{6,0},{7,1},{8,14},{9,15},{10,... | collective-permute-start | bytes 98312 | tf_op jit(solution)/shard_map/ppermute | solution.py:220
  63.9 9.6 %collective-permute-start.4 = (bf16[4,8,512]{2,1,0:T(8,128)(2,1)S(1)}, bf16[4,8,512]{2,1,0:T(8,128)(2,1)S(1)}, u32[]{:S(2)}, u32[]{:S(2)}) collective-permute-start(bf16[4,8,512]{2,1,0:T(8,128)(2,1)S(1)} %add_convert_fusion.2.own_ref), channel_id=1, source_target_pairs={{0,1},{1,0},{2,3},{3,2},{4,5},{5,4},{6,7},{7,6},{8,9},{9,8},{10,11... | collective-permute-start | bytes 98312 | tf_op jit(solution)/shard_map/ppermute | solution.py:215
  64.0 2.2 %copy-start.12 = (bf16[1,512,4096]{2,1,0:T(8,128)(2,1)S(1)}, bf16[1,512,4096]{2,1,0:T(8,128)(2,1)}, u32[]{:S(2)}) copy-start(bf16[1,512,4096]{2,1,0:T(8,128)(2,1)} %param.19) | copy-start | bytes 12582916
  66.2 2.2 %copy-start.13 = (bf16[1,512,4096]{2,1,0:T(8,128)(2,1)S(1)}, bf16[1,512,4096]{2,1,0:T(8,128)(2,1)}, u32[]{:S(2)}) copy-start(bf16[1,512,4096]{2,1,0:T(8,128)(2,1)} %param.20) | copy-start | bytes 12582916
  68.4 2.2 %copy-start.14 = (bf16[512,4096]{1,0:T(8,128)(2,1)S(1)}, bf16[512,4096]{1,0:T(8,128)(2,1)}, u32[]{:S(2)}) copy-start(bf16[512,4096]{1,0:T(8,128)(2,1)} %refs_2_.1) | copy-start | bytes 12582916
  71.4 2.0 %copy-start.15 = (bf16[512,4096]{1,0:T(8,128)(2,1)}, bf16[512,4096]{1,0:T(8,128)(2,1)S(1)}, u32[]{:S(2)}) copy-start(bf16[512,4096]{1,0:T(8,128)(2,1)S(1)} %get-tuple-element.36.w_ref) | copy-start | bytes 12582916
  73.5 2.4 %copy-start.9 = (bf16[512,4096]{1,0:T(8,128)(2,1)}, bf16[512,4096]{1,0:T(8,128)(2,1)S(1)}, u32[]{:S(2)}) copy-start(bf16[512,4096]{1,0:T(8,128)(2,1)S(1)} %get-tuple-element.32.w_ref) | copy-start | bytes 12582916
  73.5 9.3 %copy-start.20 = (f32[8,128]{1,0:T(8,128)S(1)}, f32[8,128]{1,0:T(8,128)}, u32[]{:S(2)}) copy-start(f32[8,128]{1,0:T(8,128)} %param.14) | copy-start | bytes 12292
  75.8 2.0 %copy-start.7 = (bf16[512,4096]{1,0:T(8,128)(2,1)}, bf16[512,4096]{1,0:T(8,128)(2,1)S(1)}, u32[]{:S(2)}) copy-start(bf16[512,4096]{1,0:T(8,128)(2,1)S(1)} %get-tuple-element.30.w_ref) | copy-start | bytes 12582916
  77.8 9.5 %all-to-all-start.2 = ((bf16[8,8,512]{2,1,0:T(8,128)(2,1)}), bf16[8,8,512]{2,1,0:T(8,128)(2,1)S(1)}, u32[]{:S(2)}, u32[]{:S(2)}) async-start(bf16[8,8,512]{2,1,0:T(8,128)(2,1)} %get-tuple-element.31), calls=%async_computation.2 | async-start | bytes 131072 | tf_op jit(solution)/shard_map/all_to_all | solution.py:206
  87.4 2.2 %copy-start.10 = (bf16[512,4096]{1,0:T(8,128)(2,1)S(1)}, bf16[512,4096]{1,0:T(8,128)(2,1)}, u32[]{:S(2)}) copy-start(bf16[512,4096]{1,0:T(8,128)(2,1)} %copy-done.9) | copy-start | bytes 12582916
  91.9 1.3 collective-permute-start.5
  93.1 5.1 %collective-permute-start.6 = (bf16[4,8,512]{2,1,0:T(8,128)(2,1)S(1)}, bf16[4,8,512]{2,1,0:T(8,128)(2,1)S(1)}, u32[]{:S(2)}, u32[]{:S(2)}) collective-permute-start(bf16[4,8,512]{2,1,0:T(8,128)(2,1)S(1)} %fusion.1), channel_id=1, source_target_pairs={{0,8},{8,16},{16,24},{24,0},{1,9},{9,17},{17,25},{25,1},{2,10},{10... | collective-permute-start | bytes 98312 | tf_op jit(solution)/shard_map/ppermute | solution.py:240
  94.8 3.9 %collective-permute-start.7 = (bf16[4,8,512]{2,1,0:T(8,128)(2,1)S(1)}, bf16[4,8,512]{2,1,0:T(8,128)(2,1)S(1)}, u32[]{:S(2)}, u32[]{:S(2)}) collective-permute-start(bf16[4,8,512]{2,1,0:T(8,128)(2,1)S(1)} %fusion.1), channel_id=1, source_target_pairs={{0,16},{8,24},{16,0},{24,8},{1,17},{9,25},{17,1},{25,9},{2,18},{10... | collective-permute-start | bytes 98312 | tf_op jit(solution)/shard_map/ppermute | solution.py:240
  96.0 3.9 %collective-permute-start.8 = (bf16[4,8,512]{2,1,0:T(8,128)(2,1)S(1)}, bf16[4,8,512]{2,1,0:T(8,128)(2,1)S(1)}, u32[]{:S(2)}, u32[]{:S(2)}) collective-permute-start(bf16[4,8,512]{2,1,0:T(8,128)(2,1)S(1)} %fusion.1), channel_id=1, source_target_pairs={{0,24},{8,0},{16,8},{24,16},{1,25},{9,1},{17,9},{25,17},{2,26},{10... | collective-permute-start | bytes 98312 | tf_op jit(solution)/shard_map/ppermute | solution.py:240
  108.3 1.3 collective-permute-start.9
  109.6 2.2 %copy-start.16 = (bf16[512,4096]{1,0:T(8,128)(2,1)S(1)}, bf16[512,4096]{1,0:T(8,128)(2,1)}, u32[]{:S(2)}) copy-start(bf16[512,4096]{1,0:T(8,128)(2,1)} %copy-done.15) | copy-start | bytes 12582916
  114.2 1.3 collective-permute-start.10
  124.4 13.5 %copy-start.8 = (bf16[512,4096]{1,0:T(8,128)(2,1)S(1)}, bf16[512,4096]{1,0:T(8,128)(2,1)}, u32[]{:S(2)}) copy-start(bf16[512,4096]{1,0:T(8,128)(2,1)} %copy-done.7) | copy-start | bytes 12582916
  124.4 1.3 collective-permute-start.11
  125.7 2.2 %copy-start.11 = (bf16[512,4096]{1,0:T(8,128)(2,1)S(1)}, bf16[512,4096]{1,0:T(8,128)(2,1)}, u32[]{:S(2)}) copy-start(bf16[512,4096]{1,0:T(8,128)(2,1)} %copy-done.9) | copy-start | bytes 12582916
  139.1 1.3 collective-permute-start.12
  140.4 4.5 %collective-permute-start.13 = (bf16[4,8,512]{2,1,0:T(8,128)(2,1)S(1)}, bf16[4,8,512]{2,1,0:T(8,128)(2,1)S(1)}, u32[]{:S(2)}, u32[]{:S(2)}) collective-permute-start(bf16[4,8,512]{2,1,0:T(8,128)(2,1)S(1)} %fusion.2), channel_id=1, source_target_pairs={{0,2},{1,3},{2,0},{3,1},{4,6},{5,7},{6,4},{7,5},{8,10},{9,11},{10,... | collective-permute-start | bytes 98312 | tf_op jit(solution)/shard_map/ppermute | solution.py:220
  141.2 5.2 %collective-permute-start.14 = (bf16[4,8,512]{2,1,0:T(8,128)(2,1)S(1)}, bf16[4,8,512]{2,1,0:T(8,128)(2,1)S(1)}, u32[]{:S(2)}, u32[]{:S(2)}) collective-permute-start(bf16[4,8,512]{2,1,0:T(8,128)(2,1)S(1)} %fusion.2), channel_id=1, source_target_pairs={{0,4},{1,5},{2,6},{3,7},{4,0},{5,1},{6,2},{7,3},{8,12},{9,13},{10,... | collective-permute-start | bytes 98312 | tf_op jit(solution)/shard_map/ppermute | solution.py:220
  141.9 5.7 %collective-permute-start.15 = (bf16[4,8,512]{2,1,0:T(8,128)(2,1)S(1)}, bf16[4,8,512]{2,1,0:T(8,128)(2,1)S(1)}, u32[]{:S(2)}, u32[]{:S(2)}) collective-permute-start(bf16[4,8,512]{2,1,0:T(8,128)(2,1)S(1)} %fusion.2), channel_id=1, source_target_pairs={{0,6},{1,7},{2,4},{3,5},{4,2},{5,3},{6,0},{7,1},{8,14},{9,15},{10,... | collective-permute-start | bytes 98312 | tf_op jit(solution)/shard_map/ppermute | solution.py:220
  147.7 1.3 collective-permute-start.16
  148.9 5.8 %copy-start.2 = (bf16[4,1024,2048]{2,1,0:T(8,128)(2,1)S(1)}, bf16[4,1024,2048]{2,1,0:T(8,128)(2,1)}, u32[]{:S(2)}) copy-start(bf16[4,1024,2048]{2,1,0:T(8,128)(2,1)} %copy-done) | copy-start | bytes 50331652
  154.7 14.6 %copy-start.6 = (bf16[4,256,2048]{2,1,0:T(8,128)(2,1)S(1)}, bf16[4,256,2048]{2,1,0:T(8,128)(2,1)}, u32[]{:S(2)}) copy-start(bf16[4,256,2048]{2,1,0:T(8,128)(2,1)} %copy-done.4) | copy-start | bytes 12582916
  170.6 10.1 %all-to-all-start.7 = ((bf16[8,4,8,256]{3,2,1,0:T(8,128)(2,1)}), bf16[8,4,8,256]{3,2,1,0:T(8,128)(2,1)S(1)}, u32[]{:S(2)}, u32[]{:S(2)}) async-start(bf16[8,4,8,256]{3,2,1,0:T(8,128)(2,1)} %leaf_solve_back.1), calls=%async_computation.7 | async-start | bytes 262144 | tf_op jit(solution)/shard_map/all_to_all | solution.py:210

commit v4 on v3

v4 whole, which is shorter than its diff:
```python
import jax
import jax.numpy as jnp
from jax import lax
from jax.experimental import pallas as pl
from jax.experimental.pallas import tpu as pltpu
from jax.sharding import PartitionSpec as P

F32 = jnp.float32
BF16 = jnp.bfloat16
I32 = jnp.int32
LANES = 128
UNROLL = 4

VMEM = pl.BlockSpec(memory_space=pltpu.VMEM)
SMEM = pl.BlockSpec(memory_space=pltpu.SMEM)


def pinned(w):
    return pltpu.with_memory_space_constraint(w, pltpu.VMEM)


def call(
    body, outs, ins, specs, out_specs=None, scratch=(), moved=0, limit=6 << 20, name=None
):
    return pl.pallas_call(
        body,
        out_shape=[jax.ShapeDtypeStruct(s, d) for s, d in outs],
        in_specs=list(specs),
        out_specs=out_specs or [VMEM] * len(outs),
        scratch_shapes=list(scratch),
        cost_estimate=pl.CostEstimate(flops=0, bytes_accessed=moved, transcendentals=0),
        compiler_params=pltpu.CompilerParams(vmem_limit_bytes=limit),
        name=name,
    )(*ins)


def times_transposed(x, w):
    return lax.dot_general(x, w, (((1,), (1,)), ((), ())), preferred_element_type=F32)


def times(x, w):
    return lax.dot_general(x, w, (((1,), (0,)), ((), ())), preferred_element_type=F32)


def walk(plan_ref, sets, tiles, blocks, tile, visit, carry):
    def trip(i, carry):
        at = []
        for s in range(sets):
            lo = plan_ref[s * tiles + tile] + i * UNROLL
            at += [(s, jnp.minimum(lo + u, blocks)) for u in range(UNROLL)]
        return visit(at, carry)

    return lax.fori_loop(0, plan_ref[sets * tiles + tile], trip, carry)


def pick(x, index):
    inside = (index >= 0) & (index < LANES)
    found = jnp.take_along_axis(
        x, index & (LANES - 1), axis=1, mode="promise_in_bounds"
    )
    return jnp.where(inside, found, 0.0)


def prepare(lists, first, heights, widths):
    count = len(lists)

    def one(rows_ref, scalar_ref, height_ref, list_ref, plan_ref, out_ref, first, width):
        sets, length = rows_ref.shape
        tiles, blocks = length // LANES, width // LANES
        out_ref[...] = jnp.full(out_ref.shape, -1, I32)
        used = [height_ref[s] - first for s in range(sets)]
        lane = lax.broadcasted_iota(I32, (1, LANES), 1)
        for tile in range(tiles):
            lanes = slice(tile * LANES, (tile + 1) * LANES)
            spots = lax.broadcasted_iota(I32, (LANES, LANES), 0) + (tile * LANES + 1)
            cols, trips = [], 0
            for s in range(sets):
                line = jnp.where(lane + tile * LANES < used[s], rows_ref[s : s + 1, lanes], -1)
                list_ref[s : s + 1, lanes] = line
                cols.append(jnp.transpose(jnp.broadcast_to(line, (LANES, LANES))))
                end = jnp.maximum(jnp.minimum(used[s], (tile + 1) * LANES) - 1, 0)
                lo = lax.shift_right_logical(scalar_ref[s, tile * LANES], 7)
                hi = lax.shift_right_logical(scalar_ref[s, end], 7)
                met = used[s] > tile * LANES
                plan_ref[s * tiles + tile] = jnp.where(met, lo, blocks)
                span = jnp.where(met, hi - lo + UNROLL, 0)
                trips = jnp.maximum(trips, lax.div(span, UNROLL))
            plan_ref[sets * tiles + tile] = trips

            def visit(at, carry):
                across = lax.broadcasted_iota(I32, (LANES, LANES), 1)
                got = []
                for s, block in at:
                    hit = cols[s] == across + block * LANES
                    got.append(jnp.sum(jnp.where(hit, spots, 0), axis=0, keepdims=True))
                for (s, block), g in zip(at, got):
                    out_ref[s, block] += jnp.broadcast_to(g, out_ref.shape[2:])
                return carry

            walk(plan_ref, sets, tiles, blocks, tile, visit, 0)

    def body(*refs):
        ins, outs = refs[: 3 * count], refs[3 * count :]
        row = lax.axis_index("rows")
        for i in range(count):
            one(*ins[3 * i : 3 * i + 3], *outs[3 * i : 3 * i + 3], row * first[i], widths[i])

    shapes, specs, ins = [], [], []
    for rows, height, width in zip(lists, heights, widths):
        sets, length = rows.shape
        shapes += [
            (rows.shape, I32),
            (((sets + 1) * (length // LANES),), I32),
            ((sets, width // LANES + 1, 8, LANES), I32),
        ]
        ins += [rows, rows, height]
        specs += [VMEM, SMEM, SMEM]
    got = call(
        body,
        shapes,
        ins,
        specs,
        out_specs=[VMEM, SMEM, VMEM] * count,
        moved=16 << 20,
        limit=4 << 20,
        name="prepare",
    )
    return [got[3 * i : 3 * i + 3] for i in range(count)]


def scatter_walk(plan_ref, inverse_ref, update_ref, acc_ref, tiles):
    sets, blocks = inverse_ref.shape[0], inverse_ref.shape[1] - 1
    for tile in range(tiles):

        def visit(at, carry):
            got = []
            for s, block in at:
                x = update_ref[s, :, tile * LANES : (tile + 1) * LANES]
                got.append(pick(x, inverse_ref[s, block] - tile * LANES))
            for (s, block), g in zip(at, got):
                acc_ref[block] += g
            return carry

        walk(plan_ref, sets, tiles, blocks, tile, visit, 0)


def gather_walk(plan_ref, rows_ref, source_ref, out_ref):
    sets, length = rows_ref.shape
    tiles, blocks = length // LANES, source_ref.shape[0] - 1
    for tile in range(tiles):
        index = [
            jnp.broadcast_to(
                rows_ref[s : s + 1, tile * LANES : (tile + 1) * LANES], (8, LANES)
            )
            for s in range(sets)
        ]

        def visit(at, carry):
            carry = list(carry)
            for s, block in at:
                carry[s] = carry[s] + pick(source_ref[block], index[s] - block * LANES)
            return tuple(carry)

        zero = tuple(jnp.zeros((8, LANES), F32) for _ in range(sets))
        found = walk(plan_ref, sets, tiles, blocks, tile, visit, zero)
        for s in range(sets):
            out_ref[s, :, tile * LANES : (tile + 1) * LANES] = found[s].astype(out_ref.dtype)


def joined(ref, *at):
    return jnp.concatenate([ref[(j,) + at] for j in range(ref.shape[0])], axis=1)


def split(value, n):
    w = value.shape[1] // n
    return [value[:, j * w : (j + 1) * w] for j in range(n)]


def core():
    return lax.axis_index("rows") & 1


def chip():
    return lax.axis_index("rows") // 2


def spot(r, w):
    return pl.ds(pl.multiple_of(r * w, LANES), w)


def unite(own_ref, other_ref, out_ref, *at, xor=False):
    odd, w = core(), own_ref.shape[-1]
    for k in range(own_ref.shape[0]):
        c = chip() ^ k if xor else k
        out_ref[:, spot(2 * c + odd, w)] = own_ref[(k,) + at]
        out_ref[:, spot(2 * c + 1 - odd, w)] = other_ref[(k,) + at]


def deal(value_ref, own_ref, other_ref):
    odd = core()
    chips, _, w = own_ref.shape
    for k in range(chips):
        own_ref[k] = value_ref[:, spot(2 * k + odd, w)].astype(own_ref.dtype)
        other_ref[k] = value_ref[:, spot(2 * k + 1 - odd, w)].astype(other_ref.dtype)


def all_gather(copies):
    return lax.all_to_all(copies, "rows", 0, 0)


def scatter_pieces(x):
    return lax.all_to_all(x, "rows", 0, 0)


def swap(x):
    n = lax.axis_size("rows")
    return lax.ppermute(x, "rows", [(i, i ^ 1) for i in range(n)])


def far(x, k):
    n = lax.axis_size("rows")
    return lax.ppermute(x, "rows", [(i, i ^ (2 * k)) for i in range(n)])


def chips_sum(x):
    b = x.astype(BF16)
    return x + sum(far(b, k).astype(F32) for k in range(1, lax.axis_size("rows") // 2))


def leaf_sum(x):
    n = lax.axis_size("leaf")
    b = x.astype(BF16)
    for k in range(1, n):
        x = x + lax.ppermute(b, "leaf", [(i, (i + k) % n) for i in range(n)]).astype(F32)
    return x


def shards(
    leaf_rhs,
    parent_rhs,
    root_rhs,
    leaf_inv,
    leaf_panel,
    leaf_rows,
    leaf_height,
    parent_inv,
    parent_panel,
    parent_rows,
    parent_height,
    root_inv,
):
    n = lax.axis_size("rows")
    chips = n // 2
    rcount, leaves, leaf_cols = leaf_rhs.shape
    leaf_local, leaf_width = leaf_panel.shape[1:]
    parent_cols, parent_width = parent_inv.shape[1:]
    parent_local = parent_panel.shape[1]
    root_width = root_inv.shape[1]
    root_cols = root_rhs.shape[1]
    piece = root_width // n
    tall = parent_width + root_width
    leaf_aligned = leaf_cols % LANES == 0
    root_aligned = root_cols % LANES == 0

    def flat():
        return lax.axis_index("leaf") * n + lax.axis_index("rows")

    def leaf_gather(x, copies):
        if leaf_aligned and not copies:
            own = jnp.stack([x] + [far(x, k) for k in range(1, chips)])
            return own, swap(own)
        got = all_gather(x if copies else jnp.broadcast_to(x[None], (n,) + x.shape))
        if leaf_aligned:
            return (got,)
        return (jnp.moveaxis(got, 0, 2).reshape(1, leaves, rcount, leaf_width),)

    rhs = root_rhs
    if not root_aligned:
        rhs = lax.dynamic_update_slice_in_dim(
            jnp.zeros((rcount, root_width), F32), root_rhs, flat() * root_cols, 1
        )
    lb = leaf_gather(jnp.moveaxis(leaf_rhs.astype(BF16), 1, 0), False)
    prepared = prepare(
        [leaf_rows, parent_rows],
        [leaf_local, parent_local],
        [leaf_height, parent_height],
        [tall, root_width],
    )
    lb, prepared, parent_rhs, rhs = lax.optimization_barrier(
        (lb, prepared, parent_rhs[:, 0], rhs)
    )
    (leaf_list, leaf_plan, leaf_inverse), (parent_list, parent_plan, parent_inverse) = prepared

    def leaf_solve(*refs):
        x_refs, (w_ref, y_ref, copies_ref, x_ref) = refs[: len(lb)], refs[len(lb) :]
        for s in range(leaves):
            if len(lb) == 2:
                unite(*x_refs, x_ref, s, xor=True)
                x = x_ref[...]
            else:
                x = joined(x_refs[0], s)
            y = times_transposed(x, w_ref[s])
            y_ref[s] = y
            for j in range(n):
                copies_ref[j, s] = y.astype(BF16)

    ly, lyb = call(
        leaf_solve,
        [((leaves, rcount, leaf_cols), F32), ((n, leaves, rcount, leaf_cols), BF16)],
        [*lb, pinned(leaf_inv)],
        [VMEM] * (len(lb) + 1),
        scratch=[pltpu.VMEM((rcount, leaf_width), BF16)],
        name="leaf_solve",
    )
    (lyb,) = leaf_gather(lyb, True)

    def leaf_update(
        plan_ref, x_ref, w_ref, inverse_ref, rhs_ref, own_ref, other_ref, root_ref,
        update_ref, acc_ref, sum_ref,
    ):
        acc_ref[...] = jnp.zeros(acc_ref.shape, F32)
        for s in range(leaves):
            update_ref[s] = times_transposed(joined(x_ref, s), w_ref[s])
        scatter_walk(plan_ref, inverse_ref, update_ref, acc_ref, leaf_local // LANES)
        for b in range(parent_width // LANES):
            sum_ref[:, b * LANES : (b + 1) * LANES] = -acc_ref[b]
        sum_ref[:, spot(lax.axis_index("rows"), parent_cols)] += rhs_ref[...]
        deal(sum_ref, own_ref, other_ref)
        for b in range(root_width // LANES):
            root_ref[b] = acc_ref[parent_width // LANES + b]

    own, other, root_acc = call(
        leaf_update,
        [
            ((chips, rcount, parent_cols), F32),
            ((chips, rcount, parent_cols), BF16),
            ((root_width // LANES, rcount, LANES), F32),
        ],
        [leaf_plan, lyb, pinned(leaf_panel), leaf_inverse, parent_rhs],
        [SMEM] + [VMEM] * 4,
        scratch=[
            pltpu.VMEM((leaves, rcount, leaf_local), F32),
            pltpu.VMEM((tall // LANES + 1, rcount, LANES), F32),
            pltpu.VMEM((rcount, parent_width), F32),
        ],
        name="leaf_update",
    )
    prb = chips_sum(own + swap(other).astype(F32)).astype(BF16)

    def parent_solve(own_ref, other_ref, w_ref, y_ref, copies_ref, x_ref):
        unite(own_ref, other_ref, x_ref)
        y = times_transposed(x_ref[...], w_ref[0])
        y_ref[...] = y
        for j in range(n):
            copies_ref[j] = y.astype(BF16)

    py, pyb = call(
        parent_solve,
        [((rcount, parent_cols), F32), ((n, rcount, parent_cols), BF16)],
        [prb, swap(prb), pinned(parent_inv)],
        [VMEM] * 3,
        scratch=[pltpu.VMEM((rcount, parent_width), BF16)],
        name="parent_solve",
    )
    pyb = all_gather(pyb)

    def parent_update(
        plan_ref, x_ref, w_ref, inverse_ref, root_ref, rhs_ref, own_ref, other_ref,
        update_ref, acc_ref, sum_ref,
    ):
        for b in range(root_width // LANES):
            acc_ref[b] = root_ref[b]
        update_ref[0] = times_transposed(joined(x_ref), w_ref[0])
        scatter_walk(plan_ref, inverse_ref, update_ref, acc_ref, parent_local // LANES)
        for b in range(root_width // LANES):
            sum_ref[:, b * LANES : (b + 1) * LANES] = -acc_ref[b]
        if root_aligned:
            sum_ref[:, spot(flat(), root_cols)] += rhs_ref[...]
        else:
            sum_ref[...] += rhs_ref[...]
        deal(sum_ref, own_ref, other_ref)

    own, other = call(
        parent_update,
        [((chips, rcount, piece), F32), ((chips, rcount, piece), BF16)],
        [parent_plan, pyb, pinned(parent_panel), parent_inverse, root_acc, rhs],
        [SMEM] + [VMEM] * 5,
        scratch=[
            pltpu.VMEM((1, rcount, parent_local), F32),
            pltpu.VMEM((root_width // LANES + 1, rcount, LANES), F32),
            pltpu.VMEM((rcount, root_width), F32),
        ],
        name="parent_update",
    )
    rrb = chips_sum(leaf_sum(own + swap(other).astype(F32))).astype(BF16)

    def root_solve(own_ref, other_ref, w_ref, own_out, other_out, x_ref, sum_ref):
        unite(own_ref, other_ref, x_ref)
        y = times_transposed(x_ref[...], w_ref[...]).astype(BF16)
        sum_ref[...] = times(y, w_ref[...])
        deal(sum_ref, own_out, other_out)

    own, other = call(
        root_solve,
        [((chips, rcount, piece), F32), ((chips, rcount, piece), BF16)],
        [rrb, swap(rrb), pinned(root_inv)],
        [VMEM] * 3,
        scratch=[pltpu.VMEM((rcount, root_width), BF16), pltpu.VMEM((rcount, root_width), F32)],
        name="root_solve",
    )
    rxb = chips_sum(own + swap(other).astype(F32)).astype(BF16)

    def blocks_of(source_ref, target_ref, start, width):
        for b in range(width // LANES):
            target_ref[start + b] = source_ref[:, b * LANES : (b + 1) * LANES].astype(F32)

    def parent_back(
        plan_ref, own_ref, other_ref, rows_ref, w_ref, out_ref, whole_ref, sol_ref,
        x_ref, found_ref,
    ):
        unite(own_ref, other_ref, x_ref)
        if root_aligned:
            sol_ref[...] = x_ref[:, spot(flat(), root_cols)].astype(F32)
        else:
            sol_ref[...] = x_ref[...].astype(F32)
        blocks_of(x_ref, whole_ref, 0, root_width)
        whole_ref[root_width // LANES] = jnp.zeros((rcount, LANES), F32)
        gather_walk(plan_ref, rows_ref, whole_ref, found_ref)
        term = times(found_ref[0], w_ref[0])
        for j, part in enumerate(split(term, n)):
            out_ref[j] = part.astype(BF16)

    term, root_whole, root_sol = call(
        parent_back,
        [
            ((n, rcount, parent_cols), BF16),
            ((root_width // LANES + 1, rcount, LANES), F32),
            ((rcount, root_cols if root_aligned else root_width), F32),
        ],
        [parent_plan, rxb, swap(rxb), parent_list, pinned(parent_panel)],
        [SMEM] + [VMEM] * 4,
        scratch=[
            pltpu.VMEM((rcount, root_width), BF16),
            pltpu.VMEM((1, rcount, parent_local), BF16),
        ],
        name="parent_back",
    )
    tail = scatter_pieces(term)

    def parent_solve_back(tail_ref, y_ref, w_ref, own_ref, other_ref, sum_ref):
        lost = sum(tail_ref[j].astype(F32) for j in range(n))
        sum_ref[...] = times((y_ref[...] - lost).astype(BF16), w_ref[0])
        deal(sum_ref, own_ref, other_ref)

    own, other = call(
        parent_solve_back,
        [((chips, rcount, parent_cols), F32), ((chips, rcount, parent_cols), BF16)],
        [tail, py, pinned(parent_inv)],
        [VMEM] * 3,
        scratch=[pltpu.VMEM((rcount, parent_width), F32)],
        name="parent_solve_back",
    )
    px = chips_sum(own + swap(other).astype(F32))
    pxb = px.astype(BF16)

    def ancestors(
        plan_ref, px_ref, own_ref, other_ref, root_ref, rows_ref, sol_ref,
        x_ref, whole_ref, found_ref,
    ):
        sol_ref[...] = px_ref[chip()]
        unite(own_ref, other_ref, x_ref)
        blocks_of(x_ref, whole_ref, 0, parent_width)
        for b in range(root_width // LANES + 1):
            whole_ref[parent_width // LANES + b] = root_ref[b]
        gather_walk(plan_ref, rows_ref, whole_ref, found_ref)

    def terms(x_ref, w_ref, out_ref, odd):
        for k in range(chips):
            cols = spot(2 * (chip() ^ k) + odd, leaf_cols)
            for s in range(leaves):
                out_ref[k, s] = times(x_ref[s], w_ref[s, :, cols]).astype(out_ref.dtype)

    split_terms = (chips, leaves, rcount, leaf_cols)

    def own_terms(x, w, name):
        def body(x_ref, w_ref, out_ref):
            terms(x_ref, w_ref, out_ref, core())

        return call(
            body, [(split_terms, F32)], [x, pinned(w)], [VMEM] * 2, moved=12 << 20, name=name
        )[0]

    def leaf_reduce(own, other):
        other = swap(other)
        sums = [own[k] + other[k].astype(F32) for k in range(chips)]
        return [sums[0]] + [far(sums[k].astype(BF16), k) for k in range(1, chips)]

    def all_terms(x_ref, w_ref, out_ref):
        for s in range(leaves):
            out_ref[s] = times(x_ref[s], w_ref[s]).astype(BF16)

    def pieces_apart(term):
        return jnp.moveaxis(term.reshape(leaves, rcount, n, leaf_cols), 2, 0)

    whole_term = (leaves, rcount, leaf_width)
    found_shape = (leaves, rcount, leaf_local)
    scratch = [
        pltpu.VMEM((rcount, parent_width), BF16),
        pltpu.VMEM((tall // LANES + 1, rcount, LANES), F32),
    ]

    def leaf_back(*refs):
        ins, (w_ref, out_ref, sol_ref, found_ref, x_ref, whole_ref) = refs[:6], refs[6:]
        ancestors(*ins, sol_ref, x_ref, whole_ref, found_ref)
        if leaf_aligned:
            terms(found_ref, w_ref, out_ref, 1 - core())
        else:
            all_terms(found_ref, w_ref, out_ref)

    term, parent_sol, found = call(
        leaf_back,
        [
            (split_terms if leaf_aligned else whole_term, BF16),
            ((rcount, parent_cols), F32),
            (found_shape, BF16),
        ],
        [leaf_plan, px, pxb, swap(pxb), root_whole, leaf_list, pinned(leaf_panel)],
        [SMEM] + [VMEM] * 6,
        scratch=scratch,
        name="leaf_back",
    )
    if leaf_aligned:
        tails = leaf_reduce(own_terms(found, leaf_panel, "leaf_back_own"), term)
    else:
        tails = [scatter_pieces(pieces_apart(term)).astype(F32).sum(0)]

    def leaf_solve_back(*refs):
        tail_refs, (y_ref, w_ref, out_ref, v_ref) = refs[: len(tails)], refs[len(tails) :]
        for s in range(leaves):
            lost = sum(ref[s].astype(F32) for ref in tail_refs)
            v_ref[s] = (y_ref[s] - lost).astype(BF16)
        if leaf_aligned:
            terms(v_ref, w_ref, out_ref, 1 - core())
        else:
            all_terms(v_ref, w_ref, out_ref)

    term, lvb = call(
        leaf_solve_back,
        [
            (split_terms if leaf_aligned else whole_term, BF16),
            ((leaves, rcount, leaf_cols), BF16),
        ],
        [*tails, ly, pinned(leaf_inv)],
        [VMEM] * (len(tails) + 2),
        name="leaf_solve_back",
    )
    if leaf_aligned:
        parts = leaf_reduce(own_terms(lvb, leaf_inv, "leaf_solve_back_own"), term)
        leaf_sol = sum(p.astype(F32) for p in parts)
    else:
        leaf_sol = scatter_pieces(pieces_apart(term)).astype(F32).sum(0)
    if not root_aligned:
        root_sol = lax.dynamic_slice_in_dim(root_sol, flat() * root_cols, root_cols, 1)
    return (jnp.moveaxis(leaf_sol, 0, 1), parent_sol[:, None, :], root_sol)


def solution(mesh):
    return jax.shard_map(
        shards,
        mesh=mesh,
        in_specs=(
            P(None, "leaf", "rows"),
            P(None, "leaf", "rows"),
            P(None, ("leaf", "rows")),
            P("leaf", "rows", None),
            P("leaf", "rows", None),
            P("leaf", "rows"),
            P("leaf"),
            P("leaf", "rows", None),
            P("leaf", "rows", None),
            P("leaf", "rows"),
            P("leaf"),
            P("rows", None),
        ),
        out_specs=(P(None, "leaf", "rows"), P(None, "leaf", "rows"), P(None, ("leaf", "rows"))),
        check_vma=False,
    )
```

time: 183 us -> 138 us (0.75)
  local copies, waits for them, and re-layouts: 49.4 us -> 12.8 us
  blocking collectives: 36.3 us -> 27 us
  waiting for transfers between devices: 29.2 us -> 34.6 us
  Pallas kernels: 29.2 us -> 24.2 us
  starting transfers between devices: 33.2 us -> 37.2 us
  other arithmetic: 2.4 us -> 0.23 us
    unnamed x52 -> x32, local copies, waits for them, and re-layouts: 48 us -> 12.8 us
    ppermute x6 -> x21, starting transfers between devices: 8.9 us -> 31.4 us  [far(): return lax.ppermute(x, 'rows', [(i, i ^ 2 * k) for i in range(n)])]
    all_to_all x4 -> x0, starting transfers between devices: 18.4 us -> none  [the longest x3 15 us: all_gather(): return lax.all_to_all(copies, 'rows', 0, 0)]
    ppermute x6 -> x21, waiting for transfers between devices: 6.1 us -> 19.5 us  [far(): return lax.ppermute(x, 'rows', [(i, i ^ 2 * k) for i in range(n)])]
    all_to_all x4 -> x0, waiting for transfers between devices: 13.3 us -> none  [the longest x3 7.84 us: all_gather(): return lax.all_to_all(copies, 'rows', 0, 0)]
    all_to_all x2 -> x1, blocking collectives: 19.1 us -> 8.65 us  [scatter_pieces(): return lax.all_to_all(x, 'rows', 0, 0)]
    ppermute x3, waiting for transfers between devices: 1.69 us -> 4.81 us  [leaf_sum(): lax.ppermute(b, 'leaf', [(i, (i + k) % n) for i in range(n)]).astype(F32)]
    pallas_call x11 -> x12, Pallas kernels: 26.9 us -> 24.2 us  [call(): pl.pallas_call(body, out_shape=[jax.ShapeDtypeStruct(s, d) for s, d in ou...]
  transfers between devices with their start and end apart: 21 -> 35, of which waited for: 16 -> 29; matrix products, arithmetic and copies ran while one was open for 2% -> 1% of each run, Pallas kernels for 3% -> 4%
where the time goes in v4:
time: 138 us
  starting transfers between devices  37.2 us (27%)
  waiting for transfers between devices  34.6 us (25%)
  blocking collectives  27 us (20%)
  Pallas kernels  24.2 us (18%)
  local copies, waits for them, and re-layouts  12.8 us (9%)
  between operations  1.52 us (1%)
    ppermute x21, starting transfers between devices, far(): return lax.ppermute(x, 'rows', [(i, i ^ 2 * k) for i in range(n)])  31.4 us
    pallas_call x12, Pallas kernels, call(): pl.pallas_call(body, out_shape=[jax.ShapeDtypeStruct(s, d) for s, d in ou...  24.2 us
    ppermute x21, waiting for transfers between devices, far(): return lax.ppermute(x, 'rows', [(i, i ^ 2 * k) for i in range(n)])  19.5 us
    all_to_all x2, blocking collectives, all_gather(): return lax.all_to_all(copies, 'rows', 0, 0)  18.4 us
    unnamed x32, local copies, waits for them, and re-layouts  12.8 us
    ppermute x11, waiting for transfers between devices, swap(): return lax.ppermute(x, 'rows', [(i, i ^ 1) for i in range(n)])  10.3 us
    all_to_all x1, blocking collectives, scatter_pieces(): return lax.all_to_all(x, 'rows', 0, 0)  8.65 us
    ppermute x3, starting transfers between devices, leaf_sum(): lax.ppermute(b, 'leaf', [(i, (i + k) % n) for i in range(n)]).astype(F32)  4.93 us
  transfers between devices with their start and end apart: 35, of which 29 were waited for; matrix products, arithmetic and copies ran while one was open for 1% of the time, Pallas kernels for 4%

profile of v4, /device:TPU:0, one launch (start us, length us, event | category | flops | bytes accessed | tf_op | source)
XLA Modules:
  0.0 137.6 jit_solution(7004222599274822912)
XLA Ops:
  1.4 3.0 %collective-permute-start = (bf16[4,8,256]{2,1,0:T(8,128)(2,1)S(1)}, bf16[4,8,256]{2,1,0:T(8,128)(2,1)S(1)}, u32[]{:S(2)}, u32[]{:S(2)}) collective-permute-start(bf16[4,8,256]{2,1,0:T(8,128)(2,1)S(1)} %bitcast.43), channel_id=1, source_target_pairs={{0,2},{1,3},{2,0},{3,1},{4,6},{5,7},{6,4},{7,5},{8,10},{9,11},{10,... | collective-permute-start | bytes 49160 | tf_op jit(solution)/shard_map/ppermute | solution.py:222
  4.4 2.5 %collective-permute-start.2 = (bf16[4,8,256]{2,1,0:T(8,128)(2,1)S(1)}, bf16[4,8,256]{2,1,0:T(8,128)(2,1)S(1)}, u32[]{:S(2)}, u32[]{:S(2)}) collective-permute-start(bf16[4,8,256]{2,1,0:T(8,128)(2,1)S(1)} %bitcast.44), channel_id=1, source_target_pairs={{0,6},{1,7},{2,4},{3,5},{4,2},{5,3},{6,0},{7,1},{8,14},{9,15},{10,... | collective-permute-start | bytes 49160 | tf_op jit(solution)/shard_map/ppermute | solution.py:222
  7.0 3.2 %collective-permute-done.2 = bf16[4,8,256]{2,1,0:T(8,128)(2,1)S(1)} collective-permute-done((bf16[4,8,256]{2,1,0:T(8,128)(2,1)S(1)}, bf16[4,8,256]{2,1,0:T(8,128)(2,1)S(1)}, u32[]{:S(2)}, u32[]{:S(2)}) %collective-permute-start.2) | collective-permute-done | bytes 16416 | tf_op jit(solution)/shard_map/ppermute | solution.py:222
  10.2 1.4 collective-permute-done.1
  15.1 4.2 %prepare.1 = (s32[4,1024]{1,0:T(4,128)S(1)}, s32[40]{0:T(128)S(1)}, s32[4,65,8,128]{3,2,1,0:T(8,128)S(1)}, s32[1,512]{1,0:T(1,128)S(1)}, s32[8]{0:T(128)S(1)}, /*index=5*/s32[1,33,8,128]{3,2,1,0:T(8,128)S(1)}) custom-call(s32[4,1024]{1,0:T(4,128)S(1)} %copy-done.6, s32[4,1024]{1,0:T(4,128)S(1)} %copy-done.6, s32[4]{0:T(128)S(1)} %copy-done.9, ...), custom_call_target="tpu_custom_call" | custom-call | bytes 16777216 | tf_op jit(solution)/shard_map/prepare/pallas_call | solution.py:25
  19.3 2.2 %copy-done.1 = bf16[4,256,2048]{2,1,0:T(8,128)(2,1)S(1)} copy-done((bf16[4,256,2048]{2,1,0:T(8,128)(2,1)S(1)}, bf16[4,256,2048]{2,1,0:T(8,128)(2,1)}, u32[]{:S(2)}) %copy-start.1) | copy-done | bytes 4194328
  21.5 1.2 leaf_solve.1
  22.7 9.2 %all_to_all.15.x_ref = bf16[8,4,8,256]{3,2,1,0:T(8,128)(2,1)S(1)} all-to-all(bf16[8,4,8,256]{3,2,1,0:T(8,128)(2,1)S(1)} %get-tuple-element.50), channel_id=1, replica_groups=mesh['leaf'=4,'rows'=8] {'rows'}, dimensions={0} | all-to-all | bytes 262144 | tf_op jit(solution)/shard_map/all_to_all | solution.py:208
  31.9 5.8 %copy-done = bf16[4,1024,2048]{2,1,0:T(8,128)(2,1)S(1)} copy-done((bf16[4,1024,2048]{2,1,0:T(8,128)(2,1)S(1)}, bf16[4,1024,2048]{2,1,0:T(8,128)(2,1)}, u32[]{:S(2)}) %copy-start) | copy-done | bytes 16777240
  37.6 6.1 %leaf_update.1 = (f32[4,8,512]{2,1,0:T(8,128)S(1)}, bf16[4,8,512]{2,1,0:T(8,128)(2,1)S(1)}, f32[32,8,128]{2,1,0:T(8,128)S(1)}) custom-call(s32[40]{0:T(128)S(1)} %get-tuple-element.46.plan_ref.refs_0_, bf16[8,4,8,256]{3,2,1,0:T(8,128)(2,1)S(1)} %all_to_all.15.x_ref, bf16[4,1024,2048]{2,1,0:T(8,128)(2,1)S(1)} %copy-done, ...), custom_call_target="tpu_custom_call" | custom-call | tf_op jit(solution)/shard_map/leaf_update/pallas_call | solution.py:25
  43.9 1.2 collective-permute-done.4
  46.1 1.4 %collective-permute-start.6 = (bf16[4,8,512]{2,1,0:T(8,128)(2,1)S(1)}, bf16[4,8,512]{2,1,0:T(8,128)(2,1)S(1)}, u32[]{:S(2)}, u32[]{:S(2)}) collective-permute-start(bf16[4,8,512]{2,1,0:T(8,128)(2,1)S(1)} %fusion), channel_id=1, source_target_pairs={{0,4},{1,5},{2,6},{3,7},{4,0},{5,1},{6,2},{7,3},{8,12},{9,13},{10,... | collective-permute-start | bytes 98312 | tf_op jit(solution)/shard_map/ppermute | solution.py:222
  47.5 2.0 %collective-permute-start.5 = (bf16[4,8,512]{2,1,0:T(8,128)(2,1)S(1)}, bf16[4,8,512]{2,1,0:T(8,128)(2,1)S(1)}, u32[]{:S(2)}, u32[]{:S(2)}) collective-permute-start(bf16[4,8,512]{2,1,0:T(8,128)(2,1)S(1)} %fusion), channel_id=1, source_target_pairs={{0,2},{1,3},{2,0},{3,1},{4,6},{5,7},{6,4},{7,5},{8,10},{9,11},{10,... | collective-permute-start | bytes 98312 | tf_op jit(solution)/shard_map/ppermute | solution.py:222
  49.5 1.5 %collective-permute-done.7 = bf16[4,8,512]{2,1,0:T(8,128)(2,1)S(1)} collective-permute-done((bf16[4,8,512]{2,1,0:T(8,128)(2,1)S(1)}, bf16[4,8,512]{2,1,0:T(8,128)(2,1)S(1)}, u32[]{:S(2)}, u32[]{:S(2)}) %collective-permute-start.7) | collective-permute-done | bytes 32800 | tf_op jit(solution)/shard_map/ppermute | solution.py:222
  51.7 1.2 collective-permute-done.8.other_ref
  52.9 1.2 parent_solve.1
  54.1 9.2 %all_to_all.16.x_ref = bf16[8,8,512]{2,1,0:T(8,128)(2,1)S(1)} all-to-all(bf16[8,8,512]{2,1,0:T(8,128)(2,1)S(1)} %get-tuple-element.55), channel_id=1, replica_groups=mesh['leaf'=4,'rows'=8] {'rows'}, dimensions={0} | all-to-all | bytes 131072 | tf_op jit(solution)/shard_map/all_to_all | solution.py:208
  63.3 2.1 %parent_update.1 = (f32[4,8,512]{2,1,0:T(8,128)S(1)}, bf16[4,8,512]{2,1,0:T(8,128)(2,1)S(1)}) custom-call(s32[8]{0:T(128)S(1)} %get-tuple-element.47.plan_ref, bf16[8,8,512]{2,1,0:T(8,128)(2,1)S(1)} %all_to_all.16.x_ref, bf16[1,512,4096]{2,1,0:T(8,128)(2,1)S(1)} %copy-done.3, s32[1,33,8,128]{3,2,1,0:T(8,128)S(1)} %get-tuple-element.56.inverse_ref, ...), custom_call_target="tpu_custom_call" | custom-call | tf_op jit(solution)/shard_map/parent_update/pallas_call | solution.py:25
  65.5 1.2 collective-permute-done.9
  66.7 3.0 %collective-permute-start.12 = (bf16[4,8,512]{2,1,0:T(8,128)(2,1)S(1)}, bf16[4,8,512]{2,1,0:T(8,128)(2,1)S(1)}, u32[]{:S(2)}, u32[]{:S(2)}) collective-permute-start(bf16[4,8,512]{2,1,0:T(8,128)(2,1)S(1)} %fusion.1), channel_id=1, source_target_pairs={{0,24},{8,0},{16,8},{24,16},{1,25},{9,1},{17,9},{25,17},{2,26},{10... | collective-permute-start | bytes 98312 | tf_op jit(solution)/shard_map/ppermute | solution.py:234
  69.8 1.9 %collective-permute-start.11 = (bf16[4,8,512]{2,1,0:T(8,128)(2,1)S(1)}, bf16[4,8,512]{2,1,0:T(8,128)(2,1)S(1)}, u32[]{:S(2)}, u32[]{:S(2)}) collective-permute-start(bf16[4,8,512]{2,1,0:T(8,128)(2,1)S(1)} %fusion.1), channel_id=1, source_target_pairs={{0,16},{8,24},{16,0},{24,8},{1,17},{9,25},{17,1},{25,9},{2,18},{10... | collective-permute-start | bytes 98312 | tf_op jit(solution)/shard_map/ppermute | solution.py:234
  72.1 1.6 %collective-permute-done.11 = bf16[4,8,512]{2,1,0:T(8,128)(2,1)S(1)} collective-permute-done((bf16[4,8,512]{2,1,0:T(8,128)(2,1)S(1)}, bf16[4,8,512]{2,1,0:T(8,128)(2,1)S(1)}, u32[]{:S(2)}, u32[]{:S(2)}) %collective-permute-start.11) | collective-permute-done | bytes 32800 | tf_op jit(solution)/shard_map/ppermute | solution.py:234
  73.7 2.8 %collective-permute-done.10 = bf16[4,8,512]{2,1,0:T(8,128)(2,1)S(1)} collective-permute-done((bf16[4,8,512]{2,1,0:T(8,128)(2,1)S(1)}, bf16[4,8,512]{2,1,0:T(8,128)(2,1)S(1)}, u32[]{:S(2)}, u32[]{:S(2)}) %collective-permute-start.10) | collective-permute-done | bytes 32800 | tf_op jit(solution)/shard_map/ppermute | solution.py:234
  77.1 1.7 %collective-permute-start.14 = (bf16[4,8,512]{2,1,0:T(8,128)(2,1)S(1)}, bf16[4,8,512]{2,1,0:T(8,128)(2,1)S(1)}, u32[]{:S(2)}, u32[]{:S(2)}) collective-permute-start(bf16[4,8,512]{2,1,0:T(8,128)(2,1)S(1)} %fusion.24), channel_id=1, source_target_pairs={{0,4},{1,5},{2,6},{3,7},{4,0},{5,1},{6,2},{7,3},{8,12},{9,13},{10,... | collective-permute-start | bytes 98312 | tf_op jit(solution)/shard_map/ppermute | solution.py:222
  78.8 2.2 %collective-permute-start.13 = (bf16[4,8,512]{2,1,0:T(8,128)(2,1)S(1)}, bf16[4,8,512]{2,1,0:T(8,128)(2,1)S(1)}, u32[]{:S(2)}, u32[]{:S(2)}) collective-permute-start(bf16[4,8,512]{2,1,0:T(8,128)(2,1)S(1)} %fusion.24), channel_id=1, source_target_pairs={{0,2},{1,3},{2,0},{3,1},{4,6},{5,7},{6,4},{7,5},{8,10},{9,11},{10,... | collective-permute-start | bytes 98312 | tf_op jit(solution)/shard_map/ppermute | solution.py:222
  80.9 1.3 collective-permute-done.15
  83.0 1.2 collective-permute-done.16.other_ref
  84.2 1.8 %root_solve.1 = (f32[4,8,512]{2,1,0:T(8,128)S(1)}, bf16[4,8,512]{2,1,0:T(8,128)(2,1)S(1)}) custom-call(bf16[4,8,512]{2,1,0:T(8,128)(2,1)S(1)} %add_convert_fusion.1.own_ref, bf16[4,8,512]{2,1,0:T(8,128)(2,1)S(1)} %collective-permute-done.16.other_ref, bf16[512,4096]{1,0:T(8,128)(2,1)S(1)} %copy-done.5), custom_call_target="tpu_custom_call" | custom-call | tf_op jit(solution)/shard_map/root_solve/pallas_call | solution.py:25
  87.2 2.4 %collective-permute-start.20 = (bf16[4,8,512]{2,1,0:T(8,128)(2,1)S(1)}, bf16[4,8,512]{2,1,0:T(8,128)(2,1)S(1)}, u32[]{:S(2)}, u32[]{:S(2)}) collective-permute-start(bf16[4,8,512]{2,1,0:T(8,128)(2,1)S(1)} %fusion.2), channel_id=1, source_target_pairs={{0,6},{1,7},{2,4},{3,5},{4,2},{5,3},{6,0},{7,1},{8,14},{9,15},{10,... | collective-permute-start | bytes 98312 | tf_op jit(solution)/shard_map/ppermute | solution.py:222
  89.6 1.1 collective-permute-start.19
  91.7 1.7 %collective-permute-done.20 = bf16[4,8,512]{2,1,0:T(8,128)(2,1)S(1)} collective-permute-done((bf16[4,8,512]{2,1,0:T(8,128)(2,1)S(1)}, bf16[4,8,512]{2,1,0:T(8,128)(2,1)S(1)}, u32[]{:S(2)}, u32[]{:S(2)}) %collective-permute-start.20) | collective-permute-done | bytes 32800 | tf_op jit(solution)/shard_map/ppermute | solution.py:222
  93.3 1.1 collective-permute-done.19
  94.9 1.2 collective-permute-done.21.other_ref
  96.1 2.0 %parent_back.1 = (bf16[8,8,512]{2,1,0:T(8,128)(2,1)S(1)}, f32[33,8,128]{2,1,0:T(8,128)S(1)}, f32[8,128]{1,0:T(8,128)}) custom-call(s32[8]{0:T(128)S(1)} %get-tuple-element.47.plan_ref, bf16[4,8,512]{2,1,0:T(8,128)(2,1)S(1)} %add_convert_fusion.own_ref, bf16[4,8,512]{2,1,0:T(8,128)(2,1)S(1)} %collective-permute-done.21.other_ref, ...), custom_call_target="tpu_custom_call" | custom-call | tf_op jit(solution)/shard_map/parent_back/pallas_call | solution.py:25
  98.1 8.7 %all_to_all.17.tail_ref = bf16[8,8,512]{2,1,0:T(8,128)(2,1)S(1)} all-to-all(bf16[8,8,512]{2,1,0:T(8,128)(2,1)S(1)} %get-tuple-element.64), channel_id=1, replica_groups=mesh['leaf'=4,'rows'=8] {'rows'}, dimensions={0} | all-to-all | bytes 131072 | tf_op jit(solution)/shard_map/all_to_all | solution.py:212
  107.5 1.2 collective-permute-done.22
  109.6 1.3 collective-permute-start.24
  111.0 2.2 %collective-permute-start.23 = (bf16[4,8,512]{2,1,0:T(8,128)(2,1)S(1)}, bf16[4,8,512]{2,1,0:T(8,128)(2,1)S(1)}, u32[]{:S(2)}, u32[]{:S(2)}) collective-permute-start(bf16[4,8,512]{2,1,0:T(8,128)(2,1)S(1)} %fusion.3), channel_id=1, source_target_pairs={{0,2},{1,3},{2,0},{3,1},{4,6},{5,7},{6,4},{7,5},{8,10},{9,11},{10,... | collective-permute-start | bytes 98312 | tf_op jit(solution)/shard_map/ppermute | solution.py:222
  113.1 1.6 %collective-permute-done.25 = bf16[4,8,512]{2,1,0:T(8,128)(2,1)S(1)} collective-permute-done((bf16[4,8,512]{2,1,0:T(8,128)(2,1)S(1)}, bf16[4,8,512]{2,1,0:T(8,128)(2,1)S(1)}, u32[]{:S(2)}, u32[]{:S(2)}) %collective-permute-start.25) | collective-permute-done | bytes 32800 | tf_op jit(solution)/shard_map/ppermute | solution.py:222
  115.3 1.2 collective-permute-done.26.refs_3_
  116.5 2.7 %leaf_back.1 = (bf16[4,4,8,256]{3,2,1,0:T(8,128)(2,1)S(1)}, f32[8,512]{1,0:T(8,128)S(1)}, bf16[4,8,1024]{2,1,0:T(8,128)(2,1)S(1)}) custom-call(s32[40]{0:T(128)S(1)} %get-tuple-element.46.plan_ref.refs_0_, f32[4,8,512]{2,1,0:T(8,128)S(1)} %get-tuple-element.81.refs_1_, bf16[4,8,512]{2,1,0:T(8,128)(2,1)S(1)} %get-tuple-element.80.refs_2_, ...), custom_call_target="tpu_custom_call" | custom-call | tf_op jit(solution)/shard_map/leaf_back/pallas_call | solution.py:25
  119.4 1.2 leaf_back_own.1
  120.7 1.7 %collective-permute-start.30 = (bf16[4,8,256]{2,1,0:T(8,128)(2,1)S(1)}, bf16[4,8,256]{2,1,0:T(8,128)(2,1)S(1)}, u32[]{:S(2)}, u32[]{:S(2)}) collective-permute-start(bf16[4,8,256]{2,1,0:T(8,128)(2,1)S(1)} %get-tuple-element.85), channel_id=1, source_target_pairs={{0,6},{1,7},{2,4},{3,5},{4,2},{5,3},{6,0},{7,1},{8,14},{9,15},{10,... | collective-permute-start | bytes 49160 | tf_op jit(solution)/shard_map/ppermute | solution.py:222
  122.4 1.7 %collective-permute-start.29 = (bf16[4,8,256]{2,1,0:T(8,128)(2,1)S(1)}, bf16[4,8,256]{2,1,0:T(8,128)(2,1)S(1)}, u32[]{:S(2)}, u32[]{:S(2)}) collective-permute-start(bf16[4,8,256]{2,1,0:T(8,128)(2,1)S(1)} %get-tuple-element.86), channel_id=1, source_target_pairs={{0,4},{1,5},{2,6},{3,7},{4,0},{5,1},{6,2},{7,3},{8,12},{9,13},{10,... | collective-permute-start | bytes 49160 | tf_op jit(solution)/shard_map/ppermute | solution.py:222
  125.1 1.2 collective-permute-done.30.refs_3_
  129.5 1.1 collective-permute-start.32
  130.6 1.6 %collective-permute-start.34 = (bf16[4,8,256]{2,1,0:T(8,128)(2,1)S(1)}, bf16[4,8,256]{2,1,0:T(8,128)(2,1)S(1)}, u32[]{:S(2)}, u32[]{:S(2)}) collective-permute-start(bf16[4,8,256]{2,1,0:T(8,128)(2,1)S(1)} %get-tuple-element.83), channel_id=1, source_target_pairs={{0,6},{1,7},{2,4},{3,5},{4,2},{5,3},{6,0},{7,1},{8,14},{9,15},{10,... | collective-permute-start | bytes 49160 | tf_op jit(solution)/shard_map/ppermute | solution.py:222
  133.7 2.4 %collective-permute-done.34 = bf16[4,8,256]{2,1,0:T(8,128)(2,1)S(1)} collective-permute-done((bf16[4,8,256]{2,1,0:T(8,128)(2,1)S(1)}, bf16[4,8,256]{2,1,0:T(8,128)(2,1)S(1)}, u32[]{:S(2)}, u32[]{:S(2)}) %collective-permute-start.34) | collective-permute-done | bytes 16416 | tf_op jit(solution)/shard_map/ppermute | solution.py:222
  (83 shorter events, 19.2 us)
Async XLA Ops:
  1.4 5.6 %collective-permute-start = (bf16[4,8,256]{2,1,0:T(8,128)(2,1)S(1)}, bf16[4,8,256]{2,1,0:T(8,128)(2,1)S(1)}, u32[]{:S(2)}, u32[]{:S(2)}) collective-permute-start(bf16[4,8,256]{2,1,0:T(8,128)(2,1)S(1)} %bitcast.43), channel_id=1, source_target_pairs={{0,2},{1,3},{2,0},{3,1},{4,6},{5,7},{6,4},{7,5},{8,10},{9,11},{10,... | collective-permute-start | bytes 49160 | tf_op jit(solution)/shard_map/ppermute | solution.py:222
  4.4 5.8 %collective-permute-start.2 = (bf16[4,8,256]{2,1,0:T(8,128)(2,1)S(1)}, bf16[4,8,256]{2,1,0:T(8,128)(2,1)S(1)}, u32[]{:S(2)}, u32[]{:S(2)}) collective-permute-start(bf16[4,8,256]{2,1,0:T(8,128)(2,1)S(1)} %bitcast.44), channel_id=1, source_target_pairs={{0,6},{1,7},{2,4},{3,5},{4,2},{5,3},{6,0},{7,1},{8,14},{9,15},{10,... | collective-permute-start | bytes 49160 | tf_op jit(solution)/shard_map/ppermute | solution.py:222
  6.9 4.6 %collective-permute-start.1 = (bf16[4,8,256]{2,1,0:T(8,128)(2,1)S(1)}, bf16[4,8,256]{2,1,0:T(8,128)(2,1)S(1)}, u32[]{:S(2)}, u32[]{:S(2)}) collective-permute-start(bf16[4,8,256]{2,1,0:T(8,128)(2,1)S(1)} %bitcast.45), channel_id=1, source_target_pairs={{0,4},{1,5},{2,6},{3,7},{4,0},{5,1},{6,2},{7,3},{8,12},{9,13},{10,... | collective-permute-start | bytes 49160 | tf_op jit(solution)/shard_map/ppermute | solution.py:222
  11.6 7.7 %collective-permute-start.3 = (bf16[4,4,8,256]{3,2,1,0:T(8,128)(2,1)S(1)}, bf16[4,4,8,256]{3,2,1,0:T(8,128)(2,1)S(1)}, u32[]{:S(2)}, u32[]{:S(2)}) collective-permute-start(bf16[4,4,8,256]{3,2,1,0:T(8,128)(2,1)S(1)} %pad_maximum_fusion.refs_0_), channel_id=1, source_target_pairs={{0,1},{1,0},{2,3},{3,2},{4,5},{5,4},{6,7},{7,6},{8,9},{9,8},{10,11... | collective-permute-start | bytes 196616 | tf_op jit(solution)/shard_map/ppermute | solution.py:217
  13.0 0.7 copy-start.6
  13.7 0.7 copy-start.7
  19.3 2.2 %copy-start.1 = (bf16[4,256,2048]{2,1,0:T(8,128)(2,1)S(1)}, bf16[4,256,2048]{2,1,0:T(8,128)(2,1)}, u32[]{:S(2)}) copy-start(bf16[4,256,2048]{2,1,0:T(8,128)(2,1)} %w_ref.15) | copy-start | bytes 12582916
  31.9 5.8 %copy-start = (bf16[4,1024,2048]{2,1,0:T(8,128)(2,1)S(1)}, bf16[4,1024,2048]{2,1,0:T(8,128)(2,1)}, u32[]{:S(2)}) copy-start(bf16[4,1024,2048]{2,1,0:T(8,128)(2,1)} %w_ref.14) | copy-start | bytes 50331652
  37.6 15.3 %copy-start.4 = (bf16[1,512,4096]{2,1,0:T(8,128)(2,1)S(1)}, bf16[1,512,4096]{2,1,0:T(8,128)(2,1)}, u32[]{:S(2)}) copy-start(bf16[1,512,4096]{2,1,0:T(8,128)(2,1)} %w_ref.13) | copy-start | bytes 12582916
  37.6 78.8 %slice-start = ((s8[16777216]{0:T(1024)(128)(4,1)}), s8[4194304]{0:T(1024)(128)(4,1)S(1)}, s32[]{:S(2)}) async-start(s8[16777216]{0:T(1024)(128)(4,1)} %bitcast.39), calls=%async_computation.3 | async-start | bytes 8388608
  37.6 78.8 %slice-start.1 = ((s8[16777216]{0:T(1024)(128)(4,1)}), s8[4194304]{0:T(1024)(128)(4,1)S(1)}, s32[]{:S(2)}) async-start(s8[16777216]{0:T(1024)(128)(4,1)} %bitcast.39), calls=%async_computation.4 | async-start | bytes 8388608
  43.8 19.5 %copy-start.3 = (bf16[1,512,4096]{2,1,0:T(8,128)(2,1)S(1)}, bf16[1,512,4096]{2,1,0:T(8,128)(2,1)}, u32[]{:S(2)}) copy-start(bf16[1,512,4096]{2,1,0:T(8,128)(2,1)} %w_ref.12) | copy-start | bytes 12582916
  43.8 19.5 %copy-start.8 = (f32[8,128]{1,0:T(8,128)S(1)}, f32[8,128]{1,0:T(8,128)}, u32[]{:S(2)}) copy-start(f32[8,128]{1,0:T(8,128)} %rhs_ref) | copy-start | bytes 12292
  43.8 1.3 collective-permute-start.4
  45.1 6.0 %collective-permute-start.7 = (bf16[4,8,512]{2,1,0:T(8,128)(2,1)S(1)}, bf16[4,8,512]{2,1,0:T(8,128)(2,1)S(1)}, u32[]{:S(2)}, u32[]{:S(2)}) collective-permute-start(bf16[4,8,512]{2,1,0:T(8,128)(2,1)S(1)} %fusion), channel_id=1, source_target_pairs={{0,6},{1,7},{2,4},{3,5},{4,2},{5,3},{6,0},{7,1},{8,14},{9,15},{10,... | collective-permute-start | bytes 98312 | tf_op jit(solution)/shard_map/ppermute | solution.py:222
  46.1 5.5 %collective-permute-start.6 = (bf16[4,8,512]{2,1,0:T(8,128)(2,1)S(1)}, bf16[4,8,512]{2,1,0:T(8,128)(2,1)S(1)}, u32[]{:S(2)}, u32[]{:S(2)}) collective-permute-start(bf16[4,8,512]{2,1,0:T(8,128)(2,1)S(1)} %fusion), channel_id=1, source_target_pairs={{0,4},{1,5},{2,6},{3,7},{4,0},{5,1},{6,2},{7,3},{8,12},{9,13},{10,... | collective-permute-start | bytes 98312 | tf_op jit(solution)/shard_map/ppermute | solution.py:222
  47.5 4.1 %collective-permute-start.5 = (bf16[4,8,512]{2,1,0:T(8,128)(2,1)S(1)}, bf16[4,8,512]{2,1,0:T(8,128)(2,1)S(1)}, u32[]{:S(2)}, u32[]{:S(2)}) collective-permute-start(bf16[4,8,512]{2,1,0:T(8,128)(2,1)S(1)} %fusion), channel_id=1, source_target_pairs={{0,2},{1,3},{2,0},{3,1},{4,6},{5,7},{6,4},{7,5},{8,10},{9,11},{10,... | collective-permute-start | bytes 98312 | tf_op jit(solution)/shard_map/ppermute | solution.py:222
  51.6 32.6 %copy-start.5 = (bf16[512,4096]{1,0:T(8,128)(2,1)S(1)}, bf16[512,4096]{1,0:T(8,128)(2,1)}, u32[]{:S(2)}) copy-start(bf16[512,4096]{1,0:T(8,128)(2,1)} %w_ref.11) | copy-start | bytes 12582916
  51.6 64.8 %slice-start.2 = ((s8[16777216]{0:T(1024)(128)(4,1)}), s8[4194304]{0:T(1024)(128)(4,1)S(1)}, s32[]{:S(2)}) async-start(s8[16777216]{0:T(1024)(128)(4,1)} %bitcast.39), calls=%async_computation.5 | async-start | bytes 8388608
  51.6 1.3 collective-permute-start.8
  65.4 1.3 collective-permute-start.9
  66.7 5.4 %collective-permute-start.12 = (bf16[4,8,512]{2,1,0:T(8,128)(2,1)S(1)}, bf16[4,8,512]{2,1,0:T(8,128)(2,1)S(1)}, u32[]{:S(2)}, u32[]{:S(2)}) collective-permute-start(bf16[4,8,512]{2,1,0:T(8,128)(2,1)S(1)} %fusion.1), channel_id=1, source_target_pairs={{0,24},{8,0},{16,8},{24,16},{1,25},{9,1},{17,9},{25,17},{2,26},{10... | collective-permute-start | bytes 98312 | tf_op jit(solution)/shard_map/ppermute | solution.py:234
  69.8 3.9 %collective-permute-start.11 = (bf16[4,8,512]{2,1,0:T(8,128)(2,1)S(1)}, bf16[4,8,512]{2,1,0:T(8,128)(2,1)S(1)}, u32[]{:S(2)}, u32[]{:S(2)}) collective-permute-start(bf16[4,8,512]{2,1,0:T(8,128)(2,1)S(1)} %fusion.1), channel_id=1, source_target_pairs={{0,16},{8,24},{16,0},{24,8},{1,17},{9,25},{17,1},{25,9},{2,18},{10... | collective-permute-start | bytes 98312 | tf_op jit(solution)/shard_map/ppermute | solution.py:234
  71.6 4.8 %collective-permute-start.10 = (bf16[4,8,512]{2,1,0:T(8,128)(2,1)S(1)}, bf16[4,8,512]{2,1,0:T(8,128)(2,1)S(1)}, u32[]{:S(2)}, u32[]{:S(2)}) collective-permute-start(bf16[4,8,512]{2,1,0:T(8,128)(2,1)S(1)} %fusion.1), channel_id=1, source_target_pairs={{0,8},{8,16},{16,24},{24,0},{1,9},{9,17},{17,25},{25,1},{2,10},{10... | collective-permute-start | bytes 98312 | tf_op jit(solution)/shard_map/ppermute | solution.py:234
  76.5 5.8 %collective-permute-start.15 = (bf16[4,8,512]{2,1,0:T(8,128)(2,1)S(1)}, bf16[4,8,512]{2,1,0:T(8,128)(2,1)S(1)}, u32[]{:S(2)}, u32[]{:S(2)}) collective-permute-start(bf16[4,8,512]{2,1,0:T(8,128)(2,1)S(1)} %fusion.24), channel_id=1, source_target_pairs={{0,6},{1,7},{2,4},{3,5},{4,2},{5,3},{6,0},{7,1},{8,14},{9,15},{10,... | collective-permute-start | bytes 98312 | tf_op jit(solution)/shard_map/ppermute | solution.py:222
  77.1 5.2 %collective-permute-start.14 = (bf16[4,8,512]{2,1,0:T(8,128)(2,1)S(1)}, bf16[4,8,512]{2,1,0:T(8,128)(2,1)S(1)}, u32[]{:S(2)}, u32[]{:S(2)}) collective-permute-start(bf16[4,8,512]{2,1,0:T(8,128)(2,1)S(1)} %fusion.24), channel_id=1, source_target_pairs={{0,4},{1,5},{2,6},{3,7},{4,0},{5,1},{6,2},{7,3},{8,12},{9,13},{10,... | collective-permute-start | bytes 98312 | tf_op jit(solution)/shard_map/ppermute | solution.py:222
  78.8 4.1 %collective-permute-start.13 = (bf16[4,8,512]{2,1,0:T(8,128)(2,1)S(1)}, bf16[4,8,512]{2,1,0:T(8,128)(2,1)S(1)}, u32[]{:S(2)}, u32[]{:S(2)}) collective-permute-start(bf16[4,8,512]{2,1,0:T(8,128)(2,1)S(1)} %fusion.24), channel_id=1, source_target_pairs={{0,2},{1,3},{2,0},{3,1},{4,6},{5,7},{6,4},{7,5},{8,10},{9,11},{10,... | collective-permute-start | bytes 98312 | tf_op jit(solution)/shard_map/ppermute | solution.py:222
  82.9 33.6 %slice-start.3 = ((s8[16777216]{0:T(1024)(128)(4,1)}), s8[4194304]{0:T(1024)(128)(4,1)S(1)}, s32[]{:S(2)}) async-start(s8[16777216]{0:T(1024)(128)(4,1)} %bitcast.39), calls=%async_computation.6 | async-start | bytes 8388608
  82.9 1.3 collective-permute-start.16
  86.0 1.2 collective-permute-start.17
  87.2 6.1 %collective-permute-start.20 = (bf16[4,8,512]{2,1,0:T(8,128)(2,1)S(1)}, bf16[4,8,512]{2,1,0:T(8,128)(2,1)S(1)}, u32[]{:S(2)}, u32[]{:S(2)}) collective-permute-start(bf16[4,8,512]{2,1,0:T(8,128)(2,1)S(1)} %fusion.2), channel_id=1, source_target_pairs={{0,6},{1,7},{2,4},{3,5},{4,2},{5,3},{6,0},{7,1},{8,14},{9,15},{10,... | collective-permute-start | bytes 98312 | tf_op jit(solution)/shard_map/ppermute | solution.py:222
  89.6 4.8 %collective-permute-start.19 = (bf16[4,8,512]{2,1,0:T(8,128)(2,1)S(1)}, bf16[4,8,512]{2,1,0:T(8,128)(2,1)S(1)}, u32[]{:S(2)}, u32[]{:S(2)}) collective-permute-start(bf16[4,8,512]{2,1,0:T(8,128)(2,1)S(1)} %fusion.2), channel_id=1, source_target_pairs={{0,4},{1,5},{2,6},{3,7},{4,0},{5,1},{6,2},{7,3},{8,12},{9,13},{10,... | collective-permute-start | bytes 98312 | tf_op jit(solution)/shard_map/ppermute | solution.py:222
  90.8 4.0 %collective-permute-start.18 = (bf16[4,8,512]{2,1,0:T(8,128)(2,1)S(1)}, bf16[4,8,512]{2,1,0:T(8,128)(2,1)S(1)}, u32[]{:S(2)}, u32[]{:S(2)}) collective-permute-start(bf16[4,8,512]{2,1,0:T(8,128)(2,1)S(1)} %fusion.2), channel_id=1, source_target_pairs={{0,2},{1,3},{2,0},{3,1},{4,6},{5,7},{6,4},{7,5},{8,10},{9,11},{10,... | collective-permute-start | bytes 98312 | tf_op jit(solution)/shard_map/ppermute | solution.py:222
  94.8 1.3 collective-permute-start.21
  107.5 1.2 collective-permute-start.22
  108.7 6.1 %collective-permute-start.25 = (bf16[4,8,512]{2,1,0:T(8,128)(2,1)S(1)}, bf16[4,8,512]{2,1,0:T(8,128)(2,1)S(1)}, u32[]{:S(2)}, u32[]{:S(2)}) collective-permute-start(bf16[4,8,512]{2,1,0:T(8,128)(2,1)S(1)} %fusion.3), channel_id=1, source_target_pairs={{0,6},{1,7},{2,4},{3,5},{4,2},{5,3},{6,0},{7,1},{8,14},{9,15},{10,... | collective-permute-start | bytes 98312 | tf_op jit(solution)/shard_map/ppermute | solution.py:222
  109.6 5.2 %collective-permute-start.24 = (bf16[4,8,512]{2,1,0:T(8,128)(2,1)S(1)}, bf16[4,8,512]{2,1,0:T(8,128)(2,1)S(1)}, u32[]{:S(2)}, u32[]{:S(2)}) collective-permute-start(bf16[4,8,512]{2,1,0:T(8,128)(2,1)S(1)} %fusion.3), channel_id=1, source_target_pairs={{0,4},{1,5},{2,6},{3,7},{4,0},{5,1},{6,2},{7,3},{8,12},{9,13},{10,... | collective-permute-start | bytes 98312 | tf_op jit(solution)/shard_map/ppermute | solution.py:222
  111.0 4.2 %collective-permute-start.23 = (bf16[4,8,512]{2,1,0:T(8,128)(2,1)S(1)}, bf16[4,8,512]{2,1,0:T(8,128)(2,1)S(1)}, u32[]{:S(2)}, u32[]{:S(2)}) collective-permute-start(bf16[4,8,512]{2,1,0:T(8,128)(2,1)S(1)} %fusion.3), channel_id=1, source_target_pairs={{0,2},{1,3},{2,0},{3,1},{4,6},{5,7},{6,4},{7,5},{8,10},{9,11},{10,... | collective-permute-start | bytes 98312 | tf_op jit(solution)/shard_map/ppermute | solution.py:222
  115.2 1.3 collective-permute-start.26
  119.2 1.4 %collective-permute-start.27 = (bf16[4,4,8,256]{3,2,1,0:T(8,128)(2,1)S(1)}, bf16[4,4,8,256]{3,2,1,0:T(8,128)(2,1)S(1)}, u32[]{:S(2)}, u32[]{:S(2)}) collective-permute-start(bf16[4,4,8,256]{3,2,1,0:T(8,128)(2,1)S(1)} %get-tuple-element.71), channel_id=1, source_target_pairs={{0,1},{1,0},{2,3},{3,2},{4,5},{5,4},{6,7},{7,6},{8,9},{9,8},{10,11... | collective-permute-start | bytes 196616 | tf_op jit(solution)/shard_map/ppermute | solution.py:217
  119.4 8.5 %copy-start.2 = (bf16[4,256,2048]{2,1,0:T(8,128)(2,1)S(1)}, bf16[4,256,2048]{2,1,0:T(8,128)(2,1)}, u32[]{:S(2)}) copy-start(bf16[4,256,2048]{2,1,0:T(8,128)(2,1)} %w_ref.15) | copy-start | bytes 12582916
  120.7 5.7 %collective-permute-start.30 = (bf16[4,8,256]{2,1,0:T(8,128)(2,1)S(1)}, bf16[4,8,256]{2,1,0:T(8,128)(2,1)S(1)}, u32[]{:S(2)}, u32[]{:S(2)}) collective-permute-start(bf16[4,8,256]{2,1,0:T(8,128)(2,1)S(1)} %get-tuple-element.85), channel_id=1, source_target_pairs={{0,6},{1,7},{2,4},{3,5},{4,2},{5,3},{6,0},{7,1},{8,14},{9,15},{10,... | collective-permute-start | bytes 49160 | tf_op jit(solution)/shard_map/ppermute | solution.py:222
  122.4 4.6 %collective-permute-start.29 = (bf16[4,8,256]{2,1,0:T(8,128)(2,1)S(1)}, bf16[4,8,256]{2,1,0:T(8,128)(2,1)S(1)}, u32[]{:S(2)}, u32[]{:S(2)}) collective-permute-start(bf16[4,8,256]{2,1,0:T(8,128)(2,1)S(1)} %get-tuple-element.86), channel_id=1, source_target_pairs={{0,4},{1,5},{2,6},{3,7},{4,0},{5,1},{6,2},{7,3},{8,12},{9,13},{10,... | collective-permute-start | bytes 49160 | tf_op jit(solution)/shard_map/ppermute | solution.py:222
  124.1 3.7 %collective-permute-start.28 = (bf16[4,8,256]{2,1,0:T(8,128)(2,1)S(1)}, bf16[4,8,256]{2,1,0:T(8,128)(2,1)S(1)}, u32[]{:S(2)}, u32[]{:S(2)}) collective-permute-start(bf16[4,8,256]{2,1,0:T(8,128)(2,1)S(1)} %get-tuple-element.87), channel_id=1, source_target_pairs={{0,2},{1,3},{2,0},{3,1},{4,6},{5,7},{6,4},{7,5},{8,10},{9,11},{10,... | collective-permute-start | bytes 49160 | tf_op jit(solution)/shard_map/ppermute | solution.py:222
  128.3 1.3 collective-permute-start.31
  129.5 4.2 %collective-permute-start.32 = (bf16[4,8,256]{2,1,0:T(8,128)(2,1)S(1)}, bf16[4,8,256]{2,1,0:T(8,128)(2,1)S(1)}, u32[]{:S(2)}, u32[]{:S(2)}) collective-permute-start(bf16[4,8,256]{2,1,0:T(8,128)(2,1)S(1)} %get-tuple-element.82), channel_id=1, source_target_pairs={{0,2},{1,3},{2,0},{3,1},{4,6},{5,7},{6,4},{7,5},{8,10},{9,11},{10,... | collective-permute-start | bytes 49160 | tf_op jit(solution)/shard_map/ppermute | solution.py:222
  130.6 5.5 %collective-permute-start.34 = (bf16[4,8,256]{2,1,0:T(8,128)(2,1)S(1)}, bf16[4,8,256]{2,1,0:T(8,128)(2,1)S(1)}, u32[]{:S(2)}, u32[]{:S(2)}) collective-permute-start(bf16[4,8,256]{2,1,0:T(8,128)(2,1)S(1)} %get-tuple-element.83), channel_id=1, source_target_pairs={{0,6},{1,7},{2,4},{3,5},{4,2},{5,3},{6,0},{7,1},{8,14},{9,15},{10,... | collective-permute-start | bytes 49160 | tf_op jit(solution)/shard_map/ppermute | solution.py:222
  132.3 4.6 %collective-permute-start.33 = (bf16[4,8,256]{2,1,0:T(8,128)(2,1)S(1)}, bf16[4,8,256]{2,1,0:T(8,128)(2,1)S(1)}, u32[]{:S(2)}, u32[]{:S(2)}) collective-permute-start(bf16[4,8,256]{2,1,0:T(8,128)(2,1)S(1)} %get-tuple-element.84), channel_id=1, source_target_pairs={{0,4},{1,5},{2,6},{3,7},{4,0},{5,1},{6,2},{7,3},{8,12},{9,13},{10,... | collective-permute-start | bytes 49160 | tf_op jit(solution)/shard_map/ppermute | solution.py:222
  (1 other events, 0.7 us)

commit v5 on v4

--- a/solution.py
+++ b/solution.py
@@ -24,7 +24,7 @@
 ):
     return pl.pallas_call(
         body,
-        out_shape=[jax.ShapeDtypeStruct(s, d) for s, d in outs],
+        out_shape=[jax.ShapeDtypeStruct(*o) if isinstance(o, tuple) else o for o in outs],
         in_specs=list(specs),
         out_specs=out_specs or [VMEM] * len(outs),
         scratch_shapes=list(scratch),
@@ -42,6 +42,14 @@
     return lax.dot_general(x, w, (((1,), (0,)), ((), ())), preferred_element_type=F32)
 
 
+def split_at(refs, *counts):
+    out = []
+    for c in counts:
+        out.append(refs[:c])
+        refs = refs[c:]
+    return *out, refs
+
+
 def walk(plan_ref, sets, tiles, blocks, tile, visit, carry):
     def trip(i, carry):
         at = []
@@ -61,7 +69,7 @@
     return jnp.where(inside, found, 0.0)
 
 
-def prepare(lists, first, heights, widths):
+def prepare(weights, lists, first, heights, widths):
     count = len(lists)
 
     def one(rows_ref, scalar_ref, height_ref, list_ref, plan_ref, out_ref, first, width):
@@ -99,33 +107,54 @@
 
             walk(plan_ref, sets, tiles, blocks, tile, visit, 0)
 
+    held = len(weights)
+
     def body(*refs):
-        ins, outs = refs[: 3 * count], refs[3 * count :]
+        sources, rows, heights, refs = split_at(refs, held, count, count)
+        targets, outs, lines, scalars, (weight_sems, row_sems) = split_at(
+            refs, held, 3 * count, count, count
+        )
         row = lax.axis_index("rows")
+        ahead = []
         for i in range(count):
-            one(*ins[3 * i : 3 * i + 3], *outs[3 * i : 3 * i + 3], row * first[i], widths[i])
-
-    shapes, specs, ins = [], [], []
-    for rows, height, width in zip(lists, heights, widths):
+            ahead.append(pltpu.make_async_copy(rows[i], lines[i], row_sems.at[2 * i]))
+            ahead.append(pltpu.make_async_copy(rows[i], scalars[i], row_sems.at[2 * i + 1]))
+        behind = [
+            pltpu.make_async_copy(source, target, weight_sems.at[i])
+            for i, (source, target) in enumerate(zip(sources, targets))
+        ]
+        for copy in ahead + behind:
+            copy.start()
+        for copy in ahead:
+            copy.wait()
+        for i in range(count):
+            one(lines[i], scalars[i], heights[i], *outs[3 * i : 3 * i + 3], row * first[i], widths[i])
+        for copy in behind:
+            copy.wait()
+
+    shapes = [pltpu.VMEM(w.shape, w.dtype) for w in weights]
+    for rows, width in zip(lists, widths):
         sets, length = rows.shape
         shapes += [
             (rows.shape, I32),
             (((sets + 1) * (length // LANES),), I32),
             ((sets, width // LANES + 1, 8, LANES), I32),
         ]
-        ins += [rows, rows, height]
-        specs += [VMEM, SMEM, SMEM]
+    outside = pl.BlockSpec(memory_space=pltpu.HBM)
     got = call(
         body,
         shapes,
-        ins,
-        specs,
-        out_specs=[VMEM, SMEM, VMEM] * count,
-        moved=16 << 20,
+        [pltpu.with_memory_space_constraint(x, pltpu.HBM) for x in (*weights, *lists)] + heights,
+        [outside] * (held + count) + [SMEM] * count,
+        out_specs=[VMEM] * held + [VMEM, SMEM, VMEM] * count,
+        scratch=[pltpu.VMEM(x.shape, I32) for x in lists]
+        + [pltpu.SMEM(x.shape, I32) for x in lists]
+        + [pltpu.SemaphoreType.DMA((held,)), pltpu.SemaphoreType.DMA((2 * count,))],
+        moved=20 << 20,
         limit=4 << 20,
         name="prepare",
     )
-    return [got[3 * i : 3 * i + 3] for i in range(count)]
+    return got[:held], [got[held + 3 * i : held + 3 * i + 3] for i in range(count)]
 
 
 def scatter_walk(plan_ref, inverse_ref, update_ref, acc_ref, tiles):
@@ -167,15 +196,6 @@
             out_ref[s, :, tile * LANES : (tile + 1) * LANES] = found[s].astype(out_ref.dtype)
 
 
-def joined(ref, *at):
-    return jnp.concatenate([ref[(j,) + at] for j in range(ref.shape[0])], axis=1)
-
-
-def split(value, n):
-    w = value.shape[1] // n
-    return [value[:, j * w : (j + 1) * w] for j in range(n)]
-
-
 def core():
     return lax.axis_index("rows") & 1
 
@@ -204,11 +224,7 @@
         other_ref[k] = value_ref[:, spot(2 * k + 1 - odd, w)].astype(other_ref.dtype)
 
 
-def all_gather(copies):
-    return lax.all_to_all(copies, "rows", 0, 0)
-
-
-def scatter_pieces(x):
+def all_to_all(x):
     return lax.all_to_all(x, "rows", 0, 0)
 
 
@@ -265,66 +281,70 @@
     def flat():
         return lax.axis_index("leaf") * n + lax.axis_index("rows")
 
-    def leaf_gather(x, copies):
-        if leaf_aligned and not copies:
-            own = jnp.stack([x] + [far(x, k) for k in range(1, chips)])
-            return own, swap(own)
-        got = all_gather(x if copies else jnp.broadcast_to(x[None], (n,) + x.shape))
-        if leaf_aligned:
-            return (got,)
-        return (jnp.moveaxis(got, 0, 2).reshape(1, leaves, rcount, leaf_width),)
+    def far_gather(x):
+        return jnp.stack([x] + [far(x, k) for k in range(1, chips)])
+
+    def leaf_columns(x):
+        got = all_to_all(jnp.broadcast_to(x[None], (n,) + x.shape))
+        return jnp.moveaxis(got, 0, 2).reshape(1, leaves, rcount, leaf_width)
+
+    def join_in(x_refs, x_ref, *at):
+        if len(x_refs) == 1:
+            return x_refs[0][(0,) + at]
+        unite(*x_refs, x_ref, *at, xor=True)
+        return x_ref[...]
 
     rhs = root_rhs
     if not root_aligned:
         rhs = lax.dynamic_update_slice_in_dim(
             jnp.zeros((rcount, root_width), F32), root_rhs, flat() * root_cols, 1
         )
-    lb = leaf_gather(jnp.moveaxis(leaf_rhs.astype(BF16), 1, 0), False)
-    prepared = prepare(
+    lb = jnp.moveaxis(leaf_rhs.astype(BF16), 1, 0)
+    lb = far_gather(lb) if leaf_aligned else leaf_columns(lb)
+    early, prepared = prepare(
+        [leaf_inv, leaf_panel],
         [leaf_rows, parent_rows],
         [leaf_local, parent_local],
         [leaf_height, parent_height],
         [tall, root_width],
     )
-    lb, prepared, parent_rhs, rhs = lax.optimization_barrier(
-        (lb, prepared, parent_rhs[:, 0], rhs)
-    )
+    lb, early, prepared, rhs = lax.optimization_barrier((lb, early, prepared, rhs))
+    leaf_inv_early, leaf_panel_early = early
     (leaf_list, leaf_plan, leaf_inverse), (parent_list, parent_plan, parent_inverse) = prepared
+    lb = (lb, swap(lb)) if leaf_aligned else (lb,)
 
     def leaf_solve(*refs):
-        x_refs, (w_ref, y_ref, copies_ref, x_ref) = refs[: len(lb)], refs[len(lb) :]
+        x_refs, (w_ref, y_ref, send_ref, x_ref) = refs[: len(lb)], refs[len(lb) :]
         for s in range(leaves):
-            if len(lb) == 2:
-                unite(*x_refs, x_ref, s, xor=True)
-                x = x_ref[...]
-            else:
-                x = joined(x_refs[0], s)
-            y = times_transposed(x, w_ref[s])
+            y = times_transposed(join_in(x_refs, x_ref, s), w_ref[s])
             y_ref[s] = y
-            for j in range(n):
-                copies_ref[j, s] = y.astype(BF16)
+            send_ref[s] = y.astype(BF16)
 
     ly, lyb = call(
         leaf_solve,
-        [((leaves, rcount, leaf_cols), F32), ((n, leaves, rcount, leaf_cols), BF16)],
-        [*lb, pinned(leaf_inv)],
+        [((leaves, rcount, leaf_cols), F32), ((leaves, rcount, leaf_cols), BF16)],
+        [*lb, pinned(leaf_inv_early)],
         [VMEM] * (len(lb) + 1),
         scratch=[pltpu.VMEM((rcount, leaf_width), BF16)],
         name="leaf_solve",
     )
-    (lyb,) = leaf_gather(lyb, True)
-
-    def leaf_update(
-        plan_ref, x_ref, w_ref, inverse_ref, rhs_ref, own_ref, other_ref, root_ref,
-        update_ref, acc_ref, sum_ref,
-    ):
+    if leaf_aligned:
+        lyb = far_gather(lyb)
+        lyb = (lyb, swap(lyb))
+    else:
+        lyb = (leaf_columns(lyb),)
+
+    def leaf_update(*refs):
+        x_refs, refs = refs[: len(lyb)], refs[len(lyb) :]
+        plan_ref, w_ref, inverse_ref, rhs_ref, own_ref, other_ref, root_ref, *refs = refs
+        x_ref, update_ref, acc_ref, sum_ref = refs
         acc_ref[...] = jnp.zeros(acc_ref.shape, F32)
         for s in range(leaves):
-            update_ref[s] = times_transposed(joined(x_ref, s), w_ref[s])
+            update_ref[s] = times_transposed(join_in(x_refs, x_ref, s), w_ref[s])
         scatter_walk(plan_ref, inverse_ref, update_ref, acc_ref, leaf_local // LANES)
         for b in range(parent_width // LANES):
             sum_ref[:, b * LANES : (b + 1) * LANES] = -acc_ref[b]
-        sum_ref[:, spot(lax.axis_index("rows"), parent_cols)] += rhs_ref[...]
+        sum_ref[:, spot(lax.axis_index("rows"), parent_cols)] += rhs_ref[:, 0, :]
         deal(sum_ref, own_ref, other_ref)
         for b in range(root_width // LANES):
             root_ref[b] = acc_ref[parent_width // LANES + b]
@@ -336,9 +356,10 @@
             ((chips, rcount, parent_cols), BF16),
             ((root_width // LANES, rcount, LANES), F32),
         ],
-        [leaf_plan, lyb, pinned(leaf_panel), leaf_inverse, parent_rhs],
-        [SMEM] + [VMEM] * 4,
+        [*lyb, leaf_plan, pinned(leaf_panel_early), leaf_inverse, parent_rhs],
+        [VMEM] * len(lyb) + [SMEM] + [VMEM] * 3,
         scratch=[
+            pltpu.VMEM((rcount, leaf_width), BF16),
             pltpu.VMEM((leaves, rcount, leaf_local), F32),
             pltpu.VMEM((tall // LANES + 1, rcount, LANES), F32),
             pltpu.VMEM((rcount, parent_width), F32),
@@ -347,30 +368,30 @@
     )
     prb = chips_sum(own + swap(other).astype(F32)).astype(BF16)
 
-    def parent_solve(own_ref, other_ref, w_ref, y_ref, copies_ref, x_ref):
+    def parent_solve(own_ref, other_ref, w_ref, y_ref, send_ref, x_ref):
         unite(own_ref, other_ref, x_ref)
         y = times_transposed(x_ref[...], w_ref[0])
         y_ref[...] = y
-        for j in range(n):
-            copies_ref[j] = y.astype(BF16)
+        send_ref[...] = y.astype(BF16)
 
     py, pyb = call(
         parent_solve,
-        [((rcount, parent_cols), F32), ((n, rcount, parent_cols), BF16)],
+        [((rcount, parent_cols), F32), ((rcount, parent_cols), BF16)],
         [prb, swap(prb), pinned(parent_inv)],
         [VMEM] * 3,
         scratch=[pltpu.VMEM((rcount, parent_width), BF16)],
         name="parent_solve",
     )
-    pyb = all_gather(pyb)
+    pyb = far_gather(pyb)
 
     def parent_update(
-        plan_ref, x_ref, w_ref, inverse_ref, root_ref, rhs_ref, own_ref, other_ref,
-        update_ref, acc_ref, sum_ref,
+        plan_ref, x_own_ref, x_other_ref, w_ref, inverse_ref, root_ref, rhs_ref, own_ref, other_ref,
+        x_ref, update_ref, acc_ref, sum_ref,
     ):
+        unite(x_own_ref, x_other_ref, x_ref, xor=True)
         for b in range(root_width // LANES):
             acc_ref[b] = root_ref[b]
-        update_ref[0] = times_transposed(joined(x_ref), w_ref[0])
+        update_ref[0] = times_transposed(x_ref[...], w_ref[0])
         scatter_walk(plan_ref, inverse_ref, update_ref, acc_ref, parent_local // LANES)
         for b in range(root_width // LANES):
             sum_ref[:, b * LANES : (b + 1) * LANES] = -acc_ref[b]
@@ -383,9 +404,10 @@
     own, other = call(
         parent_update,
         [((chips, rcount, piece), F32), ((chips, rcount, piece), BF16)],
-        [parent_plan, pyb, pinned(parent_panel), parent_inverse, root_acc, rhs],
-        [SMEM] + [VMEM] * 5,
+        [parent_plan, pyb, swap(pyb), pinned(parent_panel), parent_inverse, root_acc, rhs],
+        [SMEM] + [VMEM] * 6,
         scratch=[
+            pltpu.VMEM((rcount, parent_width), BF16),
             pltpu.VMEM((1, rcount, parent_local), F32),
             pltpu.VMEM((root_width // LANES + 1, rcount, LANES), F32),
             pltpu.VMEM((rcount, root_width), F32),
@@ -414,9 +436,31 @@
         for b in range(width // LANES):
             target_ref[start + b] = source_ref[:, b * LANES : (b + 1) * LANES].astype(F32)
 
+    def terms(x_ref, w_ref, out_ref, odd):
+        _, sets, _, cols = out_ref.shape
+        for k in range(chips):
+            at = spot(2 * (chip() ^ k) + odd, cols)
+            for s in range(sets):
+                out_ref[k, s] = times(x_ref[s], w_ref[s, :, at]).astype(out_ref.dtype)
+
+    def split_terms(w):
+        return (chips, w.shape[0], rcount, w.shape[2] // n)
+
+    def own_terms(x, w, name):
+        def body(x_ref, w_ref, out_ref):
+            terms(x_ref, w_ref, out_ref, core())
+
+        return call(
+            body, [(split_terms(w), F32)], [x, pinned(w)], [VMEM] * 2, moved=12 << 20, name=name
+        )[0]
+
+    def reduce(own, other):
+        other = swap(other)
+        sums = [own[k] + other[k].astype(F32) for k in range(chips)]
+        return [sums[0]] + [far(sums[k].astype(BF16), k) for k in range(1, chips)]
+
     def parent_back(
-        plan_ref, own_ref, other_ref, rows_ref, w_ref, out_ref, whole_ref, sol_ref,
-        x_ref, found_ref,
+        plan_ref, own_ref, other_ref, rows_ref, w_ref, out_ref, whole_ref, sol_ref, found_ref, x_ref,
     ):
         unite(own_ref, other_ref, x_ref)
         if root_aligned:
@@ -426,37 +470,34 @@
         blocks_of(x_ref, whole_ref, 0, root_width)
         whole_ref[root_width // LANES] = jnp.zeros((rcount, LANES), F32)
         gather_walk(plan_ref, rows_ref, whole_ref, found_ref)
-        term = times(found_ref[0], w_ref[0])
-        for j, part in enumerate(split(term, n)):
-            out_ref[j] = part.astype(BF16)
-
-    term, root_whole, root_sol = call(
+        terms(found_ref, w_ref, out_ref, 1 - core())
+
+    term, root_whole, root_sol, found = call(
         parent_back,
         [
-            ((n, rcount, parent_cols), BF16),
+            (split_terms(parent_panel), BF16),
             ((root_width // LANES + 1, rcount, LANES), F32),
             ((rcount, root_cols if root_aligned else root_width), F32),
+            ((1, rcount, parent_local), BF16),
         ],
         [parent_plan, rxb, swap(rxb), parent_list, pinned(parent_panel)],
         [SMEM] + [VMEM] * 4,
-        scratch=[
-            pltpu.VMEM((rcount, root_width), BF16),
-            pltpu.VMEM((1, rcount, parent_local), BF16),
-        ],
+        scratch=[pltpu.VMEM((rcount, root_width), BF16)],
         name="parent_back",
     )
-    tail = scatter_pieces(term)
-
-    def parent_solve_back(tail_ref, y_ref, w_ref, own_ref, other_ref, sum_ref):
-        lost = sum(tail_ref[j].astype(F32) for j in range(n))
+    tails = reduce(own_terms(found, parent_panel, "parent_back_own"), term)
+
+    def parent_solve_back(*refs):
+        tail_refs, (y_ref, w_ref, own_ref, other_ref, sum_ref) = refs[:chips], refs[chips:]
+        lost = sum(ref[0].astype(F32) for ref in tail_refs)
         sum_ref[...] = times((y_ref[...] - lost).astype(BF16), w_ref[0])
         deal(sum_ref, own_ref, other_ref)
 
     own, other = call(
         parent_solve_back,
         [((chips, rcount, parent_cols), F32), ((chips, rcount, parent_cols), BF16)],
-        [tail, py, pinned(parent_inv)],
-        [VMEM] * 3,
+        [*tails, py, pinned(parent_inv)],
+        [VMEM] * (chips + 2),
         scratch=[pltpu.VMEM((rcount, parent_width), F32)],
         name="parent_solve_back",
     )
@@ -474,27 +515,6 @@
             whole_ref[parent_width // LANES + b] = root_ref[b]
         gather_walk(plan_ref, rows_ref, whole_ref, found_ref)
 
-    def terms(x_ref, w_ref, out_ref, odd):
-        for k in range(chips):
-            cols = spot(2 * (chip() ^ k) + odd, leaf_cols)
-            for s in range(leaves):
-                out_ref[k, s] = times(x_ref[s], w_ref[s, :, cols]).astype(out_ref.dtype)
-
-    split_terms = (chips, leaves, rcount, leaf_cols)
-
-    def own_terms(x, w, name):
-        def body(x_ref, w_ref, out_ref):
-            terms(x_ref, w_ref, out_ref, core())
-
-        return call(
-            body, [(split_terms, F32)], [x, pinned(w)], [VMEM] * 2, moved=12 << 20, name=name
-        )[0]
-
-    def leaf_reduce(own, other):
-        other = swap(other)
-        sums = [own[k] + other[k].astype(F32) for k in range(chips)]
-        return [sums[0]] + [far(sums[k].astype(BF16), k) for k in range(1, chips)]
-
     def all_terms(x_ref, w_ref, out_ref):
         for s in range(leaves):
             out_ref[s] = times(x_ref[s], w_ref[s]).astype(BF16)
@@ -520,7 +540,7 @@
     term, parent_sol, found = call(
         leaf_back,
         [
-            (split_terms if leaf_aligned else whole_term, BF16),
+            (split_terms(leaf_panel) if leaf_aligned else whole_term, BF16),
             ((rcount, parent_cols), F32),
             (found_shape, BF16),
         ],
@@ -530,9 +550,9 @@
         name="leaf_back",
     )
     if leaf_aligned:
-        tails = leaf_reduce(own_terms(found, leaf_panel, "leaf_back_own"), term)
+        tails = reduce(own_terms(found, leaf_panel, "leaf_back_own"), term)
     else:
-        tails = [scatter_pieces(pieces_apart(term)).astype(F32).sum(0)]
+        tails = [all_to_all(pieces_apart(term)).astype(F32).sum(0)]
 
     def leaf_solve_back(*refs):
         tail_refs, (y_ref, w_ref, out_ref, v_ref) = refs[: len(tails)], refs[len(tails) :]
@@ -547,7 +567,7 @@
     term, lvb = call(
         leaf_solve_back,
         [
-            (split_terms if leaf_aligned else whole_term, BF16),
+            (split_terms(leaf_panel) if leaf_aligned else whole_term, BF16),
             ((leaves, rcount, leaf_cols), BF16),
         ],
         [*tails, ly, pinned(leaf_inv)],
@@ -555,10 +575,10 @@
         name="leaf_solve_back",
     )
     if leaf_aligned:
-        parts = leaf_reduce(own_terms(lvb, leaf_inv, "leaf_solve_back_own"), term)
+        parts = reduce(own_terms(lvb, leaf_inv, "leaf_solve_back_own"), term)
         leaf_sol = sum(p.astype(F32) for p in parts)
     else:
-        leaf_sol = scatter_pieces(pieces_apart(term)).astype(F32).sum(0)
+        leaf_sol = all_to_all(pieces_apart(term)).astype(F32).sum(0)
     if not root_aligned:
         root_sol = lax.dynamic_slice_in_dim(root_sol, flat() * root_cols, root_cols, 1)
     return (jnp.moveaxis(leaf_sol, 0, 1), parent_sol[:, None, :], root_sol)

time: 138 us -> 126 us (0.913)
  blocking collectives: 27 us -> 0 us
  starting transfers between devices: 37.2 us -> 50.3 us
  local copies, waits for them, and re-layouts: 12.8 us -> 2.72 us
  waiting for transfers between devices: 34.6 us -> 42.2 us
  Pallas kernels: 24.2 us -> 28 us
    all_to_all x3 -> x0, blocking collectives: 27 us -> none  [the longest x2 18.4 us: all_gather(): return lax.all_to_all(copies, 'rows', 0, 0)]
    ppermute x21 -> x30, starting transfers between devices: 31.4 us -> 44.7 us  [far(): return lax.ppermute(x, 'rows', [(i, i ^ 2 * k) for i in range(n)])]
    unnamed x32 -> x25, local copies, waits for them, and re-layouts: 12.8 us -> 2.72 us
    ppermute x21 -> x30, waiting for transfers between devices: 19.5 us -> 23.9 us  [far(): return lax.ppermute(x, 'rows', [(i, i ^ 2 * k) for i in range(n)])]
    ppermute x11 -> x14, waiting for transfers between devices: 10.3 us -> 14.3 us  [swap(): return lax.ppermute(x, 'rows', [(i, i ^ 1) for i in range(n)])]
    pallas_call x12 -> x13, Pallas kernels: 24.2 us -> 28 us  [call(): pl.pallas_call(body, out_shape=[jax.ShapeDtypeStruct(*o) if isinstance(o,...]
  transfers between devices with their start and end apart: 35 -> 47, of which waited for: 29 -> 37; matrix products, arithmetic and copies ran while one was open for 1% -> 0% of each run, Pallas kernels for 4% -> 8%
where the time goes in v5:
time: 126 us; the launch traced here: 125 us
  starting transfers between devices  50.3 us (40%)
  waiting for transfers between devices  42.2 us (33%)
  Pallas kernels  28 us (22%)
  local copies, waits for them, and re-layouts  2.72 us (2%)
  between operations  1.58 us (1%)
    ppermute x30, starting transfers between devices, far(): return lax.ppermute(x, 'rows', [(i, i ^ 2 * k) for i in range(n)])  44.7 us
    pallas_call x13, Pallas kernels, call(): pl.pallas_call(body, out_shape=[jax.ShapeDtypeStruct(*o) if isinstance(o,...  28 us
    ppermute x30, waiting for transfers between devices, far(): return lax.ppermute(x, 'rows', [(i, i ^ 2 * k) for i in range(n)])  23.9 us
    ppermute x14, waiting for transfers between devices, swap(): return lax.ppermute(x, 'rows', [(i, i ^ 1) for i in range(n)])  14.3 us
    ppermute x3, starting transfers between devices, leaf_sum(): lax.ppermute(b, 'leaf', [(i, (i + k) % n) for i in range(n)]).astype(F32)  4.17 us
    ppermute x3, waiting for transfers between devices, leaf_sum(): lax.ppermute(b, 'leaf', [(i, (i + k) % n) for i in range(n)]).astype(F32)  3.94 us
    unnamed x25, local copies, waits for them, and re-layouts  2.72 us
  transfers between devices with their start and end apart: 47, of which 37 were waited for; matrix products, arithmetic and copies ran while one was open for 0% of the time, Pallas kernels for 8%

profile of v5, /device:TPU:0, one launch (start us, length us, event | category | flops | bytes accessed | tf_op | source)
XLA Modules:
  0.0 125.1 jit_solution(5818745341329406672)
XLA Ops:
  1.4 3.0 %collective-permute-start = (bf16[4,8,256]{2,1,0:T(8,128)(2,1)S(1)}, bf16[4,8,256]{2,1,0:T(8,128)(2,1)S(1)}, u32[]{:S(2)}, u32[]{:S(2)}) collective-permute-start(bf16[4,8,256]{2,1,0:T(8,128)(2,1)S(1)} %bitcast.57), channel_id=1, source_target_pairs={{0,2},{1,3},{2,0},{3,1},{4,6},{5,7},{6,4},{7,5},{8,10},{9,11},{10,... | collective-permute-start | bytes 49160 | tf_op jit(solution)/shard_map/ppermute | solution.py:238
  4.4 2.5 %collective-permute-start.2 = (bf16[4,8,256]{2,1,0:T(8,128)(2,1)S(1)}, bf16[4,8,256]{2,1,0:T(8,128)(2,1)S(1)}, u32[]{:S(2)}, u32[]{:S(2)}) collective-permute-start(bf16[4,8,256]{2,1,0:T(8,128)(2,1)S(1)} %bitcast.58), channel_id=1, source_target_pairs={{0,6},{1,7},{2,4},{3,5},{4,2},{5,3},{6,0},{7,1},{8,14},{9,15},{10,... | collective-permute-start | bytes 49160 | tf_op jit(solution)/shard_map/ppermute | solution.py:238
  8.3 8.3 %prepare.1 = (bf16[4,256,2048]{2,1,0:T(8,128)(2,1)S(1)}, bf16[4,1024,2048]{2,1,0:T(8,128)(2,1)S(1)}, s32[4,1024]{1,0:T(4,128)S(1)}, s32[40]{0:T(128)S(1)}, s32[4...) custom-call(bf16[4,256,2048]{2,1,0:T(8,128)(2,1)} %w_ref.13, ...), custom_call_target="tpu_custom_call" | custom-call | bytes 20971520 | tf_op jit(solution)/shard_map/prepare/pallas_call | solution.py:25
  16.7 1.2 collective-permute-done.3.refs_1_
  18.0 1.2 leaf_solve.1
  19.2 2.9 %collective-permute-start.6 = (bf16[4,8,256]{2,1,0:T(8,128)(2,1)S(1)}, bf16[4,8,256]{2,1,0:T(8,128)(2,1)S(1)}, u32[]{:S(2)}, u32[]{:S(2)}) collective-permute-start(bf16[4,8,256]{2,1,0:T(8,128)(2,1)S(1)} %get-tuple-element.55), channel_id=1, source_target_pairs={{0,6},{1,7},{2,4},{3,5},{4,2},{5,3},{6,0},{7,1},{8,14},{9,15},{10,... | collective-permute-start | bytes 49160 | tf_op jit(solution)/shard_map/ppermute | solution.py:238
  22.4 1.1 collective-permute-start.4
  23.6 1.2 collective-permute-done.6
  24.7 2.1 %collective-permute-done.5 = bf16[4,8,256]{2,1,0:T(8,128)(2,1)S(1)} collective-permute-done((bf16[4,8,256]{2,1,0:T(8,128)(2,1)S(1)}, bf16[4,8,256]{2,1,0:T(8,128)(2,1)S(1)}, u32[]{:S(2)}, u32[]{:S(2)}) %collective-permute-start.5) | collective-permute-done | bytes 16416 | tf_op jit(solution)/shard_map/ppermute | solution.py:238
  26.9 1.2 collective-permute-done.7.refs_1_
  28.2 6.1 %leaf_update.1 = (f32[4,8,512]{2,1,0:T(8,128)S(1)}, bf16[4,8,512]{2,1,0:T(8,128)(2,1)S(1)}, f32[32,8,128]{2,1,0:T(8,128)S(1)}) custom-call(bf16[4,4,8,256]{3,2,1,0:T(8,128)(2,1)S(1)} %pad_maximum_fusion.1.refs_0_, bf16[4,4,8,256]{3,2,1,0:T(8,128)(2,1)S(1)} %collective-permute-done.7.refs_1_, s32[40]{0:T(128)S(1)} %get-tuple-element.51.refs_2_.refs_0_, ...), custom_call_target="tpu_custom_call" | custom-call | tf_op jit(solution)/shard_map/leaf_update/pallas_call | solution.py:25
  35.6 2.0 %collective-permute-start.11 = (bf16[4,8,512]{2,1,0:T(8,128)(2,1)S(1)}, bf16[4,8,512]{2,1,0:T(8,128)(2,1)S(1)}, u32[]{:S(2)}, u32[]{:S(2)}) collective-permute-start(bf16[4,8,512]{2,1,0:T(8,128)(2,1)S(1)} %fusion), channel_id=1, source_target_pairs={{0,6},{1,7},{2,4},{3,5},{4,2},{5,3},{6,0},{7,1},{8,14},{9,15},{10,... | collective-permute-start | bytes 98312 | tf_op jit(solution)/shard_map/ppermute | solution.py:238
  37.7 2.4 %collective-permute-start.9 = (bf16[4,8,512]{2,1,0:T(8,128)(2,1)S(1)}, bf16[4,8,512]{2,1,0:T(8,128)(2,1)S(1)}, u32[]{:S(2)}, u32[]{:S(2)}) collective-permute-start(bf16[4,8,512]{2,1,0:T(8,128)(2,1)S(1)} %fusion), channel_id=1, source_target_pairs={{0,2},{1,3},{2,0},{3,1},{4,6},{5,7},{6,4},{7,5},{8,10},{9,11},{10,... | collective-permute-start | bytes 98312 | tf_op jit(solution)/shard_map/ppermute | solution.py:238
  40.1 1.8 %collective-permute-done.11 = bf16[4,8,512]{2,1,0:T(8,128)(2,1)S(1)} collective-permute-done((bf16[4,8,512]{2,1,0:T(8,128)(2,1)S(1)}, bf16[4,8,512]{2,1,0:T(8,128)(2,1)S(1)}, u32[]{:S(2)}, u32[]{:S(2)}) %collective-permute-start.11) | collective-permute-done | bytes 32800 | tf_op jit(solution)/shard_map/ppermute | solution.py:238
  42.9 1.2 collective-permute-done.12.other_ref
  44.1 1.2 parent_solve.1
  45.3 2.1 %collective-permute-start.15 = (bf16[8,512]{1,0:T(8,128)(2,1)S(1)}, bf16[8,512]{1,0:T(8,128)(2,1)S(1)}, u32[]{:S(2)}, u32[]{:S(2)}) collective-permute-start(bf16[8,512]{1,0:T(8,128)(2,1)S(1)} %get-tuple-element.60), channel_id=1, source_target_pairs={{0,6},{1,7},{2,4},{3,5},{4,2},{5,3},{6,0},{7,1},{8,14},{9,15},{10,... | collective-permute-start | bytes 24584 | tf_op jit(solution)/shard_map/ppermute | solution.py:238
  48.0 1.7 %collective-permute-start.13 = (bf16[8,512]{1,0:T(8,128)(2,1)S(1)}, bf16[8,512]{1,0:T(8,128)(2,1)S(1)}, u32[]{:S(2)}, u32[]{:S(2)}) collective-permute-start(bf16[8,512]{1,0:T(8,128)(2,1)S(1)} %get-tuple-element.60), channel_id=1, source_target_pairs={{0,2},{1,3},{2,0},{3,1},{4,6},{5,7},{6,4},{7,5},{8,10},{9,11},{10,... | collective-permute-start | bytes 24584 | tf_op jit(solution)/shard_map/ppermute | solution.py:238
  50.8 1.2 collective-permute-done.14
  52.1 1.2 collective-permute-done.16.x_other_ref
  53.3 2.1 %parent_update.1 = (f32[4,8,512]{2,1,0:T(8,128)S(1)}, bf16[4,8,512]{2,1,0:T(8,128)(2,1)S(1)}) custom-call(s32[8]{0:T(128)S(1)} %get-tuple-element.52.plan_ref, bf16[4,8,512]{2,1,0:T(8,128)(2,1)S(1)} %pad_maximum_fusion.2.x_own_ref, bf16[4,8,512]{2,1,0:T(8,128)(2,1)S(1)} %collective-permute-done.16.x_other_ref, bf16[1,512,4096]{2,1,0:T(8,128)(2,1)S(1)} %copy-done.1, ...), custom_call_target="tpu_custom_call" | custom-call | tf_op jit(solution)/shard_map/parent_update/pallas_call | solution.py:25
  56.7 2.6 %collective-permute-start.20 = (bf16[4,8,512]{2,1,0:T(8,128)(2,1)S(1)}, bf16[4,8,512]{2,1,0:T(8,128)(2,1)S(1)}, u32[]{:S(2)}, u32[]{:S(2)}) collective-permute-start(bf16[4,8,512]{2,1,0:T(8,128)(2,1)S(1)} %fusion.1), channel_id=1, source_target_pairs={{0,24},{8,0},{16,8},{24,16},{1,25},{9,1},{17,9},{25,17},{2,26},{10... | collective-permute-start | bytes 98312 | tf_op jit(solution)/shard_map/ppermute | solution.py:250
  60.9 2.7 %collective-permute-done.19 = bf16[4,8,512]{2,1,0:T(8,128)(2,1)S(1)} collective-permute-done((bf16[4,8,512]{2,1,0:T(8,128)(2,1)S(1)}, bf16[4,8,512]{2,1,0:T(8,128)(2,1)S(1)}, u32[]{:S(2)}, u32[]{:S(2)}) %collective-permute-start.19) | collective-permute-done | bytes 32800 | tf_op jit(solution)/shard_map/ppermute | solution.py:250
  63.5 1.3 %collective-permute-done.18 = bf16[4,8,512]{2,1,0:T(8,128)(2,1)S(1)} collective-permute-done((bf16[4,8,512]{2,1,0:T(8,128)(2,1)S(1)}, bf16[4,8,512]{2,1,0:T(8,128)(2,1)S(1)}, u32[]{:S(2)}, u32[]{:S(2)}) %collective-permute-start.18) | collective-permute-done | bytes 32800 | tf_op jit(solution)/shard_map/ppermute | solution.py:250
  64.8 1.1 collective-permute-start.23
  67.1 2.2 %collective-permute-start.21 = (bf16[4,8,512]{2,1,0:T(8,128)(2,1)S(1)}, bf16[4,8,512]{2,1,0:T(8,128)(2,1)S(1)}, u32[]{:S(2)}, u32[]{:S(2)}) collective-permute-start(bf16[4,8,512]{2,1,0:T(8,128)(2,1)S(1)} %fusion.31), channel_id=1, source_target_pairs={{0,2},{1,3},{2,0},{3,1},{4,6},{5,7},{6,4},{7,5},{8,10},{9,11},{10,... | collective-permute-start | bytes 98312 | tf_op jit(solution)/shard_map/ppermute | solution.py:238
  69.3 1.3 %collective-permute-done.23 = bf16[4,8,512]{2,1,0:T(8,128)(2,1)S(1)} collective-permute-done((bf16[4,8,512]{2,1,0:T(8,128)(2,1)S(1)}, bf16[4,8,512]{2,1,0:T(8,128)(2,1)S(1)}, u32[]{:S(2)}, u32[]{:S(2)}) %collective-permute-start.23) | collective-permute-done | bytes 32800 | tf_op jit(solution)/shard_map/ppermute | solution.py:238
  71.5 1.2 collective-permute-done.24.other_ref
  72.7 1.8 %root_solve.1 = (f32[4,8,512]{2,1,0:T(8,128)S(1)}, bf16[4,8,512]{2,1,0:T(8,128)(2,1)S(1)}) custom-call(bf16[4,8,512]{2,1,0:T(8,128)(2,1)S(1)} %add_convert_fusion.1.own_ref, bf16[4,8,512]{2,1,0:T(8,128)(2,1)S(1)} %collective-permute-done.24.other_ref, bf16[512,4096]{1,0:T(8,128)(2,1)S(1)} %copy-done.3), custom_call_target="tpu_custom_call" | custom-call | tf_op jit(solution)/shard_map/root_solve/pallas_call | solution.py:25
  75.7 2.2 %collective-permute-start.28 = (bf16[4,8,512]{2,1,0:T(8,128)(2,1)S(1)}, bf16[4,8,512]{2,1,0:T(8,128)(2,1)S(1)}, u32[]{:S(2)}, u32[]{:S(2)}) collective-permute-start(bf16[4,8,512]{2,1,0:T(8,128)(2,1)S(1)} %fusion.2), channel_id=1, source_target_pairs={{0,6},{1,7},{2,4},{3,5},{4,2},{5,3},{6,0},{7,1},{8,14},{9,15},{10,... | collective-permute-start | bytes 98312 | tf_op jit(solution)/shard_map/ppermute | solution.py:238
  80.2 1.5 %collective-permute-done.28 = bf16[4,8,512]{2,1,0:T(8,128)(2,1)S(1)} collective-permute-done((bf16[4,8,512]{2,1,0:T(8,128)(2,1)S(1)}, bf16[4,8,512]{2,1,0:T(8,128)(2,1)S(1)}, u32[]{:S(2)}, u32[]{:S(2)}) %collective-permute-start.28) | collective-permute-done | bytes 32800 | tf_op jit(solution)/shard_map/ppermute | solution.py:238
  81.6 1.2 collective-permute-done.27
  83.3 1.2 collective-permute-done.29.other_ref
  84.5 1.5 %parent_back.1 = (bf16[4,1,8,512]{3,2,1,0:T(8,128)(2,1)S(1)}, f32[33,8,128]{2,1,0:T(8,128)S(1)}, f32[8,128]{1,0:T(8,128)}, bf16[1,8,512]{2,1,0:T(8,128)(2,1)S(1)}) custom-call(s32[8]{0:T(128)S(1)} %get-tuple-element.52.plan_ref, bf16[4,8,512]{2,1,0:T(8,128)(2,1)S(1)} %add_convert_fusion.own_ref, bf16[4,8,512]{2,1,0:T(8,128)(2,1)S(1)} %collective-permute-done.29.other_ref, ...), custom_call_target="tpu_custom_call" | custom-call | tf_op jit(solution)/shard_map/parent_back/pallas_call | solution.py:25
  87.2 1.6 %collective-permute-start.33 = (bf16[1,8,512]{2,1,0:T(8,128)(2,1)S(1)}, bf16[1,8,512]{2,1,0:T(8,128)(2,1)S(1)}, u32[]{:S(2)}, u32[]{:S(2)}) collective-permute-start(bf16[1,8,512]{2,1,0:T(8,128)(2,1)S(1)} %get-tuple-element.95), channel_id=1, source_target_pairs={{0,6},{1,7},{2,4},{3,5},{4,2},{5,3},{6,0},{7,1},{8,14},{9,15},{10,... | collective-permute-start | bytes 24584 | tf_op jit(solution)/shard_map/ppermute | solution.py:238
  89.7 2.0 %collective-permute-start.31 = (bf16[1,8,512]{2,1,0:T(8,128)(2,1)S(1)}, bf16[1,8,512]{2,1,0:T(8,128)(2,1)S(1)}, u32[]{:S(2)}, u32[]{:S(2)}) collective-permute-start(bf16[1,8,512]{2,1,0:T(8,128)(2,1)S(1)} %get-tuple-element.97), channel_id=1, source_target_pairs={{0,2},{1,3},{2,0},{3,1},{4,6},{5,7},{6,4},{7,5},{8,10},{9,11},{10,... | collective-permute-start | bytes 24584 | tf_op jit(solution)/shard_map/ppermute | solution.py:238
  94.1 1.2 collective-permute-done.34
  95.3 2.3 %collective-permute-start.37 = (bf16[4,8,512]{2,1,0:T(8,128)(2,1)S(1)}, bf16[4,8,512]{2,1,0:T(8,128)(2,1)S(1)}, u32[]{:S(2)}, u32[]{:S(2)}) collective-permute-start(bf16[4,8,512]{2,1,0:T(8,128)(2,1)S(1)} %fusion.3), channel_id=1, source_target_pairs={{0,6},{1,7},{2,4},{3,5},{4,2},{5,3},{6,0},{7,1},{8,14},{9,15},{10,... | collective-permute-start | bytes 98312 | tf_op jit(solution)/shard_map/ppermute | solution.py:238
  99.8 1.7 %collective-permute-done.37 = bf16[4,8,512]{2,1,0:T(8,128)(2,1)S(1)} collective-permute-done((bf16[4,8,512]{2,1,0:T(8,128)(2,1)S(1)}, bf16[4,8,512]{2,1,0:T(8,128)(2,1)S(1)}, u32[]{:S(2)}, u32[]{:S(2)}) %collective-permute-start.37) | collective-permute-done | bytes 32800 | tf_op jit(solution)/shard_map/ppermute | solution.py:238
  102.9 1.2 collective-permute-done.38.refs_3_
  104.1 2.7 %leaf_back.1 = (bf16[4,4,8,256]{3,2,1,0:T(8,128)(2,1)S(1)}, f32[8,512]{1,0:T(8,128)S(1)}, bf16[4,8,1024]{2,1,0:T(8,128)(2,1)S(1)}) custom-call(s32[40]{0:T(128)S(1)} %get-tuple-element.51.refs_2_.refs_0_, f32[4,8,512]{2,1,0:T(8,128)S(1)} %get-tuple-element.87.refs_1_, bf16[4,8,512]{2,1,0:T(8,128)(2,1)S(1)} %get-tuple-element.86.refs_2_, ...), custom_call_target="tpu_custom_call" | custom-call | tf_op jit(solution)/shard_map/leaf_back/pallas_call | solution.py:25
  107.1 1.2 leaf_back_own.1
  108.3 1.6 %collective-permute-start.42 = (bf16[4,8,256]{2,1,0:T(8,128)(2,1)S(1)}, bf16[4,8,256]{2,1,0:T(8,128)(2,1)S(1)}, u32[]{:S(2)}, u32[]{:S(2)}) collective-permute-start(bf16[4,8,256]{2,1,0:T(8,128)(2,1)S(1)} %get-tuple-element.91), channel_id=1, source_target_pairs={{0,6},{1,7},{2,4},{3,5},{4,2},{5,3},{6,0},{7,1},{8,14},{9,15},{10,... | collective-permute-start | bytes 49160 | tf_op jit(solution)/shard_map/ppermute | solution.py:238
  110.7 2.1 %collective-permute-start.40 = (bf16[4,8,256]{2,1,0:T(8,128)(2,1)S(1)}, bf16[4,8,256]{2,1,0:T(8,128)(2,1)S(1)}, u32[]{:S(2)}, u32[]{:S(2)}) collective-permute-start(bf16[4,8,256]{2,1,0:T(8,128)(2,1)S(1)} %get-tuple-element.93), channel_id=1, source_target_pairs={{0,2},{1,3},{2,0},{3,1},{4,6},{5,7},{6,4},{7,5},{8,10},{9,11},{10,... | collective-permute-start | bytes 49160 | tf_op jit(solution)/shard_map/ppermute | solution.py:238
  112.8 1.3 %collective-permute-done.42.refs_3_ = bf16[4,8,256]{2,1,0:T(8,128)(2,1)S(1)} collective-permute-done((bf16[4,8,256]{2,1,0:T(8,128)(2,1)S(1)}, bf16[4,8,256]{2,1,0:T(8,128)(2,1)S(1)}, u32[]{:S(2)}, u32[]{:S(2)}) %collective-permute-start.42) | collective-permute-done | bytes 16416 | tf_op jit(solution)/shard_map/ppermute | solution.py:238
  116.4 1.9 %collective-permute-start.44 = (bf16[4,8,256]{2,1,0:T(8,128)(2,1)S(1)}, bf16[4,8,256]{2,1,0:T(8,128)(2,1)S(1)}, u32[]{:S(2)}, u32[]{:S(2)}) collective-permute-start(bf16[4,8,256]{2,1,0:T(8,128)(2,1)S(1)} %get-tuple-element.88), channel_id=1, source_target_pairs={{0,2},{1,3},{2,0},{3,1},{4,6},{5,7},{6,4},{7,5},{8,10},{9,11},{10,... | collective-permute-start | bytes 49160 | tf_op jit(solution)/shard_map/ppermute | solution.py:238
  118.3 1.5 %collective-permute-start.46 = (bf16[4,8,256]{2,1,0:T(8,128)(2,1)S(1)}, bf16[4,8,256]{2,1,0:T(8,128)(2,1)S(1)}, u32[]{:S(2)}, u32[]{:S(2)}) collective-permute-start(bf16[4,8,256]{2,1,0:T(8,128)(2,1)S(1)} %get-tuple-element.89), channel_id=1, source_target_pairs={{0,6},{1,7},{2,4},{3,5},{4,2},{5,3},{6,0},{7,1},{8,14},{9,15},{10,... | collective-permute-start | bytes 49160 | tf_op jit(solution)/shard_map/ppermute | solution.py:238
  120.6 3.3 %collective-permute-done.46 = bf16[4,8,256]{2,1,0:T(8,128)(2,1)S(1)} collective-permute-done((bf16[4,8,256]{2,1,0:T(8,128)(2,1)S(1)}, bf16[4,8,256]{2,1,0:T(8,128)(2,1)S(1)}, u32[]{:S(2)}, u32[]{:S(2)}) %collective-permute-start.46) | collective-permute-done | bytes 16416 | tf_op jit(solution)/shard_map/ppermute | solution.py:238
  (101 shorter events, 28.4 us)
Async XLA Ops:
  1.4 15.2 %collective-permute-start = (bf16[4,8,256]{2,1,0:T(8,128)(2,1)S(1)}, bf16[4,8,256]{2,1,0:T(8,128)(2,1)S(1)}, u32[]{:S(2)}, u32[]{:S(2)}) collective-permute-start(bf16[4,8,256]{2,1,0:T(8,128)(2,1)S(1)} %bitcast.57), channel_id=1, source_target_pairs={{0,2},{1,3},{2,0},{3,1},{4,6},{5,7},{6,4},{7,5},{8,10},{9,11},{10,... | collective-permute-start | bytes 49160 | tf_op jit(solution)/shard_map/ppermute | solution.py:238
  4.4 12.2 %collective-permute-start.2 = (bf16[4,8,256]{2,1,0:T(8,128)(2,1)S(1)}, bf16[4,8,256]{2,1,0:T(8,128)(2,1)S(1)}, u32[]{:S(2)}, u32[]{:S(2)}) collective-permute-start(bf16[4,8,256]{2,1,0:T(8,128)(2,1)S(1)} %bitcast.58), channel_id=1, source_target_pairs={{0,6},{1,7},{2,4},{3,5},{4,2},{5,3},{6,0},{7,1},{8,14},{9,15},{10,... | collective-permute-start | bytes 49160 | tf_op jit(solution)/shard_map/ppermute | solution.py:238
  6.9 9.7 %collective-permute-start.1 = (bf16[4,8,256]{2,1,0:T(8,128)(2,1)S(1)}, bf16[4,8,256]{2,1,0:T(8,128)(2,1)S(1)}, u32[]{:S(2)}, u32[]{:S(2)}) collective-permute-start(bf16[4,8,256]{2,1,0:T(8,128)(2,1)S(1)} %bitcast.59), channel_id=1, source_target_pairs={{0,4},{1,5},{2,6},{3,7},{4,0},{5,1},{6,2},{7,3},{8,12},{9,13},{10,... | collective-permute-start | bytes 49160 | tf_op jit(solution)/shard_map/ppermute | solution.py:238
  16.7 1.3 %collective-permute-start.3 = (bf16[4,4,8,256]{3,2,1,0:T(8,128)(2,1)S(1)}, bf16[4,4,8,256]{3,2,1,0:T(8,128)(2,1)S(1)}, u32[]{:S(2)}, u32[]{:S(2)}) collective-permute-start(bf16[4,4,8,256]{3,2,1,0:T(8,128)(2,1)S(1)} %pad_maximum_fusion.refs_0_), channel_id=1, source_target_pairs={{0,1},{1,0},{2,3},{3,2},{4,5},{5,4},{6,7},{7,6},{8,9},{9,8},{10,11... | collective-permute-start | bytes 196616 | tf_op jit(solution)/shard_map/ppermute | solution.py:233
  19.2 5.6 %collective-permute-start.6 = (bf16[4,8,256]{2,1,0:T(8,128)(2,1)S(1)}, bf16[4,8,256]{2,1,0:T(8,128)(2,1)S(1)}, u32[]{:S(2)}, u32[]{:S(2)}) collective-permute-start(bf16[4,8,256]{2,1,0:T(8,128)(2,1)S(1)} %get-tuple-element.55), channel_id=1, source_target_pairs={{0,6},{1,7},{2,4},{3,5},{4,2},{5,3},{6,0},{7,1},{8,14},{9,15},{10,... | collective-permute-start | bytes 49160 | tf_op jit(solution)/shard_map/ppermute | solution.py:238
  22.1 4.7 %collective-permute-start.5 = (bf16[4,8,256]{2,1,0:T(8,128)(2,1)S(1)}, bf16[4,8,256]{2,1,0:T(8,128)(2,1)S(1)}, u32[]{:S(2)}, u32[]{:S(2)}) collective-permute-start(bf16[4,8,256]{2,1,0:T(8,128)(2,1)S(1)} %get-tuple-element.55), channel_id=1, source_target_pairs={{0,4},{1,5},{2,6},{3,7},{4,0},{5,1},{6,2},{7,3},{8,12},{9,13},{10,... | collective-permute-start | bytes 49160 | tf_op jit(solution)/shard_map/ppermute | solution.py:238
  22.4 4.4 %collective-permute-start.4 = (bf16[4,8,256]{2,1,0:T(8,128)(2,1)S(1)}, bf16[4,8,256]{2,1,0:T(8,128)(2,1)S(1)}, u32[]{:S(2)}, u32[]{:S(2)}) collective-permute-start(bf16[4,8,256]{2,1,0:T(8,128)(2,1)S(1)} %get-tuple-element.55), channel_id=1, source_target_pairs={{0,2},{1,3},{2,0},{3,1},{4,6},{5,7},{6,4},{7,5},{8,10},{9,11},{10,... | collective-permute-start | bytes 49160 | tf_op jit(solution)/shard_map/ppermute | solution.py:238
  26.8 1.3 %collective-permute-start.7 = (bf16[4,4,8,256]{3,2,1,0:T(8,128)(2,1)S(1)}, bf16[4,4,8,256]{3,2,1,0:T(8,128)(2,1)S(1)}, u32[]{:S(2)}, u32[]{:S(2)}) collective-permute-start(bf16[4,4,8,256]{3,2,1,0:T(8,128)(2,1)S(1)} %pad_maximum_fusion.1.refs_0_), channel_id=1, source_target_pairs={{0,1},{1,0},{2,3},{3,2},{4,5},{5,4},{6,7},{7,6},{8,9},{9,8},{10,11... | collective-permute-start | bytes 196616 | tf_op jit(solution)/shard_map/ppermute | solution.py:233
  28.2 76.0 %slice-start.1 = ((s8[16777216]{0:T(1024)(128)(4,1)}), s8[4194304]{0:T(1024)(128)(4,1)S(1)}, s32[]{:S(2)}) async-start(s8[16777216]{0:T(1024)(128)(4,1)} %bitcast.52), calls=%async_computation.1 | async-start | bytes 8388608
  34.3 1.3 %collective-permute-start.8 = (bf16[4,8,512]{2,1,0:T(8,128)(2,1)S(1)}, bf16[4,8,512]{2,1,0:T(8,128)(2,1)S(1)}, u32[]{:S(2)}, u32[]{:S(2)}) collective-permute-start(bf16[4,8,512]{2,1,0:T(8,128)(2,1)S(1)} %get-tuple-element.59), channel_id=1, source_target_pairs={{0,1},{1,0},{2,3},{3,2},{4,5},{5,4},{6,7},{7,6},{8,9},{9,8},{10,11... | collective-permute-start | bytes 98312 | tf_op jit(solution)/shard_map/ppermute | solution.py:233
  35.6 6.2 %collective-permute-start.11 = (bf16[4,8,512]{2,1,0:T(8,128)(2,1)S(1)}, bf16[4,8,512]{2,1,0:T(8,128)(2,1)S(1)}, u32[]{:S(2)}, u32[]{:S(2)}) collective-permute-start(bf16[4,8,512]{2,1,0:T(8,128)(2,1)S(1)} %fusion), channel_id=1, source_target_pairs={{0,6},{1,7},{2,4},{3,5},{4,2},{5,3},{6,0},{7,1},{8,14},{9,15},{10,... | collective-permute-start | bytes 98312 | tf_op jit(solution)/shard_map/ppermute | solution.py:238
  37.6 5.2 %collective-permute-start.10 = (bf16[4,8,512]{2,1,0:T(8,128)(2,1)S(1)}, bf16[4,8,512]{2,1,0:T(8,128)(2,1)S(1)}, u32[]{:S(2)}, u32[]{:S(2)}) collective-permute-start(bf16[4,8,512]{2,1,0:T(8,128)(2,1)S(1)} %fusion), channel_id=1, source_target_pairs={{0,4},{1,5},{2,6},{3,7},{4,0},{5,1},{6,2},{7,3},{8,12},{9,13},{10,... | collective-permute-start | bytes 98312 | tf_op jit(solution)/shard_map/ppermute | solution.py:238
  37.7 5.1 %collective-permute-start.9 = (bf16[4,8,512]{2,1,0:T(8,128)(2,1)S(1)}, bf16[4,8,512]{2,1,0:T(8,128)(2,1)S(1)}, u32[]{:S(2)}, u32[]{:S(2)}) collective-permute-start(bf16[4,8,512]{2,1,0:T(8,128)(2,1)S(1)} %fusion), channel_id=1, source_target_pairs={{0,2},{1,3},{2,0},{3,1},{4,6},{5,7},{6,4},{7,5},{8,10},{9,11},{10,... | collective-permute-start | bytes 98312 | tf_op jit(solution)/shard_map/ppermute | solution.py:238
  42.8 1.3 %collective-permute-start.12 = (bf16[4,8,512]{2,1,0:T(8,128)(2,1)S(1)}, bf16[4,8,512]{2,1,0:T(8,128)(2,1)S(1)}, u32[]{:S(2)}, u32[]{:S(2)}) collective-permute-start(bf16[4,8,512]{2,1,0:T(8,128)(2,1)S(1)} %add_convert_fusion.2.own_ref), channel_id=1, source_target_pairs={{0,1},{1,0},{2,3},{3,2},{4,5},{5,4},{6,7},{7,6},{8,9},{9,8},{10,11... | collective-permute-start | bytes 98312 | tf_op jit(solution)/shard_map/ppermute | solution.py:233
  45.3 5.5 %collective-permute-start.15 = (bf16[8,512]{1,0:T(8,128)(2,1)S(1)}, bf16[8,512]{1,0:T(8,128)(2,1)S(1)}, u32[]{:S(2)}, u32[]{:S(2)}) collective-permute-start(bf16[8,512]{1,0:T(8,128)(2,1)S(1)} %get-tuple-element.60), channel_id=1, source_target_pairs={{0,6},{1,7},{2,4},{3,5},{4,2},{5,3},{6,0},{7,1},{8,14},{9,15},{10,... | collective-permute-start | bytes 24584 | tf_op jit(solution)/shard_map/ppermute | solution.py:238
  47.4 4.5 %collective-permute-start.14 = (bf16[8,512]{1,0:T(8,128)(2,1)S(1)}, bf16[8,512]{1,0:T(8,128)(2,1)S(1)}, u32[]{:S(2)}, u32[]{:S(2)}) collective-permute-start(bf16[8,512]{1,0:T(8,128)(2,1)S(1)} %get-tuple-element.60), channel_id=1, source_target_pairs={{0,4},{1,5},{2,6},{3,7},{4,0},{5,1},{6,2},{7,3},{8,12},{9,13},{10,... | collective-permute-start | bytes 24584 | tf_op jit(solution)/shard_map/ppermute | solution.py:238
  48.0 4.0 %collective-permute-start.13 = (bf16[8,512]{1,0:T(8,128)(2,1)S(1)}, bf16[8,512]{1,0:T(8,128)(2,1)S(1)}, u32[]{:S(2)}, u32[]{:S(2)}) collective-permute-start(bf16[8,512]{1,0:T(8,128)(2,1)S(1)} %get-tuple-element.60), channel_id=1, source_target_pairs={{0,2},{1,3},{2,0},{3,1},{4,6},{5,7},{6,4},{7,5},{8,10},{9,11},{10,... | collective-permute-start | bytes 24584 | tf_op jit(solution)/shard_map/ppermute | solution.py:238
  52.0 1.3 %collective-permute-start.16 = (bf16[4,8,512]{2,1,0:T(8,128)(2,1)S(1)}, bf16[4,8,512]{2,1,0:T(8,128)(2,1)S(1)}, u32[]{:S(2)}, u32[]{:S(2)}) collective-permute-start(bf16[4,8,512]{2,1,0:T(8,128)(2,1)S(1)} %pad_maximum_fusion.2.x_own_ref), channel_id=1, source_target_pairs={{0,1},{1,0},{2,3},{3,2},{4,5},{5,4},{6,7},{7,6},{8,9},{9,8},{10,11... | collective-permute-start | bytes 98312 | tf_op jit(solution)/shard_map/ppermute | solution.py:233
  55.4 1.3 %collective-permute-start.17 = (bf16[4,8,512]{2,1,0:T(8,128)(2,1)S(1)}, bf16[4,8,512]{2,1,0:T(8,128)(2,1)S(1)}, u32[]{:S(2)}, u32[]{:S(2)}) collective-permute-start(bf16[4,8,512]{2,1,0:T(8,128)(2,1)S(1)} %get-tuple-element.65), channel_id=1, source_target_pairs={{0,1},{1,0},{2,3},{3,2},{4,5},{5,4},{6,7},{7,6},{8,9},{9,8},{10,11... | collective-permute-start | bytes 98312 | tf_op jit(solution)/shard_map/ppermute | solution.py:233
  56.7 4.2 %collective-permute-start.20 = (bf16[4,8,512]{2,1,0:T(8,128)(2,1)S(1)}, bf16[4,8,512]{2,1,0:T(8,128)(2,1)S(1)}, u32[]{:S(2)}, u32[]{:S(2)}) collective-permute-start(bf16[4,8,512]{2,1,0:T(8,128)(2,1)S(1)} %fusion.1), channel_id=1, source_target_pairs={{0,24},{8,0},{16,8},{24,16},{1,25},{9,1},{17,9},{25,17},{2,26},{10... | collective-permute-start | bytes 98312 | tf_op jit(solution)/shard_map/ppermute | solution.py:250
  59.3 4.3 %collective-permute-start.19 = (bf16[4,8,512]{2,1,0:T(8,128)(2,1)S(1)}, bf16[4,8,512]{2,1,0:T(8,128)(2,1)S(1)}, u32[]{:S(2)}, u32[]{:S(2)}) collective-permute-start(bf16[4,8,512]{2,1,0:T(8,128)(2,1)S(1)} %fusion.1), channel_id=1, source_target_pairs={{0,16},{8,24},{16,0},{24,8},{1,17},{9,25},{17,1},{25,9},{2,18},{10... | collective-permute-start | bytes 98312 | tf_op jit(solution)/shard_map/ppermute | solution.py:250
  60.0 4.8 %collective-permute-start.18 = (bf16[4,8,512]{2,1,0:T(8,128)(2,1)S(1)}, bf16[4,8,512]{2,1,0:T(8,128)(2,1)S(1)}, u32[]{:S(2)}, u32[]{:S(2)}) collective-permute-start(bf16[4,8,512]{2,1,0:T(8,128)(2,1)S(1)} %fusion.1), channel_id=1, source_target_pairs={{0,8},{8,16},{16,24},{24,0},{1,9},{9,17},{17,25},{25,1},{2,10},{10... | collective-permute-start | bytes 98312 | tf_op jit(solution)/shard_map/ppermute | solution.py:250
  64.8 5.8 %collective-permute-start.23 = (bf16[4,8,512]{2,1,0:T(8,128)(2,1)S(1)}, bf16[4,8,512]{2,1,0:T(8,128)(2,1)S(1)}, u32[]{:S(2)}, u32[]{:S(2)}) collective-permute-start(bf16[4,8,512]{2,1,0:T(8,128)(2,1)S(1)} %fusion.31), channel_id=1, source_target_pairs={{0,6},{1,7},{2,4},{3,5},{4,2},{5,3},{6,0},{7,1},{8,14},{9,15},{10,... | collective-permute-start | bytes 98312 | tf_op jit(solution)/shard_map/ppermute | solution.py:238
  66.0 5.4 %collective-permute-start.22 = (bf16[4,8,512]{2,1,0:T(8,128)(2,1)S(1)}, bf16[4,8,512]{2,1,0:T(8,128)(2,1)S(1)}, u32[]{:S(2)}, u32[]{:S(2)}) collective-permute-start(bf16[4,8,512]{2,1,0:T(8,128)(2,1)S(1)} %fusion.31), channel_id=1, source_target_pairs={{0,4},{1,5},{2,6},{3,7},{4,0},{5,1},{6,2},{7,3},{8,12},{9,13},{10,... | collective-permute-start | bytes 98312 | tf_op jit(solution)/shard_map/ppermute | solution.py:238
  67.1 4.3 %collective-permute-start.21 = (bf16[4,8,512]{2,1,0:T(8,128)(2,1)S(1)}, bf16[4,8,512]{2,1,0:T(8,128)(2,1)S(1)}, u32[]{:S(2)}, u32[]{:S(2)}) collective-permute-start(bf16[4,8,512]{2,1,0:T(8,128)(2,1)S(1)} %fusion.31), channel_id=1, source_target_pairs={{0,2},{1,3},{2,0},{3,1},{4,6},{5,7},{6,4},{7,5},{8,10},{9,11},{10,... | collective-permute-start | bytes 98312 | tf_op jit(solution)/shard_map/ppermute | solution.py:238
  71.4 1.3 %collective-permute-start.24 = (bf16[4,8,512]{2,1,0:T(8,128)(2,1)S(1)}, bf16[4,8,512]{2,1,0:T(8,128)(2,1)S(1)}, u32[]{:S(2)}, u32[]{:S(2)}) collective-permute-start(bf16[4,8,512]{2,1,0:T(8,128)(2,1)S(1)} %add_convert_fusion.1.own_ref), channel_id=1, source_target_pairs={{0,1},{1,0},{2,3},{3,2},{4,5},{5,4},{6,7},{7,6},{8,9},{9,8},{10,11... | collective-permute-start | bytes 98312 | tf_op jit(solution)/shard_map/ppermute | solution.py:233
  74.5 1.2 collective-permute-start.25
  75.7 5.9 %collective-permute-start.28 = (bf16[4,8,512]{2,1,0:T(8,128)(2,1)S(1)}, bf16[4,8,512]{2,1,0:T(8,128)(2,1)S(1)}, u32[]{:S(2)}, u32[]{:S(2)}) collective-permute-start(bf16[4,8,512]{2,1,0:T(8,128)(2,1)S(1)} %fusion.2), channel_id=1, source_target_pairs={{0,6},{1,7},{2,4},{3,5},{4,2},{5,3},{6,0},{7,1},{8,14},{9,15},{10,... | collective-permute-start | bytes 98312 | tf_op jit(solution)/shard_map/ppermute | solution.py:238
  78.0 4.9 %collective-permute-start.27 = (bf16[4,8,512]{2,1,0:T(8,128)(2,1)S(1)}, bf16[4,8,512]{2,1,0:T(8,128)(2,1)S(1)}, u32[]{:S(2)}, u32[]{:S(2)}) collective-permute-start(bf16[4,8,512]{2,1,0:T(8,128)(2,1)S(1)} %fusion.2), channel_id=1, source_target_pairs={{0,4},{1,5},{2,6},{3,7},{4,0},{5,1},{6,2},{7,3},{8,12},{9,13},{10,... | collective-permute-start | bytes 98312 | tf_op jit(solution)/shard_map/ppermute | solution.py:238
  79.1 4.1 %collective-permute-start.26 = (bf16[4,8,512]{2,1,0:T(8,128)(2,1)S(1)}, bf16[4,8,512]{2,1,0:T(8,128)(2,1)S(1)}, u32[]{:S(2)}, u32[]{:S(2)}) collective-permute-start(bf16[4,8,512]{2,1,0:T(8,128)(2,1)S(1)} %fusion.2), channel_id=1, source_target_pairs={{0,2},{1,3},{2,0},{3,1},{4,6},{5,7},{6,4},{7,5},{8,10},{9,11},{10,... | collective-permute-start | bytes 98312 | tf_op jit(solution)/shard_map/ppermute | solution.py:238
  83.2 1.3 %collective-permute-start.29 = (bf16[4,8,512]{2,1,0:T(8,128)(2,1)S(1)}, bf16[4,8,512]{2,1,0:T(8,128)(2,1)S(1)}, u32[]{:S(2)}, u32[]{:S(2)}) collective-permute-start(bf16[4,8,512]{2,1,0:T(8,128)(2,1)S(1)} %add_convert_fusion.own_ref), channel_id=1, source_target_pairs={{0,1},{1,0},{2,3},{3,2},{4,5},{5,4},{6,7},{7,6},{8,9},{9,8},{10,11... | collective-permute-start | bytes 98312 | tf_op jit(solution)/shard_map/ppermute | solution.py:233
  86.0 1.2 collective-permute-start.30
  87.2 5.5 %collective-permute-start.33 = (bf16[1,8,512]{2,1,0:T(8,128)(2,1)S(1)}, bf16[1,8,512]{2,1,0:T(8,128)(2,1)S(1)}, u32[]{:S(2)}, u32[]{:S(2)}) collective-permute-start(bf16[1,8,512]{2,1,0:T(8,128)(2,1)S(1)} %get-tuple-element.95), channel_id=1, source_target_pairs={{0,6},{1,7},{2,4},{3,5},{4,2},{5,3},{6,0},{7,1},{8,14},{9,15},{10,... | collective-permute-start | bytes 24584 | tf_op jit(solution)/shard_map/ppermute | solution.py:238
  88.8 4.6 %collective-permute-start.32 = (bf16[1,8,512]{2,1,0:T(8,128)(2,1)S(1)}, bf16[1,8,512]{2,1,0:T(8,128)(2,1)S(1)}, u32[]{:S(2)}, u32[]{:S(2)}) collective-permute-start(bf16[1,8,512]{2,1,0:T(8,128)(2,1)S(1)} %get-tuple-element.96), channel_id=1, source_target_pairs={{0,4},{1,5},{2,6},{3,7},{4,0},{5,1},{6,2},{7,3},{8,12},{9,13},{10,... | collective-permute-start | bytes 24584 | tf_op jit(solution)/shard_map/ppermute | solution.py:238
  89.7 3.7 %collective-permute-start.31 = (bf16[1,8,512]{2,1,0:T(8,128)(2,1)S(1)}, bf16[1,8,512]{2,1,0:T(8,128)(2,1)S(1)}, u32[]{:S(2)}, u32[]{:S(2)}) collective-permute-start(bf16[1,8,512]{2,1,0:T(8,128)(2,1)S(1)} %get-tuple-element.97), channel_id=1, source_target_pairs={{0,2},{1,3},{2,0},{3,1},{4,6},{5,7},{6,4},{7,5},{8,10},{9,11},{10,... | collective-permute-start | bytes 24584 | tf_op jit(solution)/shard_map/ppermute | solution.py:238
  94.1 1.2 collective-permute-start.34
  95.3 6.1 %collective-permute-start.37 = (bf16[4,8,512]{2,1,0:T(8,128)(2,1)S(1)}, bf16[4,8,512]{2,1,0:T(8,128)(2,1)S(1)}, u32[]{:S(2)}, u32[]{:S(2)}) collective-permute-start(bf16[4,8,512]{2,1,0:T(8,128)(2,1)S(1)} %fusion.3), channel_id=1, source_target_pairs={{0,6},{1,7},{2,4},{3,5},{4,2},{5,3},{6,0},{7,1},{8,14},{9,15},{10,... | collective-permute-start | bytes 98312 | tf_op jit(solution)/shard_map/ppermute | solution.py:238
  97.6 4.9 %collective-permute-start.36 = (bf16[4,8,512]{2,1,0:T(8,128)(2,1)S(1)}, bf16[4,8,512]{2,1,0:T(8,128)(2,1)S(1)}, u32[]{:S(2)}, u32[]{:S(2)}) collective-permute-start(bf16[4,8,512]{2,1,0:T(8,128)(2,1)S(1)} %fusion.3), channel_id=1, source_target_pairs={{0,4},{1,5},{2,6},{3,7},{4,0},{5,1},{6,2},{7,3},{8,12},{9,13},{10,... | collective-permute-start | bytes 98312 | tf_op jit(solution)/shard_map/ppermute | solution.py:238
  98.7 4.1 %collective-permute-start.35 = (bf16[4,8,512]{2,1,0:T(8,128)(2,1)S(1)}, bf16[4,8,512]{2,1,0:T(8,128)(2,1)S(1)}, u32[]{:S(2)}, u32[]{:S(2)}) collective-permute-start(bf16[4,8,512]{2,1,0:T(8,128)(2,1)S(1)} %fusion.3), channel_id=1, source_target_pairs={{0,2},{1,3},{2,0},{3,1},{4,6},{5,7},{6,4},{7,5},{8,10},{9,11},{10,... | collective-permute-start | bytes 98312 | tf_op jit(solution)/shard_map/ppermute | solution.py:238
  102.8 1.3 %collective-permute-start.38 = (bf16[4,8,512]{2,1,0:T(8,128)(2,1)S(1)}, bf16[4,8,512]{2,1,0:T(8,128)(2,1)S(1)}, u32[]{:S(2)}, u32[]{:S(2)}) collective-permute-start(bf16[4,8,512]{2,1,0:T(8,128)(2,1)S(1)} %get-tuple-element.86.refs_2_), channel_id=1, source_target_pairs={{0,1},{1,0},{2,3},{3,2},{4,5},{5,4},{6,7},{7,6},{8,9},{9,8},{10,11... | collective-permute-start | bytes 98312 | tf_op jit(solution)/shard_map/ppermute | solution.py:233
  106.9 1.4 %collective-permute-start.39 = (bf16[4,4,8,256]{3,2,1,0:T(8,128)(2,1)S(1)}, bf16[4,4,8,256]{3,2,1,0:T(8,128)(2,1)S(1)}, u32[]{:S(2)}, u32[]{:S(2)}) collective-permute-start(bf16[4,4,8,256]{3,2,1,0:T(8,128)(2,1)S(1)} %get-tuple-element.77), channel_id=1, source_target_pairs={{0,1},{1,0},{2,3},{3,2},{4,5},{5,4},{6,7},{7,6},{8,9},{9,8},{10,11... | collective-permute-start | bytes 196616 | tf_op jit(solution)/shard_map/ppermute | solution.py:233
  108.3 5.7 %collective-permute-start.42 = (bf16[4,8,256]{2,1,0:T(8,128)(2,1)S(1)}, bf16[4,8,256]{2,1,0:T(8,128)(2,1)S(1)}, u32[]{:S(2)}, u32[]{:S(2)}) collective-permute-start(bf16[4,8,256]{2,1,0:T(8,128)(2,1)S(1)} %get-tuple-element.91), channel_id=1, source_target_pairs={{0,6},{1,7},{2,4},{3,5},{4,2},{5,3},{6,0},{7,1},{8,14},{9,15},{10,... | collective-permute-start | bytes 49160 | tf_op jit(solution)/shard_map/ppermute | solution.py:238
  110.0 4.7 %collective-permute-start.41 = (bf16[4,8,256]{2,1,0:T(8,128)(2,1)S(1)}, bf16[4,8,256]{2,1,0:T(8,128)(2,1)S(1)}, u32[]{:S(2)}, u32[]{:S(2)}) collective-permute-start(bf16[4,8,256]{2,1,0:T(8,128)(2,1)S(1)} %get-tuple-element.92), channel_id=1, source_target_pairs={{0,4},{1,5},{2,6},{3,7},{4,0},{5,1},{6,2},{7,3},{8,12},{9,13},{10,... | collective-permute-start | bytes 49160 | tf_op jit(solution)/shard_map/ppermute | solution.py:238
  110.7 4.0 %collective-permute-start.40 = (bf16[4,8,256]{2,1,0:T(8,128)(2,1)S(1)}, bf16[4,8,256]{2,1,0:T(8,128)(2,1)S(1)}, u32[]{:S(2)}, u32[]{:S(2)}) collective-permute-start(bf16[4,8,256]{2,1,0:T(8,128)(2,1)S(1)} %get-tuple-element.93), channel_id=1, source_target_pairs={{0,2},{1,3},{2,0},{3,1},{4,6},{5,7},{6,4},{7,5},{8,10},{9,11},{10,... | collective-permute-start | bytes 49160 | tf_op jit(solution)/shard_map/ppermute | solution.py:238
  115.1 1.3 %collective-permute-start.43 = (bf16[4,4,8,256]{3,2,1,0:T(8,128)(2,1)S(1)}, bf16[4,4,8,256]{3,2,1,0:T(8,128)(2,1)S(1)}, u32[]{:S(2)}, u32[]{:S(2)}) collective-permute-start(bf16[4,4,8,256]{3,2,1,0:T(8,128)(2,1)S(1)} %get-tuple-element.80), channel_id=1, source_target_pairs={{0,1},{1,0},{2,3},{3,2},{4,5},{5,4},{6,7},{7,6},{8,9},{9,8},{10,11... | collective-permute-start | bytes 196616 | tf_op jit(solution)/shard_map/ppermute | solution.py:233
  116.4 4.2 %collective-permute-start.44 = (bf16[4,8,256]{2,1,0:T(8,128)(2,1)S(1)}, bf16[4,8,256]{2,1,0:T(8,128)(2,1)S(1)}, u32[]{:S(2)}, u32[]{:S(2)}) collective-permute-start(bf16[4,8,256]{2,1,0:T(8,128)(2,1)S(1)} %get-tuple-element.88), channel_id=1, source_target_pairs={{0,2},{1,3},{2,0},{3,1},{4,6},{5,7},{6,4},{7,5},{8,10},{9,11},{10,... | collective-permute-start | bytes 49160 | tf_op jit(solution)/shard_map/ppermute | solution.py:238
  118.3 5.5 %collective-permute-start.46 = (bf16[4,8,256]{2,1,0:T(8,128)(2,1)S(1)}, bf16[4,8,256]{2,1,0:T(8,128)(2,1)S(1)}, u32[]{:S(2)}, u32[]{:S(2)}) collective-permute-start(bf16[4,8,256]{2,1,0:T(8,128)(2,1)S(1)} %get-tuple-element.89), channel_id=1, source_target_pairs={{0,6},{1,7},{2,4},{3,5},{4,2},{5,3},{6,0},{7,1},{8,14},{9,15},{10,... | collective-permute-start | bytes 49160 | tf_op jit(solution)/shard_map/ppermute | solution.py:238
  119.8 4.6 %collective-permute-start.45 = (bf16[4,8,256]{2,1,0:T(8,128)(2,1)S(1)}, bf16[4,8,256]{2,1,0:T(8,128)(2,1)S(1)}, u32[]{:S(2)}, u32[]{:S(2)}) collective-permute-start(bf16[4,8,256]{2,1,0:T(8,128)(2,1)S(1)} %get-tuple-element.90), channel_id=1, source_target_pairs={{0,4},{1,5},{2,6},{3,7},{4,0},{5,1},{6,2},{7,3},{8,12},{9,13},{10,... | collective-permute-start | bytes 49160 | tf_op jit(solution)/shard_map/ppermute | solution.py:238
  (10 other events, 252.7 us)

commit v6 on v5

--- a/solution.py
+++ b/solution.py
@@ -17,6 +17,10 @@
 
 def pinned(w):
     return pltpu.with_memory_space_constraint(w, pltpu.VMEM)
+
+
+def outside(w):
+    return pltpu.with_memory_space_constraint(w, pltpu.HBM)
 
 
 def call(
@@ -42,14 +46,6 @@
     return lax.dot_general(x, w, (((1,), (0,)), ((), ())), preferred_element_type=F32)
 
 
-def split_at(refs, *counts):
-    out = []
-    for c in counts:
-        out.append(refs[:c])
-        refs = refs[c:]
-    return *out, refs
-
-
 def walk(plan_ref, sets, tiles, blocks, tile, visit, carry):
     def trip(i, carry):
         at = []
@@ -69,14 +65,23 @@
     return jnp.where(inside, found, 0.0)
 
 
-def prepare(weights, lists, first, heights, widths):
-    count = len(lists)
-
-    def one(rows_ref, scalar_ref, height_ref, list_ref, plan_ref, out_ref, first, width):
-        sets, length = rows_ref.shape
-        tiles, blocks = length // LANES, width // LANES
+def prepare(after, rows, first, height, width, sets):
+    of = range(*sets)
+    sets, length = rows.shape
+    tiles, blocks = length // LANES, width // LANES
+
+    def body(after_ref, given_ref, height_ref, list_ref, plan_ref, out_ref, rows_ref, scalar_ref, sems):
+        copies = [
+            pltpu.make_async_copy(given_ref, target, sems.at[i])
+            for i, target in enumerate((rows_ref, scalar_ref))
+        ]
+        for copy in copies:
+            copy.start()
         out_ref[...] = jnp.full(out_ref.shape, -1, I32)
-        used = [height_ref[s] - first for s in range(sets)]
+        start = lax.axis_index("rows") * first
+        used = [height_ref[s] - start for s in range(sets)]
+        for copy in copies:
+            copy.wait()
         lane = lax.broadcasted_iota(I32, (1, LANES), 1)
         for tile in range(tiles):
             lanes = slice(tile * LANES, (tile + 1) * LANES)
@@ -85,7 +90,8 @@
             for s in range(sets):
                 line = jnp.where(lane + tile * LANES < used[s], rows_ref[s : s + 1, lanes], -1)
                 list_ref[s : s + 1, lanes] = line
-                cols.append(jnp.transpose(jnp.broadcast_to(line, (LANES, LANES))))
+                if s in of:
+                    cols.append(jnp.transpose(jnp.broadcast_to(line, (LANES, LANES))))
                 end = jnp.maximum(jnp.minimum(used[s], (tile + 1) * LANES) - 1, 0)
                 lo = lax.shift_right_logical(scalar_ref[s, tile * LANES], 7)
                 hi = lax.shift_right_logical(scalar_ref[s, end], 7)
@@ -98,6 +104,7 @@
             def visit(at, carry):
                 across = lax.broadcasted_iota(I32, (LANES, LANES), 1)
                 got = []
+                at = [(s - of.start, block) for s, block in at if s in of]
                 for s, block in at:
                     hit = cols[s] == across + block * LANES
                     got.append(jnp.sum(jnp.where(hit, spots, 0), axis=0, keepdims=True))
@@ -107,65 +114,37 @@
 
             walk(plan_ref, sets, tiles, blocks, tile, visit, 0)
 
-    held = len(weights)
-
-    def body(*refs):
-        sources, rows, heights, refs = split_at(refs, held, count, count)
-        targets, outs, lines, scalars, (weight_sems, row_sems) = split_at(
-            refs, held, 3 * count, count, count
-        )
-        row = lax.axis_index("rows")
-        ahead = []
-        for i in range(count):
-            ahead.append(pltpu.make_async_copy(rows[i], lines[i], row_sems.at[2 * i]))
-            ahead.append(pltpu.make_async_copy(rows[i], scalars[i], row_sems.at[2 * i + 1]))
-        behind = [
-            pltpu.make_async_copy(source, target, weight_sems.at[i])
-            for i, (source, target) in enumerate(zip(sources, targets))
-        ]
-        for copy in ahead + behind:
-            copy.start()
-        for copy in ahead:
-            copy.wait()
-        for i in range(count):
-            one(lines[i], scalars[i], heights[i], *outs[3 * i : 3 * i + 3], row * first[i], widths[i])
-        for copy in behind:
-            copy.wait()
-
-    shapes = [pltpu.VMEM(w.shape, w.dtype) for w in weights]
-    for rows, width in zip(lists, widths):
-        sets, length = rows.shape
-        shapes += [
+    return call(
+        body,
+        [
             (rows.shape, I32),
-            (((sets + 1) * (length // LANES),), I32),
-            ((sets, width // LANES + 1, 8, LANES), I32),
-        ]
-    outside = pl.BlockSpec(memory_space=pltpu.HBM)
-    got = call(
-        body,
-        shapes,
-        [pltpu.with_memory_space_constraint(x, pltpu.HBM) for x in (*weights, *lists)] + heights,
-        [outside] * (held + count) + [SMEM] * count,
-        out_specs=[VMEM] * held + [VMEM, SMEM, VMEM] * count,
-        scratch=[pltpu.VMEM(x.shape, I32) for x in lists]
-        + [pltpu.SMEM(x.shape, I32) for x in lists]
-        + [pltpu.SemaphoreType.DMA((held,)), pltpu.SemaphoreType.DMA((2 * count,))],
-        moved=20 << 20,
+            (((sets + 1) * tiles,), I32),
+            ((len(of), blocks + 1, 8, LANES), I32),
+        ],
+        [after, outside(rows), height],
+        [pl.BlockSpec(memory_space=pl.ANY), pl.BlockSpec(memory_space=pltpu.HBM), SMEM],
+        out_specs=[VMEM, SMEM, VMEM],
+        scratch=[
+            pltpu.VMEM(rows.shape, I32),
+            pltpu.SMEM(rows.shape, I32),
+            pltpu.SemaphoreType.DMA((2,)),
+        ],
+        moved=8 << 20,
         limit=4 << 20,
         name="prepare",
     )
-    return got[:held], [got[held + 3 * i : held + 3 * i + 3] for i in range(count)]
-
-
-def scatter_walk(plan_ref, inverse_ref, update_ref, acc_ref, tiles):
-    sets, blocks = inverse_ref.shape[0], inverse_ref.shape[1] - 1
+
+
+def scatter_walk(plan_ref, inverse_refs, update_ref, acc_ref, tiles):
+    sets, blocks = update_ref.shape[0], inverse_refs[0].shape[1] - 1
+    inverse = [ref.at[s] for ref in inverse_refs for s in range(ref.shape[0])]
     for tile in range(tiles):
 
         def visit(at, carry):
             got = []
             for s, block in at:
                 x = update_ref[s, :, tile * LANES : (tile + 1) * LANES]
-                got.append(pick(x, inverse_ref[s, block] - tile * LANES))
+                got.append(pick(x, inverse[s][block] - tile * LANES))
             for (s, block), g in zip(at, got):
                 acc_ref[block] += g
             return carry
@@ -211,7 +190,7 @@
 def unite(own_ref, other_ref, out_ref, *at, xor=False):
     odd, w = core(), own_ref.shape[-1]
     for k in range(own_ref.shape[0]):
-        c = chip() ^ k if xor else k
+        c = chip() ^ (-k % own_ref.shape[0]) if xor else k
         out_ref[:, spot(2 * c + odd, w)] = own_ref[(k,) + at]
         out_ref[:, spot(2 * c + 1 - odd, w)] = other_ref[(k,) + at]
 
@@ -238,9 +217,14 @@
     return lax.ppermute(x, "rows", [(i, i ^ (2 * k)) for i in range(n)])
 
 
+def from_chips(piece):
+    chips = lax.axis_size("rows") // 2
+    return [far(piece(k), k) for k in range(chips - 1, 0, -1)]
+
+
 def chips_sum(x):
     b = x.astype(BF16)
-    return x + sum(far(b, k).astype(F32) for k in range(1, lax.axis_size("rows") // 2))
+    return x + sum(got.astype(F32) for got in from_chips(lambda k: b))
 
 
 def leaf_sum(x):
@@ -282,7 +266,7 @@
         return lax.axis_index("leaf") * n + lax.axis_index("rows")
 
     def far_gather(x):
-        return jnp.stack([x] + [far(x, k) for k in range(1, chips)])
+        return jnp.stack([x] + from_chips(lambda k: x))
 
     def leaf_columns(x):
         got = all_to_all(jnp.broadcast_to(x[None], (n,) + x.shape))
@@ -299,18 +283,28 @@
         rhs = lax.dynamic_update_slice_in_dim(
             jnp.zeros((rcount, root_width), F32), root_rhs, flat() * root_cols, 1
         )
-    lb = jnp.moveaxis(leaf_rhs.astype(BF16), 1, 0)
+    weights = (leaf_inv, leaf_panel, parent_inv, parent_panel, root_inv)
+
+    def round_rhs(x_ref, *refs):
+        out_ref = refs[-1]
+        for s in range(leaves):
+            out_ref[s] = x_ref[:, s, :].astype(BF16)
+
+    lb = call(
+        round_rhs,
+        [((leaves, rcount, leaf_cols), BF16)],
+        [leaf_rhs] + [outside(w) for w in weights],
+        [VMEM] + [pl.BlockSpec(memory_space=pltpu.HBM)] * len(weights),
+        name="round_rhs",
+    )[0]
+    half = leaves // 2
+
+    def prepare_leaves(after, *sets):
+        return prepare(after, leaf_rows, leaf_local, leaf_height, tall, sets)
+
+    leaf_list, leaf_plan, inverse_low = prepare_leaves(lb, 0, half)
     lb = far_gather(lb) if leaf_aligned else leaf_columns(lb)
-    early, prepared = prepare(
-        [leaf_inv, leaf_panel],
-        [leaf_rows, parent_rows],
-        [leaf_local, parent_local],
-        [leaf_height, parent_height],
-        [tall, root_width],
-    )
-    lb, early, prepared, rhs = lax.optimization_barrier((lb, early, prepared, rhs))
-    leaf_inv_early, leaf_panel_early = early
-    (leaf_list, leaf_plan, leaf_inverse), (parent_list, parent_plan, parent_inverse) = prepared
+    lb, inverse_low, rhs = lax.optimization_barrier((lb, inverse_low, rhs))
     lb = (lb, swap(lb)) if leaf_aligned else (lb,)
 
     def leaf_solve(*refs):
@@ -323,25 +317,28 @@
     ly, lyb = call(
         leaf_solve,
         [((leaves, rcount, leaf_cols), F32), ((leaves, rcount, leaf_cols), BF16)],
-        [*lb, pinned(leaf_inv_early)],
+        [*lb, pinned(leaf_inv)],
         [VMEM] * (len(lb) + 1),
         scratch=[pltpu.VMEM((rcount, leaf_width), BF16)],
         name="leaf_solve",
     )
+    inverse_high = prepare_leaves(lyb, half, leaves)[2]
     if leaf_aligned:
-        lyb = far_gather(lyb)
+        lyb, inverse_high = lax.optimization_barrier((far_gather(lyb), inverse_high))
         lyb = (lyb, swap(lyb))
     else:
         lyb = (leaf_columns(lyb),)
+    leaf_inverse = (inverse_low, inverse_high)
 
     def leaf_update(*refs):
         x_refs, refs = refs[: len(lyb)], refs[len(lyb) :]
-        plan_ref, w_ref, inverse_ref, rhs_ref, own_ref, other_ref, root_ref, *refs = refs
+        plan_ref, w_ref, *inverse_refs, rhs_ref, own_ref, other_ref, root_ref = refs[:-4]
+        refs = refs[-4:]
         x_ref, update_ref, acc_ref, sum_ref = refs
         acc_ref[...] = jnp.zeros(acc_ref.shape, F32)
         for s in range(leaves):
             update_ref[s] = times_transposed(join_in(x_refs, x_ref, s), w_ref[s])
-        scatter_walk(plan_ref, inverse_ref, update_ref, acc_ref, leaf_local // LANES)
+        scatter_walk(plan_ref, inverse_refs, update_ref, acc_ref, leaf_local // LANES)
         for b in range(parent_width // LANES):
             sum_ref[:, b * LANES : (b + 1) * LANES] = -acc_ref[b]
         sum_ref[:, spot(lax.axis_index("rows"), parent_cols)] += rhs_ref[:, 0, :]
@@ -356,8 +353,8 @@
             ((chips, rcount, parent_cols), BF16),
             ((root_width // LANES, rcount, LANES), F32),
         ],
-        [*lyb, leaf_plan, pinned(leaf_panel_early), leaf_inverse, parent_rhs],
-        [VMEM] * len(lyb) + [SMEM] + [VMEM] * 3,
+        [*lyb, leaf_plan, pinned(leaf_panel), *leaf_inverse, parent_rhs],
+        [VMEM] * len(lyb) + [SMEM] + [VMEM] * 4,
         scratch=[
             pltpu.VMEM((rcount, leaf_width), BF16),
             pltpu.VMEM((leaves, rcount, leaf_local), F32),
@@ -382,7 +379,10 @@
         scratch=[pltpu.VMEM((rcount, parent_width), BF16)],
         name="parent_solve",
     )
-    pyb = far_gather(pyb)
+    parent_list, parent_plan, parent_inverse = prepare(
+        pyb, parent_rows, parent_local, parent_height, root_width, (0, 1)
+    )
+    pyb, parent_inverse = lax.optimization_barrier((far_gather(pyb), parent_inverse))
 
     def parent_update(
         plan_ref, x_own_ref, x_other_ref, w_ref, inverse_ref, root_ref, rhs_ref, own_ref, other_ref,
@@ -392,7 +392,7 @@
         for b in range(root_width // LANES):
             acc_ref[b] = root_ref[b]
         update_ref[0] = times_transposed(x_ref[...], w_ref[0])
-        scatter_walk(plan_ref, inverse_ref, update_ref, acc_ref, parent_local // LANES)
+        scatter_walk(plan_ref, [inverse_ref], update_ref, acc_ref, parent_local // LANES)
         for b in range(root_width // LANES):
             sum_ref[:, b * LANES : (b + 1) * LANES] = -acc_ref[b]
         if root_aligned:
@@ -457,7 +457,7 @@
     def reduce(own, other):
         other = swap(other)
         sums = [own[k] + other[k].astype(F32) for k in range(chips)]
-        return [sums[0]] + [far(sums[k].astype(BF16), k) for k in range(1, chips)]
+        return [sums[0]] + from_chips(lambda k: sums[k].astype(BF16))
 
     def parent_back(
         plan_ref, own_ref, other_ref, rows_ref, w_ref, out_ref, whole_ref, sol_ref, found_ref, x_ref,

time: 126 us -> 123 us (0.976)
  waiting for transfers between devices: 42.2 us -> 35.5 us
  Pallas kernels: 28 us -> 31.9 us
    ppermute x30, waiting for transfers between devices: 23.9 us -> 18.7 us  [far(): return lax.ppermute(x, 'rows', [(i, i ^ 2 * k) for i in range(n)])]
    pallas_call x13 -> x16, Pallas kernels: 28 us -> 31.9 us  [call(): pl.pallas_call(body, out_shape=[jax.ShapeDtypeStruct(*o) if isinstance(o,...]
    ppermute x3, waiting for transfers between devices: 3.94 us -> 2.47 us  [leaf_sum(): lax.ppermute(b, 'leaf', [(i, (i + k) % n) for i in range(n)]).astype(F32)]
    unnamed x25 -> x20, local copies, waits for them, and re-layouts: 2.72 us -> 2.19 us
  transfers between devices with their start and end apart: 47 -> 47, of which waited for: 37 -> 34; matrix products, arithmetic and copies ran while one was open for 0% -> 1% of each run, Pallas kernels for 8% -> 10%
where the time goes in v6:
time: 123 us; the launch traced here: 122 us
  starting transfers between devices  51 us (41%)
  waiting for transfers between devices  35.5 us (29%)
  Pallas kernels  31.9 us (26%)
  local copies, waits for them, and re-layouts  2.19 us (2%)
  between operations  1.61 us (1%)
    ppermute x30, starting transfers between devices, far(): return lax.ppermute(x, 'rows', [(i, i ^ 2 * k) for i in range(n)])  45.7 us
    pallas_call x16, Pallas kernels, call(): pl.pallas_call(body, out_shape=[jax.ShapeDtypeStruct(*o) if isinstance(o,...  31.9 us
    ppermute x30, waiting for transfers between devices, far(): return lax.ppermute(x, 'rows', [(i, i ^ 2 * k) for i in range(n)])  18.7 us
    ppermute x14, waiting for transfers between devices, swap(): return lax.ppermute(x, 'rows', [(i, i ^ 1) for i in range(n)])  14.3 us
    ppermute x3, starting transfers between devices, leaf_sum(): lax.ppermute(b, 'leaf', [(i, (i + k) % n) for i in range(n)]).astype(F32)  3.78 us
    ppermute x3, waiting for transfers between devices, leaf_sum(): lax.ppermute(b, 'leaf', [(i, (i + k) % n) for i in range(n)]).astype(F32)  2.47 us
  transfers between devices with their start and end apart: 47, of which 34 were waited for; matrix products, arithmetic and copies ran while one was open for 1% of the time, Pallas kernels for 10%

profile of v6, /device:TPU:0, one launch (start us, length us, event | category | flops | bytes accessed | tf_op | source)
XLA Modules:
  0.0 122.5 jit_solution(5643185548077094348)
XLA Ops:
  1.6 5.1 %collective-permute-start = (bf16[4,8,256]{2,1,0:T(8,128)(2,1)S(1)}, bf16[4,8,256]{2,1,0:T(8,128)(2,1)S(1)}, u32[]{:S(2)}, u32[]{:S(2)}) collective-permute-start(bf16[4,8,256]{2,1,0:T(8,128)(2,1)S(1)} %round_rhs.1.after_ref), channel_id=1, source_target_pairs={{0,6},{1,7},{2,4},{3,5},{4,2},{5,3},{6,0},{7,1},{8,14},{9,15},{10,... | collective-permute-start | bytes 49160 | tf_op jit(solution)/shard_map/ppermute | solution.py:217
  7.4 4.2 %prepare.3 = (s32[4,1024]{1,0:T(4,128)S(1)}, s32[40]{0:T(128)S(1)}, s32[2,65,8,128]{3,2,1,0:T(8,128)S(1)}) custom-call(bf16[4,8,256]{2,1,0:T(8,128)(2,1)S(1)} %round_rhs.1.after_ref, s32[4,1024]{1,0:T(4,128)} %given_ref.4, s32[4]{0:T(128)S(1)} %copy-done.8), custom_call_target="tpu_custom_call" | custom-call | bytes 8388608 | tf_op jit(solution)/shard_map/prepare/pallas_call | solution.py:29
  11.7 1.2 %collective-permute-done.3.refs_1_ = bf16[4,4,8,256]{3,2,1,0:T(8,128)(2,1)S(1)} collective-permute-done((bf16[4,4,8,256]{3,2,1,0:T(8,128)(2,1)S(1)}, bf16[4,4,8,256]{3,2,1,0:T(8,128)(2,1)S(1)}, u32[]{:S(2)}, u32[]{:S(2)}) %collective-permute-start.3) | collective-permute-done | bytes 65568 | tf_op jit(solution)/shard_map/ppermute | solution.py:212
  12.9 1.2 leaf_solve.1
  14.1 3.3 %collective-permute-start.4 = (bf16[4,8,256]{2,1,0:T(8,128)(2,1)S(1)}, bf16[4,8,256]{2,1,0:T(8,128)(2,1)S(1)}, u32[]{:S(2)}, u32[]{:S(2)}) collective-permute-start(bf16[4,8,256]{2,1,0:T(8,128)(2,1)S(1)} %get-tuple-element.42.after_ref), channel_id=1, source_target_pairs={{0,6},{1,7},{2,4},{3,5},{4,2},{5,3},{6,0},{7,1},{8,14},{9,15},{10,... | collective-permute-start | bytes 49160 | tf_op jit(solution)/shard_map/ppermute | solution.py:217
  18.5 4.2 %prepare.4 = (s32[4,1024]{1,0:T(4,128)}, s32[40]{0:T(128)}, s32[2,65,8,128]{3,2,1,0:T(8,128)S(1)}) custom-call(bf16[4,8,256]{2,1,0:T(8,128)(2,1)S(1)} %get-tuple-element.42.after_ref, s32[4,1024]{1,0:T(4,128)} %given_ref.4, s32[4]{0:T(128)S(1)} %copy-done.8), custom_call_target="tpu_custom_call" | custom-call | bytes 8388608 | tf_op jit(solution)/shard_map/prepare/pallas_call | solution.py:29
  22.9 1.2 %collective-permute-done.7.refs_1_ = bf16[4,4,8,256]{3,2,1,0:T(8,128)(2,1)S(1)} collective-permute-done((bf16[4,4,8,256]{3,2,1,0:T(8,128)(2,1)S(1)}, bf16[4,4,8,256]{3,2,1,0:T(8,128)(2,1)S(1)}, u32[]{:S(2)}, u32[]{:S(2)}) %collective-permute-start.7) | collective-permute-done | bytes 65568 | tf_op jit(solution)/shard_map/ppermute | solution.py:212
  24.1 7.1 %leaf_update.1 = (f32[4,8,512]{2,1,0:T(8,128)S(1)}, bf16[4,8,512]{2,1,0:T(8,128)(2,1)S(1)}, f32[32,8,128]{2,1,0:T(8,128)S(1)}) custom-call(bf16[4,4,8,256]{3,2,1,0:T(8,128)(2,1)S(1)} %pad_maximum_fusion.1.refs_0_, bf16[4,4,8,256]{3,2,1,0:T(8,128)(2,1)S(1)} %collective-permute-done.7.refs_1_, s32[40]{0:T(128)S(1)} %get-tuple-element.39.refs_2_.refs_0_, ...), custom_call_target="tpu_custom_call" | custom-call | tf_op jit(solution)/shard_map/leaf_update/pallas_call | solution.py:29
  33.0 2.2 %collective-permute-start.11 = (bf16[4,8,512]{2,1,0:T(8,128)(2,1)S(1)}, bf16[4,8,512]{2,1,0:T(8,128)(2,1)S(1)}, u32[]{:S(2)}, u32[]{:S(2)}) collective-permute-start(bf16[4,8,512]{2,1,0:T(8,128)(2,1)S(1)} %fusion), channel_id=1, source_target_pairs={{0,2},{1,3},{2,0},{3,1},{4,6},{5,7},{6,4},{7,5},{8,10},{9,11},{10,... | collective-permute-start | bytes 98312 | tf_op jit(solution)/shard_map/ppermute | solution.py:217
  35.2 1.7 %collective-permute-start.9 = (bf16[4,8,512]{2,1,0:T(8,128)(2,1)S(1)}, bf16[4,8,512]{2,1,0:T(8,128)(2,1)S(1)}, u32[]{:S(2)}, u32[]{:S(2)}) collective-permute-start(bf16[4,8,512]{2,1,0:T(8,128)(2,1)S(1)} %fusion), channel_id=1, source_target_pairs={{0,6},{1,7},{2,4},{3,5},{4,2},{5,3},{6,0},{7,1},{8,14},{9,15},{10,... | collective-permute-start | bytes 98312 | tf_op jit(solution)/shard_map/ppermute | solution.py:217
  37.6 3.3 %collective-permute-done.9 = bf16[4,8,512]{2,1,0:T(8,128)(2,1)S(1)} collective-permute-done((bf16[4,8,512]{2,1,0:T(8,128)(2,1)S(1)}, bf16[4,8,512]{2,1,0:T(8,128)(2,1)S(1)}, u32[]{:S(2)}, u32[]{:S(2)}) %collective-permute-start.9) | collective-permute-done | bytes 32800 | tf_op jit(solution)/shard_map/ppermute | solution.py:217
  41.0 1.2 collective-permute-done.12.other_ref
  42.2 1.2 parent_solve.1
  43.4 2.3 %collective-permute-start.15 = (bf16[8,512]{1,0:T(8,128)(2,1)S(1)}, bf16[8,512]{1,0:T(8,128)(2,1)S(1)}, u32[]{:S(2)}, u32[]{:S(2)}) collective-permute-start(bf16[8,512]{1,0:T(8,128)(2,1)S(1)} %get-tuple-element.49.after_ref), channel_id=1, source_target_pairs={{0,2},{1,3},{2,0},{3,1},{4,6},{5,7},{6,4},{7,5},{8,10},{9,11},{10,... | collective-permute-start | bytes 24584 | tf_op jit(solution)/shard_map/ppermute | solution.py:217
  45.7 2.1 %collective-permute-start.13 = (bf16[8,512]{1,0:T(8,128)(2,1)S(1)}, bf16[8,512]{1,0:T(8,128)(2,1)S(1)}, u32[]{:S(2)}, u32[]{:S(2)}) collective-permute-start(bf16[8,512]{1,0:T(8,128)(2,1)S(1)} %get-tuple-element.49.after_ref), channel_id=1, source_target_pairs={{0,6},{1,7},{2,4},{3,5},{4,2},{5,3},{6,0},{7,1},{8,14},{9,15},{10,... | collective-permute-start | bytes 24584 | tf_op jit(solution)/shard_map/ppermute | solution.py:217
  48.5 2.0 %prepare.5 = (s32[1,512]{1,0:T(1,128)S(1)}, s32[8]{0:T(128)S(1)}, s32[1,33,8,128]{3,2,1,0:T(8,128)S(1)}) custom-call(bf16[8,512]{1,0:T(8,128)(2,1)S(1)} %get-tuple-element.49.after_ref, s32[1,512]{1,0:T(1,128)} %given_ref.5, s32[1]{0:T(128)S(6)} %copy.17.height_ref), custom_call_target="tpu_custom_call" | custom-call | bytes 8388608 | tf_op jit(solution)/shard_map/prepare/pallas_call | solution.py:29
  51.3 1.2 collective-permute-done.16.x_other_ref
  52.5 2.1 %parent_update.1 = (f32[4,8,512]{2,1,0:T(8,128)S(1)}, bf16[4,8,512]{2,1,0:T(8,128)(2,1)S(1)}) custom-call(s32[8]{0:T(128)S(1)} %get-tuple-element.50.plan_ref, bf16[4,8,512]{2,1,0:T(8,128)(2,1)S(1)} %pad_maximum_fusion.2.x_own_ref, bf16[4,8,512]{2,1,0:T(8,128)(2,1)S(1)} %collective-permute-done.16.x_other_ref, bf16[1,512,4096]{2,1,0:T(8,128)(2,1)S(1)} %copy-done.1, ...), custom_call_target="tpu_custom_call" | custom-call | tf_op jit(solution)/shard_map/parent_update/pallas_call | solution.py:29
  56.0 2.2 %collective-permute-start.19 = (bf16[4,8,512]{2,1,0:T(8,128)(2,1)S(1)}, bf16[4,8,512]{2,1,0:T(8,128)(2,1)S(1)}, u32[]{:S(2)}, u32[]{:S(2)}) collective-permute-start(bf16[4,8,512]{2,1,0:T(8,128)(2,1)S(1)} %fusion.1), channel_id=1, source_target_pairs={{0,16},{8,24},{16,0},{24,8},{1,17},{9,25},{17,1},{25,9},{2,18},{10... | collective-permute-start | bytes 98312 | tf_op jit(solution)/shard_map/ppermute | solution.py:234
  58.2 1.4 %collective-permute-start.20 = (bf16[4,8,512]{2,1,0:T(8,128)(2,1)S(1)}, bf16[4,8,512]{2,1,0:T(8,128)(2,1)S(1)}, u32[]{:S(2)}, u32[]{:S(2)}) collective-permute-start(bf16[4,8,512]{2,1,0:T(8,128)(2,1)S(1)} %fusion.1), channel_id=1, source_target_pairs={{0,24},{8,0},{16,8},{24,16},{1,25},{9,1},{17,9},{25,17},{2,26},{10... | collective-permute-start | bytes 98312 | tf_op jit(solution)/shard_map/ppermute | solution.py:234
  59.7 1.2 collective-permute-done.18
  60.8 1.3 %collective-permute-done.20 = bf16[4,8,512]{2,1,0:T(8,128)(2,1)S(1)} collective-permute-done((bf16[4,8,512]{2,1,0:T(8,128)(2,1)S(1)}, bf16[4,8,512]{2,1,0:T(8,128)(2,1)S(1)}, u32[]{:S(2)}, u32[]{:S(2)}) %collective-permute-start.20) | collective-permute-done | bytes 32800 | tf_op jit(solution)/shard_map/ppermute | solution.py:234
  62.2 2.4 %collective-permute-start.21 = (bf16[4,8,512]{2,1,0:T(8,128)(2,1)S(1)}, bf16[4,8,512]{2,1,0:T(8,128)(2,1)S(1)}, u32[]{:S(2)}, u32[]{:S(2)}) collective-permute-start(bf16[4,8,512]{2,1,0:T(8,128)(2,1)S(1)} %fusion.29), channel_id=1, source_target_pairs={{0,6},{1,7},{2,4},{3,5},{4,2},{5,3},{6,0},{7,1},{8,14},{9,15},{10,... | collective-permute-start | bytes 98312 | tf_op jit(solution)/shard_map/ppermute | solution.py:217
  64.6 2.0 %collective-permute-start.23 = (bf16[4,8,512]{2,1,0:T(8,128)(2,1)S(1)}, bf16[4,8,512]{2,1,0:T(8,128)(2,1)S(1)}, u32[]{:S(2)}, u32[]{:S(2)}) collective-permute-start(bf16[4,8,512]{2,1,0:T(8,128)(2,1)S(1)} %fusion.29), channel_id=1, source_target_pairs={{0,2},{1,3},{2,0},{3,1},{4,6},{5,7},{6,4},{7,5},{8,10},{9,11},{10,... | collective-permute-start | bytes 98312 | tf_op jit(solution)/shard_map/ppermute | solution.py:217
  66.6 1.6 %collective-permute-done.21 = bf16[4,8,512]{2,1,0:T(8,128)(2,1)S(1)} collective-permute-done((bf16[4,8,512]{2,1,0:T(8,128)(2,1)S(1)}, bf16[4,8,512]{2,1,0:T(8,128)(2,1)S(1)}, u32[]{:S(2)}, u32[]{:S(2)}) %collective-permute-start.21) | collective-permute-done | bytes 32800 | tf_op jit(solution)/shard_map/ppermute | solution.py:217
  68.2 1.2 %collective-permute-done.22 = bf16[4,8,512]{2,1,0:T(8,128)(2,1)S(1)} collective-permute-done((bf16[4,8,512]{2,1,0:T(8,128)(2,1)S(1)}, bf16[4,8,512]{2,1,0:T(8,128)(2,1)S(1)}, u32[]{:S(2)}, u32[]{:S(2)}) %collective-permute-start.22) | collective-permute-done | bytes 32800 | tf_op jit(solution)/shard_map/ppermute | solution.py:217
  69.5 1.2 collective-permute-done.24.other_ref
  70.7 1.8 %root_solve.1 = (f32[4,8,512]{2,1,0:T(8,128)S(1)}, bf16[4,8,512]{2,1,0:T(8,128)(2,1)S(1)}) custom-call(bf16[4,8,512]{2,1,0:T(8,128)(2,1)S(1)} %add_convert_fusion.1.own_ref, bf16[4,8,512]{2,1,0:T(8,128)(2,1)S(1)} %collective-permute-done.24.other_ref, bf16[512,4096]{1,0:T(8,128)(2,1)S(1)} %copy-done.4), custom_call_target="tpu_custom_call" | custom-call | tf_op jit(solution)/shard_map/root_solve/pallas_call | solution.py:29
  73.8 1.9 %collective-permute-start.26 = (bf16[4,8,512]{2,1,0:T(8,128)(2,1)S(1)}, bf16[4,8,512]{2,1,0:T(8,128)(2,1)S(1)}, u32[]{:S(2)}, u32[]{:S(2)}) collective-permute-start(bf16[4,8,512]{2,1,0:T(8,128)(2,1)S(1)} %fusion.2), channel_id=1, source_target_pairs={{0,6},{1,7},{2,4},{3,5},{4,2},{5,3},{6,0},{7,1},{8,14},{9,15},{10,... | collective-permute-start | bytes 98312 | tf_op jit(solution)/shard_map/ppermute | solution.py:217
  76.4 1.8 %collective-permute-start.28 = (bf16[4,8,512]{2,1,0:T(8,128)(2,1)S(1)}, bf16[4,8,512]{2,1,0:T(8,128)(2,1)S(1)}, u32[]{:S(2)}, u32[]{:S(2)}) collective-permute-start(bf16[4,8,512]{2,1,0:T(8,128)(2,1)S(1)} %fusion.2), channel_id=1, source_target_pairs={{0,2},{1,3},{2,0},{3,1},{4,6},{5,7},{6,4},{7,5},{8,10},{9,11},{10,... | collective-permute-start | bytes 98312 | tf_op jit(solution)/shard_map/ppermute | solution.py:217
  78.3 1.7 %collective-permute-done.26 = bf16[4,8,512]{2,1,0:T(8,128)(2,1)S(1)} collective-permute-done((bf16[4,8,512]{2,1,0:T(8,128)(2,1)S(1)}, bf16[4,8,512]{2,1,0:T(8,128)(2,1)S(1)}, u32[]{:S(2)}, u32[]{:S(2)}) %collective-permute-start.26) | collective-permute-done | bytes 32800 | tf_op jit(solution)/shard_map/ppermute | solution.py:217
  80.9 1.2 collective-permute-done.29.other_ref
  82.1 1.5 %parent_back.1 = (bf16[4,1,8,512]{3,2,1,0:T(8,128)(2,1)S(1)}, f32[33,8,128]{2,1,0:T(8,128)S(1)}, f32[8,128]{1,0:T(8,128)}, bf16[1,8,512]{2,1,0:T(8,128)(2,1)S(1)}) custom-call(s32[8]{0:T(128)S(1)} %get-tuple-element.50.plan_ref, bf16[4,8,512]{2,1,0:T(8,128)(2,1)S(1)} %add_convert_fusion.own_ref, bf16[4,8,512]{2,1,0:T(8,128)(2,1)S(1)} %collective-permute-done.29.other_ref, ...), custom_call_target="tpu_custom_call" | custom-call | tf_op jit(solution)/shard_map/parent_back/pallas_call | solution.py:29
  84.8 2.0 %collective-permute-start.31 = (bf16[1,8,512]{2,1,0:T(8,128)(2,1)S(1)}, bf16[1,8,512]{2,1,0:T(8,128)(2,1)S(1)}, u32[]{:S(2)}, u32[]{:S(2)}) collective-permute-start(bf16[1,8,512]{2,1,0:T(8,128)(2,1)S(1)} %get-tuple-element.89), channel_id=1, source_target_pairs={{0,6},{1,7},{2,4},{3,5},{4,2},{5,3},{6,0},{7,1},{8,14},{9,15},{10,... | collective-permute-start | bytes 24584 | tf_op jit(solution)/shard_map/ppermute | solution.py:217
  87.7 1.5 %collective-permute-start.33 = (bf16[1,8,512]{2,1,0:T(8,128)(2,1)S(1)}, bf16[1,8,512]{2,1,0:T(8,128)(2,1)S(1)}, u32[]{:S(2)}, u32[]{:S(2)}) collective-permute-start(bf16[1,8,512]{2,1,0:T(8,128)(2,1)S(1)} %get-tuple-element.87), channel_id=1, source_target_pairs={{0,2},{1,3},{2,0},{3,1},{4,6},{5,7},{6,4},{7,5},{8,10},{9,11},{10,... | collective-permute-start | bytes 24584 | tf_op jit(solution)/shard_map/ppermute | solution.py:217
  92.1 1.2 collective-permute-done.34
  93.4 1.9 %collective-permute-start.35 = (bf16[4,8,512]{2,1,0:T(8,128)(2,1)S(1)}, bf16[4,8,512]{2,1,0:T(8,128)(2,1)S(1)}, u32[]{:S(2)}, u32[]{:S(2)}) collective-permute-start(bf16[4,8,512]{2,1,0:T(8,128)(2,1)S(1)} %fusion.3), channel_id=1, source_target_pairs={{0,6},{1,7},{2,4},{3,5},{4,2},{5,3},{6,0},{7,1},{8,14},{9,15},{10,... | collective-permute-start | bytes 98312 | tf_op jit(solution)/shard_map/ppermute | solution.py:217
  96.3 1.5 %collective-permute-start.37 = (bf16[4,8,512]{2,1,0:T(8,128)(2,1)S(1)}, bf16[4,8,512]{2,1,0:T(8,128)(2,1)S(1)}, u32[]{:S(2)}, u32[]{:S(2)}) collective-permute-start(bf16[4,8,512]{2,1,0:T(8,128)(2,1)S(1)} %fusion.3), channel_id=1, source_target_pairs={{0,2},{1,3},{2,0},{3,1},{4,6},{5,7},{6,4},{7,5},{8,10},{9,11},{10,... | collective-permute-start | bytes 98312 | tf_op jit(solution)/shard_map/ppermute | solution.py:217
  97.8 1.6 %collective-permute-done.35 = bf16[4,8,512]{2,1,0:T(8,128)(2,1)S(1)} collective-permute-done((bf16[4,8,512]{2,1,0:T(8,128)(2,1)S(1)}, bf16[4,8,512]{2,1,0:T(8,128)(2,1)S(1)}, u32[]{:S(2)}, u32[]{:S(2)}) %collective-permute-start.35) | collective-permute-done | bytes 32800 | tf_op jit(solution)/shard_map/ppermute | solution.py:217
  100.5 1.2 collective-permute-done.38.refs_3_
  101.7 3.5 %leaf_back.1 = (bf16[4,4,8,256]{3,2,1,0:T(8,128)(2,1)S(1)}, f32[8,512]{1,0:T(8,128)S(1)}, bf16[4,8,1024]{2,1,0:T(8,128)(2,1)S(1)}) custom-call(s32[40]{0:T(128)S(1)} %get-tuple-element.39.refs_2_.refs_0_, f32[4,8,512]{2,1,0:T(8,128)S(1)} %get-tuple-element.79.refs_1_, bf16[4,8,512]{2,1,0:T(8,128)(2,1)S(1)} %get-tuple-element.78.refs_2_, ...), custom_call_target="tpu_custom_call" | custom-call | tf_op jit(solution)/shard_map/leaf_back/pallas_call | solution.py:29
  105.4 1.2 leaf_back_own.1
  106.7 1.4 %collective-permute-start.40 = (bf16[4,8,256]{2,1,0:T(8,128)(2,1)S(1)}, bf16[4,8,256]{2,1,0:T(8,128)(2,1)S(1)}, u32[]{:S(2)}, u32[]{:S(2)}) collective-permute-start(bf16[4,8,256]{2,1,0:T(8,128)(2,1)S(1)} %get-tuple-element.85), channel_id=1, source_target_pairs={{0,6},{1,7},{2,4},{3,5},{4,2},{5,3},{6,0},{7,1},{8,14},{9,15},{10,... | collective-permute-start | bytes 49160 | tf_op jit(solution)/shard_map/ppermute | solution.py:217
  108.7 2.4 %collective-permute-start.42 = (bf16[4,8,256]{2,1,0:T(8,128)(2,1)S(1)}, bf16[4,8,256]{2,1,0:T(8,128)(2,1)S(1)}, u32[]{:S(2)}, u32[]{:S(2)}) collective-permute-start(bf16[4,8,256]{2,1,0:T(8,128)(2,1)S(1)} %get-tuple-element.83), channel_id=1, source_target_pairs={{0,2},{1,3},{2,0},{3,1},{4,6},{5,7},{6,4},{7,5},{8,10},{9,11},{10,... | collective-permute-start | bytes 49160 | tf_op jit(solution)/shard_map/ppermute | solution.py:217
  111.1 1.1 collective-permute-done.40.refs_1_
  114.6 2.4 %collective-permute-start.44 = (bf16[4,8,256]{2,1,0:T(8,128)(2,1)S(1)}, bf16[4,8,256]{2,1,0:T(8,128)(2,1)S(1)}, u32[]{:S(2)}, u32[]{:S(2)}) collective-permute-start(bf16[4,8,256]{2,1,0:T(8,128)(2,1)S(1)} %get-tuple-element.80), channel_id=1, source_target_pairs={{0,6},{1,7},{2,4},{3,5},{4,2},{5,3},{6,0},{7,1},{8,14},{9,15},{10,... | collective-permute-start | bytes 49160 | tf_op jit(solution)/shard_map/ppermute | solution.py:217
  117.0 1.1 collective-permute-start.45
  120.2 1.4 %collective-permute-done.45 = bf16[4,8,256]{2,1,0:T(8,128)(2,1)S(1)} collective-permute-done((bf16[4,8,256]{2,1,0:T(8,128)(2,1)S(1)}, bf16[4,8,256]{2,1,0:T(8,128)(2,1)S(1)}, u32[]{:S(2)}, u32[]{:S(2)}) %collective-permute-start.45) | collective-permute-done | bytes 16416 | tf_op jit(solution)/shard_map/ppermute | solution.py:217
  (98 shorter events, 23.8 us)
Async XLA Ops:
  1.6 10.0 %collective-permute-start = (bf16[4,8,256]{2,1,0:T(8,128)(2,1)S(1)}, bf16[4,8,256]{2,1,0:T(8,128)(2,1)S(1)}, u32[]{:S(2)}, u32[]{:S(2)}) collective-permute-start(bf16[4,8,256]{2,1,0:T(8,128)(2,1)S(1)} %round_rhs.1.after_ref), channel_id=1, source_target_pairs={{0,6},{1,7},{2,4},{3,5},{4,2},{5,3},{6,0},{7,1},{8,14},{9,15},{10,... | collective-permute-start | bytes 49160 | tf_op jit(solution)/shard_map/ppermute | solution.py:217
  6.7 4.9 %collective-permute-start.1 = (bf16[4,8,256]{2,1,0:T(8,128)(2,1)S(1)}, bf16[4,8,256]{2,1,0:T(8,128)(2,1)S(1)}, u32[]{:S(2)}, u32[]{:S(2)}) collective-permute-start(bf16[4,8,256]{2,1,0:T(8,128)(2,1)S(1)} %round_rhs.1.after_ref), channel_id=1, source_target_pairs={{0,4},{1,5},{2,6},{3,7},{4,0},{5,1},{6,2},{7,3},{8,12},{9,13},{10,... | collective-permute-start | bytes 49160 | tf_op jit(solution)/shard_map/ppermute | solution.py:217
  6.7 4.9 %collective-permute-start.2 = (bf16[4,8,256]{2,1,0:T(8,128)(2,1)S(1)}, bf16[4,8,256]{2,1,0:T(8,128)(2,1)S(1)}, u32[]{:S(2)}, u32[]{:S(2)}) collective-permute-start(bf16[4,8,256]{2,1,0:T(8,128)(2,1)S(1)} %round_rhs.1.after_ref), channel_id=1, source_target_pairs={{0,2},{1,3},{2,0},{3,1},{4,6},{5,7},{6,4},{7,5},{8,10},{9,11},{10,... | collective-permute-start | bytes 49160 | tf_op jit(solution)/shard_map/ppermute | solution.py:217
  11.6 1.3 %collective-permute-start.3 = (bf16[4,4,8,256]{3,2,1,0:T(8,128)(2,1)S(1)}, bf16[4,4,8,256]{3,2,1,0:T(8,128)(2,1)S(1)}, u32[]{:S(2)}, u32[]{:S(2)}) collective-permute-start(bf16[4,4,8,256]{3,2,1,0:T(8,128)(2,1)S(1)} %pad_maximum_fusion.refs_0_), channel_id=1, source_target_pairs={{0,1},{1,0},{2,3},{3,2},{4,5},{5,4},{6,7},{7,6},{8,9},{9,8},{10,11... | collective-permute-start | bytes 196616 | tf_op jit(solution)/shard_map/ppermute | solution.py:212
  14.1 8.6 %collective-permute-start.4 = (bf16[4,8,256]{2,1,0:T(8,128)(2,1)S(1)}, bf16[4,8,256]{2,1,0:T(8,128)(2,1)S(1)}, u32[]{:S(2)}, u32[]{:S(2)}) collective-permute-start(bf16[4,8,256]{2,1,0:T(8,128)(2,1)S(1)} %get-tuple-element.42.after_ref), channel_id=1, source_target_pairs={{0,6},{1,7},{2,4},{3,5},{4,2},{5,3},{6,0},{7,1},{8,14},{9,15},{10,... | collective-permute-start | bytes 49160 | tf_op jit(solution)/shard_map/ppermute | solution.py:217
  17.5 5.3 %collective-permute-start.5 = (bf16[4,8,256]{2,1,0:T(8,128)(2,1)S(1)}, bf16[4,8,256]{2,1,0:T(8,128)(2,1)S(1)}, u32[]{:S(2)}, u32[]{:S(2)}) collective-permute-start(bf16[4,8,256]{2,1,0:T(8,128)(2,1)S(1)} %get-tuple-element.42.after_ref), channel_id=1, source_target_pairs={{0,4},{1,5},{2,6},{3,7},{4,0},{5,1},{6,2},{7,3},{8,12},{9,13},{10,... | collective-permute-start | bytes 49160 | tf_op jit(solution)/shard_map/ppermute | solution.py:217
  17.5 5.3 %collective-permute-start.6 = (bf16[4,8,256]{2,1,0:T(8,128)(2,1)S(1)}, bf16[4,8,256]{2,1,0:T(8,128)(2,1)S(1)}, u32[]{:S(2)}, u32[]{:S(2)}) collective-permute-start(bf16[4,8,256]{2,1,0:T(8,128)(2,1)S(1)} %get-tuple-element.42.after_ref), channel_id=1, source_target_pairs={{0,2},{1,3},{2,0},{3,1},{4,6},{5,7},{6,4},{7,5},{8,10},{9,11},{10,... | collective-permute-start | bytes 49160 | tf_op jit(solution)/shard_map/ppermute | solution.py:217
  22.8 1.3 %collective-permute-start.7 = (bf16[4,4,8,256]{3,2,1,0:T(8,128)(2,1)S(1)}, bf16[4,4,8,256]{3,2,1,0:T(8,128)(2,1)S(1)}, u32[]{:S(2)}, u32[]{:S(2)}) collective-permute-start(bf16[4,4,8,256]{3,2,1,0:T(8,128)(2,1)S(1)} %pad_maximum_fusion.1.refs_0_), channel_id=1, source_target_pairs={{0,1},{1,0},{2,3},{3,2},{4,5},{5,4},{6,7},{7,6},{8,9},{9,8},{10,11... | collective-permute-start | bytes 196616 | tf_op jit(solution)/shard_map/ppermute | solution.py:212
  31.2 1.3 %collective-permute-start.8 = (bf16[4,8,512]{2,1,0:T(8,128)(2,1)S(1)}, bf16[4,8,512]{2,1,0:T(8,128)(2,1)S(1)}, u32[]{:S(2)}, u32[]{:S(2)}) collective-permute-start(bf16[4,8,512]{2,1,0:T(8,128)(2,1)S(1)} %get-tuple-element.48), channel_id=1, source_target_pairs={{0,1},{1,0},{2,3},{3,2},{4,5},{5,4},{6,7},{7,6},{8,9},{9,8},{10,11... | collective-permute-start | bytes 98312 | tf_op jit(solution)/shard_map/ppermute | solution.py:212
  32.5 5.1 %collective-permute-start.10 = (bf16[4,8,512]{2,1,0:T(8,128)(2,1)S(1)}, bf16[4,8,512]{2,1,0:T(8,128)(2,1)S(1)}, u32[]{:S(2)}, u32[]{:S(2)}) collective-permute-start(bf16[4,8,512]{2,1,0:T(8,128)(2,1)S(1)} %fusion), channel_id=1, source_target_pairs={{0,4},{1,5},{2,6},{3,7},{4,0},{5,1},{6,2},{7,3},{8,12},{9,13},{10,... | collective-permute-start | bytes 98312 | tf_op jit(solution)/shard_map/ppermute | solution.py:217
  33.0 4.6 %collective-permute-start.11 = (bf16[4,8,512]{2,1,0:T(8,128)(2,1)S(1)}, bf16[4,8,512]{2,1,0:T(8,128)(2,1)S(1)}, u32[]{:S(2)}, u32[]{:S(2)}) collective-permute-start(bf16[4,8,512]{2,1,0:T(8,128)(2,1)S(1)} %fusion), channel_id=1, source_target_pairs={{0,2},{1,3},{2,0},{3,1},{4,6},{5,7},{6,4},{7,5},{8,10},{9,11},{10,... | collective-permute-start | bytes 98312 | tf_op jit(solution)/shard_map/ppermute | solution.py:217
  35.2 5.7 %collective-permute-start.9 = (bf16[4,8,512]{2,1,0:T(8,128)(2,1)S(1)}, bf16[4,8,512]{2,1,0:T(8,128)(2,1)S(1)}, u32[]{:S(2)}, u32[]{:S(2)}) collective-permute-start(bf16[4,8,512]{2,1,0:T(8,128)(2,1)S(1)} %fusion), channel_id=1, source_target_pairs={{0,6},{1,7},{2,4},{3,5},{4,2},{5,3},{6,0},{7,1},{8,14},{9,15},{10,... | collective-permute-start | bytes 98312 | tf_op jit(solution)/shard_map/ppermute | solution.py:217
  40.9 29.8 %copy-start.4 = (bf16[512,4096]{1,0:T(8,128)(2,1)S(1)}, bf16[512,4096]{1,0:T(8,128)(2,1)}, u32[]{:S(2)}) copy-start(bf16[512,4096]{1,0:T(8,128)(2,1)} %w_ref.9) | copy-start | bytes 12582916
  41.0 1.3 %collective-permute-start.12 = (bf16[4,8,512]{2,1,0:T(8,128)(2,1)S(1)}, bf16[4,8,512]{2,1,0:T(8,128)(2,1)S(1)}, u32[]{:S(2)}, u32[]{:S(2)}) collective-permute-start(bf16[4,8,512]{2,1,0:T(8,128)(2,1)S(1)} %add_convert_fusion.2.own_ref), channel_id=1, source_target_pairs={{0,1},{1,0},{2,3},{3,2},{4,5},{5,4},{6,7},{7,6},{8,9},{9,8},{10,11... | collective-permute-start | bytes 98312 | tf_op jit(solution)/shard_map/ppermute | solution.py:212
  43.4 7.1 %collective-permute-start.14 = (bf16[8,512]{1,0:T(8,128)(2,1)S(1)}, bf16[8,512]{1,0:T(8,128)(2,1)S(1)}, u32[]{:S(2)}, u32[]{:S(2)}) collective-permute-start(bf16[8,512]{1,0:T(8,128)(2,1)S(1)} %get-tuple-element.49.after_ref), channel_id=1, source_target_pairs={{0,4},{1,5},{2,6},{3,7},{4,0},{5,1},{6,2},{7,3},{8,12},{9,13},{10,... | collective-permute-start | bytes 24584 | tf_op jit(solution)/shard_map/ppermute | solution.py:217
  43.4 7.1 %collective-permute-start.15 = (bf16[8,512]{1,0:T(8,128)(2,1)S(1)}, bf16[8,512]{1,0:T(8,128)(2,1)S(1)}, u32[]{:S(2)}, u32[]{:S(2)}) collective-permute-start(bf16[8,512]{1,0:T(8,128)(2,1)S(1)} %get-tuple-element.49.after_ref), channel_id=1, source_target_pairs={{0,2},{1,3},{2,0},{3,1},{4,6},{5,7},{6,4},{7,5},{8,10},{9,11},{10,... | collective-permute-start | bytes 24584 | tf_op jit(solution)/shard_map/ppermute | solution.py:217
  45.7 5.4 %collective-permute-start.13 = (bf16[8,512]{1,0:T(8,128)(2,1)S(1)}, bf16[8,512]{1,0:T(8,128)(2,1)S(1)}, u32[]{:S(2)}, u32[]{:S(2)}) collective-permute-start(bf16[8,512]{1,0:T(8,128)(2,1)S(1)} %get-tuple-element.49.after_ref), channel_id=1, source_target_pairs={{0,6},{1,7},{2,4},{3,5},{4,2},{5,3},{6,0},{7,1},{8,14},{9,15},{10,... | collective-permute-start | bytes 24584 | tf_op jit(solution)/shard_map/ppermute | solution.py:217
  51.2 1.3 %collective-permute-start.16 = (bf16[4,8,512]{2,1,0:T(8,128)(2,1)S(1)}, bf16[4,8,512]{2,1,0:T(8,128)(2,1)S(1)}, u32[]{:S(2)}, u32[]{:S(2)}) collective-permute-start(bf16[4,8,512]{2,1,0:T(8,128)(2,1)S(1)} %pad_maximum_fusion.2.x_own_ref), channel_id=1, source_target_pairs={{0,1},{1,0},{2,3},{3,2},{4,5},{5,4},{6,7},{7,6},{8,9},{9,8},{10,11... | collective-permute-start | bytes 98312 | tf_op jit(solution)/shard_map/ppermute | solution.py:212
  54.6 1.3 %collective-permute-start.17 = (bf16[4,8,512]{2,1,0:T(8,128)(2,1)S(1)}, bf16[4,8,512]{2,1,0:T(8,128)(2,1)S(1)}, u32[]{:S(2)}, u32[]{:S(2)}) collective-permute-start(bf16[4,8,512]{2,1,0:T(8,128)(2,1)S(1)} %get-tuple-element.57), channel_id=1, source_target_pairs={{0,1},{1,0},{2,3},{3,2},{4,5},{5,4},{6,7},{7,6},{8,9},{9,8},{10,11... | collective-permute-start | bytes 98312 | tf_op jit(solution)/shard_map/ppermute | solution.py:212
  55.9 4.9 %collective-permute-start.18 = (bf16[4,8,512]{2,1,0:T(8,128)(2,1)S(1)}, bf16[4,8,512]{2,1,0:T(8,128)(2,1)S(1)}, u32[]{:S(2)}, u32[]{:S(2)}) collective-permute-start(bf16[4,8,512]{2,1,0:T(8,128)(2,1)S(1)} %fusion.1), channel_id=1, source_target_pairs={{0,8},{8,16},{16,24},{24,0},{1,9},{9,17},{17,25},{25,1},{2,10},{10... | collective-permute-start | bytes 98312 | tf_op jit(solution)/shard_map/ppermute | solution.py:234
  56.0 4.8 %collective-permute-start.19 = (bf16[4,8,512]{2,1,0:T(8,128)(2,1)S(1)}, bf16[4,8,512]{2,1,0:T(8,128)(2,1)S(1)}, u32[]{:S(2)}, u32[]{:S(2)}) collective-permute-start(bf16[4,8,512]{2,1,0:T(8,128)(2,1)S(1)} %fusion.1), channel_id=1, source_target_pairs={{0,16},{8,24},{16,0},{24,8},{1,17},{9,25},{17,1},{25,9},{2,18},{10... | collective-permute-start | bytes 98312 | tf_op jit(solution)/shard_map/ppermute | solution.py:234
  58.2 3.9 %collective-permute-start.20 = (bf16[4,8,512]{2,1,0:T(8,128)(2,1)S(1)}, bf16[4,8,512]{2,1,0:T(8,128)(2,1)S(1)}, u32[]{:S(2)}, u32[]{:S(2)}) collective-permute-start(bf16[4,8,512]{2,1,0:T(8,128)(2,1)S(1)} %fusion.1), channel_id=1, source_target_pairs={{0,24},{8,0},{16,8},{24,16},{1,25},{9,1},{17,9},{25,17},{2,26},{10... | collective-permute-start | bytes 98312 | tf_op jit(solution)/shard_map/ppermute | solution.py:234
  62.2 6.0 %collective-permute-start.21 = (bf16[4,8,512]{2,1,0:T(8,128)(2,1)S(1)}, bf16[4,8,512]{2,1,0:T(8,128)(2,1)S(1)}, u32[]{:S(2)}, u32[]{:S(2)}) collective-permute-start(bf16[4,8,512]{2,1,0:T(8,128)(2,1)S(1)} %fusion.29), channel_id=1, source_target_pairs={{0,6},{1,7},{2,4},{3,5},{4,2},{5,3},{6,0},{7,1},{8,14},{9,15},{10,... | collective-permute-start | bytes 98312 | tf_op jit(solution)/shard_map/ppermute | solution.py:217
  64.6 4.8 %collective-permute-start.22 = (bf16[4,8,512]{2,1,0:T(8,128)(2,1)S(1)}, bf16[4,8,512]{2,1,0:T(8,128)(2,1)S(1)}, u32[]{:S(2)}, u32[]{:S(2)}) collective-permute-start(bf16[4,8,512]{2,1,0:T(8,128)(2,1)S(1)} %fusion.29), channel_id=1, source_target_pairs={{0,4},{1,5},{2,6},{3,7},{4,0},{5,1},{6,2},{7,3},{8,12},{9,13},{10,... | collective-permute-start | bytes 98312 | tf_op jit(solution)/shard_map/ppermute | solution.py:217
  64.6 4.8 %collective-permute-start.23 = (bf16[4,8,512]{2,1,0:T(8,128)(2,1)S(1)}, bf16[4,8,512]{2,1,0:T(8,128)(2,1)S(1)}, u32[]{:S(2)}, u32[]{:S(2)}) collective-permute-start(bf16[4,8,512]{2,1,0:T(8,128)(2,1)S(1)} %fusion.29), channel_id=1, source_target_pairs={{0,2},{1,3},{2,0},{3,1},{4,6},{5,7},{6,4},{7,5},{8,10},{9,11},{10,... | collective-permute-start | bytes 98312 | tf_op jit(solution)/shard_map/ppermute | solution.py:217
  69.5 1.3 %collective-permute-start.24 = (bf16[4,8,512]{2,1,0:T(8,128)(2,1)S(1)}, bf16[4,8,512]{2,1,0:T(8,128)(2,1)S(1)}, u32[]{:S(2)}, u32[]{:S(2)}) collective-permute-start(bf16[4,8,512]{2,1,0:T(8,128)(2,1)S(1)} %add_convert_fusion.1.own_ref), channel_id=1, source_target_pairs={{0,1},{1,0},{2,3},{3,2},{4,5},{5,4},{6,7},{7,6},{8,9},{9,8},{10,11... | collective-permute-start | bytes 98312 | tf_op jit(solution)/shard_map/ppermute | solution.py:212
  72.6 1.2 collective-permute-start.25
  73.8 6.2 %collective-permute-start.26 = (bf16[4,8,512]{2,1,0:T(8,128)(2,1)S(1)}, bf16[4,8,512]{2,1,0:T(8,128)(2,1)S(1)}, u32[]{:S(2)}, u32[]{:S(2)}) collective-permute-start(bf16[4,8,512]{2,1,0:T(8,128)(2,1)S(1)} %fusion.2), channel_id=1, source_target_pairs={{0,6},{1,7},{2,4},{3,5},{4,2},{5,3},{6,0},{7,1},{8,14},{9,15},{10,... | collective-permute-start | bytes 98312 | tf_op jit(solution)/shard_map/ppermute | solution.py:217
  75.7 5.0 %collective-permute-start.27 = (bf16[4,8,512]{2,1,0:T(8,128)(2,1)S(1)}, bf16[4,8,512]{2,1,0:T(8,128)(2,1)S(1)}, u32[]{:S(2)}, u32[]{:S(2)}) collective-permute-start(bf16[4,8,512]{2,1,0:T(8,128)(2,1)S(1)} %fusion.2), channel_id=1, source_target_pairs={{0,4},{1,5},{2,6},{3,7},{4,0},{5,1},{6,2},{7,3},{8,12},{9,13},{10,... | collective-permute-start | bytes 98312 | tf_op jit(solution)/shard_map/ppermute | solution.py:217
  76.4 4.3 %collective-permute-start.28 = (bf16[4,8,512]{2,1,0:T(8,128)(2,1)S(1)}, bf16[4,8,512]{2,1,0:T(8,128)(2,1)S(1)}, u32[]{:S(2)}, u32[]{:S(2)}) collective-permute-start(bf16[4,8,512]{2,1,0:T(8,128)(2,1)S(1)} %fusion.2), channel_id=1, source_target_pairs={{0,2},{1,3},{2,0},{3,1},{4,6},{5,7},{6,4},{7,5},{8,10},{9,11},{10,... | collective-permute-start | bytes 98312 | tf_op jit(solution)/shard_map/ppermute | solution.py:217
  80.8 1.3 %collective-permute-start.29 = (bf16[4,8,512]{2,1,0:T(8,128)(2,1)S(1)}, bf16[4,8,512]{2,1,0:T(8,128)(2,1)S(1)}, u32[]{:S(2)}, u32[]{:S(2)}) collective-permute-start(bf16[4,8,512]{2,1,0:T(8,128)(2,1)S(1)} %add_convert_fusion.own_ref), channel_id=1, source_target_pairs={{0,1},{1,0},{2,3},{3,2},{4,5},{5,4},{6,7},{7,6},{8,9},{9,8},{10,11... | collective-permute-start | bytes 98312 | tf_op jit(solution)/shard_map/ppermute | solution.py:212
  83.6 1.2 collective-permute-start.30
  84.8 5.6 %collective-permute-start.31 = (bf16[1,8,512]{2,1,0:T(8,128)(2,1)S(1)}, bf16[1,8,512]{2,1,0:T(8,128)(2,1)S(1)}, u32[]{:S(2)}, u32[]{:S(2)}) collective-permute-start(bf16[1,8,512]{2,1,0:T(8,128)(2,1)S(1)} %get-tuple-element.89), channel_id=1, source_target_pairs={{0,6},{1,7},{2,4},{3,5},{4,2},{5,3},{6,0},{7,1},{8,14},{9,15},{10,... | collective-permute-start | bytes 24584 | tf_op jit(solution)/shard_map/ppermute | solution.py:217
  86.8 4.6 %collective-permute-start.32 = (bf16[1,8,512]{2,1,0:T(8,128)(2,1)S(1)}, bf16[1,8,512]{2,1,0:T(8,128)(2,1)S(1)}, u32[]{:S(2)}, u32[]{:S(2)}) collective-permute-start(bf16[1,8,512]{2,1,0:T(8,128)(2,1)S(1)} %get-tuple-element.88), channel_id=1, source_target_pairs={{0,4},{1,5},{2,6},{3,7},{4,0},{5,1},{6,2},{7,3},{8,12},{9,13},{10,... | collective-permute-start | bytes 24584 | tf_op jit(solution)/shard_map/ppermute | solution.py:217
  87.7 3.7 %collective-permute-start.33 = (bf16[1,8,512]{2,1,0:T(8,128)(2,1)S(1)}, bf16[1,8,512]{2,1,0:T(8,128)(2,1)S(1)}, u32[]{:S(2)}, u32[]{:S(2)}) collective-permute-start(bf16[1,8,512]{2,1,0:T(8,128)(2,1)S(1)} %get-tuple-element.87), channel_id=1, source_target_pairs={{0,2},{1,3},{2,0},{3,1},{4,6},{5,7},{6,4},{7,5},{8,10},{9,11},{10,... | collective-permute-start | bytes 24584 | tf_op jit(solution)/shard_map/ppermute | solution.py:217
  92.1 1.2 collective-permute-start.34
  93.4 6.1 %collective-permute-start.35 = (bf16[4,8,512]{2,1,0:T(8,128)(2,1)S(1)}, bf16[4,8,512]{2,1,0:T(8,128)(2,1)S(1)}, u32[]{:S(2)}, u32[]{:S(2)}) collective-permute-start(bf16[4,8,512]{2,1,0:T(8,128)(2,1)S(1)} %fusion.3), channel_id=1, source_target_pairs={{0,6},{1,7},{2,4},{3,5},{4,2},{5,3},{6,0},{7,1},{8,14},{9,15},{10,... | collective-permute-start | bytes 98312 | tf_op jit(solution)/shard_map/ppermute | solution.py:217
  95.2 5.0 %collective-permute-start.36 = (bf16[4,8,512]{2,1,0:T(8,128)(2,1)S(1)}, bf16[4,8,512]{2,1,0:T(8,128)(2,1)S(1)}, u32[]{:S(2)}, u32[]{:S(2)}) collective-permute-start(bf16[4,8,512]{2,1,0:T(8,128)(2,1)S(1)} %fusion.3), channel_id=1, source_target_pairs={{0,4},{1,5},{2,6},{3,7},{4,0},{5,1},{6,2},{7,3},{8,12},{9,13},{10,... | collective-permute-start | bytes 98312 | tf_op jit(solution)/shard_map/ppermute | solution.py:217
  96.3 4.1 %collective-permute-start.37 = (bf16[4,8,512]{2,1,0:T(8,128)(2,1)S(1)}, bf16[4,8,512]{2,1,0:T(8,128)(2,1)S(1)}, u32[]{:S(2)}, u32[]{:S(2)}) collective-permute-start(bf16[4,8,512]{2,1,0:T(8,128)(2,1)S(1)} %fusion.3), channel_id=1, source_target_pairs={{0,2},{1,3},{2,0},{3,1},{4,6},{5,7},{6,4},{7,5},{8,10},{9,11},{10,... | collective-permute-start | bytes 98312 | tf_op jit(solution)/shard_map/ppermute | solution.py:217
  100.5 1.3 %collective-permute-start.38 = (bf16[4,8,512]{2,1,0:T(8,128)(2,1)S(1)}, bf16[4,8,512]{2,1,0:T(8,128)(2,1)S(1)}, u32[]{:S(2)}, u32[]{:S(2)}) collective-permute-start(bf16[4,8,512]{2,1,0:T(8,128)(2,1)S(1)} %get-tuple-element.78.refs_2_), channel_id=1, source_target_pairs={{0,1},{1,0},{2,3},{3,2},{4,5},{5,4},{6,7},{7,6},{8,9},{9,8},{10,11... | collective-permute-start | bytes 98312 | tf_op jit(solution)/shard_map/ppermute | solution.py:212
  105.3 1.4 %collective-permute-start.39 = (bf16[4,4,8,256]{3,2,1,0:T(8,128)(2,1)S(1)}, bf16[4,4,8,256]{3,2,1,0:T(8,128)(2,1)S(1)}, u32[]{:S(2)}, u32[]{:S(2)}) collective-permute-start(bf16[4,4,8,256]{3,2,1,0:T(8,128)(2,1)S(1)} %get-tuple-element.69), channel_id=1, source_target_pairs={{0,1},{1,0},{2,3},{3,2},{4,5},{5,4},{6,7},{7,6},{8,9},{9,8},{10,11... | collective-permute-start | bytes 196616 | tf_op jit(solution)/shard_map/ppermute | solution.py:212
  106.7 5.6 %collective-permute-start.40 = (bf16[4,8,256]{2,1,0:T(8,128)(2,1)S(1)}, bf16[4,8,256]{2,1,0:T(8,128)(2,1)S(1)}, u32[]{:S(2)}, u32[]{:S(2)}) collective-permute-start(bf16[4,8,256]{2,1,0:T(8,128)(2,1)S(1)} %get-tuple-element.85), channel_id=1, source_target_pairs={{0,6},{1,7},{2,4},{3,5},{4,2},{5,3},{6,0},{7,1},{8,14},{9,15},{10,... | collective-permute-start | bytes 49160 | tf_op jit(solution)/shard_map/ppermute | solution.py:217
  108.1 4.6 %collective-permute-start.41 = (bf16[4,8,256]{2,1,0:T(8,128)(2,1)S(1)}, bf16[4,8,256]{2,1,0:T(8,128)(2,1)S(1)}, u32[]{:S(2)}, u32[]{:S(2)}) collective-permute-start(bf16[4,8,256]{2,1,0:T(8,128)(2,1)S(1)} %get-tuple-element.84), channel_id=1, source_target_pairs={{0,4},{1,5},{2,6},{3,7},{4,0},{5,1},{6,2},{7,3},{8,12},{9,13},{10,... | collective-permute-start | bytes 49160 | tf_op jit(solution)/shard_map/ppermute | solution.py:217
  108.7 4.2 %collective-permute-start.42 = (bf16[4,8,256]{2,1,0:T(8,128)(2,1)S(1)}, bf16[4,8,256]{2,1,0:T(8,128)(2,1)S(1)}, u32[]{:S(2)}, u32[]{:S(2)}) collective-permute-start(bf16[4,8,256]{2,1,0:T(8,128)(2,1)S(1)} %get-tuple-element.83), channel_id=1, source_target_pairs={{0,2},{1,3},{2,0},{3,1},{4,6},{5,7},{6,4},{7,5},{8,10},{9,11},{10,... | collective-permute-start | bytes 49160 | tf_op jit(solution)/shard_map/ppermute | solution.py:217
  113.3 1.3 %collective-permute-start.43 = (bf16[4,4,8,256]{3,2,1,0:T(8,128)(2,1)S(1)}, bf16[4,4,8,256]{3,2,1,0:T(8,128)(2,1)S(1)}, u32[]{:S(2)}, u32[]{:S(2)}) collective-permute-start(bf16[4,4,8,256]{3,2,1,0:T(8,128)(2,1)S(1)} %get-tuple-element.72), channel_id=1, source_target_pairs={{0,1},{1,0},{2,3},{3,2},{4,5},{5,4},{6,7},{7,6},{8,9},{9,8},{10,11... | collective-permute-start | bytes 196616 | tf_op jit(solution)/shard_map/ppermute | solution.py:212
  114.6 5.6 %collective-permute-start.44 = (bf16[4,8,256]{2,1,0:T(8,128)(2,1)S(1)}, bf16[4,8,256]{2,1,0:T(8,128)(2,1)S(1)}, u32[]{:S(2)}, u32[]{:S(2)}) collective-permute-start(bf16[4,8,256]{2,1,0:T(8,128)(2,1)S(1)} %get-tuple-element.80), channel_id=1, source_target_pairs={{0,6},{1,7},{2,4},{3,5},{4,2},{5,3},{6,0},{7,1},{8,14},{9,15},{10,... | collective-permute-start | bytes 49160 | tf_op jit(solution)/shard_map/ppermute | solution.py:217
  117.0 4.6 %collective-permute-start.45 = (bf16[4,8,256]{2,1,0:T(8,128)(2,1)S(1)}, bf16[4,8,256]{2,1,0:T(8,128)(2,1)S(1)}, u32[]{:S(2)}, u32[]{:S(2)}) collective-permute-start(bf16[4,8,256]{2,1,0:T(8,128)(2,1)S(1)} %get-tuple-element.82), channel_id=1, source_target_pairs={{0,4},{1,5},{2,6},{3,7},{4,0},{5,1},{6,2},{7,3},{8,12},{9,13},{10,... | collective-permute-start | bytes 49160 | tf_op jit(solution)/shard_map/ppermute | solution.py:217
  118.1 3.7 %collective-permute-start.46 = (bf16[4,8,256]{2,1,0:T(8,128)(2,1)S(1)}, bf16[4,8,256]{2,1,0:T(8,128)(2,1)S(1)}, u32[]{:S(2)}, u32[]{:S(2)}) collective-permute-start(bf16[4,8,256]{2,1,0:T(8,128)(2,1)S(1)} %get-tuple-element.81), channel_id=1, source_target_pairs={{0,2},{1,3},{2,0},{3,1},{4,6},{5,7},{6,4},{7,5},{8,10},{9,11},{10,... | collective-permute-start | bytes 49160 | tf_op jit(solution)/shard_map/ppermute | solution.py:217
  (8 other events, 124.8 us)

commit v7 on v6

--- a/solution.py
+++ b/solution.py
@@ -70,18 +70,13 @@
     sets, length = rows.shape
     tiles, blocks = length // LANES, width // LANES
 
-    def body(after_ref, given_ref, height_ref, list_ref, plan_ref, out_ref, rows_ref, scalar_ref, sems):
-        copies = [
-            pltpu.make_async_copy(given_ref, target, sems.at[i])
-            for i, target in enumerate((rows_ref, scalar_ref))
-        ]
-        for copy in copies:
-            copy.start()
+    def body(after_ref, rows_ref, height_ref, list_ref, plan_ref, out_ref, scalar_ref, sem):
+        copy = pltpu.make_async_copy(rows_ref, scalar_ref, sem)
+        copy.start()
         out_ref[...] = jnp.full(out_ref.shape, -1, I32)
         start = lax.axis_index("rows") * first
         used = [height_ref[s] - start for s in range(sets)]
-        for copy in copies:
-            copy.wait()
+        copy.wait()
         lane = lax.broadcasted_iota(I32, (1, LANES), 1)
         for tile in range(tiles):
             lanes = slice(tile * LANES, (tile + 1) * LANES)
@@ -121,13 +116,12 @@
             (((sets + 1) * tiles,), I32),
             ((len(of), blocks + 1, 8, LANES), I32),
         ],
-        [after, outside(rows), height],
-        [pl.BlockSpec(memory_space=pl.ANY), pl.BlockSpec(memory_space=pltpu.HBM), SMEM],
+        [after, rows, height],
+        [pl.BlockSpec(memory_space=pl.ANY), VMEM, SMEM],
         out_specs=[VMEM, SMEM, VMEM],
         scratch=[
-            pltpu.VMEM(rows.shape, I32),
             pltpu.SMEM(rows.shape, I32),
-            pltpu.SemaphoreType.DMA((2,)),
+            pltpu.SemaphoreType.DMA(()),
         ],
         moved=8 << 20,
         limit=4 << 20,
@@ -201,6 +195,37 @@
     for k in range(chips):
         own_ref[k] = value_ref[:, spot(2 * k + odd, w)].astype(own_ref.dtype)
         other_ref[k] = value_ref[:, spot(2 * k + 1 - odd, w)].astype(other_ref.dtype)
+
+
+def half_of(x_ref, w_ref, s, odd, xor):
+    at = (s,) if len(x_ref.shape) == 4 else ()
+    chips, cols = x_ref.shape[0], x_ref.shape[-1]
+    terms = []
+    for k in range(chips):
+        c = chip() ^ (-k % chips) if xor else k
+        terms.append(times_transposed(x_ref[(k,) + at], w_ref[s, :, spot(2 * c + odd, cols)]))
+    return sum(terms[1:], terms[0])
+
+
+def own_half(x, w, name, xor=False):
+    sets, rows = w.shape[:2]
+
+    def body(x_ref, w_ref, out_ref):
+        for s in range(sets):
+            out_ref[s] = half_of(x_ref, w_ref, s, core(), xor)
+
+    return call(
+        body,
+        [((sets, x.shape[-2], rows), F32)],
+        [x, pinned(w)],
+        [VMEM] * 2,
+        moved=12 << 20,
+        name=name,
+    )[0]
+
+
+def both_halves(part_ref, x_ref, w_ref, s, xor=False):
+    return part_ref[s] + half_of(x_ref, w_ref, s, 1 - core(), xor)
 
 
 def all_to_all(x):
@@ -256,6 +281,8 @@
     parent_cols, parent_width = parent_inv.shape[1:]
     parent_local = parent_panel.shape[1]
     root_width = root_inv.shape[1]
+    root_inv = root_inv[None]
+    root_local = root_inv.shape[1]
     root_cols = root_rhs.shape[1]
     piece = root_width // n
     tall = parent_width + root_width
@@ -272,18 +299,20 @@
         got = all_to_all(jnp.broadcast_to(x[None], (n,) + x.shape))
         return jnp.moveaxis(got, 0, 2).reshape(1, leaves, rcount, leaf_width)
 
-    def join_in(x_refs, x_ref, *at):
-        if len(x_refs) == 1:
-            return x_refs[0][(0,) + at]
-        unite(*x_refs, x_ref, *at, xor=True)
-        return x_ref[...]
+    def leaf_product(x_refs, w_ref, s):
+        if leaf_aligned:
+            return both_halves(*x_refs, w_ref, s, xor=True)
+        return times_transposed(x_refs[0][0, s], w_ref[s])
+
+    def leaf_halves(x, w, name):
+        return own_half(x, w, name, xor=True), swap(x)
 
     rhs = root_rhs
     if not root_aligned:
         rhs = lax.dynamic_update_slice_in_dim(
             jnp.zeros((rcount, root_width), F32), root_rhs, flat() * root_cols, 1
         )
-    weights = (leaf_inv, leaf_panel, parent_inv, parent_panel, root_inv)
+    weights = (leaf_inv, leaf_panel, parent_inv, parent_panel, root_inv, leaf_rows, parent_rows)
 
     def round_rhs(x_ref, *refs):
         out_ref = refs[-1]
@@ -305,12 +334,12 @@
     leaf_list, leaf_plan, inverse_low = prepare_leaves(lb, 0, half)
     lb = far_gather(lb) if leaf_aligned else leaf_columns(lb)
     lb, inverse_low, rhs = lax.optimization_barrier((lb, inverse_low, rhs))
-    lb = (lb, swap(lb)) if leaf_aligned else (lb,)
+    lb = leaf_halves(lb, leaf_inv, "leaf_solve_own") if leaf_aligned else (lb,)
 
     def leaf_solve(*refs):
-        x_refs, (w_ref, y_ref, send_ref, x_ref) = refs[: len(lb)], refs[len(lb) :]
+        x_refs, (w_ref, y_ref, send_ref) = refs[: len(lb)], refs[len(lb) :]
         for s in range(leaves):
-            y = times_transposed(join_in(x_refs, x_ref, s), w_ref[s])
+            y = leaf_product(x_refs, w_ref, s)
             y_ref[s] = y
             send_ref[s] = y.astype(BF16)
 
@@ -319,25 +348,23 @@
         [((leaves, rcount, leaf_cols), F32), ((leaves, rcount, leaf_cols), BF16)],
         [*lb, pinned(leaf_inv)],
         [VMEM] * (len(lb) + 1),
-        scratch=[pltpu.VMEM((rcount, leaf_width), BF16)],
         name="leaf_solve",
     )
     inverse_high = prepare_leaves(lyb, half, leaves)[2]
     if leaf_aligned:
         lyb, inverse_high = lax.optimization_barrier((far_gather(lyb), inverse_high))
-        lyb = (lyb, swap(lyb))
+        lyb = leaf_halves(lyb, leaf_panel, "leaf_update_own")
     else:
         lyb = (leaf_columns(lyb),)
     leaf_inverse = (inverse_low, inverse_high)
 
     def leaf_update(*refs):
         x_refs, refs = refs[: len(lyb)], refs[len(lyb) :]
-        plan_ref, w_ref, *inverse_refs, rhs_ref, own_ref, other_ref, root_ref = refs[:-4]
-        refs = refs[-4:]
-        x_ref, update_ref, acc_ref, sum_ref = refs
+        plan_ref, w_ref, *inverse_refs, rhs_ref, own_ref, other_ref, root_ref = refs[:-3]
+        update_ref, acc_ref, sum_ref = refs[-3:]
         acc_ref[...] = jnp.zeros(acc_ref.shape, F32)
         for s in range(leaves):
-            update_ref[s] = times_transposed(join_in(x_refs, x_ref, s), w_ref[s])
+            update_ref[s] = leaf_product(x_refs, w_ref, s)
         scatter_walk(plan_ref, inverse_refs, update_ref, acc_ref, leaf_local // LANES)
         for b in range(parent_width // LANES):
             sum_ref[:, b * LANES : (b + 1) * LANES] = -acc_ref[b]
@@ -356,7 +383,6 @@
         [*lyb, leaf_plan, pinned(leaf_panel), *leaf_inverse, parent_rhs],
         [VMEM] * len(lyb) + [SMEM] + [VMEM] * 4,
         scratch=[
-            pltpu.VMEM((rcount, leaf_width), BF16),
             pltpu.VMEM((leaves, rcount, leaf_local), F32),
             pltpu.VMEM((tall // LANES + 1, rcount, LANES), F32),
             pltpu.VMEM((rcount, parent_width), F32),
@@ -365,18 +391,16 @@
     )
     prb = chips_sum(own + swap(other).astype(F32)).astype(BF16)
 
-    def parent_solve(own_ref, other_ref, w_ref, y_ref, send_ref, x_ref):
-        unite(own_ref, other_ref, x_ref)
-        y = times_transposed(x_ref[...], w_ref[0])
+    def parent_solve(part_ref, x_ref, w_ref, y_ref, send_ref):
+        y = both_halves(part_ref, x_ref, w_ref, 0)
         y_ref[...] = y
         send_ref[...] = y.astype(BF16)
 
     py, pyb = call(
         parent_solve,
         [((rcount, parent_cols), F32), ((rcount, parent_cols), BF16)],
-        [prb, swap(prb), pinned(parent_inv)],
+        [own_half(prb, parent_inv, "parent_solve_own"), swap(prb), pinned(parent_inv)],
         [VMEM] * 3,
-        scratch=[pltpu.VMEM((rcount, parent_width), BF16)],
         name="parent_solve",
     )
     parent_list, parent_plan, parent_inverse = prepare(
@@ -385,13 +409,12 @@
     pyb, parent_inverse = lax.optimization_barrier((far_gather(pyb), parent_inverse))
 
     def parent_update(
-        plan_ref, x_own_ref, x_other_ref, w_ref, inverse_ref, root_ref, rhs_ref, own_ref, other_ref,
-        x_ref, update_ref, acc_ref, sum_ref,
+        plan_ref, part_ref, x_ref, w_ref, inverse_ref, root_ref, rhs_ref, own_ref, other_ref,
+        update_ref, acc_ref, sum_ref,
     ):
-        unite(x_own_ref, x_other_ref, x_ref, xor=True)
         for b in range(root_width // LANES):
             acc_ref[b] = root_ref[b]
-        update_ref[0] = times_transposed(x_ref[...], w_ref[0])
+        update_ref[0] = both_halves(part_ref, x_ref, w_ref, 0, xor=True)
         scatter_walk(plan_ref, [inverse_ref], update_ref, acc_ref, parent_local // LANES)
         for b in range(root_width // LANES):
             sum_ref[:, b * LANES : (b + 1) * LANES] = -acc_ref[b]
@@ -404,10 +427,17 @@
     own, other = call(
         parent_update,
         [((chips, rcount, piece), F32), ((chips, rcount, piece), BF16)],
-        [parent_plan, pyb, swap(pyb), pinned(parent_panel), parent_inverse, root_acc, rhs],
+        [
+            parent_plan,
+            own_half(pyb, parent_panel, "parent_update_own", xor=True),
+            swap(pyb),
+            pinned(parent_panel),
+            parent_inverse,
+            root_acc,
+            rhs,
+        ],
         [SMEM] + [VMEM] * 6,
         scratch=[
-            pltpu.VMEM((rcount, parent_width), BF16),
             pltpu.VMEM((1, rcount, parent_local), F32),
             pltpu.VMEM((root_width // LANES + 1, rcount, LANES), F32),
             pltpu.VMEM((rcount, root_width), F32),
@@ -416,43 +446,44 @@
     )
     rrb = chips_sum(leaf_sum(own + swap(other).astype(F32))).astype(BF16)
 
-    def root_solve(own_ref, other_ref, w_ref, own_out, other_out, x_ref, sum_ref):
-        unite(own_ref, other_ref, x_ref)
-        y = times_transposed(x_ref[...], w_ref[...]).astype(BF16)
-        sum_ref[...] = times(y, w_ref[...])
-        deal(sum_ref, own_out, other_out)
-
-    own, other = call(
+    def terms(x_ref, w_ref, out_ref, odd, xor=True):
+        _, sets, _, cols = out_ref.shape
+        for k in range(chips):
+            at = spot(2 * (chip() ^ k if xor else k) + odd, cols)
+            for s in range(sets):
+                out_ref[k, s] = times(x_ref[s], w_ref[s, :, at]).astype(out_ref.dtype)
+
+    def split_terms(w):
+        return (chips, w.shape[0], rcount, w.shape[2] // n)
+
+    def own_terms(x, w, name, xor=True):
+        def body(x_ref, w_ref, out_ref):
+            terms(x_ref, w_ref, out_ref, core(), xor)
+
+        return call(
+            body, [(split_terms(w), F32)], [x, pinned(w)], [VMEM] * 2, moved=12 << 20, name=name
+        )[0]
+
+    def total(x, w, other, name):
+        own = own_terms(x, w, name, xor=False)
+        return chips_sum((own + swap(other).astype(F32))[:, 0])
+
+    def root_solve(part_ref, x_ref, w_ref, out_ref, y_ref):
+        y_ref[0] = both_halves(part_ref, x_ref, w_ref, 0).astype(BF16)
+        terms(y_ref, w_ref, out_ref, 1 - core(), xor=False)
+
+    term, ryb = call(
         root_solve,
-        [((chips, rcount, piece), F32), ((chips, rcount, piece), BF16)],
-        [rrb, swap(rrb), pinned(root_inv)],
+        [(split_terms(root_inv), BF16), ((1, rcount, root_local), BF16)],
+        [own_half(rrb, root_inv, "root_solve_own"), swap(rrb), pinned(root_inv)],
         [VMEM] * 3,
-        scratch=[pltpu.VMEM((rcount, root_width), BF16), pltpu.VMEM((rcount, root_width), F32)],
         name="root_solve",
     )
-    rxb = chips_sum(own + swap(other).astype(F32)).astype(BF16)
+    rxb = total(ryb, root_inv, term, "root_solve_back_own").astype(BF16)
 
     def blocks_of(source_ref, target_ref, start, width):
         for b in range(width // LANES):
             target_ref[start + b] = source_ref[:, b * LANES : (b + 1) * LANES].astype(F32)
-
-    def terms(x_ref, w_ref, out_ref, odd):
-        _, sets, _, cols = out_ref.shape
-        for k in range(chips):
-            at = spot(2 * (chip() ^ k) + odd, cols)
-            for s in range(sets):
-                out_ref[k, s] = times(x_ref[s], w_ref[s, :, at]).astype(out_ref.dtype)
-
-    def split_terms(w):
-        return (chips, w.shape[0], rcount, w.shape[2] // n)
-
-    def own_terms(x, w, name):
-        def body(x_ref, w_ref, out_ref):
-            terms(x_ref, w_ref, out_ref, core())
-
-        return call(
-            body, [(split_terms(w), F32)], [x, pinned(w)], [VMEM] * 2, moved=12 << 20, name=name
-        )[0]
 
     def reduce(own, other):
         other = swap(other)
@@ -488,20 +519,19 @@
     tails = reduce(own_terms(found, parent_panel, "parent_back_own"), term)
 
     def parent_solve_back(*refs):
-        tail_refs, (y_ref, w_ref, own_ref, other_ref, sum_ref) = refs[:chips], refs[chips:]
+        tail_refs, (y_ref, w_ref, out_ref, v_ref) = refs[:chips], refs[chips:]
         lost = sum(ref[0].astype(F32) for ref in tail_refs)
-        sum_ref[...] = times((y_ref[...] - lost).astype(BF16), w_ref[0])
-        deal(sum_ref, own_ref, other_ref)
-
-    own, other = call(
+        v_ref[0] = (y_ref[...] - lost).astype(BF16)
+        terms(v_ref, w_ref, out_ref, 1 - core(), xor=False)
+
+    term, pvb = call(
         parent_solve_back,
-        [((chips, rcount, parent_cols), F32), ((chips, rcount, parent_cols), BF16)],
+        [(split_terms(parent_inv), BF16), ((1, rcount, parent_cols), BF16)],
         [*tails, py, pinned(parent_inv)],
         [VMEM] * (chips + 2),
-        scratch=[pltpu.VMEM((rcount, parent_width), F32)],
         name="parent_solve_back",
     )
-    px = chips_sum(own + swap(other).astype(F32))
+    px = total(pvb, parent_inv, term, "parent_solve_back_own")
     pxb = px.astype(BF16)
 
     def ancestors(

time: 123 us -> 118 us (0.959)
  waiting for transfers between devices: 35.5 us -> 29.8 us
  starting transfers between devices: 51 us -> 52.3 us
    ppermute x14, waiting for transfers between devices: 14.3 us -> 9.46 us  [swap(): return lax.ppermute(x, 'rows', [(i, i ^ 1) for i in range(n)])]
    pallas_call x16 -> x23, Pallas kernels: 31.9 us -> 31.9 us  [call(): pl.pallas_call(body, out_shape=[jax.ShapeDtypeStruct(*o) if isinstance(o,...]
  transfers between devices with their start and end apart: 47 -> 47, of which waited for: 34 -> 35; matrix products, arithmetic and copies ran while one was open for 1% -> 1% of each run, Pallas kernels for 10% -> 15%
where the time goes in v7:
time: 118 us
  starting transfers between devices  52.3 us (44%)
  Pallas kernels  31.9 us (27%)
  waiting for transfers between devices  29.8 us (25%)
  local copies, waits for them, and re-layouts  2.23 us (2%)
  between operations  1.71 us (1%)
    ppermute x30, starting transfers between devices, far(): return lax.ppermute(x, 'rows', [(i, i ^ 2 * k) for i in range(n)])  45.8 us
    pallas_call x23, Pallas kernels, call(): pl.pallas_call(body, out_shape=[jax.ShapeDtypeStruct(*o) if isinstance(o,...  31.9 us
    ppermute x30, waiting for transfers between devices, far(): return lax.ppermute(x, 'rows', [(i, i ^ 2 * k) for i in range(n)])  18 us
    ppermute x14, waiting for transfers between devices, swap(): return lax.ppermute(x, 'rows', [(i, i ^ 1) for i in range(n)])  9.46 us
    ppermute x3, starting transfers between devices, leaf_sum(): lax.ppermute(b, 'leaf', [(i, (i + k) % n) for i in range(n)]).astype(F32)  4.26 us
  transfers between devices with their start and end apart: 47, of which 35 were waited for; matrix products, arithmetic and copies ran while one was open for 1% of the time, Pallas kernels for 15%

profile of v7, /device:TPU:0, one launch (start us, length us, event | category | flops | bytes accessed | tf_op | source)
XLA Modules:
  0.0 118.3 jit_solution(16162923785187928867)
XLA Ops:
  1.6 5.1 %collective-permute-start = (bf16[4,8,256]{2,1,0:T(8,128)(2,1)S(1)}, bf16[4,8,256]{2,1,0:T(8,128)(2,1)S(1)}, u32[]{:S(2)}, u32[]{:S(2)}) collective-permute-start(bf16[4,8,256]{2,1,0:T(8,128)(2,1)S(1)} %round_rhs.1.after_ref), channel_id=1, source_target_pairs={{0,6},{1,7},{2,4},{3,5},{4,2},{5,3},{6,0},{7,1},{8,14},{9,15},{10,... | collective-permute-start | bytes 49160 | tf_op jit(solution)/shard_map/ppermute | solution.py:242
  7.4 3.9 %prepare.3 = (s32[4,1024]{1,0:T(4,128)S(1)}, s32[40]{0:T(128)S(1)}, s32[2,65,8,128]{3,2,1,0:T(8,128)S(1)}) custom-call(bf16[4,8,256]{2,1,0:T(8,128)(2,1)S(1)} %round_rhs.1.after_ref, s32[4,1024]{1,0:T(4,128)S(1)} %copy-done.4, s32[4]{0:T(128)S(1)} %copy-done.9), custom_call_target="tpu_custom_call" | custom-call | bytes 8388608 | tf_op jit(solution)/shard_map/prepare/pallas_call | solution.py:29
  13.3 3.4 %collective-permute-start.4 = (bf16[4,8,256]{2,1,0:T(8,128)(2,1)S(1)}, bf16[4,8,256]{2,1,0:T(8,128)(2,1)S(1)}, u32[]{:S(2)}, u32[]{:S(2)}) collective-permute-start(bf16[4,8,256]{2,1,0:T(8,128)(2,1)S(1)} %get-tuple-element.42.after_ref), channel_id=1, source_target_pairs={{0,6},{1,7},{2,4},{3,5},{4,2},{5,3},{6,0},{7,1},{8,14},{9,15},{10,... | collective-permute-start | bytes 49160 | tf_op jit(solution)/shard_map/ppermute | solution.py:242
  16.7 1.1 collective-permute-start.6
  17.8 3.9 %prepare.4 = (s32[4,1024]{1,0:T(4,128)}, s32[40]{0:T(128)}, s32[2,65,8,128]{3,2,1,0:T(8,128)S(1)}) custom-call(bf16[4,8,256]{2,1,0:T(8,128)(2,1)S(1)} %get-tuple-element.42.after_ref, s32[4,1024]{1,0:T(4,128)S(1)} %copy-done.4, s32[4]{0:T(128)S(1)} %copy-done.9), custom_call_target="tpu_custom_call" | custom-call | bytes 8388608 | tf_op jit(solution)/shard_map/prepare/pallas_call | solution.py:29
  21.9 2.3 %leaf_update_own.1.refs_0_ = f32[4,8,1024]{2,1,0:T(8,128)S(1)} custom-call(bf16[4,4,8,256]{3,2,1,0:T(8,128)(2,1)S(1)} %pad_maximum_fusion.1.x_ref, bf16[4,1024,2048]{2,1,0:T(8,128)(2,1)S(1)} %bitcast.73), custom_call_target="tpu_custom_call" | custom-call | bytes 12582912 | tf_op jit(solution)/shard_map/leaf_update_own/pallas_call | solution.py:29
  24.2 4.8 %leaf_update.1 = (f32[4,8,512]{2,1,0:T(8,128)S(1)}, bf16[4,8,512]{2,1,0:T(8,128)(2,1)S(1)}, f32[32,8,128]{2,1,0:T(8,128)S(1)}) custom-call(f32[4,8,1024]{2,1,0:T(8,128)S(1)} %leaf_update_own.1.refs_0_, bf16[4,4,8,256]{3,2,1,0:T(8,128)(2,1)S(1)} %collective-permute-done.7.refs_1_, s32[40]{0:T(128)S(1)} %get-tuple-element.39.refs_2_.refs_0_, ...), custom_call_target="tpu_custom_call" | custom-call | tf_op jit(solution)/shard_map/leaf_update/pallas_call | solution.py:29
  31.5 1.7 %collective-permute-start.11 = (bf16[4,8,512]{2,1,0:T(8,128)(2,1)S(1)}, bf16[4,8,512]{2,1,0:T(8,128)(2,1)S(1)}, u32[]{:S(2)}, u32[]{:S(2)}) collective-permute-start(bf16[4,8,512]{2,1,0:T(8,128)(2,1)S(1)} %fusion.1), channel_id=1, source_target_pairs={{0,2},{1,3},{2,0},{3,1},{4,6},{5,7},{6,4},{7,5},{8,10},{9,11},{10,... | collective-permute-start | bytes 98312 | tf_op jit(solution)/shard_map/ppermute | solution.py:242
  33.2 1.9 %collective-permute-start.9 = (bf16[4,8,512]{2,1,0:T(8,128)(2,1)S(1)}, bf16[4,8,512]{2,1,0:T(8,128)(2,1)S(1)}, u32[]{:S(2)}, u32[]{:S(2)}) collective-permute-start(bf16[4,8,512]{2,1,0:T(8,128)(2,1)S(1)} %fusion.1), channel_id=1, source_target_pairs={{0,6},{1,7},{2,4},{3,5},{4,2},{5,3},{6,0},{7,1},{8,14},{9,15},{10,... | collective-permute-start | bytes 98312 | tf_op jit(solution)/shard_map/ppermute | solution.py:242
  35.8 3.2 %collective-permute-done.9 = bf16[4,8,512]{2,1,0:T(8,128)(2,1)S(1)} collective-permute-done((bf16[4,8,512]{2,1,0:T(8,128)(2,1)S(1)}, bf16[4,8,512]{2,1,0:T(8,128)(2,1)S(1)}, u32[]{:S(2)}, u32[]{:S(2)}) %collective-permute-start.9) | collective-permute-done | bytes 32800 | tf_op jit(solution)/shard_map/ppermute | solution.py:242
  40.9 1.9 %collective-permute-start.13 = (bf16[8,512]{1,0:T(8,128)(2,1)S(1)}, bf16[8,512]{1,0:T(8,128)(2,1)S(1)}, u32[]{:S(2)}, u32[]{:S(2)}) collective-permute-start(bf16[8,512]{1,0:T(8,128)(2,1)S(1)} %get-tuple-element.49.after_ref), channel_id=1, source_target_pairs={{0,6},{1,7},{2,4},{3,5},{4,2},{5,3},{6,0},{7,1},{8,14},{9,15},{10,... | collective-permute-start | bytes 24584 | tf_op jit(solution)/shard_map/ppermute | solution.py:242
  42.8 2.5 %collective-permute-start.15 = (bf16[8,512]{1,0:T(8,128)(2,1)S(1)}, bf16[8,512]{1,0:T(8,128)(2,1)S(1)}, u32[]{:S(2)}, u32[]{:S(2)}) collective-permute-start(bf16[8,512]{1,0:T(8,128)(2,1)S(1)} %get-tuple-element.49.after_ref), channel_id=1, source_target_pairs={{0,2},{1,3},{2,0},{3,1},{4,6},{5,7},{6,4},{7,5},{8,10},{9,11},{10,... | collective-permute-start | bytes 24584 | tf_op jit(solution)/shard_map/ppermute | solution.py:242
  46.0 1.8 %prepare.5 = (s32[1,512]{1,0:T(1,128)S(1)}, s32[8]{0:T(128)S(1)}, s32[1,33,8,128]{3,2,1,0:T(8,128)S(1)}) custom-call(bf16[8,512]{1,0:T(8,128)(2,1)S(1)} %get-tuple-element.49.after_ref, s32[1,512]{1,0:T(1,128)S(1)} %copy-done.7, s32[1]{0:T(128)S(6)} %copy.21.height_ref), custom_call_target="tpu_custom_call" | custom-call | bytes 8388608 | tf_op jit(solution)/shard_map/prepare/pallas_call | solution.py:29
  49.1 1.8 %parent_update.1 = (f32[4,8,512]{2,1,0:T(8,128)S(1)}, bf16[4,8,512]{2,1,0:T(8,128)(2,1)S(1)}) custom-call(s32[8]{0:T(128)S(1)} %get-tuple-element.50.plan_ref, f32[1,8,512]{2,1,0:T(8,128)S(1)} %parent_update_own.1.part_ref, bf16[4,8,512]{2,1,0:T(8,128)(2,1)S(1)} %collective-permute-done.16.x_ref, bf16[1,512,4096]{2,1,0:T(8,128)(2,1)S(1)} %copy-done, ...), custom_call_target="tpu_custom_call" | custom-call | tf_op jit(solution)/shard_map/parent_update/pallas_call | solution.py:29
  51.1 1.0 collective-permute-done.17
  52.2 1.4 %collective-permute-start.18 = (bf16[4,8,512]{2,1,0:T(8,128)(2,1)S(1)}, bf16[4,8,512]{2,1,0:T(8,128)(2,1)S(1)}, u32[]{:S(2)}, u32[]{:S(2)}) collective-permute-start(bf16[4,8,512]{2,1,0:T(8,128)(2,1)S(1)} %fusion.2), channel_id=1, source_target_pairs={{0,8},{8,16},{16,24},{24,0},{1,9},{9,17},{17,25},{25,1},{2,10},{10... | collective-permute-start | bytes 98312 | tf_op jit(solution)/shard_map/ppermute | solution.py:259
  53.6 1.3 %collective-permute-start.19 = (bf16[4,8,512]{2,1,0:T(8,128)(2,1)S(1)}, bf16[4,8,512]{2,1,0:T(8,128)(2,1)S(1)}, u32[]{:S(2)}, u32[]{:S(2)}) collective-permute-start(bf16[4,8,512]{2,1,0:T(8,128)(2,1)S(1)} %fusion.2), channel_id=1, source_target_pairs={{0,16},{8,24},{16,0},{24,8},{1,17},{9,25},{17,1},{25,9},{2,18},{10... | collective-permute-start | bytes 98312 | tf_op jit(solution)/shard_map/ppermute | solution.py:259
  54.9 1.6 %collective-permute-start.20 = (bf16[4,8,512]{2,1,0:T(8,128)(2,1)S(1)}, bf16[4,8,512]{2,1,0:T(8,128)(2,1)S(1)}, u32[]{:S(2)}, u32[]{:S(2)}) collective-permute-start(bf16[4,8,512]{2,1,0:T(8,128)(2,1)S(1)} %fusion.2), channel_id=1, source_target_pairs={{0,24},{8,0},{16,8},{24,16},{1,25},{9,1},{17,9},{25,17},{2,26},{10... | collective-permute-start | bytes 98312 | tf_op jit(solution)/shard_map/ppermute | solution.py:259
  57.5 1.3 %collective-permute-done.20 = bf16[4,8,512]{2,1,0:T(8,128)(2,1)S(1)} collective-permute-done((bf16[4,8,512]{2,1,0:T(8,128)(2,1)S(1)}, bf16[4,8,512]{2,1,0:T(8,128)(2,1)S(1)}, u32[]{:S(2)}, u32[]{:S(2)}) %collective-permute-start.20) | collective-permute-done | bytes 32800 | tf_op jit(solution)/shard_map/ppermute | solution.py:259
  58.8 1.2 %collective-permute-start.21 = (bf16[4,8,512]{2,1,0:T(8,128)(2,1)S(1)}, bf16[4,8,512]{2,1,0:T(8,128)(2,1)S(1)}, u32[]{:S(2)}, u32[]{:S(2)}) collective-permute-start(bf16[4,8,512]{2,1,0:T(8,128)(2,1)S(1)} %fusion.28), channel_id=1, source_target_pairs={{0,6},{1,7},{2,4},{3,5},{4,2},{5,3},{6,0},{7,1},{8,14},{9,15},{10,... | collective-permute-start | bytes 98312 | tf_op jit(solution)/shard_map/ppermute | solution.py:242
  60.1 1.4 %collective-permute-start.22 = (bf16[4,8,512]{2,1,0:T(8,128)(2,1)S(1)}, bf16[4,8,512]{2,1,0:T(8,128)(2,1)S(1)}, u32[]{:S(2)}, u32[]{:S(2)}) collective-permute-start(bf16[4,8,512]{2,1,0:T(8,128)(2,1)S(1)} %fusion.28), channel_id=1, source_target_pairs={{0,4},{1,5},{2,6},{3,7},{4,0},{5,1},{6,2},{7,3},{8,12},{9,13},{10,... | collective-permute-start | bytes 98312 | tf_op jit(solution)/shard_map/ppermute | solution.py:242
  61.5 1.8 %collective-permute-start.23 = (bf16[4,8,512]{2,1,0:T(8,128)(2,1)S(1)}, bf16[4,8,512]{2,1,0:T(8,128)(2,1)S(1)}, u32[]{:S(2)}, u32[]{:S(2)}) collective-permute-start(bf16[4,8,512]{2,1,0:T(8,128)(2,1)S(1)} %fusion.28), channel_id=1, source_target_pairs={{0,2},{1,3},{2,0},{3,1},{4,6},{5,7},{6,4},{7,5},{8,10},{9,11},{10,... | collective-permute-start | bytes 98312 | tf_op jit(solution)/shard_map/ppermute | solution.py:242
  63.3 1.3 %collective-permute-done.21 = bf16[4,8,512]{2,1,0:T(8,128)(2,1)S(1)} collective-permute-done((bf16[4,8,512]{2,1,0:T(8,128)(2,1)S(1)}, bf16[4,8,512]{2,1,0:T(8,128)(2,1)S(1)}, u32[]{:S(2)}, u32[]{:S(2)}) %collective-permute-start.21) | collective-permute-done | bytes 32800 | tf_op jit(solution)/shard_map/ppermute | solution.py:242
  67.0 1.0 root_solve.1
  69.2 1.9 %collective-permute-start.26 = (bf16[4,8,512]{2,1,0:T(8,128)(2,1)S(1)}, bf16[4,8,512]{2,1,0:T(8,128)(2,1)S(1)}, u32[]{:S(2)}, u32[]{:S(2)}) collective-permute-start(bf16[4,8,512]{2,1,0:T(8,128)(2,1)S(1)} %bitcast_convert_fusion.1), channel_id=1, source_target_pairs={{0,6},{1,7},{2,4},{3,5},{4,2},{5,3},{6,0},{7,1},{8,14},{9,15},{10,... | collective-permute-start | bytes 98312 | tf_op jit(solution)/shard_map/ppermute | solution.py:242
  71.1 1.1 collective-permute-start.27
  72.3 1.4 %collective-permute-start.28 = (bf16[4,8,512]{2,1,0:T(8,128)(2,1)S(1)}, bf16[4,8,512]{2,1,0:T(8,128)(2,1)S(1)}, u32[]{:S(2)}, u32[]{:S(2)}) collective-permute-start(bf16[4,8,512]{2,1,0:T(8,128)(2,1)S(1)} %bitcast_convert_fusion.1), channel_id=1, source_target_pairs={{0,2},{1,3},{2,0},{3,1},{4,6},{5,7},{6,4},{7,5},{8,10},{9,11},{10,... | collective-permute-start | bytes 98312 | tf_op jit(solution)/shard_map/ppermute | solution.py:242
  73.7 1.4 %collective-permute-done.26 = bf16[4,8,512]{2,1,0:T(8,128)(2,1)S(1)} collective-permute-done((bf16[4,8,512]{2,1,0:T(8,128)(2,1)S(1)}, bf16[4,8,512]{2,1,0:T(8,128)(2,1)S(1)}, u32[]{:S(2)}, u32[]{:S(2)}) %collective-permute-start.26) | collective-permute-done | bytes 32800 | tf_op jit(solution)/shard_map/ppermute | solution.py:242
  75.1 1.2 %collective-permute-done.27 = bf16[4,8,512]{2,1,0:T(8,128)(2,1)S(1)} collective-permute-done((bf16[4,8,512]{2,1,0:T(8,128)(2,1)S(1)}, bf16[4,8,512]{2,1,0:T(8,128)(2,1)S(1)}, u32[]{:S(2)}, u32[]{:S(2)}) %collective-permute-start.27) | collective-permute-done | bytes 32800 | tf_op jit(solution)/shard_map/ppermute | solution.py:242
  76.7 1.2 %collective-permute-done.29.other_ref = bf16[4,8,512]{2,1,0:T(8,128)(2,1)S(1)} collective-permute-done((bf16[4,8,512]{2,1,0:T(8,128)(2,1)S(1)}, bf16[4,8,512]{2,1,0:T(8,128)(2,1)S(1)}, u32[]{:S(2)}, u32[]{:S(2)}) %collective-permute-start.29) | collective-permute-done | bytes 32800 | tf_op jit(solution)/shard_map/ppermute | solution.py:237
  77.9 1.7 %parent_back.1 = (bf16[4,1,8,512]{3,2,1,0:T(8,128)(2,1)S(1)}, f32[33,8,128]{2,1,0:T(8,128)S(1)}, f32[8,128]{1,0:T(8,128)}, bf16[1,8,512]{2,1,0:T(8,128)(2,1)S(1)}) custom-call(s32[8]{0:T(128)S(1)} %get-tuple-element.50.plan_ref, bf16[4,8,512]{2,1,0:T(8,128)(2,1)S(1)} %fusion.own_ref, bf16[4,8,512]{2,1,0:T(8,128)(2,1)S(1)} %collective-permute-done.29.other_ref, ...), custom_call_target="tpu_custom_call" | custom-call | tf_op jit(solution)/shard_map/parent_back/pallas_call | solution.py:29
  80.8 1.2 collective-permute-start.31
  82.8 2.4 %collective-permute-start.33 = (bf16[1,8,512]{2,1,0:T(8,128)(2,1)S(1)}, bf16[1,8,512]{2,1,0:T(8,128)(2,1)S(1)}, u32[]{:S(2)}, u32[]{:S(2)}) collective-permute-start(bf16[1,8,512]{2,1,0:T(8,128)(2,1)S(1)} %get-tuple-element.87), channel_id=1, source_target_pairs={{0,2},{1,3},{2,0},{3,1},{4,6},{5,7},{6,4},{7,5},{8,10},{9,11},{10,... | collective-permute-start | bytes 24584 | tf_op jit(solution)/shard_map/ppermute | solution.py:242
  85.3 1.1 collective-permute-done.31.refs_1_
  88.5 2.4 %collective-permute-start.35 = (bf16[4,8,512]{2,1,0:T(8,128)(2,1)S(1)}, bf16[4,8,512]{2,1,0:T(8,128)(2,1)S(1)}, u32[]{:S(2)}, u32[]{:S(2)}) collective-permute-start(bf16[4,8,512]{2,1,0:T(8,128)(2,1)S(1)} %bitcast_convert_fusion), channel_id=1, source_target_pairs={{0,6},{1,7},{2,4},{3,5},{4,2},{5,3},{6,0},{7,1},{8,14},{9,15},{10,... | collective-permute-start | bytes 98312 | tf_op jit(solution)/shard_map/ppermute | solution.py:242
  90.9 1.1 collective-permute-start.36
  92.1 0.9 collective-permute-start.37
  93.0 1.7 %collective-permute-done.35 = bf16[4,8,512]{2,1,0:T(8,128)(2,1)S(1)} collective-permute-done((bf16[4,8,512]{2,1,0:T(8,128)(2,1)S(1)}, bf16[4,8,512]{2,1,0:T(8,128)(2,1)S(1)}, u32[]{:S(2)}, u32[]{:S(2)}) %collective-permute-start.35) | collective-permute-done | bytes 32800 | tf_op jit(solution)/shard_map/ppermute | solution.py:242
  94.6 1.1 collective-permute-done.36
  96.2 1.2 %collective-permute-done.38.refs_3_ = bf16[4,8,512]{2,1,0:T(8,128)(2,1)S(1)} collective-permute-done((bf16[4,8,512]{2,1,0:T(8,128)(2,1)S(1)}, bf16[4,8,512]{2,1,0:T(8,128)(2,1)S(1)}, u32[]{:S(2)}, u32[]{:S(2)}) %collective-permute-start.38) | collective-permute-done | bytes 32800 | tf_op jit(solution)/shard_map/ppermute | solution.py:237
  97.4 3.4 %leaf_back.1 = (bf16[4,4,8,256]{3,2,1,0:T(8,128)(2,1)S(1)}, f32[8,512]{1,0:T(8,128)S(1)}, bf16[4,8,1024]{2,1,0:T(8,128)(2,1)S(1)}) custom-call(s32[40]{0:T(128)S(1)} %get-tuple-element.39.refs_2_.refs_0_, f32[4,8,512]{2,1,0:T(8,128)S(1)} %get-tuple-element.79.refs_1_, bf16[4,8,512]{2,1,0:T(8,128)(2,1)S(1)} %get-tuple-element.78.refs_2_, ...), custom_call_target="tpu_custom_call" | custom-call | tf_op jit(solution)/shard_map/leaf_back/pallas_call | solution.py:29
  101.2 1.2 %leaf_back_own.1 = f32[4,4,8,256]{3,2,1,0:T(8,128)S(1)} custom-call(bf16[4,8,1024]{2,1,0:T(8,128)(2,1)S(1)} %get-tuple-element.68.x_ref, bf16[4,1024,2048]{2,1,0:T(8,128)(2,1)S(1)} %bitcast.73), custom_call_target="tpu_custom_call" | custom-call | bytes 12582912 | tf_op jit(solution)/shard_map/leaf_back_own/pallas_call | solution.py:29
  103.9 3.1 %collective-permute-start.42 = (bf16[4,8,256]{2,1,0:T(8,128)(2,1)S(1)}, bf16[4,8,256]{2,1,0:T(8,128)(2,1)S(1)}, u32[]{:S(2)}, u32[]{:S(2)}) collective-permute-start(bf16[4,8,256]{2,1,0:T(8,128)(2,1)S(1)} %get-tuple-element.83), channel_id=1, source_target_pairs={{0,2},{1,3},{2,0},{3,1},{4,6},{5,7},{6,4},{7,5},{8,10},{9,11},{10,... | collective-permute-start | bytes 49160 | tf_op jit(solution)/shard_map/ppermute | solution.py:242
  106.9 1.3 %collective-permute-done.40.refs_1_ = bf16[4,8,256]{2,1,0:T(8,128)(2,1)S(1)} collective-permute-done((bf16[4,8,256]{2,1,0:T(8,128)(2,1)S(1)}, bf16[4,8,256]{2,1,0:T(8,128)(2,1)S(1)}, u32[]{:S(2)}, u32[]{:S(2)}) %collective-permute-start.40) | collective-permute-done | bytes 16416 | tf_op jit(solution)/shard_map/ppermute | solution.py:242
  110.3 2.4 %collective-permute-start.44 = (bf16[4,8,256]{2,1,0:T(8,128)(2,1)S(1)}, bf16[4,8,256]{2,1,0:T(8,128)(2,1)S(1)}, u32[]{:S(2)}, u32[]{:S(2)}) collective-permute-start(bf16[4,8,256]{2,1,0:T(8,128)(2,1)S(1)} %get-tuple-element.80), channel_id=1, source_target_pairs={{0,6},{1,7},{2,4},{3,5},{4,2},{5,3},{6,0},{7,1},{8,14},{9,15},{10,... | collective-permute-start | bytes 49160 | tf_op jit(solution)/shard_map/ppermute | solution.py:242
  112.8 1.1 collective-permute-start.45
  113.9 0.9 collective-permute-start.46
  115.9 1.5 %collective-permute-done.45 = bf16[4,8,256]{2,1,0:T(8,128)(2,1)S(1)} collective-permute-done((bf16[4,8,256]{2,1,0:T(8,128)(2,1)S(1)}, bf16[4,8,256]{2,1,0:T(8,128)(2,1)S(1)}, u32[]{:S(2)}, u32[]{:S(2)}) %collective-permute-start.45) | collective-permute-done | bytes 16416 | tf_op jit(solution)/shard_map/ppermute | solution.py:242
  (116 shorter events, 26.0 us)
Async XLA Ops:
  0.6 21.2 %slice-start = ((s8[16777216]{0:T(1024)(128)(4,1)}), s8[4194304]{0:T(1024)(128)(4,1)S(1)}, s32[]{:S(2)}) async-start(s8[16777216]{0:T(1024)(128)(4,1)} %bitcast.72), calls=%async_computation | async-start | bytes 8388608
  1.6 9.6 %collective-permute-start = (bf16[4,8,256]{2,1,0:T(8,128)(2,1)S(1)}, bf16[4,8,256]{2,1,0:T(8,128)(2,1)S(1)}, u32[]{:S(2)}, u32[]{:S(2)}) collective-permute-start(bf16[4,8,256]{2,1,0:T(8,128)(2,1)S(1)} %round_rhs.1.after_ref), channel_id=1, source_target_pairs={{0,6},{1,7},{2,4},{3,5},{4,2},{5,3},{6,0},{7,1},{8,14},{9,15},{10,... | collective-permute-start | bytes 49160 | tf_op jit(solution)/shard_map/ppermute | solution.py:242
  6.7 4.6 %collective-permute-start.1 = (bf16[4,8,256]{2,1,0:T(8,128)(2,1)S(1)}, bf16[4,8,256]{2,1,0:T(8,128)(2,1)S(1)}, u32[]{:S(2)}, u32[]{:S(2)}) collective-permute-start(bf16[4,8,256]{2,1,0:T(8,128)(2,1)S(1)} %round_rhs.1.after_ref), channel_id=1, source_target_pairs={{0,4},{1,5},{2,6},{3,7},{4,0},{5,1},{6,2},{7,3},{8,12},{9,13},{10,... | collective-permute-start | bytes 49160 | tf_op jit(solution)/shard_map/ppermute | solution.py:242
  6.7 4.6 %collective-permute-start.2 = (bf16[4,8,256]{2,1,0:T(8,128)(2,1)S(1)}, bf16[4,8,256]{2,1,0:T(8,128)(2,1)S(1)}, u32[]{:S(2)}, u32[]{:S(2)}) collective-permute-start(bf16[4,8,256]{2,1,0:T(8,128)(2,1)S(1)} %round_rhs.1.after_ref), channel_id=1, source_target_pairs={{0,2},{1,3},{2,0},{3,1},{4,6},{5,7},{6,4},{7,5},{8,10},{9,11},{10,... | collective-permute-start | bytes 49160 | tf_op jit(solution)/shard_map/ppermute | solution.py:242
  11.4 1.3 %collective-permute-start.3 = (bf16[4,4,8,256]{3,2,1,0:T(8,128)(2,1)S(1)}, bf16[4,4,8,256]{3,2,1,0:T(8,128)(2,1)S(1)}, u32[]{:S(2)}, u32[]{:S(2)}) collective-permute-start(bf16[4,4,8,256]{3,2,1,0:T(8,128)(2,1)S(1)} %pad_maximum_fusion.x_ref), channel_id=1, source_target_pairs={{0,1},{1,0},{2,3},{3,2},{4,5},{5,4},{6,7},{7,6},{8,9},{9,8},{10,11... | collective-permute-start | bytes 196616 | tf_op jit(solution)/shard_map/ppermute | solution.py:237
  13.3 8.3 %collective-permute-start.4 = (bf16[4,8,256]{2,1,0:T(8,128)(2,1)S(1)}, bf16[4,8,256]{2,1,0:T(8,128)(2,1)S(1)}, u32[]{:S(2)}, u32[]{:S(2)}) collective-permute-start(bf16[4,8,256]{2,1,0:T(8,128)(2,1)S(1)} %get-tuple-element.42.after_ref), channel_id=1, source_target_pairs={{0,6},{1,7},{2,4},{3,5},{4,2},{5,3},{6,0},{7,1},{8,14},{9,15},{10,... | collective-permute-start | bytes 49160 | tf_op jit(solution)/shard_map/ppermute | solution.py:242
  16.7 5.0 %collective-permute-start.5 = (bf16[4,8,256]{2,1,0:T(8,128)(2,1)S(1)}, bf16[4,8,256]{2,1,0:T(8,128)(2,1)S(1)}, u32[]{:S(2)}, u32[]{:S(2)}) collective-permute-start(bf16[4,8,256]{2,1,0:T(8,128)(2,1)S(1)} %get-tuple-element.42.after_ref), channel_id=1, source_target_pairs={{0,4},{1,5},{2,6},{3,7},{4,0},{5,1},{6,2},{7,3},{8,12},{9,13},{10,... | collective-permute-start | bytes 49160 | tf_op jit(solution)/shard_map/ppermute | solution.py:242
  16.7 5.0 %collective-permute-start.6 = (bf16[4,8,256]{2,1,0:T(8,128)(2,1)S(1)}, bf16[4,8,256]{2,1,0:T(8,128)(2,1)S(1)}, u32[]{:S(2)}, u32[]{:S(2)}) collective-permute-start(bf16[4,8,256]{2,1,0:T(8,128)(2,1)S(1)} %get-tuple-element.42.after_ref), channel_id=1, source_target_pairs={{0,2},{1,3},{2,0},{3,1},{4,6},{5,7},{6,4},{7,5},{8,10},{9,11},{10,... | collective-permute-start | bytes 49160 | tf_op jit(solution)/shard_map/ppermute | solution.py:242
  21.7 2.4 %collective-permute-start.7 = (bf16[4,4,8,256]{3,2,1,0:T(8,128)(2,1)S(1)}, bf16[4,4,8,256]{3,2,1,0:T(8,128)(2,1)S(1)}, u32[]{:S(2)}, u32[]{:S(2)}) collective-permute-start(bf16[4,4,8,256]{3,2,1,0:T(8,128)(2,1)S(1)} %pad_maximum_fusion.1.x_ref), channel_id=1, source_target_pairs={{0,1},{1,0},{2,3},{3,2},{4,5},{5,4},{6,7},{7,6},{8,9},{9,8},{10,11... | collective-permute-start | bytes 196616 | tf_op jit(solution)/shard_map/ppermute | solution.py:237
  29.0 1.7 %collective-permute-start.8 = (bf16[4,8,512]{2,1,0:T(8,128)(2,1)S(1)}, bf16[4,8,512]{2,1,0:T(8,128)(2,1)S(1)}, u32[]{:S(2)}, u32[]{:S(2)}) collective-permute-start(bf16[4,8,512]{2,1,0:T(8,128)(2,1)S(1)} %get-tuple-element.48), channel_id=1, source_target_pairs={{0,1},{1,0},{2,3},{3,2},{4,5},{5,4},{6,7},{7,6},{8,9},{9,8},{10,11... | collective-permute-start | bytes 98312 | tf_op jit(solution)/shard_map/ppermute | solution.py:237
  30.7 5.1 %collective-permute-start.10 = (bf16[4,8,512]{2,1,0:T(8,128)(2,1)S(1)}, bf16[4,8,512]{2,1,0:T(8,128)(2,1)S(1)}, u32[]{:S(2)}, u32[]{:S(2)}) collective-permute-start(bf16[4,8,512]{2,1,0:T(8,128)(2,1)S(1)} %fusion.1), channel_id=1, source_target_pairs={{0,4},{1,5},{2,6},{3,7},{4,0},{5,1},{6,2},{7,3},{8,12},{9,13},{10,... | collective-permute-start | bytes 98312 | tf_op jit(solution)/shard_map/ppermute | solution.py:242
  31.5 4.3 %collective-permute-start.11 = (bf16[4,8,512]{2,1,0:T(8,128)(2,1)S(1)}, bf16[4,8,512]{2,1,0:T(8,128)(2,1)S(1)}, u32[]{:S(2)}, u32[]{:S(2)}) collective-permute-start(bf16[4,8,512]{2,1,0:T(8,128)(2,1)S(1)} %fusion.1), channel_id=1, source_target_pairs={{0,2},{1,3},{2,0},{3,1},{4,6},{5,7},{6,4},{7,5},{8,10},{9,11},{10,... | collective-permute-start | bytes 98312 | tf_op jit(solution)/shard_map/ppermute | solution.py:242
  33.2 5.7 %collective-permute-start.9 = (bf16[4,8,512]{2,1,0:T(8,128)(2,1)S(1)}, bf16[4,8,512]{2,1,0:T(8,128)(2,1)S(1)}, u32[]{:S(2)}, u32[]{:S(2)}) collective-permute-start(bf16[4,8,512]{2,1,0:T(8,128)(2,1)S(1)} %fusion.1), channel_id=1, source_target_pairs={{0,6},{1,7},{2,4},{3,5},{4,2},{5,3},{6,0},{7,1},{8,14},{9,15},{10,... | collective-permute-start | bytes 98312 | tf_op jit(solution)/shard_map/ppermute | solution.py:242
  39.0 1.3 %collective-permute-start.12 = (bf16[4,8,512]{2,1,0:T(8,128)(2,1)S(1)}, bf16[4,8,512]{2,1,0:T(8,128)(2,1)S(1)}, u32[]{:S(2)}, u32[]{:S(2)}) collective-permute-start(bf16[4,8,512]{2,1,0:T(8,128)(2,1)S(1)} %add_convert_fusion.1.x_ref), channel_id=1, source_target_pairs={{0,1},{1,0},{2,3},{3,2},{4,5},{5,4},{6,7},{7,6},{8,9},{9,8},{10,11... | collective-permute-start | bytes 98312 | tf_op jit(solution)/shard_map/ppermute | solution.py:237
  40.9 6.9 %collective-permute-start.13 = (bf16[8,512]{1,0:T(8,128)(2,1)S(1)}, bf16[8,512]{1,0:T(8,128)(2,1)S(1)}, u32[]{:S(2)}, u32[]{:S(2)}) collective-permute-start(bf16[8,512]{1,0:T(8,128)(2,1)S(1)} %get-tuple-element.49.after_ref), channel_id=1, source_target_pairs={{0,6},{1,7},{2,4},{3,5},{4,2},{5,3},{6,0},{7,1},{8,14},{9,15},{10,... | collective-permute-start | bytes 24584 | tf_op jit(solution)/shard_map/ppermute | solution.py:242
  42.8 5.0 %collective-permute-start.14 = (bf16[8,512]{1,0:T(8,128)(2,1)S(1)}, bf16[8,512]{1,0:T(8,128)(2,1)S(1)}, u32[]{:S(2)}, u32[]{:S(2)}) collective-permute-start(bf16[8,512]{1,0:T(8,128)(2,1)S(1)} %get-tuple-element.49.after_ref), channel_id=1, source_target_pairs={{0,4},{1,5},{2,6},{3,7},{4,0},{5,1},{6,2},{7,3},{8,12},{9,13},{10,... | collective-permute-start | bytes 24584 | tf_op jit(solution)/shard_map/ppermute | solution.py:242
  42.8 5.0 %collective-permute-start.15 = (bf16[8,512]{1,0:T(8,128)(2,1)S(1)}, bf16[8,512]{1,0:T(8,128)(2,1)S(1)}, u32[]{:S(2)}, u32[]{:S(2)}) collective-permute-start(bf16[8,512]{1,0:T(8,128)(2,1)S(1)} %get-tuple-element.49.after_ref), channel_id=1, source_target_pairs={{0,2},{1,3},{2,0},{3,1},{4,6},{5,7},{6,4},{7,5},{8,10},{9,11},{10,... | collective-permute-start | bytes 24584 | tf_op jit(solution)/shard_map/ppermute | solution.py:242
  47.9 1.3 %collective-permute-start.16 = (bf16[4,8,512]{2,1,0:T(8,128)(2,1)S(1)}, bf16[4,8,512]{2,1,0:T(8,128)(2,1)S(1)}, u32[]{:S(2)}, u32[]{:S(2)}) collective-permute-start(bf16[4,8,512]{2,1,0:T(8,128)(2,1)S(1)} %pad_maximum_fusion.2.x_ref), channel_id=1, source_target_pairs={{0,1},{1,0},{2,3},{3,2},{4,5},{5,4},{6,7},{7,6},{8,9},{9,8},{10,11... | collective-permute-start | bytes 98312 | tf_op jit(solution)/shard_map/ppermute | solution.py:237
  50.9 1.3 %collective-permute-start.17 = (bf16[4,8,512]{2,1,0:T(8,128)(2,1)S(1)}, bf16[4,8,512]{2,1,0:T(8,128)(2,1)S(1)}, u32[]{:S(2)}, u32[]{:S(2)}) collective-permute-start(bf16[4,8,512]{2,1,0:T(8,128)(2,1)S(1)} %get-tuple-element.57), channel_id=1, source_target_pairs={{0,1},{1,0},{2,3},{3,2},{4,5},{5,4},{6,7},{7,6},{8,9},{9,8},{10,11... | collective-permute-start | bytes 98312 | tf_op jit(solution)/shard_map/ppermute | solution.py:237
  52.2 4.9 %collective-permute-start.18 = (bf16[4,8,512]{2,1,0:T(8,128)(2,1)S(1)}, bf16[4,8,512]{2,1,0:T(8,128)(2,1)S(1)}, u32[]{:S(2)}, u32[]{:S(2)}) collective-permute-start(bf16[4,8,512]{2,1,0:T(8,128)(2,1)S(1)} %fusion.2), channel_id=1, source_target_pairs={{0,8},{8,16},{16,24},{24,0},{1,9},{9,17},{17,25},{25,1},{2,10},{10... | collective-permute-start | bytes 98312 | tf_op jit(solution)/shard_map/ppermute | solution.py:259
  53.6 3.9 %collective-permute-start.19 = (bf16[4,8,512]{2,1,0:T(8,128)(2,1)S(1)}, bf16[4,8,512]{2,1,0:T(8,128)(2,1)S(1)}, u32[]{:S(2)}, u32[]{:S(2)}) collective-permute-start(bf16[4,8,512]{2,1,0:T(8,128)(2,1)S(1)} %fusion.2), channel_id=1, source_target_pairs={{0,16},{8,24},{16,0},{24,8},{1,17},{9,25},{17,1},{25,9},{2,18},{10... | collective-permute-start | bytes 98312 | tf_op jit(solution)/shard_map/ppermute | solution.py:259
  54.9 3.9 %collective-permute-start.20 = (bf16[4,8,512]{2,1,0:T(8,128)(2,1)S(1)}, bf16[4,8,512]{2,1,0:T(8,128)(2,1)S(1)}, u32[]{:S(2)}, u32[]{:S(2)}) collective-permute-start(bf16[4,8,512]{2,1,0:T(8,128)(2,1)S(1)} %fusion.2), channel_id=1, source_target_pairs={{0,24},{8,0},{16,8},{24,16},{1,25},{9,1},{17,9},{25,17},{2,26},{10... | collective-permute-start | bytes 98312 | tf_op jit(solution)/shard_map/ppermute | solution.py:259
  58.8 5.8 %collective-permute-start.21 = (bf16[4,8,512]{2,1,0:T(8,128)(2,1)S(1)}, bf16[4,8,512]{2,1,0:T(8,128)(2,1)S(1)}, u32[]{:S(2)}, u32[]{:S(2)}) collective-permute-start(bf16[4,8,512]{2,1,0:T(8,128)(2,1)S(1)} %fusion.28), channel_id=1, source_target_pairs={{0,6},{1,7},{2,4},{3,5},{4,2},{5,3},{6,0},{7,1},{8,14},{9,15},{10,... | collective-permute-start | bytes 98312 | tf_op jit(solution)/shard_map/ppermute | solution.py:242
  60.1 5.3 %collective-permute-start.22 = (bf16[4,8,512]{2,1,0:T(8,128)(2,1)S(1)}, bf16[4,8,512]{2,1,0:T(8,128)(2,1)S(1)}, u32[]{:S(2)}, u32[]{:S(2)}) collective-permute-start(bf16[4,8,512]{2,1,0:T(8,128)(2,1)S(1)} %fusion.28), channel_id=1, source_target_pairs={{0,4},{1,5},{2,6},{3,7},{4,0},{5,1},{6,2},{7,3},{8,12},{9,13},{10,... | collective-permute-start | bytes 98312 | tf_op jit(solution)/shard_map/ppermute | solution.py:242
  61.5 4.2 %collective-permute-start.23 = (bf16[4,8,512]{2,1,0:T(8,128)(2,1)S(1)}, bf16[4,8,512]{2,1,0:T(8,128)(2,1)S(1)}, u32[]{:S(2)}, u32[]{:S(2)}) collective-permute-start(bf16[4,8,512]{2,1,0:T(8,128)(2,1)S(1)} %fusion.28), channel_id=1, source_target_pairs={{0,2},{1,3},{2,0},{3,1},{4,6},{5,7},{6,4},{7,5},{8,10},{9,11},{10,... | collective-permute-start | bytes 98312 | tf_op jit(solution)/shard_map/ppermute | solution.py:242
  65.7 1.3 %collective-permute-start.24 = (bf16[4,8,512]{2,1,0:T(8,128)(2,1)S(1)}, bf16[4,8,512]{2,1,0:T(8,128)(2,1)S(1)}, u32[]{:S(2)}, u32[]{:S(2)}) collective-permute-start(bf16[4,8,512]{2,1,0:T(8,128)(2,1)S(1)} %add_convert_fusion.x_ref), channel_id=1, source_target_pairs={{0,1},{1,0},{2,3},{3,2},{4,5},{5,4},{6,7},{7,6},{8,9},{9,8},{10,11... | collective-permute-start | bytes 98312 | tf_op jit(solution)/shard_map/ppermute | solution.py:237
  68.0 1.2 %collective-permute-start.25 = (bf16[4,1,8,512]{3,2,0,1:T(8,128)(2,1)S(1)}, bf16[4,1,8,512]{3,2,0,1:T(8,128)(2,1)S(1)}, u32[]{:S(2)}, u32[]{:S(2)}) collective-permute-start(bf16[4,1,8,512]{3,2,0,1:T(8,128)(2,1)S(1)} %bitcast.83), channel_id=1, source_target_pairs={{0,1},{1,0},{2,3},{3,2},{4,5},{5,4},{6,7},{7,6},{8,9},{9,8},{10,11... | collective-permute-start | bytes 98312 | tf_op jit(solution)/shard_map/ppermute | solution.py:237
  69.2 5.9 %collective-permute-start.26 = (bf16[4,8,512]{2,1,0:T(8,128)(2,1)S(1)}, bf16[4,8,512]{2,1,0:T(8,128)(2,1)S(1)}, u32[]{:S(2)}, u32[]{:S(2)}) collective-permute-start(bf16[4,8,512]{2,1,0:T(8,128)(2,1)S(1)} %bitcast_convert_fusion.1), channel_id=1, source_target_pairs={{0,6},{1,7},{2,4},{3,5},{4,2},{5,3},{6,0},{7,1},{8,14},{9,15},{10,... | collective-permute-start | bytes 98312 | tf_op jit(solution)/shard_map/ppermute | solution.py:242
  71.1 5.2 %collective-permute-start.27 = (bf16[4,8,512]{2,1,0:T(8,128)(2,1)S(1)}, bf16[4,8,512]{2,1,0:T(8,128)(2,1)S(1)}, u32[]{:S(2)}, u32[]{:S(2)}) collective-permute-start(bf16[4,8,512]{2,1,0:T(8,128)(2,1)S(1)} %bitcast_convert_fusion.1), channel_id=1, source_target_pairs={{0,4},{1,5},{2,6},{3,7},{4,0},{5,1},{6,2},{7,3},{8,12},{9,13},{10,... | collective-permute-start | bytes 98312 | tf_op jit(solution)/shard_map/ppermute | solution.py:242
  72.3 4.3 %collective-permute-start.28 = (bf16[4,8,512]{2,1,0:T(8,128)(2,1)S(1)}, bf16[4,8,512]{2,1,0:T(8,128)(2,1)S(1)}, u32[]{:S(2)}, u32[]{:S(2)}) collective-permute-start(bf16[4,8,512]{2,1,0:T(8,128)(2,1)S(1)} %bitcast_convert_fusion.1), channel_id=1, source_target_pairs={{0,2},{1,3},{2,0},{3,1},{4,6},{5,7},{6,4},{7,5},{8,10},{9,11},{10,... | collective-permute-start | bytes 98312 | tf_op jit(solution)/shard_map/ppermute | solution.py:242
  76.6 1.3 %collective-permute-start.29 = (bf16[4,8,512]{2,1,0:T(8,128)(2,1)S(1)}, bf16[4,8,512]{2,1,0:T(8,128)(2,1)S(1)}, u32[]{:S(2)}, u32[]{:S(2)}) collective-permute-start(bf16[4,8,512]{2,1,0:T(8,128)(2,1)S(1)} %fusion.own_ref), channel_id=1, source_target_pairs={{0,1},{1,0},{2,3},{3,2},{4,5},{5,4},{6,7},{7,6},{8,9},{9,8},{10,11... | collective-permute-start | bytes 98312 | tf_op jit(solution)/shard_map/ppermute | solution.py:237
  79.6 1.2 %collective-permute-start.30 = (bf16[4,1,8,512]{3,2,1,0:T(8,128)(2,1)S(1)}, bf16[4,1,8,512]{3,2,1,0:T(8,128)(2,1)S(1)}, u32[]{:S(2)}, u32[]{:S(2)}) collective-permute-start(bf16[4,1,8,512]{3,2,1,0:T(8,128)(2,1)S(1)} %get-tuple-element.62), channel_id=1, source_target_pairs={{0,1},{1,0},{2,3},{3,2},{4,5},{5,4},{6,7},{7,6},{8,9},{9,8},{10,11... | collective-permute-start | bytes 98312 | tf_op jit(solution)/shard_map/ppermute | solution.py:237
  80.8 5.5 %collective-permute-start.31 = (bf16[1,8,512]{2,1,0:T(8,128)(2,1)S(1)}, bf16[1,8,512]{2,1,0:T(8,128)(2,1)S(1)}, u32[]{:S(2)}, u32[]{:S(2)}) collective-permute-start(bf16[1,8,512]{2,1,0:T(8,128)(2,1)S(1)} %get-tuple-element.89), channel_id=1, source_target_pairs={{0,6},{1,7},{2,4},{3,5},{4,2},{5,3},{6,0},{7,1},{8,14},{9,15},{10,... | collective-permute-start | bytes 24584 | tf_op jit(solution)/shard_map/ppermute | solution.py:242
  82.0 4.5 %collective-permute-start.32 = (bf16[1,8,512]{2,1,0:T(8,128)(2,1)S(1)}, bf16[1,8,512]{2,1,0:T(8,128)(2,1)S(1)}, u32[]{:S(2)}, u32[]{:S(2)}) collective-permute-start(bf16[1,8,512]{2,1,0:T(8,128)(2,1)S(1)} %get-tuple-element.88), channel_id=1, source_target_pairs={{0,4},{1,5},{2,6},{3,7},{4,0},{5,1},{6,2},{7,3},{8,12},{9,13},{10,... | collective-permute-start | bytes 24584 | tf_op jit(solution)/shard_map/ppermute | solution.py:242
  82.8 4.1 %collective-permute-start.33 = (bf16[1,8,512]{2,1,0:T(8,128)(2,1)S(1)}, bf16[1,8,512]{2,1,0:T(8,128)(2,1)S(1)}, u32[]{:S(2)}, u32[]{:S(2)}) collective-permute-start(bf16[1,8,512]{2,1,0:T(8,128)(2,1)S(1)} %get-tuple-element.87), channel_id=1, source_target_pairs={{0,2},{1,3},{2,0},{3,1},{4,6},{5,7},{6,4},{7,5},{8,10},{9,11},{10,... | collective-permute-start | bytes 24584 | tf_op jit(solution)/shard_map/ppermute | solution.py:242
  87.3 1.2 %collective-permute-start.34 = (bf16[4,1,8,512]{3,2,0,1:T(8,128)(2,1)S(1)}, bf16[4,1,8,512]{3,2,0,1:T(8,128)(2,1)S(1)}, u32[]{:S(2)}, u32[]{:S(2)}) collective-permute-start(bf16[4,1,8,512]{3,2,0,1:T(8,128)(2,1)S(1)} %bitcast.82), channel_id=1, source_target_pairs={{0,1},{1,0},{2,3},{3,2},{4,5},{5,4},{6,7},{7,6},{8,9},{9,8},{10,11... | collective-permute-start | bytes 98312 | tf_op jit(solution)/shard_map/ppermute | solution.py:237
  88.5 6.1 %collective-permute-start.35 = (bf16[4,8,512]{2,1,0:T(8,128)(2,1)S(1)}, bf16[4,8,512]{2,1,0:T(8,128)(2,1)S(1)}, u32[]{:S(2)}, u32[]{:S(2)}) collective-permute-start(bf16[4,8,512]{2,1,0:T(8,128)(2,1)S(1)} %bitcast_convert_fusion), channel_id=1, source_target_pairs={{0,6},{1,7},{2,4},{3,5},{4,2},{5,3},{6,0},{7,1},{8,14},{9,15},{10,... | collective-permute-start | bytes 98312 | tf_op jit(solution)/shard_map/ppermute | solution.py:242
  90.9 4.8 %collective-permute-start.36 = (bf16[4,8,512]{2,1,0:T(8,128)(2,1)S(1)}, bf16[4,8,512]{2,1,0:T(8,128)(2,1)S(1)}, u32[]{:S(2)}, u32[]{:S(2)}) collective-permute-start(bf16[4,8,512]{2,1,0:T(8,128)(2,1)S(1)} %bitcast_convert_fusion), channel_id=1, source_target_pairs={{0,4},{1,5},{2,6},{3,7},{4,0},{5,1},{6,2},{7,3},{8,12},{9,13},{10,... | collective-permute-start | bytes 98312 | tf_op jit(solution)/shard_map/ppermute | solution.py:242
  92.1 4.0 %collective-permute-start.37 = (bf16[4,8,512]{2,1,0:T(8,128)(2,1)S(1)}, bf16[4,8,512]{2,1,0:T(8,128)(2,1)S(1)}, u32[]{:S(2)}, u32[]{:S(2)}) collective-permute-start(bf16[4,8,512]{2,1,0:T(8,128)(2,1)S(1)} %bitcast_convert_fusion), channel_id=1, source_target_pairs={{0,2},{1,3},{2,0},{3,1},{4,6},{5,7},{6,4},{7,5},{8,10},{9,11},{10,... | collective-permute-start | bytes 98312 | tf_op jit(solution)/shard_map/ppermute | solution.py:242
  96.1 1.3 %collective-permute-start.38 = (bf16[4,8,512]{2,1,0:T(8,128)(2,1)S(1)}, bf16[4,8,512]{2,1,0:T(8,128)(2,1)S(1)}, u32[]{:S(2)}, u32[]{:S(2)}) collective-permute-start(bf16[4,8,512]{2,1,0:T(8,128)(2,1)S(1)} %get-tuple-element.78.refs_2_), channel_id=1, source_target_pairs={{0,1},{1,0},{2,3},{3,2},{4,5},{5,4},{6,7},{7,6},{8,9},{9,8},{10,11... | collective-permute-start | bytes 98312 | tf_op jit(solution)/shard_map/ppermute | solution.py:237
  100.8 1.6 %collective-permute-start.39 = (bf16[4,4,8,256]{3,2,1,0:T(8,128)(2,1)S(1)}, bf16[4,4,8,256]{3,2,1,0:T(8,128)(2,1)S(1)}, u32[]{:S(2)}, u32[]{:S(2)}) collective-permute-start(bf16[4,4,8,256]{3,2,1,0:T(8,128)(2,1)S(1)} %get-tuple-element.69), channel_id=1, source_target_pairs={{0,1},{1,0},{2,3},{3,2},{4,5},{5,4},{6,7},{7,6},{8,9},{9,8},{10,11... | collective-permute-start | bytes 196616 | tf_op jit(solution)/shard_map/ppermute | solution.py:237
  102.5 5.8 %collective-permute-start.40 = (bf16[4,8,256]{2,1,0:T(8,128)(2,1)S(1)}, bf16[4,8,256]{2,1,0:T(8,128)(2,1)S(1)}, u32[]{:S(2)}, u32[]{:S(2)}) collective-permute-start(bf16[4,8,256]{2,1,0:T(8,128)(2,1)S(1)} %get-tuple-element.85), channel_id=1, source_target_pairs={{0,6},{1,7},{2,4},{3,5},{4,2},{5,3},{6,0},{7,1},{8,14},{9,15},{10,... | collective-permute-start | bytes 49160 | tf_op jit(solution)/shard_map/ppermute | solution.py:242
  103.0 5.2 %collective-permute-start.41 = (bf16[4,8,256]{2,1,0:T(8,128)(2,1)S(1)}, bf16[4,8,256]{2,1,0:T(8,128)(2,1)S(1)}, u32[]{:S(2)}, u32[]{:S(2)}) collective-permute-start(bf16[4,8,256]{2,1,0:T(8,128)(2,1)S(1)} %get-tuple-element.84), channel_id=1, source_target_pairs={{0,4},{1,5},{2,6},{3,7},{4,0},{5,1},{6,2},{7,3},{8,12},{9,13},{10,... | collective-permute-start | bytes 49160 | tf_op jit(solution)/shard_map/ppermute | solution.py:242
  103.9 4.8 %collective-permute-start.42 = (bf16[4,8,256]{2,1,0:T(8,128)(2,1)S(1)}, bf16[4,8,256]{2,1,0:T(8,128)(2,1)S(1)}, u32[]{:S(2)}, u32[]{:S(2)}) collective-permute-start(bf16[4,8,256]{2,1,0:T(8,128)(2,1)S(1)} %get-tuple-element.83), channel_id=1, source_target_pairs={{0,2},{1,3},{2,0},{3,1},{4,6},{5,7},{6,4},{7,5},{8,10},{9,11},{10,... | collective-permute-start | bytes 49160 | tf_op jit(solution)/shard_map/ppermute | solution.py:242
  109.0 1.3 %collective-permute-start.43 = (bf16[4,4,8,256]{3,2,1,0:T(8,128)(2,1)S(1)}, bf16[4,4,8,256]{3,2,1,0:T(8,128)(2,1)S(1)}, u32[]{:S(2)}, u32[]{:S(2)}) collective-permute-start(bf16[4,4,8,256]{3,2,1,0:T(8,128)(2,1)S(1)} %get-tuple-element.72), channel_id=1, source_target_pairs={{0,1},{1,0},{2,3},{3,2},{4,5},{5,4},{6,7},{7,6},{8,9},{9,8},{10,11... | collective-permute-start | bytes 196616 | tf_op jit(solution)/shard_map/ppermute | solution.py:237
  110.3 5.6 %collective-permute-start.44 = (bf16[4,8,256]{2,1,0:T(8,128)(2,1)S(1)}, bf16[4,8,256]{2,1,0:T(8,128)(2,1)S(1)}, u32[]{:S(2)}, u32[]{:S(2)}) collective-permute-start(bf16[4,8,256]{2,1,0:T(8,128)(2,1)S(1)} %get-tuple-element.80), channel_id=1, source_target_pairs={{0,6},{1,7},{2,4},{3,5},{4,2},{5,3},{6,0},{7,1},{8,14},{9,15},{10,... | collective-permute-start | bytes 49160 | tf_op jit(solution)/shard_map/ppermute | solution.py:242
  112.8 4.6 %collective-permute-start.45 = (bf16[4,8,256]{2,1,0:T(8,128)(2,1)S(1)}, bf16[4,8,256]{2,1,0:T(8,128)(2,1)S(1)}, u32[]{:S(2)}, u32[]{:S(2)}) collective-permute-start(bf16[4,8,256]{2,1,0:T(8,128)(2,1)S(1)} %get-tuple-element.82), channel_id=1, source_target_pairs={{0,4},{1,5},{2,6},{3,7},{4,0},{5,1},{6,2},{7,3},{8,12},{9,13},{10,... | collective-permute-start | bytes 49160 | tf_op jit(solution)/shard_map/ppermute | solution.py:242
  113.9 3.7 %collective-permute-start.46 = (bf16[4,8,256]{2,1,0:T(8,128)(2,1)S(1)}, bf16[4,8,256]{2,1,0:T(8,128)(2,1)S(1)}, u32[]{:S(2)}, u32[]{:S(2)}) collective-permute-start(bf16[4,8,256]{2,1,0:T(8,128)(2,1)S(1)} %get-tuple-element.81), channel_id=1, source_target_pairs={{0,2},{1,3},{2,0},{3,1},{4,6},{5,7},{6,4},{7,5},{8,10},{9,11},{10,... | collective-permute-start | bytes 49160 | tf_op jit(solution)/shard_map/ppermute | solution.py:242
  (13 other events, 144.0 us)

commit v8 on v7

--- a/solution.py
+++ b/solution.py
@@ -9,7 +9,8 @@
 BF16 = jnp.bfloat16
 I32 = jnp.int32
 LANES = 128
-UNROLL = 4
+BLOCKS = 8
+NONE = 1 << 24
 
 VMEM = pl.BlockSpec(memory_space=pltpu.VMEM)
 SMEM = pl.BlockSpec(memory_space=pltpu.SMEM)
@@ -46,127 +47,118 @@
     return lax.dot_general(x, w, (((1,), (0,)), ((), ())), preferred_element_type=F32)
 
 
-def walk(plan_ref, sets, tiles, blocks, tile, visit, carry):
-    def trip(i, carry):
-        at = []
+def prepare(after, lists):
+    count = len(lists)
+
+    def one(first, rows_ref, height_ref, list_ref, plan_ref, scalar_ref):
+        sets, length = rows_ref.shape
+        tiles = length // LANES
+        start = lax.axis_index("rows") * first
+        lane = lax.broadcasted_iota(I32, (1, LANES), 1)
+        rounds = 0
         for s in range(sets):
-            lo = plan_ref[s * tiles + tile] + i * UNROLL
-            at += [(s, jnp.minimum(lo + u, blocks)) for u in range(UNROLL)]
-        return visit(at, carry)
-
-    return lax.fori_loop(0, plan_ref[sets * tiles + tile], trip, carry)
+            used = height_ref[s] - start
+            for tile in range(tiles):
+                lanes = slice(tile * LANES, (tile + 1) * LANES)
+                line = rows_ref[s : s + 1, lanes]
+                list_ref[s : s + 1, lanes] = jnp.where(lane + tile * LANES < used, line, NONE)
+                end = jnp.maximum(jnp.minimum(used, (tile + 1) * LANES) - 1, 0)
+                lo = lax.shift_right_logical(scalar_ref[s, tile * LANES], 7)
+                hi = lax.shift_right_logical(scalar_ref[s, end], 7)
+                met = used > tile * LANES
+                plan_ref[s * tiles + tile] = jnp.where(met, lo, 0)
+                span = jnp.where(met, hi - lo + BLOCKS, 0)
+                rounds = jnp.maximum(rounds, lax.shift_right_logical(span, 3))
+        plan_ref[sets * tiles] = rounds
+
+    def body(*refs):
+        ins, outs = refs[1 : 2 * count + 1], refs[2 * count + 1 : 4 * count + 1]
+        scalars, sems = refs[4 * count + 1 : -1], refs[-1]
+        copies = [
+            pltpu.make_async_copy(ins[2 * i], scalars[i], sems.at[i]) for i in range(count)
+        ]
+        for copy in copies:
+            copy.start()
+        for i, copy in enumerate(copies):
+            copy.wait()
+            one(lists[i][1], *ins[2 * i : 2 * i + 2], *outs[2 * i : 2 * i + 2], scalars[i])
+
+    shapes, ins = [], [after]
+    for rows, _, height in lists:
+        sets, length = rows.shape
+        shapes += [(rows.shape, I32), ((sets * (length // LANES) + 1,), I32)]
+        ins += [rows, height]
+    return call(
+        body,
+        shapes,
+        ins,
+        [pl.BlockSpec(memory_space=pl.ANY)] + [VMEM, SMEM] * count,
+        out_specs=[VMEM, SMEM] * count,
+        scratch=[pltpu.SMEM(x[0].shape, I32) for x in lists] + [pltpu.SemaphoreType.DMA((count,))],
+        moved=4 << 20,
+        limit=4 << 20,
+        name="prepare",
+    )
+
+
+def walk(plan_ref, list_ref, blocks, visit):
+    sets, length = list_ref.shape
+    tiles = length // LANES
+
+    def take_round(i, first):
+        for tile in range(tiles):
+            lanes = slice(tile * LANES, (tile + 1) * LANES)
+            for s in range(sets):
+                line = jnp.broadcast_to(list_ref[s : s + 1, lanes], (BLOCKS, LANES))
+                lo = jnp.minimum(plan_ref[s * tiles + tile] + i * BLOCKS, blocks)
+                visit(s, lanes, line, lo, first)
+
+    take_round(0, True)
+
+    def again(i, carry):
+        take_round(i, False)
+        return carry
+
+    lax.fori_loop(1, plan_ref[sets * tiles], again, 0)
+
+
+def along(x, index):
+    return jnp.take_along_axis(x, index, axis=1, mode="promise_in_bounds")
 
 
 def pick(x, index):
     inside = (index >= 0) & (index < LANES)
-    found = jnp.take_along_axis(
-        x, index & (LANES - 1), axis=1, mode="promise_in_bounds"
-    )
-    return jnp.where(inside, found, 0.0)
-
-
-def prepare(after, rows, first, height, width, sets):
-    of = range(*sets)
-    sets, length = rows.shape
-    tiles, blocks = length // LANES, width // LANES
-
-    def body(after_ref, rows_ref, height_ref, list_ref, plan_ref, out_ref, scalar_ref, sem):
-        copy = pltpu.make_async_copy(rows_ref, scalar_ref, sem)
-        copy.start()
-        out_ref[...] = jnp.full(out_ref.shape, -1, I32)
-        start = lax.axis_index("rows") * first
-        used = [height_ref[s] - start for s in range(sets)]
-        copy.wait()
-        lane = lax.broadcasted_iota(I32, (1, LANES), 1)
-        for tile in range(tiles):
-            lanes = slice(tile * LANES, (tile + 1) * LANES)
-            spots = lax.broadcasted_iota(I32, (LANES, LANES), 0) + (tile * LANES + 1)
-            cols, trips = [], 0
-            for s in range(sets):
-                line = jnp.where(lane + tile * LANES < used[s], rows_ref[s : s + 1, lanes], -1)
-                list_ref[s : s + 1, lanes] = line
-                if s in of:
-                    cols.append(jnp.transpose(jnp.broadcast_to(line, (LANES, LANES))))
-                end = jnp.maximum(jnp.minimum(used[s], (tile + 1) * LANES) - 1, 0)
-                lo = lax.shift_right_logical(scalar_ref[s, tile * LANES], 7)
-                hi = lax.shift_right_logical(scalar_ref[s, end], 7)
-                met = used[s] > tile * LANES
-                plan_ref[s * tiles + tile] = jnp.where(met, lo, blocks)
-                span = jnp.where(met, hi - lo + UNROLL, 0)
-                trips = jnp.maximum(trips, lax.div(span, UNROLL))
-            plan_ref[sets * tiles + tile] = trips
-
-            def visit(at, carry):
-                across = lax.broadcasted_iota(I32, (LANES, LANES), 1)
-                got = []
-                at = [(s - of.start, block) for s, block in at if s in of]
-                for s, block in at:
-                    hit = cols[s] == across + block * LANES
-                    got.append(jnp.sum(jnp.where(hit, spots, 0), axis=0, keepdims=True))
-                for (s, block), g in zip(at, got):
-                    out_ref[s, block] += jnp.broadcast_to(g, out_ref.shape[2:])
-                return carry
-
-            walk(plan_ref, sets, tiles, blocks, tile, visit, 0)
-
-    return call(
-        body,
-        [
-            (rows.shape, I32),
-            (((sets + 1) * tiles,), I32),
-            ((len(of), blocks + 1, 8, LANES), I32),
-        ],
-        [after, rows, height],
-        [pl.BlockSpec(memory_space=pl.ANY), VMEM, SMEM],
-        out_specs=[VMEM, SMEM, VMEM],
-        scratch=[
-            pltpu.SMEM(rows.shape, I32),
-            pltpu.SemaphoreType.DMA(()),
-        ],
-        moved=8 << 20,
-        limit=4 << 20,
-        name="prepare",
-    )
-
-
-def scatter_walk(plan_ref, inverse_refs, update_ref, acc_ref, tiles):
-    sets, blocks = update_ref.shape[0], inverse_refs[0].shape[1] - 1
-    inverse = [ref.at[s] for ref in inverse_refs for s in range(ref.shape[0])]
-    for tile in range(tiles):
-
-        def visit(at, carry):
-            got = []
-            for s, block in at:
-                x = update_ref[s, :, tile * LANES : (tile + 1) * LANES]
-                got.append(pick(x, inverse[s][block] - tile * LANES))
-            for (s, block), g in zip(at, got):
-                acc_ref[block] += g
-            return carry
-
-        walk(plan_ref, sets, tiles, blocks, tile, visit, 0)
-
-
-def gather_walk(plan_ref, rows_ref, source_ref, out_ref):
-    sets, length = rows_ref.shape
-    tiles, blocks = length // LANES, source_ref.shape[0] - 1
-    for tile in range(tiles):
-        index = [
-            jnp.broadcast_to(
-                rows_ref[s : s + 1, tile * LANES : (tile + 1) * LANES], (8, LANES)
-            )
-            for s in range(sets)
-        ]
-
-        def visit(at, carry):
-            carry = list(carry)
-            for s, block in at:
-                carry[s] = carry[s] + pick(source_ref[block], index[s] - block * LANES)
-            return tuple(carry)
-
-        zero = tuple(jnp.zeros((8, LANES), F32) for _ in range(sets))
-        found = walk(plan_ref, sets, tiles, blocks, tile, visit, zero)
-        for s in range(sets):
-            out_ref[s, :, tile * LANES : (tile + 1) * LANES] = found[s].astype(out_ref.dtype)
+    return jnp.where(inside, along(x, index & (LANES - 1)), 0.0)
+
+
+def position(line, lo):
+    block = lax.broadcasted_iota(I32, line.shape, 0) + lo
+    target = block * LANES + lax.broadcasted_iota(I32, line.shape, 1)
+    below = jnp.zeros(line.shape, I32)
+    step = LANES // 2
+    while step:
+        below = jnp.where(along(line, below + (step - 1)) < target, below + step, below)
+        step //= 2
+    return jnp.where(along(line, below) == target, below, -1)
+
+
+def scatter_walk(plan_ref, list_ref, update_ref, acc_ref):
+    def visit(s, lanes, line, lo, first):
+        x, at = update_ref[s, :, lanes], position(line, lo)
+        parts = [pick(x, jnp.broadcast_to(at[u : u + 1], x.shape)) for u in range(BLOCKS)]
+        acc_ref[pl.ds(lo, BLOCKS)] += jnp.stack(parts)
+
+    walk(plan_ref, list_ref, acc_ref.shape[0] - BLOCKS, visit)
+
+
+def gather_walk(plan_ref, list_ref, source_ref, out_ref):
+    def visit(s, lanes, line, lo, first):
+        x = source_ref[pl.ds(lo, BLOCKS)]
+        parts = [pick(x[u], line - (lo + u) * LANES) for u in range(BLOCKS)]
+        found = sum(parts[1:], parts[0]).astype(out_ref.dtype)
+        out_ref[s, :, lanes] = found if first else out_ref[s, :, lanes] + found
+
+    walk(plan_ref, list_ref, source_ref.shape[0] - BLOCKS, visit)
 
 
 def core():
@@ -184,7 +176,7 @@
 def unite(own_ref, other_ref, out_ref, *at, xor=False):
     odd, w = core(), own_ref.shape[-1]
     for k in range(own_ref.shape[0]):
-        c = chip() ^ (-k % own_ref.shape[0]) if xor else k
+        c = chip() ^ k if xor else k
         out_ref[:, spot(2 * c + odd, w)] = own_ref[(k,) + at]
         out_ref[:, spot(2 * c + 1 - odd, w)] = other_ref[(k,) + at]
 
@@ -202,7 +194,7 @@
     chips, cols = x_ref.shape[0], x_ref.shape[-1]
     terms = []
     for k in range(chips):
-        c = chip() ^ (-k % chips) if xor else k
+        c = chip() ^ k if xor else k
         terms.append(times_transposed(x_ref[(k,) + at], w_ref[s, :, spot(2 * c + odd, cols)]))
     return sum(terms[1:], terms[0])
 
@@ -243,8 +235,7 @@
 
 
 def from_chips(piece):
-    chips = lax.axis_size("rows") // 2
-    return [far(piece(k), k) for k in range(chips - 1, 0, -1)]
+    return [far(piece(k), k) for k in range(1, lax.axis_size("rows") // 2)]
 
 
 def chips_sum(x):
@@ -326,14 +317,13 @@
         [VMEM] + [pl.BlockSpec(memory_space=pltpu.HBM)] * len(weights),
         name="round_rhs",
     )[0]
-    half = leaves // 2
-
-    def prepare_leaves(after, *sets):
-        return prepare(after, leaf_rows, leaf_local, leaf_height, tall, sets)
-
-    leaf_list, leaf_plan, inverse_low = prepare_leaves(lb, 0, half)
+    prepared = prepare(
+        lb,
+        [(leaf_rows, leaf_local, leaf_height), (parent_rows, parent_local, parent_height)],
+    )
     lb = far_gather(lb) if leaf_aligned else leaf_columns(lb)
-    lb, inverse_low, rhs = lax.optimization_barrier((lb, inverse_low, rhs))
+    lb, prepared, rhs = lax.optimization_barrier((lb, prepared, rhs))
+    leaf_list, leaf_plan, parent_list, parent_plan = prepared
     lb = leaf_halves(lb, leaf_inv, "leaf_solve_own") if leaf_aligned else (lb,)
 
     def leaf_solve(*refs):
@@ -350,22 +340,19 @@
         [VMEM] * (len(lb) + 1),
         name="leaf_solve",
     )
-    inverse_high = prepare_leaves(lyb, half, leaves)[2]
     if leaf_aligned:
-        lyb, inverse_high = lax.optimization_barrier((far_gather(lyb), inverse_high))
-        lyb = leaf_halves(lyb, leaf_panel, "leaf_update_own")
+        lyb = leaf_halves(far_gather(lyb), leaf_panel, "leaf_update_own")
     else:
         lyb = (leaf_columns(lyb),)
-    leaf_inverse = (inverse_low, inverse_high)
 
     def leaf_update(*refs):
         x_refs, refs = refs[: len(lyb)], refs[len(lyb) :]
-        plan_ref, w_ref, *inverse_refs, rhs_ref, own_ref, other_ref, root_ref = refs[:-3]
-        update_ref, acc_ref, sum_ref = refs[-3:]
+        plan_ref, w_ref, list_ref, rhs_ref, own_ref, other_ref, root_ref, *refs = refs
+        update_ref, acc_ref, sum_ref = refs
         acc_ref[...] = jnp.zeros(acc_ref.shape, F32)
         for s in range(leaves):
             update_ref[s] = leaf_product(x_refs, w_ref, s)
-        scatter_walk(plan_ref, inverse_refs, update_ref, acc_ref, leaf_local // LANES)
+        scatter_walk(plan_ref, list_ref, update_ref, acc_ref)
         for b in range(parent_width // LANES):
             sum_ref[:, b * LANES : (b + 1) * LANES] = -acc_ref[b]
         sum_ref[:, spot(lax.axis_index("rows"), parent_cols)] += rhs_ref[:, 0, :]
@@ -380,11 +367,11 @@
             ((chips, rcount, parent_cols), BF16),
             ((root_width // LANES, rcount, LANES), F32),
         ],
-        [*lyb, leaf_plan, pinned(leaf_panel), *leaf_inverse, parent_rhs],
-        [VMEM] * len(lyb) + [SMEM] + [VMEM] * 4,
+        [*lyb, leaf_plan, pinned(leaf_panel), leaf_list, parent_rhs],
+        [VMEM] * len(lyb) + [SMEM] + [VMEM] * 3,
         scratch=[
             pltpu.VMEM((leaves, rcount, leaf_local), F32),
-            pltpu.VMEM((tall // LANES + 1, rcount, LANES), F32),
+            pltpu.VMEM((tall // LANES + BLOCKS, rcount, LANES), F32),
             pltpu.VMEM((rcount, parent_width), F32),
         ],
         name="leaf_update",
@@ -403,19 +390,16 @@
         [VMEM] * 3,
         name="parent_solve",
     )
-    parent_list, parent_plan, parent_inverse = prepare(
-        pyb, parent_rows, parent_local, parent_height, root_width, (0, 1)
-    )
-    pyb, parent_inverse = lax.optimization_barrier((far_gather(pyb), parent_inverse))
+    pyb = far_gather(pyb)
 
     def parent_update(
-        plan_ref, part_ref, x_ref, w_ref, inverse_ref, root_ref, rhs_ref, own_ref, other_ref,
+        plan_ref, part_ref, x_ref, w_ref, list_ref, root_ref, rhs_ref, own_ref, other_ref,
         update_ref, acc_ref, sum_ref,
     ):
         for b in range(root_width // LANES):
             acc_ref[b] = root_ref[b]
         update_ref[0] = both_halves(part_ref, x_ref, w_ref, 0, xor=True)
-        scatter_walk(plan_ref, [inverse_ref], update_ref, acc_ref, parent_local // LANES)
+        scatter_walk(plan_ref, list_ref, update_ref, acc_ref)
         for b in range(root_width // LANES):
             sum_ref[:, b * LANES : (b + 1) * LANES] = -acc_ref[b]
         if root_aligned:
@@ -432,14 +416,14 @@
             own_half(pyb, parent_panel, "parent_update_own", xor=True),
             swap(pyb),
             pinned(parent_panel),
-            parent_inverse,
+            parent_list,
             root_acc,
             rhs,
         ],
         [SMEM] + [VMEM] * 6,
         scratch=[
             pltpu.VMEM((1, rcount, parent_local), F32),
-            pltpu.VMEM((root_width // LANES + 1, rcount, LANES), F32),
+            pltpu.VMEM((root_width // LANES + BLOCKS, rcount, LANES), F32),
             pltpu.VMEM((rcount, root_width), F32),
         ],
         name="parent_update",
@@ -499,7 +483,6 @@
         else:
             sol_ref[...] = x_ref[...].astype(F32)
         blocks_of(x_ref, whole_ref, 0, root_width)
-        whole_ref[root_width // LANES] = jnp.zeros((rcount, LANES), F32)
         gather_walk(plan_ref, rows_ref, whole_ref, found_ref)
         terms(found_ref, w_ref, out_ref, 1 - core())
 
@@ -507,7 +490,7 @@
         parent_back,
         [
             (split_terms(parent_panel), BF16),
-            ((root_width // LANES + 1, rcount, LANES), F32),
+            ((root_width // LANES + BLOCKS, rcount, LANES), F32),
             ((rcount, root_cols if root_aligned else root_width), F32),
             ((1, rcount, parent_local), BF16),
         ],
@@ -541,7 +524,7 @@
         sol_ref[...] = px_ref[chip()]
         unite(own_ref, other_ref, x_ref)
         blocks_of(x_ref, whole_ref, 0, parent_width)
-        for b in range(root_width // LANES + 1):
+        for b in range(root_width // LANES):
             whole_ref[parent_width // LANES + b] = root_ref[b]
         gather_walk(plan_ref, rows_ref, whole_ref, found_ref)
 
@@ -556,7 +539,7 @@
     found_shape = (leaves, rcount, leaf_local)
     scratch = [
         pltpu.VMEM((rcount, parent_width), BF16),
-        pltpu.VMEM((tall // LANES + 1, rcount, LANES), F32),
+        pltpu.VMEM((tall // LANES + BLOCKS, rcount, LANES), F32),
     ]
 
     def leaf_back(*refs):

time: 118 us -> 115 us (0.975)
  Pallas kernels: 31.9 us -> 21.6 us
  waiting for transfers between devices: 29.8 us -> 39.1 us
  starting transfers between devices: 52.3 us -> 50.3 us
    pallas_call x23 -> x21, Pallas kernels: 31.9 us -> 21.6 us  [call(): pl.pallas_call(body, out_shape=[jax.ShapeDtypeStruct(*o) if isinstance(o,...]
    ppermute x30, waiting for transfers between devices: 18 us -> 25.4 us  [far(): return lax.ppermute(x, 'rows', [(i, i ^ 2 * k) for i in range(n)])]
    ppermute x3, waiting for transfers between devices: 2.35 us -> 4.21 us  [leaf_sum(): lax.ppermute(b, 'leaf', [(i, (i + k) % n) for i in range(n)]).astype(F32)]
  transfers between devices with their start and end apart: 47 -> 47, of which waited for: 35 -> 37; matrix products, arithmetic and copies ran while one was open for 1% -> 1% of each run, Pallas kernels for 15% -> 9%
where the time goes in v8:
time: 115 us
  starting transfers between devices  50.3 us (44%)
  waiting for transfers between devices  39.1 us (34%)
  Pallas kernels  21.6 us (19%)
  local copies, waits for them, and re-layouts  2.06 us (2%)
  between operations  1.87 us (2%)
    ppermute x30, starting transfers between devices, far(): return lax.ppermute(x, 'rows', [(i, i ^ 2 * k) for i in range(n)])  44.9 us
    ppermute x30, waiting for transfers between devices, far(): return lax.ppermute(x, 'rows', [(i, i ^ 2 * k) for i in range(n)])  25.4 us
    pallas_call x21, Pallas kernels, call(): pl.pallas_call(body, out_shape=[jax.ShapeDtypeStruct(*o) if isinstance(o,...  21.6 us
    ppermute x14, waiting for transfers between devices, swap(): return lax.ppermute(x, 'rows', [(i, i ^ 1) for i in range(n)])  9.46 us
    ppermute x3, waiting for transfers between devices, leaf_sum(): lax.ppermute(b, 'leaf', [(i, (i + k) % n) for i in range(n)]).astype(F32)  4.21 us
    ppermute x3, starting transfers between devices, leaf_sum(): lax.ppermute(b, 'leaf', [(i, (i + k) % n) for i in range(n)]).astype(F32)  3.59 us
  transfers between devices with their start and end apart: 47, of which 37 were waited for; matrix products, arithmetic and copies ran while one was open for 1% of the time, Pallas kernels for 9%

profile of v8, /device:TPU:0, one launch (start us, length us, event | category | flops | bytes accessed | tf_op | source)
XLA Modules:
  0.0 115.2 jit_solution(10255917524048702698)
XLA Ops:
  1.5 5.1 %collective-permute-start.2 = (bf16[4,8,256]{2,1,0:T(8,128)(2,1)S(1)}, bf16[4,8,256]{2,1,0:T(8,128)(2,1)S(1)}, u32[]{:S(2)}, u32[]{:S(2)}) collective-permute-start(bf16[4,8,256]{2,1,0:T(8,128)(2,1)S(1)} %round_rhs.1.refs_0_), channel_id=1, source_target_pairs={{0,6},{1,7},{2,4},{3,5},{4,2},{5,3},{6,0},{7,1},{8,14},{9,15},{10,... | collective-permute-start | bytes 49160 | tf_op jit(solution)/shard_map/ppermute | solution.py:234
  8.2 2.2 %prepare.1 = (s32[4,1024]{1,0:T(4,128)S(1)}, s32[33]{0:T(128)S(1)}, s32[1,512]{1,0:T(1,128)S(1)}, s32[5]{0:T(128)S(1)}) custom-call(bf16[4,8,256]{2,1,0:T(8,128)(2,1)S(1)} %round_rhs.1.refs_0_, s32[4,1024]{1,0:T(4,128)S(1)} %copy-done.5, s32[4]{0:T(128)S(1)} %copy-done.10, s32[1,512]{1,0:T(1,128)S(1)} %copy-done.8, s32[1]{0:T(128)S(6)} %copy.21.refs_4_), custom_call_target="tpu_custom_call" | custom-call | bytes 4194304 | tf_op jit(solution)/shard_map/prepare/pallas_call | solution.py:30
  13.2 3.5 %collective-permute-start.6 = (bf16[4,8,256]{2,1,0:T(8,128)(2,1)S(1)}, bf16[4,8,256]{2,1,0:T(8,128)(2,1)S(1)}, u32[]{:S(2)}, u32[]{:S(2)}) collective-permute-start(bf16[4,8,256]{2,1,0:T(8,128)(2,1)S(1)} %get-tuple-element.42), channel_id=1, source_target_pairs={{0,6},{1,7},{2,4},{3,5},{4,2},{5,3},{6,0},{7,1},{8,14},{9,15},{10,... | collective-permute-start | bytes 49160 | tf_op jit(solution)/shard_map/ppermute | solution.py:234
  16.7 0.9 collective-permute-start.4
  17.6 1.3 %collective-permute-done.6 = bf16[4,8,256]{2,1,0:T(8,128)(2,1)S(1)} collective-permute-done((bf16[4,8,256]{2,1,0:T(8,128)(2,1)S(1)}, bf16[4,8,256]{2,1,0:T(8,128)(2,1)S(1)}, u32[]{:S(2)}, u32[]{:S(2)}) %collective-permute-start.6) | collective-permute-done | bytes 16416 | tf_op jit(solution)/shard_map/ppermute | solution.py:234
  18.9 2.4 %collective-permute-done.5 = bf16[4,8,256]{2,1,0:T(8,128)(2,1)S(1)} collective-permute-done((bf16[4,8,256]{2,1,0:T(8,128)(2,1)S(1)}, bf16[4,8,256]{2,1,0:T(8,128)(2,1)S(1)}, u32[]{:S(2)}, u32[]{:S(2)}) %collective-permute-start.5) | collective-permute-done | bytes 16416 | tf_op jit(solution)/shard_map/ppermute | solution.py:234
  21.4 2.3 %leaf_update_own.1.refs_0_ = f32[4,8,1024]{2,1,0:T(8,128)S(1)} custom-call(bf16[4,4,8,256]{3,2,1,0:T(8,128)(2,1)S(1)} %pad_maximum_fusion.1.x_ref, bf16[4,1024,2048]{2,1,0:T(8,128)(2,1)S(1)} %copy-done), custom_call_target="tpu_custom_call" | custom-call | bytes 12582912 | tf_op jit(solution)/shard_map/leaf_update_own/pallas_call | solution.py:30
  23.7 3.4 %leaf_update.1 = (f32[4,8,512]{2,1,0:T(8,128)S(1)}, bf16[4,8,512]{2,1,0:T(8,128)(2,1)S(1)}, f32[32,8,128]{2,1,0:T(8,128)S(1)}) custom-call(f32[4,8,1024]{2,1,0:T(8,128)S(1)} %leaf_update_own.1.refs_0_, bf16[4,4,8,256]{3,2,1,0:T(8,128)(2,1)S(1)} %collective-permute-done.7.refs_1_, s32[33]{0:T(128)S(1)} %get-tuple-element.39.refs_2_.refs_0_, ...), custom_call_target="tpu_custom_call" | custom-call | tf_op jit(solution)/shard_map/leaf_update/pallas_call | solution.py:30
  28.6 1.5 %collective-permute-start.11 = (bf16[4,8,512]{2,1,0:T(8,128)(2,1)S(1)}, bf16[4,8,512]{2,1,0:T(8,128)(2,1)S(1)}, u32[]{:S(2)}, u32[]{:S(2)}) collective-permute-start(bf16[4,8,512]{2,1,0:T(8,128)(2,1)S(1)} %fusion.1), channel_id=1, source_target_pairs={{0,6},{1,7},{2,4},{3,5},{4,2},{5,3},{6,0},{7,1},{8,14},{9,15},{10,... | collective-permute-start | bytes 98312 | tf_op jit(solution)/shard_map/ppermute | solution.py:234
  30.8 2.3 %collective-permute-start.9 = (bf16[4,8,512]{2,1,0:T(8,128)(2,1)S(1)}, bf16[4,8,512]{2,1,0:T(8,128)(2,1)S(1)}, u32[]{:S(2)}, u32[]{:S(2)}) collective-permute-start(bf16[4,8,512]{2,1,0:T(8,128)(2,1)S(1)} %fusion.1), channel_id=1, source_target_pairs={{0,2},{1,3},{2,0},{3,1},{4,6},{5,7},{6,4},{7,5},{8,10},{9,11},{10,... | collective-permute-start | bytes 98312 | tf_op jit(solution)/shard_map/ppermute | solution.py:234
  33.0 1.5 %collective-permute-done.11 = bf16[4,8,512]{2,1,0:T(8,128)(2,1)S(1)} collective-permute-done((bf16[4,8,512]{2,1,0:T(8,128)(2,1)S(1)}, bf16[4,8,512]{2,1,0:T(8,128)(2,1)S(1)}, u32[]{:S(2)}, u32[]{:S(2)}) %collective-permute-start.11) | collective-permute-done | bytes 32800 | tf_op jit(solution)/shard_map/ppermute | solution.py:234
  37.5 2.2 %collective-permute-start.15 = (bf16[8,512]{1,0:T(8,128)(2,1)S(1)}, bf16[8,512]{1,0:T(8,128)(2,1)S(1)}, u32[]{:S(2)}, u32[]{:S(2)}) collective-permute-start(bf16[8,512]{1,0:T(8,128)(2,1)S(1)} %get-tuple-element.46), channel_id=1, source_target_pairs={{0,6},{1,7},{2,4},{3,5},{4,2},{5,3},{6,0},{7,1},{8,14},{9,15},{10,... | collective-permute-start | bytes 24584 | tf_op jit(solution)/shard_map/ppermute | solution.py:234
  40.4 1.5 %collective-permute-start.13 = (bf16[8,512]{1,0:T(8,128)(2,1)S(1)}, bf16[8,512]{1,0:T(8,128)(2,1)S(1)}, u32[]{:S(2)}, u32[]{:S(2)}) collective-permute-start(bf16[8,512]{1,0:T(8,128)(2,1)S(1)} %get-tuple-element.46), channel_id=1, source_target_pairs={{0,2},{1,3},{2,0},{3,1},{4,6},{5,7},{6,4},{7,5},{8,10},{9,11},{10,... | collective-permute-start | bytes 24584 | tf_op jit(solution)/shard_map/ppermute | solution.py:234
  41.9 1.1 collective-permute-done.15
  42.9 1.3 %collective-permute-done.14 = bf16[8,512]{1,0:T(8,128)(2,1)S(1)} collective-permute-done((bf16[8,512]{1,0:T(8,128)(2,1)S(1)}, bf16[8,512]{1,0:T(8,128)(2,1)S(1)}, u32[]{:S(2)}, u32[]{:S(2)}) %collective-permute-start.14) | collective-permute-done | bytes 8224 | tf_op jit(solution)/shard_map/ppermute | solution.py:234
  45.5 1.4 %parent_update.1 = (f32[4,8,512]{2,1,0:T(8,128)S(1)}, bf16[4,8,512]{2,1,0:T(8,128)(2,1)S(1)}) custom-call(s32[5]{0:T(128)S(1)} %get-tuple-element.40.plan_ref, f32[1,8,512]{2,1,0:T(8,128)S(1)} %parent_update_own.1.part_ref, bf16[4,8,512]{2,1,0:T(8,128)(2,1)S(1)} %collective-permute-done.16.x_ref, bf16[1,512,4096]{2,1,0:T(8,128)(2,1)S(1)} %copy-done.1, ...), custom_call_target="tpu_custom_call" | custom-call | tf_op jit(solution)/shard_map/parent_update/pallas_call | solution.py:30
  47.1 1.0 collective-permute-done.17
  48.2 2.5 %collective-permute-start.20 = (bf16[4,8,512]{2,1,0:T(8,128)(2,1)S(1)}, bf16[4,8,512]{2,1,0:T(8,128)(2,1)S(1)}, u32[]{:S(2)}, u32[]{:S(2)}) collective-permute-start(bf16[4,8,512]{2,1,0:T(8,128)(2,1)S(1)} %fusion.2), channel_id=1, source_target_pairs={{0,24},{8,0},{16,8},{24,16},{1,25},{9,1},{17,9},{25,17},{2,26},{10... | collective-permute-start | bytes 98312 | tf_op jit(solution)/shard_map/ppermute | solution.py:250
  52.3 2.7 %collective-permute-done.19 = bf16[4,8,512]{2,1,0:T(8,128)(2,1)S(1)} collective-permute-done((bf16[4,8,512]{2,1,0:T(8,128)(2,1)S(1)}, bf16[4,8,512]{2,1,0:T(8,128)(2,1)S(1)}, u32[]{:S(2)}, u32[]{:S(2)}) %collective-permute-start.19) | collective-permute-done | bytes 32800 | tf_op jit(solution)/shard_map/ppermute | solution.py:250
  54.9 1.0 collective-permute-done.18
  56.0 1.8 %collective-permute-start.23 = (bf16[4,8,512]{2,1,0:T(8,128)(2,1)S(1)}, bf16[4,8,512]{2,1,0:T(8,128)(2,1)S(1)}, u32[]{:S(2)}, u32[]{:S(2)}) collective-permute-start(bf16[4,8,512]{2,1,0:T(8,128)(2,1)S(1)} %fusion.28), channel_id=1, source_target_pairs={{0,6},{1,7},{2,4},{3,5},{4,2},{5,3},{6,0},{7,1},{8,14},{9,15},{10,... | collective-permute-start | bytes 98312 | tf_op jit(solution)/shard_map/ppermute | solution.py:234
  57.8 1.0 collective-permute-start.22
  58.8 1.6 %collective-permute-start.21 = (bf16[4,8,512]{2,1,0:T(8,128)(2,1)S(1)}, bf16[4,8,512]{2,1,0:T(8,128)(2,1)S(1)}, u32[]{:S(2)}, u32[]{:S(2)}) collective-permute-start(bf16[4,8,512]{2,1,0:T(8,128)(2,1)S(1)} %fusion.28), channel_id=1, source_target_pairs={{0,2},{1,3},{2,0},{3,1},{4,6},{5,7},{6,4},{7,5},{8,10},{9,11},{10,... | collective-permute-start | bytes 98312 | tf_op jit(solution)/shard_map/ppermute | solution.py:234
  60.5 1.3 %collective-permute-done.23 = bf16[4,8,512]{2,1,0:T(8,128)(2,1)S(1)} collective-permute-done((bf16[4,8,512]{2,1,0:T(8,128)(2,1)S(1)}, bf16[4,8,512]{2,1,0:T(8,128)(2,1)S(1)}, u32[]{:S(2)}, u32[]{:S(2)}) %collective-permute-start.23) | collective-permute-done | bytes 32800 | tf_op jit(solution)/shard_map/ppermute | solution.py:234
  64.3 1.0 root_solve.1
  66.5 2.3 %collective-permute-start.28 = (bf16[4,8,512]{2,1,0:T(8,128)(2,1)S(1)}, bf16[4,8,512]{2,1,0:T(8,128)(2,1)S(1)}, u32[]{:S(2)}, u32[]{:S(2)}) collective-permute-start(bf16[4,8,512]{2,1,0:T(8,128)(2,1)S(1)} %bitcast_convert_fusion.1), channel_id=1, source_target_pairs={{0,6},{1,7},{2,4},{3,5},{4,2},{5,3},{6,0},{7,1},{8,14},{9,15},{10,... | collective-permute-start | bytes 98312 | tf_op jit(solution)/shard_map/ppermute | solution.py:234
  69.4 1.5 %collective-permute-start.26 = (bf16[4,8,512]{2,1,0:T(8,128)(2,1)S(1)}, bf16[4,8,512]{2,1,0:T(8,128)(2,1)S(1)}, u32[]{:S(2)}, u32[]{:S(2)}) collective-permute-start(bf16[4,8,512]{2,1,0:T(8,128)(2,1)S(1)} %bitcast_convert_fusion.1), channel_id=1, source_target_pairs={{0,2},{1,3},{2,0},{3,1},{4,6},{5,7},{6,4},{7,5},{8,10},{9,11},{10,... | collective-permute-start | bytes 98312 | tf_op jit(solution)/shard_map/ppermute | solution.py:234
  71.0 1.4 %collective-permute-done.28 = bf16[4,8,512]{2,1,0:T(8,128)(2,1)S(1)} collective-permute-done((bf16[4,8,512]{2,1,0:T(8,128)(2,1)S(1)}, bf16[4,8,512]{2,1,0:T(8,128)(2,1)S(1)}, u32[]{:S(2)}, u32[]{:S(2)}) %collective-permute-start.28) | collective-permute-done | bytes 32800 | tf_op jit(solution)/shard_map/ppermute | solution.py:234
  72.4 1.3 %collective-permute-done.27 = bf16[4,8,512]{2,1,0:T(8,128)(2,1)S(1)} collective-permute-done((bf16[4,8,512]{2,1,0:T(8,128)(2,1)S(1)}, bf16[4,8,512]{2,1,0:T(8,128)(2,1)S(1)}, u32[]{:S(2)}, u32[]{:S(2)}) %collective-permute-start.27) | collective-permute-done | bytes 32800 | tf_op jit(solution)/shard_map/ppermute | solution.py:234
  73.8 1.2 %collective-permute-done.29.other_ref = bf16[4,8,512]{2,1,0:T(8,128)(2,1)S(1)} collective-permute-done((bf16[4,8,512]{2,1,0:T(8,128)(2,1)S(1)}, bf16[4,8,512]{2,1,0:T(8,128)(2,1)S(1)}, u32[]{:S(2)}, u32[]{:S(2)}) %collective-permute-start.29) | collective-permute-done | bytes 32800 | tf_op jit(solution)/shard_map/ppermute | solution.py:229
  75.0 1.3 %parent_back.1 = (bf16[4,1,8,512]{3,2,1,0:T(8,128)(2,1)S(1)}, f32[40,8,128]{2,1,0:T(8,128)S(1)}, f32[8,128]{1,0:T(8,128)}, bf16[1,8,512]{2,1,0:T(8,128)(2,1)S(1)}) custom-call(s32[5]{0:T(128)S(1)} %get-tuple-element.40.plan_ref, bf16[4,8,512]{2,1,0:T(8,128)(2,1)S(1)} %fusion.own_ref, bf16[4,8,512]{2,1,0:T(8,128)(2,1)S(1)} %collective-permute-done.29.other_ref, ...), custom_call_target="tpu_custom_call" | custom-call | tf_op jit(solution)/shard_map/parent_back/pallas_call | solution.py:30
  77.6 1.9 %collective-permute-start.33 = (bf16[1,8,512]{2,1,0:T(8,128)(2,1)S(1)}, bf16[1,8,512]{2,1,0:T(8,128)(2,1)S(1)}, u32[]{:S(2)}, u32[]{:S(2)}) collective-permute-start(bf16[1,8,512]{2,1,0:T(8,128)(2,1)S(1)} %get-tuple-element.79), channel_id=1, source_target_pairs={{0,6},{1,7},{2,4},{3,5},{4,2},{5,3},{6,0},{7,1},{8,14},{9,15},{10,... | collective-permute-start | bytes 24584 | tf_op jit(solution)/shard_map/ppermute | solution.py:234
  80.2 1.8 %collective-permute-start.31 = (bf16[1,8,512]{2,1,0:T(8,128)(2,1)S(1)}, bf16[1,8,512]{2,1,0:T(8,128)(2,1)S(1)}, u32[]{:S(2)}, u32[]{:S(2)}) collective-permute-start(bf16[1,8,512]{2,1,0:T(8,128)(2,1)S(1)} %get-tuple-element.81), channel_id=1, source_target_pairs={{0,2},{1,3},{2,0},{3,1},{4,6},{5,7},{6,4},{7,5},{8,10},{9,11},{10,... | collective-permute-start | bytes 24584 | tf_op jit(solution)/shard_map/ppermute | solution.py:234
  82.0 1.1 collective-permute-done.33.refs_3_
  85.6 2.3 %collective-permute-start.37 = (bf16[4,8,512]{2,1,0:T(8,128)(2,1)S(1)}, bf16[4,8,512]{2,1,0:T(8,128)(2,1)S(1)}, u32[]{:S(2)}, u32[]{:S(2)}) collective-permute-start(bf16[4,8,512]{2,1,0:T(8,128)(2,1)S(1)} %bitcast_convert_fusion), channel_id=1, source_target_pairs={{0,6},{1,7},{2,4},{3,5},{4,2},{5,3},{6,0},{7,1},{8,14},{9,15},{10,... | collective-permute-start | bytes 98312 | tf_op jit(solution)/shard_map/ppermute | solution.py:234
  87.9 1.0 collective-permute-start.36
  88.8 1.2 %collective-permute-start.35 = (bf16[4,8,512]{2,1,0:T(8,128)(2,1)S(1)}, bf16[4,8,512]{2,1,0:T(8,128)(2,1)S(1)}, u32[]{:S(2)}, u32[]{:S(2)}) collective-permute-start(bf16[4,8,512]{2,1,0:T(8,128)(2,1)S(1)} %bitcast_convert_fusion), channel_id=1, source_target_pairs={{0,2},{1,3},{2,0},{3,1},{4,6},{5,7},{6,4},{7,5},{8,10},{9,11},{10,... | collective-permute-start | bytes 98312 | tf_op jit(solution)/shard_map/ppermute | solution.py:234
  90.1 1.6 %collective-permute-done.37 = bf16[4,8,512]{2,1,0:T(8,128)(2,1)S(1)} collective-permute-done((bf16[4,8,512]{2,1,0:T(8,128)(2,1)S(1)}, bf16[4,8,512]{2,1,0:T(8,128)(2,1)S(1)}, u32[]{:S(2)}, u32[]{:S(2)}) %collective-permute-start.37) | collective-permute-done | bytes 32800 | tf_op jit(solution)/shard_map/ppermute | solution.py:234
  91.7 1.2 %collective-permute-done.36 = bf16[4,8,512]{2,1,0:T(8,128)(2,1)S(1)} collective-permute-done((bf16[4,8,512]{2,1,0:T(8,128)(2,1)S(1)}, bf16[4,8,512]{2,1,0:T(8,128)(2,1)S(1)}, u32[]{:S(2)}, u32[]{:S(2)}) %collective-permute-start.36) | collective-permute-done | bytes 32800 | tf_op jit(solution)/shard_map/ppermute | solution.py:234
  93.2 1.2 %collective-permute-done.38.refs_3_ = bf16[4,8,512]{2,1,0:T(8,128)(2,1)S(1)} collective-permute-done((bf16[4,8,512]{2,1,0:T(8,128)(2,1)S(1)}, bf16[4,8,512]{2,1,0:T(8,128)(2,1)S(1)}, u32[]{:S(2)}, u32[]{:S(2)}) %collective-permute-start.38) | collective-permute-done | bytes 32800 | tf_op jit(solution)/shard_map/ppermute | solution.py:229
  94.4 2.6 %leaf_back.1 = (bf16[4,4,8,256]{3,2,1,0:T(8,128)(2,1)S(1)}, f32[8,512]{1,0:T(8,128)S(1)}, bf16[4,8,1024]{2,1,0:T(8,128)(2,1)S(1)}) custom-call(s32[33]{0:T(128)S(1)} %get-tuple-element.39.refs_2_.refs_0_, f32[4,8,512]{2,1,0:T(8,128)S(1)} %get-tuple-element.71.refs_1_, bf16[4,8,512]{2,1,0:T(8,128)(2,1)S(1)} %get-tuple-element.70.refs_2_, ...), custom_call_target="tpu_custom_call" | custom-call | tf_op jit(solution)/shard_map/leaf_back/pallas_call | solution.py:30
  97.1 1.2 %leaf_back_own.1 = f32[4,4,8,256]{3,2,1,0:T(8,128)S(1)} custom-call(bf16[4,8,1024]{2,1,0:T(8,128)(2,1)S(1)} %get-tuple-element.60.x_ref, bf16[4,1024,2048]{2,1,0:T(8,128)(2,1)S(1)} %copy-done), custom_call_target="tpu_custom_call" | custom-call | bytes 12582912 | tf_op jit(solution)/shard_map/leaf_back_own/pallas_call | solution.py:30
  98.4 1.6 %collective-permute-start.42 = (bf16[4,8,256]{2,1,0:T(8,128)(2,1)S(1)}, bf16[4,8,256]{2,1,0:T(8,128)(2,1)S(1)}, u32[]{:S(2)}, u32[]{:S(2)}) collective-permute-start(bf16[4,8,256]{2,1,0:T(8,128)(2,1)S(1)} %get-tuple-element.75), channel_id=1, source_target_pairs={{0,6},{1,7},{2,4},{3,5},{4,2},{5,3},{6,0},{7,1},{8,14},{9,15},{10,... | collective-permute-start | bytes 49160 | tf_op jit(solution)/shard_map/ppermute | solution.py:234
  100.8 2.0 %collective-permute-start.40 = (bf16[4,8,256]{2,1,0:T(8,128)(2,1)S(1)}, bf16[4,8,256]{2,1,0:T(8,128)(2,1)S(1)}, u32[]{:S(2)}, u32[]{:S(2)}) collective-permute-start(bf16[4,8,256]{2,1,0:T(8,128)(2,1)S(1)} %get-tuple-element.77), channel_id=1, source_target_pairs={{0,2},{1,3},{2,0},{3,1},{4,6},{5,7},{6,4},{7,5},{8,10},{9,11},{10,... | collective-permute-start | bytes 49160 | tf_op jit(solution)/shard_map/ppermute | solution.py:234
  102.8 1.3 %collective-permute-done.42.refs_3_ = bf16[4,8,256]{2,1,0:T(8,128)(2,1)S(1)} collective-permute-done((bf16[4,8,256]{2,1,0:T(8,128)(2,1)S(1)}, bf16[4,8,256]{2,1,0:T(8,128)(2,1)S(1)}, u32[]{:S(2)}, u32[]{:S(2)}) %collective-permute-start.42) | collective-permute-done | bytes 16416 | tf_op jit(solution)/shard_map/ppermute | solution.py:234
  106.5 1.8 %collective-permute-start.44 = (bf16[4,8,256]{2,1,0:T(8,128)(2,1)S(1)}, bf16[4,8,256]{2,1,0:T(8,128)(2,1)S(1)}, u32[]{:S(2)}, u32[]{:S(2)}) collective-permute-start(bf16[4,8,256]{2,1,0:T(8,128)(2,1)S(1)} %get-tuple-element.72), channel_id=1, source_target_pairs={{0,2},{1,3},{2,0},{3,1},{4,6},{5,7},{6,4},{7,5},{8,10},{9,11},{10,... | collective-permute-start | bytes 49160 | tf_op jit(solution)/shard_map/ppermute | solution.py:234
  108.3 1.6 %collective-permute-start.46 = (bf16[4,8,256]{2,1,0:T(8,128)(2,1)S(1)}, bf16[4,8,256]{2,1,0:T(8,128)(2,1)S(1)}, u32[]{:S(2)}, u32[]{:S(2)}) collective-permute-start(bf16[4,8,256]{2,1,0:T(8,128)(2,1)S(1)} %get-tuple-element.73), channel_id=1, source_target_pairs={{0,6},{1,7},{2,4},{3,5},{4,2},{5,3},{6,0},{7,1},{8,14},{9,15},{10,... | collective-permute-start | bytes 49160 | tf_op jit(solution)/shard_map/ppermute | solution.py:234
  110.7 3.1 %collective-permute-done.46 = bf16[4,8,256]{2,1,0:T(8,128)(2,1)S(1)} collective-permute-done((bf16[4,8,256]{2,1,0:T(8,128)(2,1)S(1)}, bf16[4,8,256]{2,1,0:T(8,128)(2,1)S(1)}, u32[]{:S(2)}, u32[]{:S(2)}) %collective-permute-start.46) | collective-permute-done | bytes 16416 | tf_op jit(solution)/shard_map/ppermute | solution.py:234
  (107 shorter events, 27.9 us)
Async XLA Ops:
  1.4 20.0 %copy-start = (bf16[4,1024,2048]{2,1,0:T(8,128)(2,1)S(1)}, bf16[4,1024,2048]{2,1,0:T(8,128)(2,1)}, u32[]{:S(2)}) copy-start(bf16[4,1024,2048]{2,1,0:T(8,128)(2,1)} %w_ref.20) | copy-start | bytes 50331652
  1.5 8.9 %collective-permute-start.2 = (bf16[4,8,256]{2,1,0:T(8,128)(2,1)S(1)}, bf16[4,8,256]{2,1,0:T(8,128)(2,1)S(1)}, u32[]{:S(2)}, u32[]{:S(2)}) collective-permute-start(bf16[4,8,256]{2,1,0:T(8,128)(2,1)S(1)} %round_rhs.1.refs_0_), channel_id=1, source_target_pairs={{0,6},{1,7},{2,4},{3,5},{4,2},{5,3},{6,0},{7,1},{8,14},{9,15},{10,... | collective-permute-start | bytes 49160 | tf_op jit(solution)/shard_map/ppermute | solution.py:234
  6.6 4.6 %collective-permute-start.1 = (bf16[4,8,256]{2,1,0:T(8,128)(2,1)S(1)}, bf16[4,8,256]{2,1,0:T(8,128)(2,1)S(1)}, u32[]{:S(2)}, u32[]{:S(2)}) collective-permute-start(bf16[4,8,256]{2,1,0:T(8,128)(2,1)S(1)} %round_rhs.1.refs_0_), channel_id=1, source_target_pairs={{0,4},{1,5},{2,6},{3,7},{4,0},{5,1},{6,2},{7,3},{8,12},{9,13},{10,... | collective-permute-start | bytes 49160 | tf_op jit(solution)/shard_map/ppermute | solution.py:234
  6.6 4.6 %collective-permute-start = (bf16[4,8,256]{2,1,0:T(8,128)(2,1)S(1)}, bf16[4,8,256]{2,1,0:T(8,128)(2,1)S(1)}, u32[]{:S(2)}, u32[]{:S(2)}) collective-permute-start(bf16[4,8,256]{2,1,0:T(8,128)(2,1)S(1)} %round_rhs.1.refs_0_), channel_id=1, source_target_pairs={{0,2},{1,3},{2,0},{3,1},{4,6},{5,7},{6,4},{7,5},{8,10},{9,11},{10,... | collective-permute-start | bytes 49160 | tf_op jit(solution)/shard_map/ppermute | solution.py:234
  11.2 1.3 %collective-permute-start.3 = (bf16[4,4,8,256]{3,2,1,0:T(8,128)(2,1)S(1)}, bf16[4,4,8,256]{3,2,1,0:T(8,128)(2,1)S(1)}, u32[]{:S(2)}, u32[]{:S(2)}) collective-permute-start(bf16[4,4,8,256]{3,2,1,0:T(8,128)(2,1)S(1)} %pad_maximum_fusion.x_ref), channel_id=1, source_target_pairs={{0,1},{1,0},{2,3},{3,2},{4,5},{5,4},{6,7},{7,6},{8,9},{9,8},{10,11... | collective-permute-start | bytes 196616 | tf_op jit(solution)/shard_map/ppermute | solution.py:229
  13.2 5.7 %collective-permute-start.6 = (bf16[4,8,256]{2,1,0:T(8,128)(2,1)S(1)}, bf16[4,8,256]{2,1,0:T(8,128)(2,1)S(1)}, u32[]{:S(2)}, u32[]{:S(2)}) collective-permute-start(bf16[4,8,256]{2,1,0:T(8,128)(2,1)S(1)} %get-tuple-element.42), channel_id=1, source_target_pairs={{0,6},{1,7},{2,4},{3,5},{4,2},{5,3},{6,0},{7,1},{8,14},{9,15},{10,... | collective-permute-start | bytes 49160 | tf_op jit(solution)/shard_map/ppermute | solution.py:234
  16.7 4.6 %collective-permute-start.5 = (bf16[4,8,256]{2,1,0:T(8,128)(2,1)S(1)}, bf16[4,8,256]{2,1,0:T(8,128)(2,1)S(1)}, u32[]{:S(2)}, u32[]{:S(2)}) collective-permute-start(bf16[4,8,256]{2,1,0:T(8,128)(2,1)S(1)} %get-tuple-element.42), channel_id=1, source_target_pairs={{0,4},{1,5},{2,6},{3,7},{4,0},{5,1},{6,2},{7,3},{8,12},{9,13},{10,... | collective-permute-start | bytes 49160 | tf_op jit(solution)/shard_map/ppermute | solution.py:234
  16.7 4.6 %collective-permute-start.4 = (bf16[4,8,256]{2,1,0:T(8,128)(2,1)S(1)}, bf16[4,8,256]{2,1,0:T(8,128)(2,1)S(1)}, u32[]{:S(2)}, u32[]{:S(2)}) collective-permute-start(bf16[4,8,256]{2,1,0:T(8,128)(2,1)S(1)} %get-tuple-element.42), channel_id=1, source_target_pairs={{0,2},{1,3},{2,0},{3,1},{4,6},{5,7},{6,4},{7,5},{8,10},{9,11},{10,... | collective-permute-start | bytes 49160 | tf_op jit(solution)/shard_map/ppermute | solution.py:234
  21.3 2.4 %collective-permute-start.7 = (bf16[4,4,8,256]{3,2,1,0:T(8,128)(2,1)S(1)}, bf16[4,4,8,256]{3,2,1,0:T(8,128)(2,1)S(1)}, u32[]{:S(2)}, u32[]{:S(2)}) collective-permute-start(bf16[4,4,8,256]{3,2,1,0:T(8,128)(2,1)S(1)} %pad_maximum_fusion.1.x_ref), channel_id=1, source_target_pairs={{0,1},{1,0},{2,3},{3,2},{4,5},{5,4},{6,7},{7,6},{8,9},{9,8},{10,11... | collective-permute-start | bytes 196616 | tf_op jit(solution)/shard_map/ppermute | solution.py:229
  27.2 1.4 %collective-permute-start.8 = (bf16[4,8,512]{2,1,0:T(8,128)(2,1)S(1)}, bf16[4,8,512]{2,1,0:T(8,128)(2,1)S(1)}, u32[]{:S(2)}, u32[]{:S(2)}) collective-permute-start(bf16[4,8,512]{2,1,0:T(8,128)(2,1)S(1)} %get-tuple-element.45), channel_id=1, source_target_pairs={{0,1},{1,0},{2,3},{3,2},{4,5},{5,4},{6,7},{7,6},{8,9},{9,8},{10,11... | collective-permute-start | bytes 98312 | tf_op jit(solution)/shard_map/ppermute | solution.py:229
  28.6 5.9 %collective-permute-start.11 = (bf16[4,8,512]{2,1,0:T(8,128)(2,1)S(1)}, bf16[4,8,512]{2,1,0:T(8,128)(2,1)S(1)}, u32[]{:S(2)}, u32[]{:S(2)}) collective-permute-start(bf16[4,8,512]{2,1,0:T(8,128)(2,1)S(1)} %fusion.1), channel_id=1, source_target_pairs={{0,6},{1,7},{2,4},{3,5},{4,2},{5,3},{6,0},{7,1},{8,14},{9,15},{10,... | collective-permute-start | bytes 98312 | tf_op jit(solution)/shard_map/ppermute | solution.py:234
  30.1 5.1 %collective-permute-start.10 = (bf16[4,8,512]{2,1,0:T(8,128)(2,1)S(1)}, bf16[4,8,512]{2,1,0:T(8,128)(2,1)S(1)}, u32[]{:S(2)}, u32[]{:S(2)}) collective-permute-start(bf16[4,8,512]{2,1,0:T(8,128)(2,1)S(1)} %fusion.1), channel_id=1, source_target_pairs={{0,4},{1,5},{2,6},{3,7},{4,0},{5,1},{6,2},{7,3},{8,12},{9,13},{10,... | collective-permute-start | bytes 98312 | tf_op jit(solution)/shard_map/ppermute | solution.py:234
  30.8 4.7 %collective-permute-start.9 = (bf16[4,8,512]{2,1,0:T(8,128)(2,1)S(1)}, bf16[4,8,512]{2,1,0:T(8,128)(2,1)S(1)}, u32[]{:S(2)}, u32[]{:S(2)}) collective-permute-start(bf16[4,8,512]{2,1,0:T(8,128)(2,1)S(1)} %fusion.1), channel_id=1, source_target_pairs={{0,2},{1,3},{2,0},{3,1},{4,6},{5,7},{6,4},{7,5},{8,10},{9,11},{10,... | collective-permute-start | bytes 98312 | tf_op jit(solution)/shard_map/ppermute | solution.py:234
  35.5 1.3 %collective-permute-start.12 = (bf16[4,8,512]{2,1,0:T(8,128)(2,1)S(1)}, bf16[4,8,512]{2,1,0:T(8,128)(2,1)S(1)}, u32[]{:S(2)}, u32[]{:S(2)}) collective-permute-start(bf16[4,8,512]{2,1,0:T(8,128)(2,1)S(1)} %add_convert_fusion.1.x_ref), channel_id=1, source_target_pairs={{0,1},{1,0},{2,3},{3,2},{4,5},{5,4},{6,7},{7,6},{8,9},{9,8},{10,11... | collective-permute-start | bytes 98312 | tf_op jit(solution)/shard_map/ppermute | solution.py:229
  37.5 5.5 %collective-permute-start.15 = (bf16[8,512]{1,0:T(8,128)(2,1)S(1)}, bf16[8,512]{1,0:T(8,128)(2,1)S(1)}, u32[]{:S(2)}, u32[]{:S(2)}) collective-permute-start(bf16[8,512]{1,0:T(8,128)(2,1)S(1)} %get-tuple-element.46), channel_id=1, source_target_pairs={{0,6},{1,7},{2,4},{3,5},{4,2},{5,3},{6,0},{7,1},{8,14},{9,15},{10,... | collective-permute-start | bytes 24584 | tf_op jit(solution)/shard_map/ppermute | solution.py:234
  39.7 4.5 %collective-permute-start.14 = (bf16[8,512]{1,0:T(8,128)(2,1)S(1)}, bf16[8,512]{1,0:T(8,128)(2,1)S(1)}, u32[]{:S(2)}, u32[]{:S(2)}) collective-permute-start(bf16[8,512]{1,0:T(8,128)(2,1)S(1)} %get-tuple-element.46), channel_id=1, source_target_pairs={{0,4},{1,5},{2,6},{3,7},{4,0},{5,1},{6,2},{7,3},{8,12},{9,13},{10,... | collective-permute-start | bytes 24584 | tf_op jit(solution)/shard_map/ppermute | solution.py:234
  40.4 3.8 %collective-permute-start.13 = (bf16[8,512]{1,0:T(8,128)(2,1)S(1)}, bf16[8,512]{1,0:T(8,128)(2,1)S(1)}, u32[]{:S(2)}, u32[]{:S(2)}) collective-permute-start(bf16[8,512]{1,0:T(8,128)(2,1)S(1)} %get-tuple-element.46), channel_id=1, source_target_pairs={{0,2},{1,3},{2,0},{3,1},{4,6},{5,7},{6,4},{7,5},{8,10},{9,11},{10,... | collective-permute-start | bytes 24584 | tf_op jit(solution)/shard_map/ppermute | solution.py:234
  44.2 1.3 %collective-permute-start.16 = (bf16[4,8,512]{2,1,0:T(8,128)(2,1)S(1)}, bf16[4,8,512]{2,1,0:T(8,128)(2,1)S(1)}, u32[]{:S(2)}, u32[]{:S(2)}) collective-permute-start(bf16[4,8,512]{2,1,0:T(8,128)(2,1)S(1)} %pad_maximum_fusion.2.x_ref), channel_id=1, source_target_pairs={{0,1},{1,0},{2,3},{3,2},{4,5},{5,4},{6,7},{7,6},{8,9},{9,8},{10,11... | collective-permute-start | bytes 98312 | tf_op jit(solution)/shard_map/ppermute | solution.py:229
  46.9 1.3 %collective-permute-start.17 = (bf16[4,8,512]{2,1,0:T(8,128)(2,1)S(1)}, bf16[4,8,512]{2,1,0:T(8,128)(2,1)S(1)}, u32[]{:S(2)}, u32[]{:S(2)}) collective-permute-start(bf16[4,8,512]{2,1,0:T(8,128)(2,1)S(1)} %get-tuple-element.51), channel_id=1, source_target_pairs={{0,1},{1,0},{2,3},{3,2},{4,5},{5,4},{6,7},{7,6},{8,9},{9,8},{10,11... | collective-permute-start | bytes 98312 | tf_op jit(solution)/shard_map/ppermute | solution.py:229
  48.2 4.1 %collective-permute-start.20 = (bf16[4,8,512]{2,1,0:T(8,128)(2,1)S(1)}, bf16[4,8,512]{2,1,0:T(8,128)(2,1)S(1)}, u32[]{:S(2)}, u32[]{:S(2)}) collective-permute-start(bf16[4,8,512]{2,1,0:T(8,128)(2,1)S(1)} %fusion.2), channel_id=1, source_target_pairs={{0,24},{8,0},{16,8},{24,16},{1,25},{9,1},{17,9},{25,17},{2,26},{10... | collective-permute-start | bytes 98312 | tf_op jit(solution)/shard_map/ppermute | solution.py:250
  50.7 4.3 %collective-permute-start.19 = (bf16[4,8,512]{2,1,0:T(8,128)(2,1)S(1)}, bf16[4,8,512]{2,1,0:T(8,128)(2,1)S(1)}, u32[]{:S(2)}, u32[]{:S(2)}) collective-permute-start(bf16[4,8,512]{2,1,0:T(8,128)(2,1)S(1)} %fusion.2), channel_id=1, source_target_pairs={{0,16},{8,24},{16,0},{24,8},{1,17},{9,25},{17,1},{25,9},{2,18},{10... | collective-permute-start | bytes 98312 | tf_op jit(solution)/shard_map/ppermute | solution.py:250
  51.2 4.8 %collective-permute-start.18 = (bf16[4,8,512]{2,1,0:T(8,128)(2,1)S(1)}, bf16[4,8,512]{2,1,0:T(8,128)(2,1)S(1)}, u32[]{:S(2)}, u32[]{:S(2)}) collective-permute-start(bf16[4,8,512]{2,1,0:T(8,128)(2,1)S(1)} %fusion.2), channel_id=1, source_target_pairs={{0,8},{8,16},{16,24},{24,0},{1,9},{9,17},{17,25},{25,1},{2,10},{10... | collective-permute-start | bytes 98312 | tf_op jit(solution)/shard_map/ppermute | solution.py:250
  56.0 5.8 %collective-permute-start.23 = (bf16[4,8,512]{2,1,0:T(8,128)(2,1)S(1)}, bf16[4,8,512]{2,1,0:T(8,128)(2,1)S(1)}, u32[]{:S(2)}, u32[]{:S(2)}) collective-permute-start(bf16[4,8,512]{2,1,0:T(8,128)(2,1)S(1)} %fusion.28), channel_id=1, source_target_pairs={{0,6},{1,7},{2,4},{3,5},{4,2},{5,3},{6,0},{7,1},{8,14},{9,15},{10,... | collective-permute-start | bytes 98312 | tf_op jit(solution)/shard_map/ppermute | solution.py:234
  57.8 4.8 %collective-permute-start.22 = (bf16[4,8,512]{2,1,0:T(8,128)(2,1)S(1)}, bf16[4,8,512]{2,1,0:T(8,128)(2,1)S(1)}, u32[]{:S(2)}, u32[]{:S(2)}) collective-permute-start(bf16[4,8,512]{2,1,0:T(8,128)(2,1)S(1)} %fusion.28), channel_id=1, source_target_pairs={{0,4},{1,5},{2,6},{3,7},{4,0},{5,1},{6,2},{7,3},{8,12},{9,13},{10,... | collective-permute-start | bytes 98312 | tf_op jit(solution)/shard_map/ppermute | solution.py:234
  58.8 4.1 %collective-permute-start.21 = (bf16[4,8,512]{2,1,0:T(8,128)(2,1)S(1)}, bf16[4,8,512]{2,1,0:T(8,128)(2,1)S(1)}, u32[]{:S(2)}, u32[]{:S(2)}) collective-permute-start(bf16[4,8,512]{2,1,0:T(8,128)(2,1)S(1)} %fusion.28), channel_id=1, source_target_pairs={{0,2},{1,3},{2,0},{3,1},{4,6},{5,7},{6,4},{7,5},{8,10},{9,11},{10,... | collective-permute-start | bytes 98312 | tf_op jit(solution)/shard_map/ppermute | solution.py:234
  63.0 1.3 %collective-permute-start.24 = (bf16[4,8,512]{2,1,0:T(8,128)(2,1)S(1)}, bf16[4,8,512]{2,1,0:T(8,128)(2,1)S(1)}, u32[]{:S(2)}, u32[]{:S(2)}) collective-permute-start(bf16[4,8,512]{2,1,0:T(8,128)(2,1)S(1)} %add_convert_fusion.x_ref), channel_id=1, source_target_pairs={{0,1},{1,0},{2,3},{3,2},{4,5},{5,4},{6,7},{7,6},{8,9},{9,8},{10,11... | collective-permute-start | bytes 98312 | tf_op jit(solution)/shard_map/ppermute | solution.py:229
  65.3 1.2 %collective-permute-start.25 = (bf16[4,1,8,512]{3,2,0,1:T(8,128)(2,1)S(1)}, bf16[4,1,8,512]{3,2,0,1:T(8,128)(2,1)S(1)}, u32[]{:S(2)}, u32[]{:S(2)}) collective-permute-start(bf16[4,1,8,512]{3,2,0,1:T(8,128)(2,1)S(1)} %bitcast.81), channel_id=1, source_target_pairs={{0,1},{1,0},{2,3},{3,2},{4,5},{5,4},{6,7},{7,6},{8,9},{9,8},{10,11... | collective-permute-start | bytes 98312 | tf_op jit(solution)/shard_map/ppermute | solution.py:229
  66.5 5.9 %collective-permute-start.28 = (bf16[4,8,512]{2,1,0:T(8,128)(2,1)S(1)}, bf16[4,8,512]{2,1,0:T(8,128)(2,1)S(1)}, u32[]{:S(2)}, u32[]{:S(2)}) collective-permute-start(bf16[4,8,512]{2,1,0:T(8,128)(2,1)S(1)} %bitcast_convert_fusion.1), channel_id=1, source_target_pairs={{0,6},{1,7},{2,4},{3,5},{4,2},{5,3},{6,0},{7,1},{8,14},{9,15},{10,... | collective-permute-start | bytes 98312 | tf_op jit(solution)/shard_map/ppermute | solution.py:234
  68.8 4.9 %collective-permute-start.27 = (bf16[4,8,512]{2,1,0:T(8,128)(2,1)S(1)}, bf16[4,8,512]{2,1,0:T(8,128)(2,1)S(1)}, u32[]{:S(2)}, u32[]{:S(2)}) collective-permute-start(bf16[4,8,512]{2,1,0:T(8,128)(2,1)S(1)} %bitcast_convert_fusion.1), channel_id=1, source_target_pairs={{0,4},{1,5},{2,6},{3,7},{4,0},{5,1},{6,2},{7,3},{8,12},{9,13},{10,... | collective-permute-start | bytes 98312 | tf_op jit(solution)/shard_map/ppermute | solution.py:234
  69.4 4.3 %collective-permute-start.26 = (bf16[4,8,512]{2,1,0:T(8,128)(2,1)S(1)}, bf16[4,8,512]{2,1,0:T(8,128)(2,1)S(1)}, u32[]{:S(2)}, u32[]{:S(2)}) collective-permute-start(bf16[4,8,512]{2,1,0:T(8,128)(2,1)S(1)} %bitcast_convert_fusion.1), channel_id=1, source_target_pairs={{0,2},{1,3},{2,0},{3,1},{4,6},{5,7},{6,4},{7,5},{8,10},{9,11},{10,... | collective-permute-start | bytes 98312 | tf_op jit(solution)/shard_map/ppermute | solution.py:234
  73.7 1.3 %collective-permute-start.29 = (bf16[4,8,512]{2,1,0:T(8,128)(2,1)S(1)}, bf16[4,8,512]{2,1,0:T(8,128)(2,1)S(1)}, u32[]{:S(2)}, u32[]{:S(2)}) collective-permute-start(bf16[4,8,512]{2,1,0:T(8,128)(2,1)S(1)} %fusion.own_ref), channel_id=1, source_target_pairs={{0,1},{1,0},{2,3},{3,2},{4,5},{5,4},{6,7},{7,6},{8,9},{9,8},{10,11... | collective-permute-start | bytes 98312 | tf_op jit(solution)/shard_map/ppermute | solution.py:229
  76.3 1.2 %collective-permute-start.30 = (bf16[4,1,8,512]{3,2,1,0:T(8,128)(2,1)S(1)}, bf16[4,1,8,512]{3,2,1,0:T(8,128)(2,1)S(1)}, u32[]{:S(2)}, u32[]{:S(2)}) collective-permute-start(bf16[4,1,8,512]{3,2,1,0:T(8,128)(2,1)S(1)} %get-tuple-element.55), channel_id=1, source_target_pairs={{0,1},{1,0},{2,3},{3,2},{4,5},{5,4},{6,7},{7,6},{8,9},{9,8},{10,11... | collective-permute-start | bytes 98312 | tf_op jit(solution)/shard_map/ppermute | solution.py:229
  77.6 5.6 %collective-permute-start.33 = (bf16[1,8,512]{2,1,0:T(8,128)(2,1)S(1)}, bf16[1,8,512]{2,1,0:T(8,128)(2,1)S(1)}, u32[]{:S(2)}, u32[]{:S(2)}) collective-permute-start(bf16[1,8,512]{2,1,0:T(8,128)(2,1)S(1)} %get-tuple-element.79), channel_id=1, source_target_pairs={{0,6},{1,7},{2,4},{3,5},{4,2},{5,3},{6,0},{7,1},{8,14},{9,15},{10,... | collective-permute-start | bytes 24584 | tf_op jit(solution)/shard_map/ppermute | solution.py:234
  79.4 4.6 %collective-permute-start.32 = (bf16[1,8,512]{2,1,0:T(8,128)(2,1)S(1)}, bf16[1,8,512]{2,1,0:T(8,128)(2,1)S(1)}, u32[]{:S(2)}, u32[]{:S(2)}) collective-permute-start(bf16[1,8,512]{2,1,0:T(8,128)(2,1)S(1)} %get-tuple-element.80), channel_id=1, source_target_pairs={{0,4},{1,5},{2,6},{3,7},{4,0},{5,1},{6,2},{7,3},{8,12},{9,13},{10,... | collective-permute-start | bytes 24584 | tf_op jit(solution)/shard_map/ppermute | solution.py:234
  80.2 3.7 %collective-permute-start.31 = (bf16[1,8,512]{2,1,0:T(8,128)(2,1)S(1)}, bf16[1,8,512]{2,1,0:T(8,128)(2,1)S(1)}, u32[]{:S(2)}, u32[]{:S(2)}) collective-permute-start(bf16[1,8,512]{2,1,0:T(8,128)(2,1)S(1)} %get-tuple-element.81), channel_id=1, source_target_pairs={{0,2},{1,3},{2,0},{3,1},{4,6},{5,7},{6,4},{7,5},{8,10},{9,11},{10,... | collective-permute-start | bytes 24584 | tf_op jit(solution)/shard_map/ppermute | solution.py:234
  84.4 1.2 %collective-permute-start.34 = (bf16[4,1,8,512]{3,2,0,1:T(8,128)(2,1)S(1)}, bf16[4,1,8,512]{3,2,0,1:T(8,128)(2,1)S(1)}, u32[]{:S(2)}, u32[]{:S(2)}) collective-permute-start(bf16[4,1,8,512]{3,2,0,1:T(8,128)(2,1)S(1)} %bitcast.80), channel_id=1, source_target_pairs={{0,1},{1,0},{2,3},{3,2},{4,5},{5,4},{6,7},{7,6},{8,9},{9,8},{10,11... | collective-permute-start | bytes 98312 | tf_op jit(solution)/shard_map/ppermute | solution.py:229
  85.6 6.1 %collective-permute-start.37 = (bf16[4,8,512]{2,1,0:T(8,128)(2,1)S(1)}, bf16[4,8,512]{2,1,0:T(8,128)(2,1)S(1)}, u32[]{:S(2)}, u32[]{:S(2)}) collective-permute-start(bf16[4,8,512]{2,1,0:T(8,128)(2,1)S(1)} %bitcast_convert_fusion), channel_id=1, source_target_pairs={{0,6},{1,7},{2,4},{3,5},{4,2},{5,3},{6,0},{7,1},{8,14},{9,15},{10,... | collective-permute-start | bytes 98312 | tf_op jit(solution)/shard_map/ppermute | solution.py:234
  87.9 5.0 %collective-permute-start.36 = (bf16[4,8,512]{2,1,0:T(8,128)(2,1)S(1)}, bf16[4,8,512]{2,1,0:T(8,128)(2,1)S(1)}, u32[]{:S(2)}, u32[]{:S(2)}) collective-permute-start(bf16[4,8,512]{2,1,0:T(8,128)(2,1)S(1)} %bitcast_convert_fusion), channel_id=1, source_target_pairs={{0,4},{1,5},{2,6},{3,7},{4,0},{5,1},{6,2},{7,3},{8,12},{9,13},{10,... | collective-permute-start | bytes 98312 | tf_op jit(solution)/shard_map/ppermute | solution.py:234
  88.8 4.3 %collective-permute-start.35 = (bf16[4,8,512]{2,1,0:T(8,128)(2,1)S(1)}, bf16[4,8,512]{2,1,0:T(8,128)(2,1)S(1)}, u32[]{:S(2)}, u32[]{:S(2)}) collective-permute-start(bf16[4,8,512]{2,1,0:T(8,128)(2,1)S(1)} %bitcast_convert_fusion), channel_id=1, source_target_pairs={{0,2},{1,3},{2,0},{3,1},{4,6},{5,7},{6,4},{7,5},{8,10},{9,11},{10,... | collective-permute-start | bytes 98312 | tf_op jit(solution)/shard_map/ppermute | solution.py:234
  93.1 1.3 %collective-permute-start.38 = (bf16[4,8,512]{2,1,0:T(8,128)(2,1)S(1)}, bf16[4,8,512]{2,1,0:T(8,128)(2,1)S(1)}, u32[]{:S(2)}, u32[]{:S(2)}) collective-permute-start(bf16[4,8,512]{2,1,0:T(8,128)(2,1)S(1)} %get-tuple-element.70.refs_2_), channel_id=1, source_target_pairs={{0,1},{1,0},{2,3},{3,2},{4,5},{5,4},{6,7},{7,6},{8,9},{9,8},{10,11... | collective-permute-start | bytes 98312 | tf_op jit(solution)/shard_map/ppermute | solution.py:229
  97.0 1.4 %collective-permute-start.39 = (bf16[4,4,8,256]{3,2,1,0:T(8,128)(2,1)S(1)}, bf16[4,4,8,256]{3,2,1,0:T(8,128)(2,1)S(1)}, u32[]{:S(2)}, u32[]{:S(2)}) collective-permute-start(bf16[4,4,8,256]{3,2,1,0:T(8,128)(2,1)S(1)} %get-tuple-element.61), channel_id=1, source_target_pairs={{0,1},{1,0},{2,3},{3,2},{4,5},{5,4},{6,7},{7,6},{8,9},{9,8},{10,11... | collective-permute-start | bytes 196616 | tf_op jit(solution)/shard_map/ppermute | solution.py:229
  98.4 5.7 %collective-permute-start.42 = (bf16[4,8,256]{2,1,0:T(8,128)(2,1)S(1)}, bf16[4,8,256]{2,1,0:T(8,128)(2,1)S(1)}, u32[]{:S(2)}, u32[]{:S(2)}) collective-permute-start(bf16[4,8,256]{2,1,0:T(8,128)(2,1)S(1)} %get-tuple-element.75), channel_id=1, source_target_pairs={{0,6},{1,7},{2,4},{3,5},{4,2},{5,3},{6,0},{7,1},{8,14},{9,15},{10,... | collective-permute-start | bytes 49160 | tf_op jit(solution)/shard_map/ppermute | solution.py:234
  100.0 4.8 %collective-permute-start.41 = (bf16[4,8,256]{2,1,0:T(8,128)(2,1)S(1)}, bf16[4,8,256]{2,1,0:T(8,128)(2,1)S(1)}, u32[]{:S(2)}, u32[]{:S(2)}) collective-permute-start(bf16[4,8,256]{2,1,0:T(8,128)(2,1)S(1)} %get-tuple-element.76), channel_id=1, source_target_pairs={{0,4},{1,5},{2,6},{3,7},{4,0},{5,1},{6,2},{7,3},{8,12},{9,13},{10,... | collective-permute-start | bytes 49160 | tf_op jit(solution)/shard_map/ppermute | solution.py:234
  100.8 4.0 %collective-permute-start.40 = (bf16[4,8,256]{2,1,0:T(8,128)(2,1)S(1)}, bf16[4,8,256]{2,1,0:T(8,128)(2,1)S(1)}, u32[]{:S(2)}, u32[]{:S(2)}) collective-permute-start(bf16[4,8,256]{2,1,0:T(8,128)(2,1)S(1)} %get-tuple-element.77), channel_id=1, source_target_pairs={{0,2},{1,3},{2,0},{3,1},{4,6},{5,7},{6,4},{7,5},{8,10},{9,11},{10,... | collective-permute-start | bytes 49160 | tf_op jit(solution)/shard_map/ppermute | solution.py:234
  105.2 1.3 %collective-permute-start.43 = (bf16[4,4,8,256]{3,2,1,0:T(8,128)(2,1)S(1)}, bf16[4,4,8,256]{3,2,1,0:T(8,128)(2,1)S(1)}, u32[]{:S(2)}, u32[]{:S(2)}) collective-permute-start(bf16[4,4,8,256]{3,2,1,0:T(8,128)(2,1)S(1)} %get-tuple-element.64), channel_id=1, source_target_pairs={{0,1},{1,0},{2,3},{3,2},{4,5},{5,4},{6,7},{7,6},{8,9},{9,8},{10,11... | collective-permute-start | bytes 196616 | tf_op jit(solution)/shard_map/ppermute | solution.py:229
  106.5 4.2 %collective-permute-start.44 = (bf16[4,8,256]{2,1,0:T(8,128)(2,1)S(1)}, bf16[4,8,256]{2,1,0:T(8,128)(2,1)S(1)}, u32[]{:S(2)}, u32[]{:S(2)}) collective-permute-start(bf16[4,8,256]{2,1,0:T(8,128)(2,1)S(1)} %get-tuple-element.72), channel_id=1, source_target_pairs={{0,2},{1,3},{2,0},{3,1},{4,6},{5,7},{6,4},{7,5},{8,10},{9,11},{10,... | collective-permute-start | bytes 49160 | tf_op jit(solution)/shard_map/ppermute | solution.py:234
  108.3 5.5 %collective-permute-start.46 = (bf16[4,8,256]{2,1,0:T(8,128)(2,1)S(1)}, bf16[4,8,256]{2,1,0:T(8,128)(2,1)S(1)}, u32[]{:S(2)}, u32[]{:S(2)}) collective-permute-start(bf16[4,8,256]{2,1,0:T(8,128)(2,1)S(1)} %get-tuple-element.73), channel_id=1, source_target_pairs={{0,6},{1,7},{2,4},{3,5},{4,2},{5,3},{6,0},{7,1},{8,14},{9,15},{10,... | collective-permute-start | bytes 49160 | tf_op jit(solution)/shard_map/ppermute | solution.py:234
  109.9 4.6 %collective-permute-start.45 = (bf16[4,8,256]{2,1,0:T(8,128)(2,1)S(1)}, bf16[4,8,256]{2,1,0:T(8,128)(2,1)S(1)}, u32[]{:S(2)}, u32[]{:S(2)}) collective-permute-start(bf16[4,8,256]{2,1,0:T(8,128)(2,1)S(1)} %get-tuple-element.74), channel_id=1, source_target_pairs={{0,4},{1,5},{2,6},{3,7},{4,0},{5,1},{6,2},{7,3},{8,12},{9,13},{10,... | collective-permute-start | bytes 49160 | tf_op jit(solution)/shard_map/ppermute | solution.py:234
  (10 other events, 82.1 us)

commit v9 on v8

--- a/solution.py
+++ b/solution.py
@@ -161,6 +161,13 @@
     walk(plan_ref, list_ref, source_ref.shape[0] - BLOCKS, visit)
 
 
+def far_order(chips):
+    order = list(range(chips))
+    if chips > 3:
+        order[-2:] = [chips - 1, chips - 2]
+    return order
+
+
 def core():
     return lax.axis_index("rows") & 1
 
@@ -175,8 +182,8 @@
 
 def unite(own_ref, other_ref, out_ref, *at, xor=False):
     odd, w = core(), own_ref.shape[-1]
-    for k in range(own_ref.shape[0]):
-        c = chip() ^ k if xor else k
+    for k, j in enumerate(far_order(own_ref.shape[0])):
+        c = chip() ^ j if xor else k
         out_ref[:, spot(2 * c + odd, w)] = own_ref[(k,) + at]
         out_ref[:, spot(2 * c + 1 - odd, w)] = other_ref[(k,) + at]
 
@@ -189,29 +196,49 @@
         other_ref[k] = value_ref[:, spot(2 * k + 1 - odd, w)].astype(other_ref.dtype)
 
 
-def half_of(x_ref, w_ref, s, odd, xor):
+def half_of(x_ref, w_ref, s, odd, xor, start=0):
     at = (s,) if len(x_ref.shape) == 4 else ()
     chips, cols = x_ref.shape[0], x_ref.shape[-1]
-    terms = []
-    for k in range(chips):
-        c = chip() ^ k if xor else k
-        terms.append(times_transposed(x_ref[(k,) + at], w_ref[s, :, spot(2 * c + odd, cols)]))
-    return sum(terms[1:], terms[0])
-
-
-def own_half(x, w, name, xor=False):
+    picked, columns = [], []
+    for k, j in list(enumerate(far_order(chips)))[start:]:
+        c = chip() ^ j if xor else k
+        picked.append(x_ref[(k,) + at])
+        columns.append(w_ref[s, :, spot(2 * c + odd, cols)])
+    return times_transposed(jnp.concatenate(picked, axis=1), jnp.concatenate(columns, axis=1))
+
+
+def own_half(x, w, name, xor=False, first=None):
+    sets, rows = w.shape[:2]
+
+    def body(x_ref, w_ref, *refs):
+        for s in range(sets):
+            got = half_of(x_ref, w_ref, s, core(), xor, len(refs) - 1)
+            refs[-1][s] = got if first is None else got + refs[0][s]
+
+    return call(
+        body,
+        [((sets, x.shape[-2], rows), F32)],
+        [x, pinned(w)] + ([] if first is None else [first]),
+        [VMEM] * (2 if first is None else 3),
+        moved=12 << 20,
+        name=name,
+    )[0]
+
+
+def own_piece(x, w, name):
     sets, rows = w.shape[:2]
 
     def body(x_ref, w_ref, out_ref):
         for s in range(sets):
-            out_ref[s] = half_of(x_ref, w_ref, s, core(), xor)
+            columns = spot(lax.axis_index("rows"), x_ref.shape[-1])
+            out_ref[s] = times_transposed(x_ref[s], w_ref[s, :, columns])
 
     return call(
         body,
         [((sets, x.shape[-2], rows), F32)],
         [x, pinned(w)],
         [VMEM] * 2,
-        moved=12 << 20,
+        moved=4 << 20,
         name=name,
     )[0]
 
@@ -235,7 +262,7 @@
 
 
 def from_chips(piece):
-    return [far(piece(k), k) for k in range(1, lax.axis_size("rows") // 2)]
+    return [far(piece(k), k) for k in far_order(lax.axis_size("rows") // 2)[1:]]
 
 
 def chips_sum(x):
@@ -295,8 +322,8 @@
             return both_halves(*x_refs, w_ref, s, xor=True)
         return times_transposed(x_refs[0][0, s], w_ref[s])
 
-    def leaf_halves(x, w, name):
-        return own_half(x, w, name, xor=True), swap(x)
+    def leaf_halves(x, w, name, first=None):
+        return own_half(x, w, name, True, first), swap(x)
 
     rhs = root_rhs
     if not root_aligned:
@@ -341,7 +368,9 @@
         name="leaf_solve",
     )
     if leaf_aligned:
-        lyb = leaf_halves(far_gather(lyb), leaf_panel, "leaf_update_own")
+        first = own_piece(lyb, leaf_panel, "leaf_update_first")
+        lyb, first = lax.optimization_barrier((far_gather(lyb), first))
+        lyb = leaf_halves(lyb, leaf_panel, "leaf_update_own", first)
     else:
         lyb = (leaf_columns(lyb),)
 

time: 115 us -> 114 us (level)
  starting transfers between devices: 50.3 us -> 44.3 us
  waiting for transfers between devices: 39.1 us -> 43.9 us
    ppermute x30, starting transfers between devices: 44.9 us -> 38.9 us  [far(): return lax.ppermute(x, 'rows', [(i, i ^ 2 * k) for i in range(n)])]
    ppermute x30, waiting for transfers between devices: 25.4 us -> 30.2 us  [far(): return lax.ppermute(x, 'rows', [(i, i ^ 2 * k) for i in range(n)])]
    pallas_call x21 -> x22, Pallas kernels: 21.6 us -> 21.5 us  [call(): pl.pallas_call(body, out_shape=[jax.ShapeDtypeStruct(*o) if isinstance(o,...]
  transfers between devices with their start and end apart: 47 -> 47, of which waited for: 37 -> 39; matrix products, arithmetic and copies ran while one was open for 1% -> 1% of each run, Pallas kernels for 9% -> 9%
where the time goes in v9:
time: 114 us
  starting transfers between devices  44.3 us (39%)
  waiting for transfers between devices  43.9 us (39%)
  Pallas kernels  21.5 us (19%)
  local copies, waits for them, and re-layouts  2.06 us (2%)
  between operations  1.94 us (2%)
    ppermute x30, starting transfers between devices, far(): return lax.ppermute(x, 'rows', [(i, i ^ 2 * k) for i in range(n)])  38.9 us
    ppermute x30, waiting for transfers between devices, far(): return lax.ppermute(x, 'rows', [(i, i ^ 2 * k) for i in range(n)])  30.2 us
    pallas_call x22, Pallas kernels, call(): pl.pallas_call(body, out_shape=[jax.ShapeDtypeStruct(*o) if isinstance(o,...  21.5 us
    ppermute x14, waiting for transfers between devices, swap(): return lax.ppermute(x, 'rows', [(i, i ^ 1) for i in range(n)])  9.46 us
    ppermute x3, waiting for transfers between devices, leaf_sum(): lax.ppermute(b, 'leaf', [(i, (i + k) % n) for i in range(n)]).astype(F32)  4.21 us
    ppermute x3, starting transfers between devices, leaf_sum(): lax.ppermute(b, 'leaf', [(i, (i + k) % n) for i in range(n)]).astype(F32)  3.59 us
  transfers between devices with their start and end apart: 47, of which 39 were waited for; matrix products, arithmetic and copies ran while one was open for 1% of the time, Pallas kernels for 9%

profile of v9, /device:TPU:0, one launch (start us, length us, event | category | flops | bytes accessed | tf_op | source)
XLA Modules:
  0.0 113.9 jit_solution(13477225735507513734)
XLA Ops:
  1.5 4.1 %collective-permute-start.2 = (bf16[4,8,256]{2,1,0:T(8,128)(2,1)S(1)}, bf16[4,8,256]{2,1,0:T(8,128)(2,1)S(1)}, u32[]{:S(2)}, u32[]{:S(2)}) collective-permute-start(bf16[4,8,256]{2,1,0:T(8,128)(2,1)S(1)} %round_rhs.1.refs_0_), channel_id=1, source_target_pairs={{0,4},{1,5},{2,6},{3,7},{4,0},{5,1},{6,2},{7,3},{8,12},{9,13},{10,... | collective-permute-start | bytes 49160 | tf_op jit(solution)/shard_map/ppermute | solution.py:261
  5.6 1.3 %collective-permute-start.1 = (bf16[4,8,256]{2,1,0:T(8,128)(2,1)S(1)}, bf16[4,8,256]{2,1,0:T(8,128)(2,1)S(1)}, u32[]{:S(2)}, u32[]{:S(2)}) collective-permute-start(bf16[4,8,256]{2,1,0:T(8,128)(2,1)S(1)} %round_rhs.1.refs_0_), channel_id=1, source_target_pairs={{0,6},{1,7},{2,4},{3,5},{4,2},{5,3},{6,0},{7,1},{8,14},{9,15},{10,... | collective-permute-start | bytes 49160 | tf_op jit(solution)/shard_map/ppermute | solution.py:261
  8.2 2.2 %prepare.1 = (s32[4,1024]{1,0:T(4,128)S(1)}, s32[33]{0:T(128)S(1)}, s32[1,512]{1,0:T(1,128)S(1)}, s32[5]{0:T(128)S(1)}) custom-call(bf16[4,8,256]{2,1,0:T(8,128)(2,1)S(1)} %round_rhs.1.refs_0_, s32[4,1024]{1,0:T(4,128)S(1)} %copy-done.5, s32[4]{0:T(128)S(1)} %copy-done.10, s32[1,512]{1,0:T(1,128)S(1)} %copy-done.8, s32[1]{0:T(128)S(6)} %copy.21.refs_4_), custom_call_target="tpu_custom_call" | custom-call | bytes 4194304 | tf_op jit(solution)/shard_map/prepare/pallas_call | solution.py:30
  13.1 2.6 %collective-permute-start.6 = (bf16[4,8,256]{2,1,0:T(8,128)(2,1)S(1)}, bf16[4,8,256]{2,1,0:T(8,128)(2,1)S(1)}, u32[]{:S(2)}, u32[]{:S(2)}) collective-permute-start(bf16[4,8,256]{2,1,0:T(8,128)(2,1)S(1)} %get-tuple-element.44.x_ref), channel_id=1, source_target_pairs={{0,4},{1,5},{2,6},{3,7},{4,0},{5,1},{6,2},{7,3},{8,12},{9,13},{10,... | collective-permute-start | bytes 49160 | tf_op jit(solution)/shard_map/ppermute | solution.py:261
  15.6 1.3 %collective-permute-start.5 = (bf16[4,8,256]{2,1,0:T(8,128)(2,1)S(1)}, bf16[4,8,256]{2,1,0:T(8,128)(2,1)S(1)}, u32[]{:S(2)}, u32[]{:S(2)}) collective-permute-start(bf16[4,8,256]{2,1,0:T(8,128)(2,1)S(1)} %get-tuple-element.44.x_ref), channel_id=1, source_target_pairs={{0,6},{1,7},{2,4},{3,5},{4,2},{5,3},{6,0},{7,1},{8,14},{9,15},{10,... | collective-permute-start | bytes 49160 | tf_op jit(solution)/shard_map/ppermute | solution.py:261
  17.8 3.4 %collective-permute-done.5 = bf16[4,8,256]{2,1,0:T(8,128)(2,1)S(1)} collective-permute-done((bf16[4,8,256]{2,1,0:T(8,128)(2,1)S(1)}, bf16[4,8,256]{2,1,0:T(8,128)(2,1)S(1)}, u32[]{:S(2)}, u32[]{:S(2)}) %collective-permute-start.5) | collective-permute-done | bytes 16416 | tf_op jit(solution)/shard_map/ppermute | solution.py:261
  21.3 1.7 %leaf_update_own.1.refs_0_ = f32[4,8,1024]{2,1,0:T(8,128)S(1)} custom-call(bf16[4,4,8,256]{3,2,1,0:T(8,128)(2,1)S(1)} %pad_maximum_fusion.1.x_ref, bf16[4,1024,2048]{2,1,0:T(8,128)(2,1)S(1)} %copy-done, f32[4,8,1024]{2,1,0:T(8,128)S(1)} %leaf_update_first.1.refs_0_), custom_call_target="tpu_custom_call" | custom-call | bytes 12582912 | tf_op jit(solution)/shard_map/leaf_update_own/pallas_call | solution.py:30
  23.1 3.1 %leaf_update.1 = (f32[4,8,512]{2,1,0:T(8,128)S(1)}, bf16[4,8,512]{2,1,0:T(8,128)(2,1)S(1)}, f32[32,8,128]{2,1,0:T(8,128)S(1)}) custom-call(f32[4,8,1024]{2,1,0:T(8,128)S(1)} %leaf_update_own.1.refs_0_, bf16[4,4,8,256]{3,2,1,0:T(8,128)(2,1)S(1)} %collective-permute-done.7.refs_1_, s32[33]{0:T(128)S(1)} %get-tuple-element.41.refs_2_.refs_0_, ...), custom_call_target="tpu_custom_call" | custom-call | tf_op jit(solution)/shard_map/leaf_update/pallas_call | solution.py:30
  28.4 1.4 %collective-permute-start.10 = (bf16[4,8,512]{2,1,0:T(8,128)(2,1)S(1)}, bf16[4,8,512]{2,1,0:T(8,128)(2,1)S(1)}, u32[]{:S(2)}, u32[]{:S(2)}) collective-permute-start(bf16[4,8,512]{2,1,0:T(8,128)(2,1)S(1)} %fusion.1), channel_id=1, source_target_pairs={{0,6},{1,7},{2,4},{3,5},{4,2},{5,3},{6,0},{7,1},{8,14},{9,15},{10,... | collective-permute-start | bytes 98312 | tf_op jit(solution)/shard_map/ppermute | solution.py:261
  29.8 1.4 %collective-permute-start.9 = (bf16[4,8,512]{2,1,0:T(8,128)(2,1)S(1)}, bf16[4,8,512]{2,1,0:T(8,128)(2,1)S(1)}, u32[]{:S(2)}, u32[]{:S(2)}) collective-permute-start(bf16[4,8,512]{2,1,0:T(8,128)(2,1)S(1)} %fusion.1), channel_id=1, source_target_pairs={{0,2},{1,3},{2,0},{3,1},{4,6},{5,7},{6,4},{7,5},{8,10},{9,11},{10,... | collective-permute-start | bytes 98312 | tf_op jit(solution)/shard_map/ppermute | solution.py:261
  31.2 1.4 %collective-permute-done.11 = bf16[4,8,512]{2,1,0:T(8,128)(2,1)S(1)} collective-permute-done((bf16[4,8,512]{2,1,0:T(8,128)(2,1)S(1)}, bf16[4,8,512]{2,1,0:T(8,128)(2,1)S(1)}, u32[]{:S(2)}, u32[]{:S(2)}) %collective-permute-start.11) | collective-permute-done | bytes 32800 | tf_op jit(solution)/shard_map/ppermute | solution.py:261
  32.6 1.6 %collective-permute-done.10 = bf16[4,8,512]{2,1,0:T(8,128)(2,1)S(1)} collective-permute-done((bf16[4,8,512]{2,1,0:T(8,128)(2,1)S(1)}, bf16[4,8,512]{2,1,0:T(8,128)(2,1)S(1)}, u32[]{:S(2)}, u32[]{:S(2)}) %collective-permute-start.10) | collective-permute-done | bytes 32800 | tf_op jit(solution)/shard_map/ppermute | solution.py:261
  36.2 1.4 %collective-permute-start.15 = (bf16[8,512]{1,0:T(8,128)(2,1)S(1)}, bf16[8,512]{1,0:T(8,128)(2,1)S(1)}, u32[]{:S(2)}, u32[]{:S(2)}) collective-permute-start(bf16[8,512]{1,0:T(8,128)(2,1)S(1)} %get-tuple-element.50), channel_id=1, source_target_pairs={{0,4},{1,5},{2,6},{3,7},{4,0},{5,1},{6,2},{7,3},{8,12},{9,13},{10,... | collective-permute-start | bytes 24584 | tf_op jit(solution)/shard_map/ppermute | solution.py:261
  37.6 1.8 %collective-permute-start.14 = (bf16[8,512]{1,0:T(8,128)(2,1)S(1)}, bf16[8,512]{1,0:T(8,128)(2,1)S(1)}, u32[]{:S(2)}, u32[]{:S(2)}) collective-permute-start(bf16[8,512]{1,0:T(8,128)(2,1)S(1)} %get-tuple-element.50), channel_id=1, source_target_pairs={{0,6},{1,7},{2,4},{3,5},{4,2},{5,3},{6,0},{7,1},{8,14},{9,15},{10,... | collective-permute-start | bytes 24584 | tf_op jit(solution)/shard_map/ppermute | solution.py:261
  39.7 1.1 collective-permute-done.15
  40.8 2.4 %collective-permute-done.14 = bf16[8,512]{1,0:T(8,128)(2,1)S(1)} collective-permute-done((bf16[8,512]{1,0:T(8,128)(2,1)S(1)}, bf16[8,512]{1,0:T(8,128)(2,1)S(1)}, u32[]{:S(2)}, u32[]{:S(2)}) %collective-permute-start.14) | collective-permute-done | bytes 8224 | tf_op jit(solution)/shard_map/ppermute | solution.py:261
  44.5 1.4 %parent_update.1 = (f32[4,8,512]{2,1,0:T(8,128)S(1)}, bf16[4,8,512]{2,1,0:T(8,128)(2,1)S(1)}) custom-call(s32[5]{0:T(128)S(1)} %get-tuple-element.42.plan_ref, f32[1,8,512]{2,1,0:T(8,128)S(1)} %parent_update_own.1.part_ref, bf16[4,8,512]{2,1,0:T(8,128)(2,1)S(1)} %collective-permute-done.16.x_ref, bf16[1,512,4096]{2,1,0:T(8,128)(2,1)S(1)} %copy-done.1, ...), custom_call_target="tpu_custom_call" | custom-call | tf_op jit(solution)/shard_map/parent_update/pallas_call | solution.py:30
  46.1 1.0 collective-permute-done.17
  47.1 2.5 %collective-permute-start.20 = (bf16[4,8,512]{2,1,0:T(8,128)(2,1)S(1)}, bf16[4,8,512]{2,1,0:T(8,128)(2,1)S(1)}, u32[]{:S(2)}, u32[]{:S(2)}) collective-permute-start(bf16[4,8,512]{2,1,0:T(8,128)(2,1)S(1)} %fusion.2), channel_id=1, source_target_pairs={{0,24},{8,0},{16,8},{24,16},{1,25},{9,1},{17,9},{25,17},{2,26},{10... | collective-permute-start | bytes 98312 | tf_op jit(solution)/shard_map/ppermute | solution.py:277
  51.2 2.7 %collective-permute-done.19 = bf16[4,8,512]{2,1,0:T(8,128)(2,1)S(1)} collective-permute-done((bf16[4,8,512]{2,1,0:T(8,128)(2,1)S(1)}, bf16[4,8,512]{2,1,0:T(8,128)(2,1)S(1)}, u32[]{:S(2)}, u32[]{:S(2)}) %collective-permute-start.19) | collective-permute-done | bytes 32800 | tf_op jit(solution)/shard_map/ppermute | solution.py:277
  53.9 1.0 collective-permute-done.18
  55.7 1.9 %collective-permute-start.22 = (bf16[4,8,512]{2,1,0:T(8,128)(2,1)S(1)}, bf16[4,8,512]{2,1,0:T(8,128)(2,1)S(1)}, u32[]{:S(2)}, u32[]{:S(2)}) collective-permute-start(bf16[4,8,512]{2,1,0:T(8,128)(2,1)S(1)} %fusion.28), channel_id=1, source_target_pairs={{0,6},{1,7},{2,4},{3,5},{4,2},{5,3},{6,0},{7,1},{8,14},{9,15},{10,... | collective-permute-start | bytes 98312 | tf_op jit(solution)/shard_map/ppermute | solution.py:261
  58.5 1.5 %collective-permute-done.23 = bf16[4,8,512]{2,1,0:T(8,128)(2,1)S(1)} collective-permute-done((bf16[4,8,512]{2,1,0:T(8,128)(2,1)S(1)}, bf16[4,8,512]{2,1,0:T(8,128)(2,1)S(1)}, u32[]{:S(2)}, u32[]{:S(2)}) %collective-permute-start.23) | collective-permute-done | bytes 32800 | tf_op jit(solution)/shard_map/ppermute | solution.py:261
  60.0 1.4 %collective-permute-done.22 = bf16[4,8,512]{2,1,0:T(8,128)(2,1)S(1)} collective-permute-done((bf16[4,8,512]{2,1,0:T(8,128)(2,1)S(1)}, bf16[4,8,512]{2,1,0:T(8,128)(2,1)S(1)}, u32[]{:S(2)}, u32[]{:S(2)}) %collective-permute-start.22) | collective-permute-done | bytes 32800 | tf_op jit(solution)/shard_map/ppermute | solution.py:261
  65.3 1.2 %collective-permute-start.28 = (bf16[4,8,512]{2,1,0:T(8,128)(2,1)S(1)}, bf16[4,8,512]{2,1,0:T(8,128)(2,1)S(1)}, u32[]{:S(2)}, u32[]{:S(2)}) collective-permute-start(bf16[4,8,512]{2,1,0:T(8,128)(2,1)S(1)} %bitcast_convert_fusion.1), channel_id=1, source_target_pairs={{0,4},{1,5},{2,6},{3,7},{4,0},{5,1},{6,2},{7,3},{8,12},{9,13},{10,... | collective-permute-start | bytes 98312 | tf_op jit(solution)/shard_map/ppermute | solution.py:261
  66.5 1.9 %collective-permute-start.27 = (bf16[4,8,512]{2,1,0:T(8,128)(2,1)S(1)}, bf16[4,8,512]{2,1,0:T(8,128)(2,1)S(1)}, u32[]{:S(2)}, u32[]{:S(2)}) collective-permute-start(bf16[4,8,512]{2,1,0:T(8,128)(2,1)S(1)} %bitcast_convert_fusion.1), channel_id=1, source_target_pairs={{0,6},{1,7},{2,4},{3,5},{4,2},{5,3},{6,0},{7,1},{8,14},{9,15},{10,... | collective-permute-start | bytes 98312 | tf_op jit(solution)/shard_map/ppermute | solution.py:261
  68.8 2.1 %collective-permute-done.28 = bf16[4,8,512]{2,1,0:T(8,128)(2,1)S(1)} collective-permute-done((bf16[4,8,512]{2,1,0:T(8,128)(2,1)S(1)}, bf16[4,8,512]{2,1,0:T(8,128)(2,1)S(1)}, u32[]{:S(2)}, u32[]{:S(2)}) %collective-permute-start.28) | collective-permute-done | bytes 32800 | tf_op jit(solution)/shard_map/ppermute | solution.py:261
  70.9 1.3 %collective-permute-done.27 = bf16[4,8,512]{2,1,0:T(8,128)(2,1)S(1)} collective-permute-done((bf16[4,8,512]{2,1,0:T(8,128)(2,1)S(1)}, bf16[4,8,512]{2,1,0:T(8,128)(2,1)S(1)}, u32[]{:S(2)}, u32[]{:S(2)}) %collective-permute-start.27) | collective-permute-done | bytes 32800 | tf_op jit(solution)/shard_map/ppermute | solution.py:261
  72.7 1.2 %collective-permute-done.29.other_ref = bf16[4,8,512]{2,1,0:T(8,128)(2,1)S(1)} collective-permute-done((bf16[4,8,512]{2,1,0:T(8,128)(2,1)S(1)}, bf16[4,8,512]{2,1,0:T(8,128)(2,1)S(1)}, u32[]{:S(2)}, u32[]{:S(2)}) %collective-permute-start.29) | collective-permute-done | bytes 32800 | tf_op jit(solution)/shard_map/ppermute | solution.py:256
  73.9 1.3 %parent_back.1 = (bf16[4,1,8,512]{3,2,1,0:T(8,128)(2,1)S(1)}, f32[40,8,128]{2,1,0:T(8,128)S(1)}, f32[8,128]{1,0:T(8,128)}, bf16[1,8,512]{2,1,0:T(8,128)(2,1)S(1)}) custom-call(s32[5]{0:T(128)S(1)} %get-tuple-element.42.plan_ref, bf16[4,8,512]{2,1,0:T(8,128)(2,1)S(1)} %fusion.own_ref, bf16[4,8,512]{2,1,0:T(8,128)(2,1)S(1)} %collective-permute-done.29.other_ref, ...), custom_call_target="tpu_custom_call" | custom-call | tf_op jit(solution)/shard_map/parent_back/pallas_call | solution.py:30
  77.1 1.9 %collective-permute-start.32 = (bf16[1,8,512]{2,1,0:T(8,128)(2,1)S(1)}, bf16[1,8,512]{2,1,0:T(8,128)(2,1)S(1)}, u32[]{:S(2)}, u32[]{:S(2)}) collective-permute-start(bf16[1,8,512]{2,1,0:T(8,128)(2,1)S(1)} %get-tuple-element.84), channel_id=1, source_target_pairs={{0,6},{1,7},{2,4},{3,5},{4,2},{5,3},{6,0},{7,1},{8,14},{9,15},{10,... | collective-permute-start | bytes 24584 | tf_op jit(solution)/shard_map/ppermute | solution.py:261
  80.0 1.1 collective-permute-done.33.refs_3_
  81.0 1.5 %collective-permute-done.32.refs_2_ = bf16[1,8,512]{2,1,0:T(8,128)(2,1)S(1)} collective-permute-done((bf16[1,8,512]{2,1,0:T(8,128)(2,1)S(1)}, bf16[1,8,512]{2,1,0:T(8,128)(2,1)S(1)}, u32[]{:S(2)}, u32[]{:S(2)}) %collective-permute-start.32) | collective-permute-done | bytes 8224 | tf_op jit(solution)/shard_map/ppermute | solution.py:261
  84.3 1.4 %collective-permute-start.37 = (bf16[4,8,512]{2,1,0:T(8,128)(2,1)S(1)}, bf16[4,8,512]{2,1,0:T(8,128)(2,1)S(1)}, u32[]{:S(2)}, u32[]{:S(2)}) collective-permute-start(bf16[4,8,512]{2,1,0:T(8,128)(2,1)S(1)} %bitcast_convert_fusion), channel_id=1, source_target_pairs={{0,4},{1,5},{2,6},{3,7},{4,0},{5,1},{6,2},{7,3},{8,12},{9,13},{10,... | collective-permute-start | bytes 98312 | tf_op jit(solution)/shard_map/ppermute | solution.py:261
  85.7 1.9 %collective-permute-start.36 = (bf16[4,8,512]{2,1,0:T(8,128)(2,1)S(1)}, bf16[4,8,512]{2,1,0:T(8,128)(2,1)S(1)}, u32[]{:S(2)}, u32[]{:S(2)}) collective-permute-start(bf16[4,8,512]{2,1,0:T(8,128)(2,1)S(1)} %bitcast_convert_fusion), channel_id=1, source_target_pairs={{0,6},{1,7},{2,4},{3,5},{4,2},{5,3},{6,0},{7,1},{8,14},{9,15},{10,... | collective-permute-start | bytes 98312 | tf_op jit(solution)/shard_map/ppermute | solution.py:261
  87.8 2.0 %collective-permute-done.37 = bf16[4,8,512]{2,1,0:T(8,128)(2,1)S(1)} collective-permute-done((bf16[4,8,512]{2,1,0:T(8,128)(2,1)S(1)}, bf16[4,8,512]{2,1,0:T(8,128)(2,1)S(1)}, u32[]{:S(2)}, u32[]{:S(2)}) %collective-permute-start.37) | collective-permute-done | bytes 32800 | tf_op jit(solution)/shard_map/ppermute | solution.py:261
  89.8 1.7 %collective-permute-done.36 = bf16[4,8,512]{2,1,0:T(8,128)(2,1)S(1)} collective-permute-done((bf16[4,8,512]{2,1,0:T(8,128)(2,1)S(1)}, bf16[4,8,512]{2,1,0:T(8,128)(2,1)S(1)}, u32[]{:S(2)}, u32[]{:S(2)}) %collective-permute-start.36) | collective-permute-done | bytes 32800 | tf_op jit(solution)/shard_map/ppermute | solution.py:261
  91.9 1.2 %collective-permute-done.38.refs_3_ = bf16[4,8,512]{2,1,0:T(8,128)(2,1)S(1)} collective-permute-done((bf16[4,8,512]{2,1,0:T(8,128)(2,1)S(1)}, bf16[4,8,512]{2,1,0:T(8,128)(2,1)S(1)}, u32[]{:S(2)}, u32[]{:S(2)}) %collective-permute-start.38) | collective-permute-done | bytes 32800 | tf_op jit(solution)/shard_map/ppermute | solution.py:256
  93.1 2.6 %leaf_back.1 = (bf16[4,4,8,256]{3,2,1,0:T(8,128)(2,1)S(1)}, f32[8,512]{1,0:T(8,128)S(1)}, bf16[4,8,1024]{2,1,0:T(8,128)(2,1)S(1)}) custom-call(s32[33]{0:T(128)S(1)} %get-tuple-element.41.refs_2_.refs_0_, f32[4,8,512]{2,1,0:T(8,128)S(1)} %get-tuple-element.75.refs_1_, bf16[4,8,512]{2,1,0:T(8,128)(2,1)S(1)} %get-tuple-element.74.refs_2_, ...), custom_call_target="tpu_custom_call" | custom-call | tf_op jit(solution)/shard_map/leaf_back/pallas_call | solution.py:30
  95.8 1.2 %leaf_back_own.1 = f32[4,4,8,256]{3,2,1,0:T(8,128)S(1)} custom-call(bf16[4,8,1024]{2,1,0:T(8,128)(2,1)S(1)} %get-tuple-element.64.x_ref, bf16[4,1024,2048]{2,1,0:T(8,128)(2,1)S(1)} %copy-done), custom_call_target="tpu_custom_call" | custom-call | bytes 12582912 | tf_op jit(solution)/shard_map/leaf_back_own/pallas_call | solution.py:30
  97.7 1.9 %collective-permute-start.41 = (bf16[4,8,256]{2,1,0:T(8,128)(2,1)S(1)}, bf16[4,8,256]{2,1,0:T(8,128)(2,1)S(1)}, u32[]{:S(2)}, u32[]{:S(2)}) collective-permute-start(bf16[4,8,256]{2,1,0:T(8,128)(2,1)S(1)} %get-tuple-element.80), channel_id=1, source_target_pairs={{0,6},{1,7},{2,4},{3,5},{4,2},{5,3},{6,0},{7,1},{8,14},{9,15},{10,... | collective-permute-start | bytes 49160 | tf_op jit(solution)/shard_map/ppermute | solution.py:261
  99.6 1.0 collective-permute-start.40
  100.6 1.2 %collective-permute-done.42.refs_3_ = bf16[4,8,256]{2,1,0:T(8,128)(2,1)S(1)} collective-permute-done((bf16[4,8,256]{2,1,0:T(8,128)(2,1)S(1)}, bf16[4,8,256]{2,1,0:T(8,128)(2,1)S(1)}, u32[]{:S(2)}, u32[]{:S(2)}) %collective-permute-start.42) | collective-permute-done | bytes 16416 | tf_op jit(solution)/shard_map/ppermute | solution.py:261
  101.8 1.5 %collective-permute-done.41.refs_2_ = bf16[4,8,256]{2,1,0:T(8,128)(2,1)S(1)} collective-permute-done((bf16[4,8,256]{2,1,0:T(8,128)(2,1)S(1)}, bf16[4,8,256]{2,1,0:T(8,128)(2,1)S(1)}, u32[]{:S(2)}, u32[]{:S(2)}) %collective-permute-start.41) | collective-permute-done | bytes 16416 | tf_op jit(solution)/shard_map/ppermute | solution.py:261
  105.1 1.0 collective-permute-start.44
  106.1 1.6 %collective-permute-start.46 = (bf16[4,8,256]{2,1,0:T(8,128)(2,1)S(1)}, bf16[4,8,256]{2,1,0:T(8,128)(2,1)S(1)}, u32[]{:S(2)}, u32[]{:S(2)}) collective-permute-start(bf16[4,8,256]{2,1,0:T(8,128)(2,1)S(1)} %get-tuple-element.77), channel_id=1, source_target_pairs={{0,4},{1,5},{2,6},{3,7},{4,0},{5,1},{6,2},{7,3},{8,12},{9,13},{10,... | collective-permute-start | bytes 49160 | tf_op jit(solution)/shard_map/ppermute | solution.py:261
  107.7 1.9 %collective-permute-start.45 = (bf16[4,8,256]{2,1,0:T(8,128)(2,1)S(1)}, bf16[4,8,256]{2,1,0:T(8,128)(2,1)S(1)}, u32[]{:S(2)}, u32[]{:S(2)}) collective-permute-start(bf16[4,8,256]{2,1,0:T(8,128)(2,1)S(1)} %get-tuple-element.78), channel_id=1, source_target_pairs={{0,6},{1,7},{2,4},{3,5},{4,2},{5,3},{6,0},{7,1},{8,14},{9,15},{10,... | collective-permute-start | bytes 49160 | tf_op jit(solution)/shard_map/ppermute | solution.py:261
  110.8 2.5 %collective-permute-done.45 = bf16[4,8,256]{2,1,0:T(8,128)(2,1)S(1)} collective-permute-done((bf16[4,8,256]{2,1,0:T(8,128)(2,1)S(1)}, bf16[4,8,256]{2,1,0:T(8,128)(2,1)S(1)}, u32[]{:S(2)}, u32[]{:S(2)}) %collective-permute-start.45) | collective-permute-done | bytes 16416 | tf_op jit(solution)/shard_map/ppermute | solution.py:261
  (108 shorter events, 28.1 us)
Async XLA Ops:
  1.5 8.9 %collective-permute-start.2 = (bf16[4,8,256]{2,1,0:T(8,128)(2,1)S(1)}, bf16[4,8,256]{2,1,0:T(8,128)(2,1)S(1)}, u32[]{:S(2)}, u32[]{:S(2)}) collective-permute-start(bf16[4,8,256]{2,1,0:T(8,128)(2,1)S(1)} %round_rhs.1.refs_0_), channel_id=1, source_target_pairs={{0,4},{1,5},{2,6},{3,7},{4,0},{5,1},{6,2},{7,3},{8,12},{9,13},{10,... | collective-permute-start | bytes 49160 | tf_op jit(solution)/shard_map/ppermute | solution.py:261
  5.6 5.5 %collective-permute-start.1 = (bf16[4,8,256]{2,1,0:T(8,128)(2,1)S(1)}, bf16[4,8,256]{2,1,0:T(8,128)(2,1)S(1)}, u32[]{:S(2)}, u32[]{:S(2)}) collective-permute-start(bf16[4,8,256]{2,1,0:T(8,128)(2,1)S(1)} %round_rhs.1.refs_0_), channel_id=1, source_target_pairs={{0,6},{1,7},{2,4},{3,5},{4,2},{5,3},{6,0},{7,1},{8,14},{9,15},{10,... | collective-permute-start | bytes 49160 | tf_op jit(solution)/shard_map/ppermute | solution.py:261
  6.9 4.2 %collective-permute-start = (bf16[4,8,256]{2,1,0:T(8,128)(2,1)S(1)}, bf16[4,8,256]{2,1,0:T(8,128)(2,1)S(1)}, u32[]{:S(2)}, u32[]{:S(2)}) collective-permute-start(bf16[4,8,256]{2,1,0:T(8,128)(2,1)S(1)} %round_rhs.1.refs_0_), channel_id=1, source_target_pairs={{0,2},{1,3},{2,0},{3,1},{4,6},{5,7},{6,4},{7,5},{8,10},{9,11},{10,... | collective-permute-start | bytes 49160 | tf_op jit(solution)/shard_map/ppermute | solution.py:261
  11.1 1.3 %collective-permute-start.3 = (bf16[4,4,8,256]{3,2,1,0:T(8,128)(2,1)S(1)}, bf16[4,4,8,256]{3,2,1,0:T(8,128)(2,1)S(1)}, u32[]{:S(2)}, u32[]{:S(2)}) collective-permute-start(bf16[4,4,8,256]{3,2,1,0:T(8,128)(2,1)S(1)} %pad_maximum_fusion.x_ref), channel_id=1, source_target_pairs={{0,1},{1,0},{2,3},{3,2},{4,5},{5,4},{6,7},{7,6},{8,9},{9,8},{10,11... | collective-permute-start | bytes 196616 | tf_op jit(solution)/shard_map/ppermute | solution.py:256
  13.1 4.7 %collective-permute-start.6 = (bf16[4,8,256]{2,1,0:T(8,128)(2,1)S(1)}, bf16[4,8,256]{2,1,0:T(8,128)(2,1)S(1)}, u32[]{:S(2)}, u32[]{:S(2)}) collective-permute-start(bf16[4,8,256]{2,1,0:T(8,128)(2,1)S(1)} %get-tuple-element.44.x_ref), channel_id=1, source_target_pairs={{0,4},{1,5},{2,6},{3,7},{4,0},{5,1},{6,2},{7,3},{8,12},{9,13},{10,... | collective-permute-start | bytes 49160 | tf_op jit(solution)/shard_map/ppermute | solution.py:261
  15.6 5.5 %collective-permute-start.5 = (bf16[4,8,256]{2,1,0:T(8,128)(2,1)S(1)}, bf16[4,8,256]{2,1,0:T(8,128)(2,1)S(1)}, u32[]{:S(2)}, u32[]{:S(2)}) collective-permute-start(bf16[4,8,256]{2,1,0:T(8,128)(2,1)S(1)} %get-tuple-element.44.x_ref), channel_id=1, source_target_pairs={{0,6},{1,7},{2,4},{3,5},{4,2},{5,3},{6,0},{7,1},{8,14},{9,15},{10,... | collective-permute-start | bytes 49160 | tf_op jit(solution)/shard_map/ppermute | solution.py:261
  17.0 4.2 %collective-permute-start.4 = (bf16[4,8,256]{2,1,0:T(8,128)(2,1)S(1)}, bf16[4,8,256]{2,1,0:T(8,128)(2,1)S(1)}, u32[]{:S(2)}, u32[]{:S(2)}) collective-permute-start(bf16[4,8,256]{2,1,0:T(8,128)(2,1)S(1)} %get-tuple-element.44.x_ref), channel_id=1, source_target_pairs={{0,2},{1,3},{2,0},{3,1},{4,6},{5,7},{6,4},{7,5},{8,10},{9,11},{10,... | collective-permute-start | bytes 49160 | tf_op jit(solution)/shard_map/ppermute | solution.py:261
  21.2 1.8 %collective-permute-start.7 = (bf16[4,4,8,256]{3,2,1,0:T(8,128)(2,1)S(1)}, bf16[4,4,8,256]{3,2,1,0:T(8,128)(2,1)S(1)}, u32[]{:S(2)}, u32[]{:S(2)}) collective-permute-start(bf16[4,4,8,256]{3,2,1,0:T(8,128)(2,1)S(1)} %pad_maximum_fusion.1.x_ref), channel_id=1, source_target_pairs={{0,1},{1,0},{2,3},{3,2},{4,5},{5,4},{6,7},{7,6},{8,9},{9,8},{10,11... | collective-permute-start | bytes 196616 | tf_op jit(solution)/shard_map/ppermute | solution.py:256
  26.2 1.4 %collective-permute-start.8 = (bf16[4,8,512]{2,1,0:T(8,128)(2,1)S(1)}, bf16[4,8,512]{2,1,0:T(8,128)(2,1)S(1)}, u32[]{:S(2)}, u32[]{:S(2)}) collective-permute-start(bf16[4,8,512]{2,1,0:T(8,128)(2,1)S(1)} %get-tuple-element.49), channel_id=1, source_target_pairs={{0,1},{1,0},{2,3},{3,2},{4,5},{5,4},{6,7},{7,6},{8,9},{9,8},{10,11... | collective-permute-start | bytes 98312 | tf_op jit(solution)/shard_map/ppermute | solution.py:256
  27.6 5.0 %collective-permute-start.11 = (bf16[4,8,512]{2,1,0:T(8,128)(2,1)S(1)}, bf16[4,8,512]{2,1,0:T(8,128)(2,1)S(1)}, u32[]{:S(2)}, u32[]{:S(2)}) collective-permute-start(bf16[4,8,512]{2,1,0:T(8,128)(2,1)S(1)} %fusion.1), channel_id=1, source_target_pairs={{0,4},{1,5},{2,6},{3,7},{4,0},{5,1},{6,2},{7,3},{8,12},{9,13},{10,... | collective-permute-start | bytes 98312 | tf_op jit(solution)/shard_map/ppermute | solution.py:261
  28.4 5.8 %collective-permute-start.10 = (bf16[4,8,512]{2,1,0:T(8,128)(2,1)S(1)}, bf16[4,8,512]{2,1,0:T(8,128)(2,1)S(1)}, u32[]{:S(2)}, u32[]{:S(2)}) collective-permute-start(bf16[4,8,512]{2,1,0:T(8,128)(2,1)S(1)} %fusion.1), channel_id=1, source_target_pairs={{0,6},{1,7},{2,4},{3,5},{4,2},{5,3},{6,0},{7,1},{8,14},{9,15},{10,... | collective-permute-start | bytes 98312 | tf_op jit(solution)/shard_map/ppermute | solution.py:261
  29.8 4.5 %collective-permute-start.9 = (bf16[4,8,512]{2,1,0:T(8,128)(2,1)S(1)}, bf16[4,8,512]{2,1,0:T(8,128)(2,1)S(1)}, u32[]{:S(2)}, u32[]{:S(2)}) collective-permute-start(bf16[4,8,512]{2,1,0:T(8,128)(2,1)S(1)} %fusion.1), channel_id=1, source_target_pairs={{0,2},{1,3},{2,0},{3,1},{4,6},{5,7},{6,4},{7,5},{8,10},{9,11},{10,... | collective-permute-start | bytes 98312 | tf_op jit(solution)/shard_map/ppermute | solution.py:261
  34.3 1.3 %collective-permute-start.12 = (bf16[4,8,512]{2,1,0:T(8,128)(2,1)S(1)}, bf16[4,8,512]{2,1,0:T(8,128)(2,1)S(1)}, u32[]{:S(2)}, u32[]{:S(2)}) collective-permute-start(bf16[4,8,512]{2,1,0:T(8,128)(2,1)S(1)} %add_convert_fusion.1.x_ref), channel_id=1, source_target_pairs={{0,1},{1,0},{2,3},{3,2},{4,5},{5,4},{6,7},{7,6},{8,9},{9,8},{10,11... | collective-permute-start | bytes 98312 | tf_op jit(solution)/shard_map/ppermute | solution.py:256
  36.2 4.6 %collective-permute-start.15 = (bf16[8,512]{1,0:T(8,128)(2,1)S(1)}, bf16[8,512]{1,0:T(8,128)(2,1)S(1)}, u32[]{:S(2)}, u32[]{:S(2)}) collective-permute-start(bf16[8,512]{1,0:T(8,128)(2,1)S(1)} %get-tuple-element.50), channel_id=1, source_target_pairs={{0,4},{1,5},{2,6},{3,7},{4,0},{5,1},{6,2},{7,3},{8,12},{9,13},{10,... | collective-permute-start | bytes 24584 | tf_op jit(solution)/shard_map/ppermute | solution.py:261
  37.6 5.5 %collective-permute-start.14 = (bf16[8,512]{1,0:T(8,128)(2,1)S(1)}, bf16[8,512]{1,0:T(8,128)(2,1)S(1)}, u32[]{:S(2)}, u32[]{:S(2)}) collective-permute-start(bf16[8,512]{1,0:T(8,128)(2,1)S(1)} %get-tuple-element.50), channel_id=1, source_target_pairs={{0,6},{1,7},{2,4},{3,5},{4,2},{5,3},{6,0},{7,1},{8,14},{9,15},{10,... | collective-permute-start | bytes 24584 | tf_op jit(solution)/shard_map/ppermute | solution.py:261
  39.4 3.7 %collective-permute-start.13 = (bf16[8,512]{1,0:T(8,128)(2,1)S(1)}, bf16[8,512]{1,0:T(8,128)(2,1)S(1)}, u32[]{:S(2)}, u32[]{:S(2)}) collective-permute-start(bf16[8,512]{1,0:T(8,128)(2,1)S(1)} %get-tuple-element.50), channel_id=1, source_target_pairs={{0,2},{1,3},{2,0},{3,1},{4,6},{5,7},{6,4},{7,5},{8,10},{9,11},{10,... | collective-permute-start | bytes 24584 | tf_op jit(solution)/shard_map/ppermute | solution.py:261
  43.2 18.7 %copy-start.4 = (bf16[512,4096]{1,0:T(8,128)(2,1)S(1)}, bf16[512,4096]{1,0:T(8,128)(2,1)}, u32[]{:S(2)}) copy-start(bf16[512,4096]{1,0:T(8,128)(2,1)} %param.23) | copy-start | bytes 12582916
  43.2 1.3 %collective-permute-start.16 = (bf16[4,8,512]{2,1,0:T(8,128)(2,1)S(1)}, bf16[4,8,512]{2,1,0:T(8,128)(2,1)S(1)}, u32[]{:S(2)}, u32[]{:S(2)}) collective-permute-start(bf16[4,8,512]{2,1,0:T(8,128)(2,1)S(1)} %pad_maximum_fusion.2.x_ref), channel_id=1, source_target_pairs={{0,1},{1,0},{2,3},{3,2},{4,5},{5,4},{6,7},{7,6},{8,9},{9,8},{10,11... | collective-permute-start | bytes 98312 | tf_op jit(solution)/shard_map/ppermute | solution.py:256
  45.8 1.3 %collective-permute-start.17 = (bf16[4,8,512]{2,1,0:T(8,128)(2,1)S(1)}, bf16[4,8,512]{2,1,0:T(8,128)(2,1)S(1)}, u32[]{:S(2)}, u32[]{:S(2)}) collective-permute-start(bf16[4,8,512]{2,1,0:T(8,128)(2,1)S(1)} %get-tuple-element.55), channel_id=1, source_target_pairs={{0,1},{1,0},{2,3},{3,2},{4,5},{5,4},{6,7},{7,6},{8,9},{9,8},{10,11... | collective-permute-start | bytes 98312 | tf_op jit(solution)/shard_map/ppermute | solution.py:256
  47.1 4.1 %collective-permute-start.20 = (bf16[4,8,512]{2,1,0:T(8,128)(2,1)S(1)}, bf16[4,8,512]{2,1,0:T(8,128)(2,1)S(1)}, u32[]{:S(2)}, u32[]{:S(2)}) collective-permute-start(bf16[4,8,512]{2,1,0:T(8,128)(2,1)S(1)} %fusion.2), channel_id=1, source_target_pairs={{0,24},{8,0},{16,8},{24,16},{1,25},{9,1},{17,9},{25,17},{2,26},{10... | collective-permute-start | bytes 98312 | tf_op jit(solution)/shard_map/ppermute | solution.py:277
  49.6 4.3 %collective-permute-start.19 = (bf16[4,8,512]{2,1,0:T(8,128)(2,1)S(1)}, bf16[4,8,512]{2,1,0:T(8,128)(2,1)S(1)}, u32[]{:S(2)}, u32[]{:S(2)}) collective-permute-start(bf16[4,8,512]{2,1,0:T(8,128)(2,1)S(1)} %fusion.2), channel_id=1, source_target_pairs={{0,16},{8,24},{16,0},{24,8},{1,17},{9,25},{17,1},{25,9},{2,18},{10... | collective-permute-start | bytes 98312 | tf_op jit(solution)/shard_map/ppermute | solution.py:277
  50.1 4.8 %collective-permute-start.18 = (bf16[4,8,512]{2,1,0:T(8,128)(2,1)S(1)}, bf16[4,8,512]{2,1,0:T(8,128)(2,1)S(1)}, u32[]{:S(2)}, u32[]{:S(2)}) collective-permute-start(bf16[4,8,512]{2,1,0:T(8,128)(2,1)S(1)} %fusion.2), channel_id=1, source_target_pairs={{0,8},{8,16},{16,24},{24,0},{1,9},{9,17},{17,25},{25,1},{2,10},{10... | collective-permute-start | bytes 98312 | tf_op jit(solution)/shard_map/ppermute | solution.py:277
  54.9 5.1 %collective-permute-start.23 = (bf16[4,8,512]{2,1,0:T(8,128)(2,1)S(1)}, bf16[4,8,512]{2,1,0:T(8,128)(2,1)S(1)}, u32[]{:S(2)}, u32[]{:S(2)}) collective-permute-start(bf16[4,8,512]{2,1,0:T(8,128)(2,1)S(1)} %fusion.28), channel_id=1, source_target_pairs={{0,4},{1,5},{2,6},{3,7},{4,0},{5,1},{6,2},{7,3},{8,12},{9,13},{10,... | collective-permute-start | bytes 98312 | tf_op jit(solution)/shard_map/ppermute | solution.py:261
  55.7 5.7 %collective-permute-start.22 = (bf16[4,8,512]{2,1,0:T(8,128)(2,1)S(1)}, bf16[4,8,512]{2,1,0:T(8,128)(2,1)S(1)}, u32[]{:S(2)}, u32[]{:S(2)}) collective-permute-start(bf16[4,8,512]{2,1,0:T(8,128)(2,1)S(1)} %fusion.28), channel_id=1, source_target_pairs={{0,6},{1,7},{2,4},{3,5},{4,2},{5,3},{6,0},{7,1},{8,14},{9,15},{10,... | collective-permute-start | bytes 98312 | tf_op jit(solution)/shard_map/ppermute | solution.py:261
  57.6 4.1 %collective-permute-start.21 = (bf16[4,8,512]{2,1,0:T(8,128)(2,1)S(1)}, bf16[4,8,512]{2,1,0:T(8,128)(2,1)S(1)}, u32[]{:S(2)}, u32[]{:S(2)}) collective-permute-start(bf16[4,8,512]{2,1,0:T(8,128)(2,1)S(1)} %fusion.28), channel_id=1, source_target_pairs={{0,2},{1,3},{2,0},{3,1},{4,6},{5,7},{6,4},{7,5},{8,10},{9,11},{10,... | collective-permute-start | bytes 98312 | tf_op jit(solution)/shard_map/ppermute | solution.py:261
  61.8 1.3 %collective-permute-start.24 = (bf16[4,8,512]{2,1,0:T(8,128)(2,1)S(1)}, bf16[4,8,512]{2,1,0:T(8,128)(2,1)S(1)}, u32[]{:S(2)}, u32[]{:S(2)}) collective-permute-start(bf16[4,8,512]{2,1,0:T(8,128)(2,1)S(1)} %add_convert_fusion.x_ref), channel_id=1, source_target_pairs={{0,1},{1,0},{2,3},{3,2},{4,5},{5,4},{6,7},{7,6},{8,9},{9,8},{10,11... | collective-permute-start | bytes 98312 | tf_op jit(solution)/shard_map/ppermute | solution.py:256
  64.0 1.2 %collective-permute-start.25 = (bf16[4,1,8,512]{3,2,0,1:T(8,128)(2,1)S(1)}, bf16[4,1,8,512]{3,2,0,1:T(8,128)(2,1)S(1)}, u32[]{:S(2)}, u32[]{:S(2)}) collective-permute-start(bf16[4,1,8,512]{3,2,0,1:T(8,128)(2,1)S(1)} %bitcast.81), channel_id=1, source_target_pairs={{0,1},{1,0},{2,3},{3,2},{4,5},{5,4},{6,7},{7,6},{8,9},{9,8},{10,11... | collective-permute-start | bytes 98312 | tf_op jit(solution)/shard_map/ppermute | solution.py:256
  65.3 5.6 %collective-permute-start.28 = (bf16[4,8,512]{2,1,0:T(8,128)(2,1)S(1)}, bf16[4,8,512]{2,1,0:T(8,128)(2,1)S(1)}, u32[]{:S(2)}, u32[]{:S(2)}) collective-permute-start(bf16[4,8,512]{2,1,0:T(8,128)(2,1)S(1)} %bitcast_convert_fusion.1), channel_id=1, source_target_pairs={{0,4},{1,5},{2,6},{3,7},{4,0},{5,1},{6,2},{7,3},{8,12},{9,13},{10,... | collective-permute-start | bytes 98312 | tf_op jit(solution)/shard_map/ppermute | solution.py:261
  66.5 5.7 %collective-permute-start.27 = (bf16[4,8,512]{2,1,0:T(8,128)(2,1)S(1)}, bf16[4,8,512]{2,1,0:T(8,128)(2,1)S(1)}, u32[]{:S(2)}, u32[]{:S(2)}) collective-permute-start(bf16[4,8,512]{2,1,0:T(8,128)(2,1)S(1)} %bitcast_convert_fusion.1), channel_id=1, source_target_pairs={{0,6},{1,7},{2,4},{3,5},{4,2},{5,3},{6,0},{7,1},{8,14},{9,15},{10,... | collective-permute-start | bytes 98312 | tf_op jit(solution)/shard_map/ppermute | solution.py:261
  68.4 4.2 %collective-permute-start.26 = (bf16[4,8,512]{2,1,0:T(8,128)(2,1)S(1)}, bf16[4,8,512]{2,1,0:T(8,128)(2,1)S(1)}, u32[]{:S(2)}, u32[]{:S(2)}) collective-permute-start(bf16[4,8,512]{2,1,0:T(8,128)(2,1)S(1)} %bitcast_convert_fusion.1), channel_id=1, source_target_pairs={{0,2},{1,3},{2,0},{3,1},{4,6},{5,7},{6,4},{7,5},{8,10},{9,11},{10,... | collective-permute-start | bytes 98312 | tf_op jit(solution)/shard_map/ppermute | solution.py:261
  72.6 1.3 %collective-permute-start.29 = (bf16[4,8,512]{2,1,0:T(8,128)(2,1)S(1)}, bf16[4,8,512]{2,1,0:T(8,128)(2,1)S(1)}, u32[]{:S(2)}, u32[]{:S(2)}) collective-permute-start(bf16[4,8,512]{2,1,0:T(8,128)(2,1)S(1)} %fusion.own_ref), channel_id=1, source_target_pairs={{0,1},{1,0},{2,3},{3,2},{4,5},{5,4},{6,7},{7,6},{8,9},{9,8},{10,11... | collective-permute-start | bytes 98312 | tf_op jit(solution)/shard_map/ppermute | solution.py:256
  75.2 1.2 %collective-permute-start.30 = (bf16[4,1,8,512]{3,2,1,0:T(8,128)(2,1)S(1)}, bf16[4,1,8,512]{3,2,1,0:T(8,128)(2,1)S(1)}, u32[]{:S(2)}, u32[]{:S(2)}) collective-permute-start(bf16[4,1,8,512]{3,2,1,0:T(8,128)(2,1)S(1)} %get-tuple-element.59), channel_id=1, source_target_pairs={{0,1},{1,0},{2,3},{3,2},{4,5},{5,4},{6,7},{7,6},{8,9},{9,8},{10,11... | collective-permute-start | bytes 98312 | tf_op jit(solution)/shard_map/ppermute | solution.py:256
  76.4 4.6 %collective-permute-start.33 = (bf16[1,8,512]{2,1,0:T(8,128)(2,1)S(1)}, bf16[1,8,512]{2,1,0:T(8,128)(2,1)S(1)}, u32[]{:S(2)}, u32[]{:S(2)}) collective-permute-start(bf16[1,8,512]{2,1,0:T(8,128)(2,1)S(1)} %get-tuple-element.83), channel_id=1, source_target_pairs={{0,4},{1,5},{2,6},{3,7},{4,0},{5,1},{6,2},{7,3},{8,12},{9,13},{10,... | collective-permute-start | bytes 24584 | tf_op jit(solution)/shard_map/ppermute | solution.py:261
  77.1 5.4 %collective-permute-start.32 = (bf16[1,8,512]{2,1,0:T(8,128)(2,1)S(1)}, bf16[1,8,512]{2,1,0:T(8,128)(2,1)S(1)}, u32[]{:S(2)}, u32[]{:S(2)}) collective-permute-start(bf16[1,8,512]{2,1,0:T(8,128)(2,1)S(1)} %get-tuple-element.84), channel_id=1, source_target_pairs={{0,6},{1,7},{2,4},{3,5},{4,2},{5,3},{6,0},{7,1},{8,14},{9,15},{10,... | collective-permute-start | bytes 24584 | tf_op jit(solution)/shard_map/ppermute | solution.py:261
  79.0 3.7 %collective-permute-start.31 = (bf16[1,8,512]{2,1,0:T(8,128)(2,1)S(1)}, bf16[1,8,512]{2,1,0:T(8,128)(2,1)S(1)}, u32[]{:S(2)}, u32[]{:S(2)}) collective-permute-start(bf16[1,8,512]{2,1,0:T(8,128)(2,1)S(1)} %get-tuple-element.85), channel_id=1, source_target_pairs={{0,2},{1,3},{2,0},{3,1},{4,6},{5,7},{6,4},{7,5},{8,10},{9,11},{10,... | collective-permute-start | bytes 24584 | tf_op jit(solution)/shard_map/ppermute | solution.py:261
  83.0 1.2 %collective-permute-start.34 = (bf16[4,1,8,512]{3,2,0,1:T(8,128)(2,1)S(1)}, bf16[4,1,8,512]{3,2,0,1:T(8,128)(2,1)S(1)}, u32[]{:S(2)}, u32[]{:S(2)}) collective-permute-start(bf16[4,1,8,512]{3,2,0,1:T(8,128)(2,1)S(1)} %bitcast.80), channel_id=1, source_target_pairs={{0,1},{1,0},{2,3},{3,2},{4,5},{5,4},{6,7},{7,6},{8,9},{9,8},{10,11... | collective-permute-start | bytes 98312 | tf_op jit(solution)/shard_map/ppermute | solution.py:256
  84.3 5.5 %collective-permute-start.37 = (bf16[4,8,512]{2,1,0:T(8,128)(2,1)S(1)}, bf16[4,8,512]{2,1,0:T(8,128)(2,1)S(1)}, u32[]{:S(2)}, u32[]{:S(2)}) collective-permute-start(bf16[4,8,512]{2,1,0:T(8,128)(2,1)S(1)} %bitcast_convert_fusion), channel_id=1, source_target_pairs={{0,4},{1,5},{2,6},{3,7},{4,0},{5,1},{6,2},{7,3},{8,12},{9,13},{10,... | collective-permute-start | bytes 98312 | tf_op jit(solution)/shard_map/ppermute | solution.py:261
  85.7 5.7 %collective-permute-start.36 = (bf16[4,8,512]{2,1,0:T(8,128)(2,1)S(1)}, bf16[4,8,512]{2,1,0:T(8,128)(2,1)S(1)}, u32[]{:S(2)}, u32[]{:S(2)}) collective-permute-start(bf16[4,8,512]{2,1,0:T(8,128)(2,1)S(1)} %bitcast_convert_fusion), channel_id=1, source_target_pairs={{0,6},{1,7},{2,4},{3,5},{4,2},{5,3},{6,0},{7,1},{8,14},{9,15},{10,... | collective-permute-start | bytes 98312 | tf_op jit(solution)/shard_map/ppermute | solution.py:261
  87.7 4.1 %collective-permute-start.35 = (bf16[4,8,512]{2,1,0:T(8,128)(2,1)S(1)}, bf16[4,8,512]{2,1,0:T(8,128)(2,1)S(1)}, u32[]{:S(2)}, u32[]{:S(2)}) collective-permute-start(bf16[4,8,512]{2,1,0:T(8,128)(2,1)S(1)} %bitcast_convert_fusion), channel_id=1, source_target_pairs={{0,2},{1,3},{2,0},{3,1},{4,6},{5,7},{6,4},{7,5},{8,10},{9,11},{10,... | collective-permute-start | bytes 98312 | tf_op jit(solution)/shard_map/ppermute | solution.py:261
  91.8 1.3 %collective-permute-start.38 = (bf16[4,8,512]{2,1,0:T(8,128)(2,1)S(1)}, bf16[4,8,512]{2,1,0:T(8,128)(2,1)S(1)}, u32[]{:S(2)}, u32[]{:S(2)}) collective-permute-start(bf16[4,8,512]{2,1,0:T(8,128)(2,1)S(1)} %get-tuple-element.74.refs_2_), channel_id=1, source_target_pairs={{0,1},{1,0},{2,3},{3,2},{4,5},{5,4},{6,7},{7,6},{8,9},{9,8},{10,11... | collective-permute-start | bytes 98312 | tf_op jit(solution)/shard_map/ppermute | solution.py:256
  95.7 1.4 %collective-permute-start.39 = (bf16[4,4,8,256]{3,2,1,0:T(8,128)(2,1)S(1)}, bf16[4,4,8,256]{3,2,1,0:T(8,128)(2,1)S(1)}, u32[]{:S(2)}, u32[]{:S(2)}) collective-permute-start(bf16[4,4,8,256]{3,2,1,0:T(8,128)(2,1)S(1)} %get-tuple-element.65), channel_id=1, source_target_pairs={{0,1},{1,0},{2,3},{3,2},{4,5},{5,4},{6,7},{7,6},{8,9},{9,8},{10,11... | collective-permute-start | bytes 196616 | tf_op jit(solution)/shard_map/ppermute | solution.py:256
  97.1 4.7 %collective-permute-start.42 = (bf16[4,8,256]{2,1,0:T(8,128)(2,1)S(1)}, bf16[4,8,256]{2,1,0:T(8,128)(2,1)S(1)}, u32[]{:S(2)}, u32[]{:S(2)}) collective-permute-start(bf16[4,8,256]{2,1,0:T(8,128)(2,1)S(1)} %get-tuple-element.79), channel_id=1, source_target_pairs={{0,4},{1,5},{2,6},{3,7},{4,0},{5,1},{6,2},{7,3},{8,12},{9,13},{10,... | collective-permute-start | bytes 49160 | tf_op jit(solution)/shard_map/ppermute | solution.py:261
  97.7 5.6 %collective-permute-start.41 = (bf16[4,8,256]{2,1,0:T(8,128)(2,1)S(1)}, bf16[4,8,256]{2,1,0:T(8,128)(2,1)S(1)}, u32[]{:S(2)}, u32[]{:S(2)}) collective-permute-start(bf16[4,8,256]{2,1,0:T(8,128)(2,1)S(1)} %get-tuple-element.80), channel_id=1, source_target_pairs={{0,6},{1,7},{2,4},{3,5},{4,2},{5,3},{6,0},{7,1},{8,14},{9,15},{10,... | collective-permute-start | bytes 49160 | tf_op jit(solution)/shard_map/ppermute | solution.py:261
  99.6 3.8 %collective-permute-start.40 = (bf16[4,8,256]{2,1,0:T(8,128)(2,1)S(1)}, bf16[4,8,256]{2,1,0:T(8,128)(2,1)S(1)}, u32[]{:S(2)}, u32[]{:S(2)}) collective-permute-start(bf16[4,8,256]{2,1,0:T(8,128)(2,1)S(1)} %get-tuple-element.81), channel_id=1, source_target_pairs={{0,2},{1,3},{2,0},{3,1},{4,6},{5,7},{6,4},{7,5},{8,10},{9,11},{10,... | collective-permute-start | bytes 49160 | tf_op jit(solution)/shard_map/ppermute | solution.py:261
  103.8 1.3 %collective-permute-start.43 = (bf16[4,4,8,256]{3,2,1,0:T(8,128)(2,1)S(1)}, bf16[4,4,8,256]{3,2,1,0:T(8,128)(2,1)S(1)}, u32[]{:S(2)}, u32[]{:S(2)}) collective-permute-start(bf16[4,4,8,256]{3,2,1,0:T(8,128)(2,1)S(1)} %get-tuple-element.68), channel_id=1, source_target_pairs={{0,1},{1,0},{2,3},{3,2},{4,5},{5,4},{6,7},{7,6},{8,9},{9,8},{10,11... | collective-permute-start | bytes 196616 | tf_op jit(solution)/shard_map/ppermute | solution.py:256
  105.1 5.1 %collective-permute-start.44 = (bf16[4,8,256]{2,1,0:T(8,128)(2,1)S(1)}, bf16[4,8,256]{2,1,0:T(8,128)(2,1)S(1)}, u32[]{:S(2)}, u32[]{:S(2)}) collective-permute-start(bf16[4,8,256]{2,1,0:T(8,128)(2,1)S(1)} %get-tuple-element.76), channel_id=1, source_target_pairs={{0,2},{1,3},{2,0},{3,1},{4,6},{5,7},{6,4},{7,5},{8,10},{9,11},{10,... | collective-permute-start | bytes 49160 | tf_op jit(solution)/shard_map/ppermute | solution.py:261
  106.1 4.6 %collective-permute-start.46 = (bf16[4,8,256]{2,1,0:T(8,128)(2,1)S(1)}, bf16[4,8,256]{2,1,0:T(8,128)(2,1)S(1)}, u32[]{:S(2)}, u32[]{:S(2)}) collective-permute-start(bf16[4,8,256]{2,1,0:T(8,128)(2,1)S(1)} %get-tuple-element.77), channel_id=1, source_target_pairs={{0,4},{1,5},{2,6},{3,7},{4,0},{5,1},{6,2},{7,3},{8,12},{9,13},{10,... | collective-permute-start | bytes 49160 | tf_op jit(solution)/shard_map/ppermute | solution.py:261
  107.7 5.5 %collective-permute-start.45 = (bf16[4,8,256]{2,1,0:T(8,128)(2,1)S(1)}, bf16[4,8,256]{2,1,0:T(8,128)(2,1)S(1)}, u32[]{:S(2)}, u32[]{:S(2)}) collective-permute-start(bf16[4,8,256]{2,1,0:T(8,128)(2,1)S(1)} %get-tuple-element.78), channel_id=1, source_target_pairs={{0,6},{1,7},{2,4},{3,5},{4,2},{5,3},{6,0},{7,1},{8,14},{9,15},{10,... | collective-permute-start | bytes 49160 | tf_op jit(solution)/shard_map/ppermute | solution.py:261
  (10 other events, 78.0 us)

commit v10 on v9

--- a/solution.py
+++ b/solution.py
@@ -142,9 +142,31 @@
     return jnp.where(along(line, below) == target, below, -1)
 
 
-def scatter_walk(plan_ref, list_ref, update_ref, acc_ref):
+def find(plan, targets, width):
+    sets, length = targets.shape
+
+    def body(plan_ref, list_ref, out_ref):
+        tiles = length // LANES
+        for tile in range(tiles):
+            for s in range(sets):
+                line = list_ref[s : s + 1, tile * LANES : (tile + 1) * LANES]
+                lo = plan_ref[s * tiles + tile]
+                out_ref[s, tile] = position(jnp.broadcast_to(line, (BLOCKS, LANES)), lo)
+
+    return call(
+        body,
+        [((sets, length // LANES, BLOCKS, LANES), I32)],
+        [plan, targets],
+        [SMEM, VMEM],
+        moved=2 << 20,
+        name="find",
+    )[0]
+
+
+def scatter_walk(plan_ref, list_ref, at_ref, update_ref, acc_ref):
     def visit(s, lanes, line, lo, first):
-        x, at = update_ref[s, :, lanes], position(line, lo)
+        x = update_ref[s, :, lanes]
+        at = at_ref[s, lanes.start // LANES] if first else position(line, lo)
         parts = [pick(x, jnp.broadcast_to(at[u : u + 1], x.shape)) for u in range(BLOCKS)]
         acc_ref[pl.ds(lo, BLOCKS)] += jnp.stack(parts)
 
@@ -162,10 +184,7 @@
 
 
 def far_order(chips):
-    order = list(range(chips))
-    if chips > 3:
-        order[-2:] = [chips - 1, chips - 2]
-    return order
+    return [0] + list(range(2, chips)) + [1] if chips > 1 else [0]
 
 
 def core():
@@ -196,48 +215,51 @@
         other_ref[k] = value_ref[:, spot(2 * k + 1 - odd, w)].astype(other_ref.dtype)
 
 
-def half_of(x_ref, w_ref, s, odd, xor, start=0):
+def half_of(x_ref, w_ref, s, odd, xor, but=()):
     at = (s,) if len(x_ref.shape) == 4 else ()
     chips, cols = x_ref.shape[0], x_ref.shape[-1]
     picked, columns = [], []
-    for k, j in list(enumerate(far_order(chips)))[start:]:
+    for k, j in enumerate(far_order(chips)):
+        if j in but:
+            continue
         c = chip() ^ j if xor else k
         picked.append(x_ref[(k,) + at])
         columns.append(w_ref[s, :, spot(2 * c + odd, cols)])
     return times_transposed(jnp.concatenate(picked, axis=1), jnp.concatenate(columns, axis=1))
 
 
-def own_half(x, w, name, xor=False, first=None):
+def own_half(x, w, name, xor=False, done=None, but=()):
     sets, rows = w.shape[:2]
 
     def body(x_ref, w_ref, *refs):
         for s in range(sets):
-            got = half_of(x_ref, w_ref, s, core(), xor, len(refs) - 1)
-            refs[-1][s] = got if first is None else got + refs[0][s]
+            got = half_of(x_ref, w_ref, s, core(), xor, but)
+            refs[-1][s] = got if done is None else got + refs[0][s]
 
     return call(
         body,
         [((sets, x.shape[-2], rows), F32)],
-        [x, pinned(w)] + ([] if first is None else [first]),
-        [VMEM] * (2 if first is None else 3),
+        [x, pinned(w)] + ([] if done is None else [done]),
+        [VMEM] * (2 if done is None else 3),
         moved=12 << 20,
         name=name,
     )[0]
 
 
-def own_piece(x, w, name):
+def one_piece(x, w, k, name, done=None):
     sets, rows = w.shape[:2]
 
-    def body(x_ref, w_ref, out_ref):
+    def body(x_ref, w_ref, *refs):
+        columns = spot(2 * (chip() ^ k) + core(), x_ref.shape[-1])
         for s in range(sets):
-            columns = spot(lax.axis_index("rows"), x_ref.shape[-1])
-            out_ref[s] = times_transposed(x_ref[s], w_ref[s, :, columns])
+            got = times_transposed(x_ref[s], w_ref[s, :, columns])
+            refs[-1][s] = got if done is None else got + refs[0][s]
 
     return call(
         body,
         [((sets, x.shape[-2], rows), F32)],
-        [x, pinned(w)],
-        [VMEM] * 2,
+        [x, pinned(w)] + ([] if done is None else [done]),
+        [VMEM] * (2 if done is None else 3),
         moved=4 << 20,
         name=name,
     )[0]
@@ -322,8 +344,8 @@
             return both_halves(*x_refs, w_ref, s, xor=True)
         return times_transposed(x_refs[0][0, s], w_ref[s])
 
-    def leaf_halves(x, w, name, first=None):
-        return own_half(x, w, name, True, first), swap(x)
+    def leaf_halves(x, w, name, done=None, but=()):
+        return own_half(x, w, name, True, done, but), swap(x)
 
     rhs = root_rhs
     if not root_aligned:
@@ -344,14 +366,12 @@
         [VMEM] + [pl.BlockSpec(memory_space=pltpu.HBM)] * len(weights),
         name="round_rhs",
     )[0]
-    prepared = prepare(
-        lb,
-        [(leaf_rows, leaf_local, leaf_height), (parent_rows, parent_local, parent_height)],
-    )
+    prepared = prepare(lb, [(leaf_rows, leaf_local, leaf_height)])
     lb = far_gather(lb) if leaf_aligned else leaf_columns(lb)
     lb, prepared, rhs = lax.optimization_barrier((lb, prepared, rhs))
-    leaf_list, leaf_plan, parent_list, parent_plan = prepared
+    leaf_list, leaf_plan = prepared
     lb = leaf_halves(lb, leaf_inv, "leaf_solve_own") if leaf_aligned else (lb,)
+    lb, leaf_at = lax.optimization_barrier((lb, find(leaf_plan, leaf_list, tall)))
 
     def leaf_solve(*refs):
         x_refs, (w_ref, y_ref, send_ref) = refs[: len(lb)], refs[len(lb) :]
@@ -368,20 +388,20 @@
         name="leaf_solve",
     )
     if leaf_aligned:
-        first = own_piece(lyb, leaf_panel, "leaf_update_first")
-        lyb, first = lax.optimization_barrier((far_gather(lyb), first))
-        lyb = leaf_halves(lyb, leaf_panel, "leaf_update_own", first)
+        done = one_piece(lyb, leaf_panel, 0, "leaf_update_first")
+        lyb, done = lax.optimization_barrier((far_gather(lyb), done))
+        lyb = leaf_halves(lyb, leaf_panel, "leaf_update_own", done, (0,))
     else:
         lyb = (leaf_columns(lyb),)
 
     def leaf_update(*refs):
         x_refs, refs = refs[: len(lyb)], refs[len(lyb) :]
-        plan_ref, w_ref, list_ref, rhs_ref, own_ref, other_ref, root_ref, *refs = refs
+        plan_ref, w_ref, list_ref, at_ref, rhs_ref, own_ref, other_ref, root_ref, *refs = refs
         update_ref, acc_ref, sum_ref = refs
         acc_ref[...] = jnp.zeros(acc_ref.shape, F32)
         for s in range(leaves):
             update_ref[s] = leaf_product(x_refs, w_ref, s)
-        scatter_walk(plan_ref, list_ref, update_ref, acc_ref)
+        scatter_walk(plan_ref, list_ref, at_ref, update_ref, acc_ref)
         for b in range(parent_width // LANES):
             sum_ref[:, b * LANES : (b + 1) * LANES] = -acc_ref[b]
         sum_ref[:, spot(lax.axis_index("rows"), parent_cols)] += rhs_ref[:, 0, :]
@@ -396,8 +416,8 @@
             ((chips, rcount, parent_cols), BF16),
             ((root_width // LANES, rcount, LANES), F32),
         ],
-        [*lyb, leaf_plan, pinned(leaf_panel), leaf_list, parent_rhs],
-        [VMEM] * len(lyb) + [SMEM] + [VMEM] * 3,
+        [*lyb, leaf_plan, pinned(leaf_panel), leaf_list, leaf_at, parent_rhs],
+        [VMEM] * len(lyb) + [SMEM] + [VMEM] * 4,
         scratch=[
             pltpu.VMEM((leaves, rcount, leaf_local), F32),
             pltpu.VMEM((tall // LANES + BLOCKS, rcount, LANES), F32),
@@ -405,7 +425,13 @@
         ],
         name="leaf_update",
     )
-    prb = chips_sum(own + swap(other).astype(F32)).astype(BF16)
+    own = own + swap(other).astype(F32)
+    prepared = prepare(own, [(parent_rows, parent_local, parent_height)])
+    prb, prepared = lax.optimization_barrier((chips_sum(own).astype(BF16), prepared))
+    parent_list, parent_plan = prepared
+    parent_at = find(parent_plan, parent_list, root_width)
+
+    prb_other, parent_at = lax.optimization_barrier((swap(prb), parent_at))
 
     def parent_solve(part_ref, x_ref, w_ref, y_ref, send_ref):
         y = both_halves(part_ref, x_ref, w_ref, 0)
@@ -415,20 +441,20 @@
     py, pyb = call(
         parent_solve,
         [((rcount, parent_cols), F32), ((rcount, parent_cols), BF16)],
-        [own_half(prb, parent_inv, "parent_solve_own"), swap(prb), pinned(parent_inv)],
+        [own_half(prb, parent_inv, "parent_solve_own"), prb_other, pinned(parent_inv)],
         [VMEM] * 3,
         name="parent_solve",
     )
     pyb = far_gather(pyb)
 
     def parent_update(
-        plan_ref, part_ref, x_ref, w_ref, list_ref, root_ref, rhs_ref, own_ref, other_ref,
+        plan_ref, part_ref, x_ref, w_ref, list_ref, at_ref, root_ref, rhs_ref, own_ref, other_ref,
         update_ref, acc_ref, sum_ref,
     ):
         for b in range(root_width // LANES):
             acc_ref[b] = root_ref[b]
         update_ref[0] = both_halves(part_ref, x_ref, w_ref, 0, xor=True)
-        scatter_walk(plan_ref, list_ref, update_ref, acc_ref)
+        scatter_walk(plan_ref, list_ref, at_ref, update_ref, acc_ref)
         for b in range(root_width // LANES):
             sum_ref[:, b * LANES : (b + 1) * LANES] = -acc_ref[b]
         if root_aligned:
@@ -446,10 +472,11 @@
             swap(pyb),
             pinned(parent_panel),
             parent_list,
+            parent_at,
             root_acc,
             rhs,
         ],
-        [SMEM] + [VMEM] * 6,
+        [SMEM] + [VMEM] * 7,
         scratch=[
             pltpu.VMEM((1, rcount, parent_local), F32),
             pltpu.VMEM((root_width // LANES + BLOCKS, rcount, LANES), F32),

time: 114 us -> 114 us (level)
  waiting for transfers between devices: 43.9 us -> 38.9 us
  Pallas kernels: 21.5 us -> 25.1 us
  starting transfers between devices: 44.3 us -> 45.6 us
    pallas_call x22 -> x25, Pallas kernels: 21.5 us -> 25.1 us  [call(): pl.pallas_call(body, out_shape=[jax.ShapeDtypeStruct(*o) if isinstance(o,...]
    ppermute x30, waiting for transfers between devices: 30.2 us -> 28 us  [far(): return lax.ppermute(x, 'rows', [(i, i ^ 2 * k) for i in range(n)])]
    ppermute x3, waiting for transfers between devices: 4.21 us -> 2.47 us  [leaf_sum(): lax.ppermute(b, 'leaf', [(i, (i + k) % n) for i in range(n)]).astype(F32)]
  transfers between devices with their start and end apart: 47 -> 47, of which waited for: 39 -> 39; matrix products, arithmetic and copies ran while one was open for 1% -> 1% of each run, Pallas kernels for 9% -> 12%
where the time goes in v10:
time: 114 us; the launch traced here: 113 us
  starting transfers between devices  45.6 us (40%)
  waiting for transfers between devices  38.9 us (34%)
  Pallas kernels  25.1 us (22%)
  local copies, waits for them, and re-layouts  2.04 us (2%)
  between operations  1.62 us (1%)
    ppermute x30, starting transfers between devices, far(): return lax.ppermute(x, 'rows', [(i, i ^ 2 * k) for i in range(n)])  39.4 us
    ppermute x30, waiting for transfers between devices, far(): return lax.ppermute(x, 'rows', [(i, i ^ 2 * k) for i in range(n)])  28 us
    pallas_call x25, Pallas kernels, call(): pl.pallas_call(body, out_shape=[jax.ShapeDtypeStruct(*o) if isinstance(o,...  25.1 us
    ppermute x14, waiting for transfers between devices, swap(): return lax.ppermute(x, 'rows', [(i, i ^ 1) for i in range(n)])  8.38 us
    ppermute x3, starting transfers between devices, leaf_sum(): lax.ppermute(b, 'leaf', [(i, (i + k) % n) for i in range(n)]).astype(F32)  4.5 us
    ppermute x3, waiting for transfers between devices, leaf_sum(): lax.ppermute(b, 'leaf', [(i, (i + k) % n) for i in range(n)]).astype(F32)  2.47 us
  transfers between devices with their start and end apart: 47, of which 39 were waited for; matrix products, arithmetic and copies ran while one was open for 1% of the time, Pallas kernels for 12%

profile of v10, /device:TPU:0, one launch (start us, length us, event | category | flops | bytes accessed | tf_op | source)
XLA Modules:
  0.0 113.5 jit_solution(10206499466630387639)
XLA Ops:
  1.4 4.1 %collective-permute-start = (bf16[4,8,256]{2,1,0:T(8,128)(2,1)S(1)}, bf16[4,8,256]{2,1,0:T(8,128)(2,1)S(1)}, u32[]{:S(2)}, u32[]{:S(2)}) collective-permute-start(bf16[4,8,256]{2,1,0:T(8,128)(2,1)S(1)} %round_rhs.1.refs_0_), channel_id=1, source_target_pairs={{0,4},{1,5},{2,6},{3,7},{4,0},{5,1},{6,2},{7,3},{8,12},{9,13},{10,... | collective-permute-start | bytes 49160 | tf_op jit(solution)/shard_map/ppermute | solution.py:283
  5.6 1.3 %collective-permute-start.1 = (bf16[4,8,256]{2,1,0:T(8,128)(2,1)S(1)}, bf16[4,8,256]{2,1,0:T(8,128)(2,1)S(1)}, u32[]{:S(2)}, u32[]{:S(2)}) collective-permute-start(bf16[4,8,256]{2,1,0:T(8,128)(2,1)S(1)} %round_rhs.1.refs_0_), channel_id=1, source_target_pairs={{0,6},{1,7},{2,4},{3,5},{4,2},{5,3},{6,0},{7,1},{8,14},{9,15},{10,... | collective-permute-start | bytes 49160 | tf_op jit(solution)/shard_map/ppermute | solution.py:283
  7.1 2.2 %prepare.2 = (s32[4,1024]{1,0:T(4,128)S(1)}, s32[33]{0:T(128)S(1)}) custom-call(bf16[4,8,256]{2,1,0:T(8,128)(2,1)S(1)} %round_rhs.1.refs_0_, s32[4,1024]{1,0:T(4,128)S(1)} %copy-done.5, s32[4]{0:T(128)S(1)} %copy-done.10), custom_call_target="tpu_custom_call" | custom-call | bytes 4194304 | tf_op jit(solution)/shard_map/prepare/pallas_call | solution.py:30
  9.3 1.8 %collective-permute-done.1 = bf16[4,8,256]{2,1,0:T(8,128)(2,1)S(1)} collective-permute-done((bf16[4,8,256]{2,1,0:T(8,128)(2,1)S(1)}, bf16[4,8,256]{2,1,0:T(8,128)(2,1)S(1)}, u32[]{:S(2)}, u32[]{:S(2)}) %collective-permute-start.1) | collective-permute-done | bytes 16416 | tf_op jit(solution)/shard_map/ppermute | solution.py:283
  11.9 1.3 %find.2.refs_5_ = s32[4,8,8,128]{3,2,1,0:T(8,128)S(1)} custom-call(s32[33]{0:T(128)S(1)} %get-tuple-element.45.plan_ref.refs_2_.refs_0_, s32[4,1024]{1,0:T(4,128)S(1)} %get-tuple-element.47.list_ref.refs_4_.refs_5_), custom_call_target="tpu_custom_call" | custom-call | bytes 2097152 | tf_op jit(solution)/shard_map/find/pallas_call | solution.py:30
  13.9 1.3 %collective-permute-start.4 = (bf16[4,8,256]{2,1,0:T(8,128)(2,1)S(1)}, bf16[4,8,256]{2,1,0:T(8,128)(2,1)S(1)}, u32[]{:S(2)}, u32[]{:S(2)}) collective-permute-start(bf16[4,8,256]{2,1,0:T(8,128)(2,1)S(1)} %get-tuple-element.50.x_ref), channel_id=1, source_target_pairs={{0,4},{1,5},{2,6},{3,7},{4,0},{5,1},{6,2},{7,3},{8,12},{9,13},{10,... | collective-permute-start | bytes 49160 | tf_op jit(solution)/shard_map/ppermute | solution.py:283
  15.1 1.2 %collective-permute-start.5 = (bf16[4,8,256]{2,1,0:T(8,128)(2,1)S(1)}, bf16[4,8,256]{2,1,0:T(8,128)(2,1)S(1)}, u32[]{:S(2)}, u32[]{:S(2)}) collective-permute-start(bf16[4,8,256]{2,1,0:T(8,128)(2,1)S(1)} %get-tuple-element.50.x_ref), channel_id=1, source_target_pairs={{0,6},{1,7},{2,4},{3,5},{4,2},{5,3},{6,0},{7,1},{8,14},{9,15},{10,... | collective-permute-start | bytes 49160 | tf_op jit(solution)/shard_map/ppermute | solution.py:283
  16.3 1.1 collective-permute-start.6
  18.5 2.1 %collective-permute-done.5 = bf16[4,8,256]{2,1,0:T(8,128)(2,1)S(1)} collective-permute-done((bf16[4,8,256]{2,1,0:T(8,128)(2,1)S(1)}, bf16[4,8,256]{2,1,0:T(8,128)(2,1)S(1)}, u32[]{:S(2)}, u32[]{:S(2)}) %collective-permute-start.5) | collective-permute-done | bytes 16416 | tf_op jit(solution)/shard_map/ppermute | solution.py:283
  20.8 1.7 %leaf_update_own.1.refs_0_ = f32[4,8,1024]{2,1,0:T(8,128)S(1)} custom-call(bf16[4,4,8,256]{3,2,1,0:T(8,128)(2,1)S(1)} %pad_maximum_fusion.1.x_ref, bf16[4,1024,2048]{2,1,0:T(8,128)(2,1)S(1)} %copy-done, f32[4,8,1024]{2,1,0:T(8,128)S(1)} %leaf_update_first.1.refs_0_), custom_call_target="tpu_custom_call" | custom-call | bytes 12582912 | tf_op jit(solution)/shard_map/leaf_update_own/pallas_call | solution.py:30
  22.5 3.1 %leaf_update.1 = (f32[4,8,512]{2,1,0:T(8,128)S(1)}, bf16[4,8,512]{2,1,0:T(8,128)(2,1)S(1)}, f32[32,8,128]{2,1,0:T(8,128)S(1)}) custom-call(f32[4,8,1024]{2,1,0:T(8,128)S(1)} %leaf_update_own.1.refs_0_, bf16[4,4,8,256]{3,2,1,0:T(8,128)(2,1)S(1)} %collective-permute-done.7.refs_1_, s32[33]{0:T(128)S(1)} %get-tuple-element.45.plan_ref.refs_2_.refs_0_, ...), custom_call_target="tpu_custom_call" | custom-call | tf_op jit(solution)/shard_map/leaf_update/pallas_call | solution.py:30
  27.0 2.1 %collective-permute-start.10 = (bf16[4,8,512]{2,1,0:T(8,128)(2,1)S(1)}, bf16[4,8,512]{2,1,0:T(8,128)(2,1)S(1)}, u32[]{:S(2)}, u32[]{:S(2)}) collective-permute-start(bf16[4,8,512]{2,1,0:T(8,128)(2,1)S(1)} %get-tuple-element.88), channel_id=1, source_target_pairs={{0,6},{1,7},{2,4},{3,5},{4,2},{5,3},{6,0},{7,1},{8,14},{9,15},{10,... | collective-permute-start | bytes 98312 | tf_op jit(solution)/shard_map/ppermute | solution.py:283
  29.1 2.4 %collective-permute-start.9 = (bf16[4,8,512]{2,1,0:T(8,128)(2,1)S(1)}, bf16[4,8,512]{2,1,0:T(8,128)(2,1)S(1)}, u32[]{:S(2)}, u32[]{:S(2)}) collective-permute-start(bf16[4,8,512]{2,1,0:T(8,128)(2,1)S(1)} %get-tuple-element.88), channel_id=1, source_target_pairs={{0,4},{1,5},{2,6},{3,7},{4,0},{5,1},{6,2},{7,3},{8,12},{9,13},{10,... | collective-permute-start | bytes 98312 | tf_op jit(solution)/shard_map/ppermute | solution.py:283
  32.1 1.2 %prepare.3 = (s32[1,512]{1,0:T(1,128)S(1)}, s32[5]{0:T(128)S(1)}) custom-call(f32[4,8,512]{2,1,0:T(8,128)S(1)} %get-tuple-element.89.refs_0_, s32[1,512]{1,0:T(1,128)S(1)} %copy-done.8, s32[1]{0:T(128)S(6)} %copy.21.refs_2_), custom_call_target="tpu_custom_call" | custom-call | bytes 4194304 | tf_op jit(solution)/shard_map/prepare/pallas_call | solution.py:30
  34.7 1.1 %find.3.at_ref = s32[1,4,8,128]{3,2,1,0:T(8,128)S(1)} custom-call(s32[5]{0:T(128)S(1)} %get-tuple-element.58.plan_ref, s32[1,512]{1,0:T(1,128)S(1)} %get-tuple-element.60.list_ref.rows_ref), custom_call_target="tpu_custom_call" | custom-call | bytes 2097152 | tf_op jit(solution)/shard_map/find/pallas_call | solution.py:30
  36.5 2.4 %collective-permute-start.13 = (bf16[8,512]{1,0:T(8,128)(2,1)S(1)}, bf16[8,512]{1,0:T(8,128)(2,1)S(1)}, u32[]{:S(2)}, u32[]{:S(2)}) collective-permute-start(bf16[8,512]{1,0:T(8,128)(2,1)S(1)} %get-tuple-element.62), channel_id=1, source_target_pairs={{0,4},{1,5},{2,6},{3,7},{4,0},{5,1},{6,2},{7,3},{8,12},{9,13},{10,... | collective-permute-start | bytes 24584 | tf_op jit(solution)/shard_map/ppermute | solution.py:283
  38.9 2.0 %collective-permute-start.14 = (bf16[8,512]{1,0:T(8,128)(2,1)S(1)}, bf16[8,512]{1,0:T(8,128)(2,1)S(1)}, u32[]{:S(2)}, u32[]{:S(2)}) collective-permute-start(bf16[8,512]{1,0:T(8,128)(2,1)S(1)} %get-tuple-element.62), channel_id=1, source_target_pairs={{0,6},{1,7},{2,4},{3,5},{4,2},{5,3},{6,0},{7,1},{8,14},{9,15},{10,... | collective-permute-start | bytes 24584 | tf_op jit(solution)/shard_map/ppermute | solution.py:283
  41.1 3.2 %collective-permute-done.14 = bf16[8,512]{1,0:T(8,128)(2,1)S(1)} collective-permute-done((bf16[8,512]{1,0:T(8,128)(2,1)S(1)}, bf16[8,512]{1,0:T(8,128)(2,1)S(1)}, u32[]{:S(2)}, u32[]{:S(2)}) %collective-permute-start.14) | collective-permute-done | bytes 8224 | tf_op jit(solution)/shard_map/ppermute | solution.py:283
  45.9 1.4 %parent_update.1 = (f32[4,8,512]{2,1,0:T(8,128)S(1)}, bf16[4,8,512]{2,1,0:T(8,128)(2,1)S(1)}) custom-call(s32[5]{0:T(128)S(1)} %get-tuple-element.58.plan_ref, f32[1,8,512]{2,1,0:T(8,128)S(1)} %parent_update_own.1.part_ref, bf16[4,8,512]{2,1,0:T(8,128)(2,1)S(1)} %collective-permute-done.16.x_ref, bf16[1,512,4096]{2,1,0:T(8,128)(2,1)S(1)} %copy-done.1, ...), custom_call_target="tpu_custom_call" | custom-call | tf_op jit(solution)/shard_map/parent_update/pallas_call | solution.py:30
  48.5 1.5 %collective-permute-start.18 = (bf16[4,8,512]{2,1,0:T(8,128)(2,1)S(1)}, bf16[4,8,512]{2,1,0:T(8,128)(2,1)S(1)}, u32[]{:S(2)}, u32[]{:S(2)}) collective-permute-start(bf16[4,8,512]{2,1,0:T(8,128)(2,1)S(1)} %fusion.1), channel_id=1, source_target_pairs={{0,8},{8,16},{16,24},{24,0},{1,9},{9,17},{17,25},{25,1},{2,10},{10... | collective-permute-start | bytes 98312 | tf_op jit(solution)/shard_map/ppermute | solution.py:299
  50.1 1.5 %collective-permute-start.19 = (bf16[4,8,512]{2,1,0:T(8,128)(2,1)S(1)}, bf16[4,8,512]{2,1,0:T(8,128)(2,1)S(1)}, u32[]{:S(2)}, u32[]{:S(2)}) collective-permute-start(bf16[4,8,512]{2,1,0:T(8,128)(2,1)S(1)} %fusion.1), channel_id=1, source_target_pairs={{0,16},{8,24},{16,0},{24,8},{1,17},{9,25},{17,1},{25,9},{2,18},{10... | collective-permute-start | bytes 98312 | tf_op jit(solution)/shard_map/ppermute | solution.py:299
  51.6 1.4 %collective-permute-start.20 = (bf16[4,8,512]{2,1,0:T(8,128)(2,1)S(1)}, bf16[4,8,512]{2,1,0:T(8,128)(2,1)S(1)}, u32[]{:S(2)}, u32[]{:S(2)}) collective-permute-start(bf16[4,8,512]{2,1,0:T(8,128)(2,1)S(1)} %fusion.1), channel_id=1, source_target_pairs={{0,24},{8,0},{16,8},{24,16},{1,25},{9,1},{17,9},{25,17},{2,26},{10... | collective-permute-start | bytes 98312 | tf_op jit(solution)/shard_map/ppermute | solution.py:299
  54.0 1.5 %collective-permute-done.20 = bf16[4,8,512]{2,1,0:T(8,128)(2,1)S(1)} collective-permute-done((bf16[4,8,512]{2,1,0:T(8,128)(2,1)S(1)}, bf16[4,8,512]{2,1,0:T(8,128)(2,1)S(1)}, u32[]{:S(2)}, u32[]{:S(2)}) %collective-permute-start.20) | collective-permute-done | bytes 32800 | tf_op jit(solution)/shard_map/ppermute | solution.py:299
  56.0 2.0 %collective-permute-start.22 = (bf16[4,8,512]{2,1,0:T(8,128)(2,1)S(1)}, bf16[4,8,512]{2,1,0:T(8,128)(2,1)S(1)}, u32[]{:S(2)}, u32[]{:S(2)}) collective-permute-start(bf16[4,8,512]{2,1,0:T(8,128)(2,1)S(1)} %fusion.27), channel_id=1, source_target_pairs={{0,6},{1,7},{2,4},{3,5},{4,2},{5,3},{6,0},{7,1},{8,14},{9,15},{10,... | collective-permute-start | bytes 98312 | tf_op jit(solution)/shard_map/ppermute | solution.py:283
  59.1 1.4 %collective-permute-done.21 = bf16[4,8,512]{2,1,0:T(8,128)(2,1)S(1)} collective-permute-done((bf16[4,8,512]{2,1,0:T(8,128)(2,1)S(1)}, bf16[4,8,512]{2,1,0:T(8,128)(2,1)S(1)}, u32[]{:S(2)}, u32[]{:S(2)}) %collective-permute-start.21) | collective-permute-done | bytes 32800 | tf_op jit(solution)/shard_map/ppermute | solution.py:283
  60.5 1.2 %collective-permute-done.22 = bf16[4,8,512]{2,1,0:T(8,128)(2,1)S(1)} collective-permute-done((bf16[4,8,512]{2,1,0:T(8,128)(2,1)S(1)}, bf16[4,8,512]{2,1,0:T(8,128)(2,1)S(1)}, u32[]{:S(2)}, u32[]{:S(2)}) %collective-permute-start.22) | collective-permute-done | bytes 32800 | tf_op jit(solution)/shard_map/ppermute | solution.py:283
  65.6 1.4 %collective-permute-start.26 = (bf16[4,8,512]{2,1,0:T(8,128)(2,1)S(1)}, bf16[4,8,512]{2,1,0:T(8,128)(2,1)S(1)}, u32[]{:S(2)}, u32[]{:S(2)}) collective-permute-start(bf16[4,8,512]{2,1,0:T(8,128)(2,1)S(1)} %bitcast_convert_fusion.1), channel_id=1, source_target_pairs={{0,4},{1,5},{2,6},{3,7},{4,0},{5,1},{6,2},{7,3},{8,12},{9,13},{10,... | collective-permute-start | bytes 98312 | tf_op jit(solution)/shard_map/ppermute | solution.py:283
  67.0 1.9 %collective-permute-start.27 = (bf16[4,8,512]{2,1,0:T(8,128)(2,1)S(1)}, bf16[4,8,512]{2,1,0:T(8,128)(2,1)S(1)}, u32[]{:S(2)}, u32[]{:S(2)}) collective-permute-start(bf16[4,8,512]{2,1,0:T(8,128)(2,1)S(1)} %bitcast_convert_fusion.1), channel_id=1, source_target_pairs={{0,6},{1,7},{2,4},{3,5},{4,2},{5,3},{6,0},{7,1},{8,14},{9,15},{10,... | collective-permute-start | bytes 98312 | tf_op jit(solution)/shard_map/ppermute | solution.py:283
  69.2 2.0 %collective-permute-done.26 = bf16[4,8,512]{2,1,0:T(8,128)(2,1)S(1)} collective-permute-done((bf16[4,8,512]{2,1,0:T(8,128)(2,1)S(1)}, bf16[4,8,512]{2,1,0:T(8,128)(2,1)S(1)}, u32[]{:S(2)}, u32[]{:S(2)}) %collective-permute-start.26) | collective-permute-done | bytes 32800 | tf_op jit(solution)/shard_map/ppermute | solution.py:283
  71.2 1.6 %collective-permute-done.27 = bf16[4,8,512]{2,1,0:T(8,128)(2,1)S(1)} collective-permute-done((bf16[4,8,512]{2,1,0:T(8,128)(2,1)S(1)}, bf16[4,8,512]{2,1,0:T(8,128)(2,1)S(1)}, u32[]{:S(2)}, u32[]{:S(2)}) %collective-permute-start.27) | collective-permute-done | bytes 32800 | tf_op jit(solution)/shard_map/ppermute | solution.py:283
  73.2 1.2 %collective-permute-done.29.other_ref = bf16[4,8,512]{2,1,0:T(8,128)(2,1)S(1)} collective-permute-done((bf16[4,8,512]{2,1,0:T(8,128)(2,1)S(1)}, bf16[4,8,512]{2,1,0:T(8,128)(2,1)S(1)}, u32[]{:S(2)}, u32[]{:S(2)}) %collective-permute-start.29) | collective-permute-done | bytes 32800 | tf_op jit(solution)/shard_map/ppermute | solution.py:278
  74.4 1.3 %parent_back.1 = (bf16[4,1,8,512]{3,2,1,0:T(8,128)(2,1)S(1)}, f32[40,8,128]{2,1,0:T(8,128)S(1)}, f32[8,128]{1,0:T(8,128)}, bf16[1,8,512]{2,1,0:T(8,128)(2,1)S(1)}) custom-call(s32[5]{0:T(128)S(1)} %get-tuple-element.58.plan_ref, bf16[4,8,512]{2,1,0:T(8,128)(2,1)S(1)} %fusion.own_ref, bf16[4,8,512]{2,1,0:T(8,128)(2,1)S(1)} %collective-permute-done.29.other_ref, ...), custom_call_target="tpu_custom_call" | custom-call | tf_op jit(solution)/shard_map/parent_back/pallas_call | solution.py:30
  77.6 1.9 %collective-permute-start.32 = (bf16[1,8,512]{2,1,0:T(8,128)(2,1)S(1)}, bf16[1,8,512]{2,1,0:T(8,128)(2,1)S(1)}, u32[]{:S(2)}, u32[]{:S(2)}) collective-permute-start(bf16[1,8,512]{2,1,0:T(8,128)(2,1)S(1)} %get-tuple-element.98), channel_id=1, source_target_pairs={{0,6},{1,7},{2,4},{3,5},{4,2},{5,3},{6,0},{7,1},{8,14},{9,15},{10,... | collective-permute-start | bytes 24584 | tf_op jit(solution)/shard_map/ppermute | solution.py:283
  80.5 1.1 collective-permute-done.31.refs_1_
  81.6 1.4 %collective-permute-done.32.refs_2_ = bf16[1,8,512]{2,1,0:T(8,128)(2,1)S(1)} collective-permute-done((bf16[1,8,512]{2,1,0:T(8,128)(2,1)S(1)}, bf16[1,8,512]{2,1,0:T(8,128)(2,1)S(1)}, u32[]{:S(2)}, u32[]{:S(2)}) %collective-permute-start.32) | collective-permute-done | bytes 8224 | tf_op jit(solution)/shard_map/ppermute | solution.py:283
  84.8 1.5 %collective-permute-start.35 = (bf16[4,8,512]{2,1,0:T(8,128)(2,1)S(1)}, bf16[4,8,512]{2,1,0:T(8,128)(2,1)S(1)}, u32[]{:S(2)}, u32[]{:S(2)}) collective-permute-start(bf16[4,8,512]{2,1,0:T(8,128)(2,1)S(1)} %bitcast_convert_fusion), channel_id=1, source_target_pairs={{0,4},{1,5},{2,6},{3,7},{4,0},{5,1},{6,2},{7,3},{8,12},{9,13},{10,... | collective-permute-start | bytes 98312 | tf_op jit(solution)/shard_map/ppermute | solution.py:283
  86.3 1.9 %collective-permute-start.36 = (bf16[4,8,512]{2,1,0:T(8,128)(2,1)S(1)}, bf16[4,8,512]{2,1,0:T(8,128)(2,1)S(1)}, u32[]{:S(2)}, u32[]{:S(2)}) collective-permute-start(bf16[4,8,512]{2,1,0:T(8,128)(2,1)S(1)} %bitcast_convert_fusion), channel_id=1, source_target_pairs={{0,6},{1,7},{2,4},{3,5},{4,2},{5,3},{6,0},{7,1},{8,14},{9,15},{10,... | collective-permute-start | bytes 98312 | tf_op jit(solution)/shard_map/ppermute | solution.py:283
  88.3 2.0 %collective-permute-done.35 = bf16[4,8,512]{2,1,0:T(8,128)(2,1)S(1)} collective-permute-done((bf16[4,8,512]{2,1,0:T(8,128)(2,1)S(1)}, bf16[4,8,512]{2,1,0:T(8,128)(2,1)S(1)}, u32[]{:S(2)}, u32[]{:S(2)}) %collective-permute-start.35) | collective-permute-done | bytes 32800 | tf_op jit(solution)/shard_map/ppermute | solution.py:283
  90.3 1.7 %collective-permute-done.36 = bf16[4,8,512]{2,1,0:T(8,128)(2,1)S(1)} collective-permute-done((bf16[4,8,512]{2,1,0:T(8,128)(2,1)S(1)}, bf16[4,8,512]{2,1,0:T(8,128)(2,1)S(1)}, u32[]{:S(2)}, u32[]{:S(2)}) %collective-permute-start.36) | collective-permute-done | bytes 32800 | tf_op jit(solution)/shard_map/ppermute | solution.py:283
  92.5 1.2 %collective-permute-done.38.refs_3_ = bf16[4,8,512]{2,1,0:T(8,128)(2,1)S(1)} collective-permute-done((bf16[4,8,512]{2,1,0:T(8,128)(2,1)S(1)}, bf16[4,8,512]{2,1,0:T(8,128)(2,1)S(1)}, u32[]{:S(2)}, u32[]{:S(2)}) %collective-permute-start.38) | collective-permute-done | bytes 32800 | tf_op jit(solution)/shard_map/ppermute | solution.py:278
  93.7 2.6 %leaf_back.1 = (bf16[4,4,8,256]{3,2,1,0:T(8,128)(2,1)S(1)}, f32[8,512]{1,0:T(8,128)S(1)}, bf16[4,8,1024]{2,1,0:T(8,128)(2,1)S(1)}) custom-call(s32[33]{0:T(128)S(1)} %get-tuple-element.45.plan_ref.refs_2_.refs_0_, f32[4,8,512]{2,1,0:T(8,128)S(1)} %get-tuple-element.87.refs_1_, bf16[4,8,512]{2,1,0:T(8,128)(2,1)S(1)} %get-tuple-element.86.refs_2_, ...), custom_call_target="tpu_custom_call" | custom-call | tf_op jit(solution)/shard_map/leaf_back/pallas_call | solution.py:30
  96.4 1.2 %leaf_back_own.1 = f32[4,4,8,256]{3,2,1,0:T(8,128)S(1)} custom-call(bf16[4,8,1024]{2,1,0:T(8,128)(2,1)S(1)} %get-tuple-element.76.x_ref, bf16[4,1024,2048]{2,1,0:T(8,128)(2,1)S(1)} %copy-done), custom_call_target="tpu_custom_call" | custom-call | bytes 12582912 | tf_op jit(solution)/shard_map/leaf_back_own/pallas_call | solution.py:30
  98.3 1.9 %collective-permute-start.41 = (bf16[4,8,256]{2,1,0:T(8,128)(2,1)S(1)}, bf16[4,8,256]{2,1,0:T(8,128)(2,1)S(1)}, u32[]{:S(2)}, u32[]{:S(2)}) collective-permute-start(bf16[4,8,256]{2,1,0:T(8,128)(2,1)S(1)} %get-tuple-element.94), channel_id=1, source_target_pairs={{0,6},{1,7},{2,4},{3,5},{4,2},{5,3},{6,0},{7,1},{8,14},{9,15},{10,... | collective-permute-start | bytes 49160 | tf_op jit(solution)/shard_map/ppermute | solution.py:283
  101.2 1.2 %collective-permute-done.40.refs_1_ = bf16[4,8,256]{2,1,0:T(8,128)(2,1)S(1)} collective-permute-done((bf16[4,8,256]{2,1,0:T(8,128)(2,1)S(1)}, bf16[4,8,256]{2,1,0:T(8,128)(2,1)S(1)}, u32[]{:S(2)}, u32[]{:S(2)}) %collective-permute-start.40) | collective-permute-done | bytes 16416 | tf_op jit(solution)/shard_map/ppermute | solution.py:283
  102.4 1.4 %collective-permute-done.41.refs_2_ = bf16[4,8,256]{2,1,0:T(8,128)(2,1)S(1)} collective-permute-done((bf16[4,8,256]{2,1,0:T(8,128)(2,1)S(1)}, bf16[4,8,256]{2,1,0:T(8,128)(2,1)S(1)}, u32[]{:S(2)}, u32[]{:S(2)}) %collective-permute-start.41) | collective-permute-done | bytes 16416 | tf_op jit(solution)/shard_map/ppermute | solution.py:283
  105.7 1.4 %collective-permute-start.44 = (bf16[4,8,256]{2,1,0:T(8,128)(2,1)S(1)}, bf16[4,8,256]{2,1,0:T(8,128)(2,1)S(1)}, u32[]{:S(2)}, u32[]{:S(2)}) collective-permute-start(bf16[4,8,256]{2,1,0:T(8,128)(2,1)S(1)} %get-tuple-element.90), channel_id=1, source_target_pairs={{0,4},{1,5},{2,6},{3,7},{4,0},{5,1},{6,2},{7,3},{8,12},{9,13},{10,... | collective-permute-start | bytes 49160 | tf_op jit(solution)/shard_map/ppermute | solution.py:283
  107.1 1.9 %collective-permute-start.45 = (bf16[4,8,256]{2,1,0:T(8,128)(2,1)S(1)}, bf16[4,8,256]{2,1,0:T(8,128)(2,1)S(1)}, u32[]{:S(2)}, u32[]{:S(2)}) collective-permute-start(bf16[4,8,256]{2,1,0:T(8,128)(2,1)S(1)} %get-tuple-element.92), channel_id=1, source_target_pairs={{0,6},{1,7},{2,4},{3,5},{4,2},{5,3},{6,0},{7,1},{8,14},{9,15},{10,... | collective-permute-start | bytes 49160 | tf_op jit(solution)/shard_map/ppermute | solution.py:283
  110.5 2.2 %collective-permute-done.45 = bf16[4,8,256]{2,1,0:T(8,128)(2,1)S(1)} collective-permute-done((bf16[4,8,256]{2,1,0:T(8,128)(2,1)S(1)}, bf16[4,8,256]{2,1,0:T(8,128)(2,1)S(1)}, u32[]{:S(2)}, u32[]{:S(2)}) %collective-permute-start.45) | collective-permute-done | bytes 16416 | tf_op jit(solution)/shard_map/ppermute | solution.py:283
  (111 shorter events, 28.2 us)
Async XLA Ops:
  1.4 7.9 %collective-permute-start = (bf16[4,8,256]{2,1,0:T(8,128)(2,1)S(1)}, bf16[4,8,256]{2,1,0:T(8,128)(2,1)S(1)}, u32[]{:S(2)}, u32[]{:S(2)}) collective-permute-start(bf16[4,8,256]{2,1,0:T(8,128)(2,1)S(1)} %round_rhs.1.refs_0_), channel_id=1, source_target_pairs={{0,4},{1,5},{2,6},{3,7},{4,0},{5,1},{6,2},{7,3},{8,12},{9,13},{10,... | collective-permute-start | bytes 49160 | tf_op jit(solution)/shard_map/ppermute | solution.py:283
  5.6 5.5 %collective-permute-start.1 = (bf16[4,8,256]{2,1,0:T(8,128)(2,1)S(1)}, bf16[4,8,256]{2,1,0:T(8,128)(2,1)S(1)}, u32[]{:S(2)}, u32[]{:S(2)}) collective-permute-start(bf16[4,8,256]{2,1,0:T(8,128)(2,1)S(1)} %round_rhs.1.refs_0_), channel_id=1, source_target_pairs={{0,6},{1,7},{2,4},{3,5},{4,2},{5,3},{6,0},{7,1},{8,14},{9,15},{10,... | collective-permute-start | bytes 49160 | tf_op jit(solution)/shard_map/ppermute | solution.py:283
  6.9 4.2 %collective-permute-start.2 = (bf16[4,8,256]{2,1,0:T(8,128)(2,1)S(1)}, bf16[4,8,256]{2,1,0:T(8,128)(2,1)S(1)}, u32[]{:S(2)}, u32[]{:S(2)}) collective-permute-start(bf16[4,8,256]{2,1,0:T(8,128)(2,1)S(1)} %round_rhs.1.refs_0_), channel_id=1, source_target_pairs={{0,2},{1,3},{2,0},{3,1},{4,6},{5,7},{6,4},{7,5},{8,10},{9,11},{10,... | collective-permute-start | bytes 49160 | tf_op jit(solution)/shard_map/ppermute | solution.py:283
  11.1 2.1 %collective-permute-start.3 = (bf16[4,4,8,256]{3,2,1,0:T(8,128)(2,1)S(1)}, bf16[4,4,8,256]{3,2,1,0:T(8,128)(2,1)S(1)}, u32[]{:S(2)}, u32[]{:S(2)}) collective-permute-start(bf16[4,4,8,256]{3,2,1,0:T(8,128)(2,1)S(1)} %pad_maximum_fusion.x_ref), channel_id=1, source_target_pairs={{0,1},{1,0},{2,3},{3,2},{4,5},{5,4},{6,7},{7,6},{8,9},{9,8},{10,11... | collective-permute-start | bytes 196616 | tf_op jit(solution)/shard_map/ppermute | solution.py:278
  13.9 4.7 %collective-permute-start.4 = (bf16[4,8,256]{2,1,0:T(8,128)(2,1)S(1)}, bf16[4,8,256]{2,1,0:T(8,128)(2,1)S(1)}, u32[]{:S(2)}, u32[]{:S(2)}) collective-permute-start(bf16[4,8,256]{2,1,0:T(8,128)(2,1)S(1)} %get-tuple-element.50.x_ref), channel_id=1, source_target_pairs={{0,4},{1,5},{2,6},{3,7},{4,0},{5,1},{6,2},{7,3},{8,12},{9,13},{10,... | collective-permute-start | bytes 49160 | tf_op jit(solution)/shard_map/ppermute | solution.py:283
  15.1 5.5 %collective-permute-start.5 = (bf16[4,8,256]{2,1,0:T(8,128)(2,1)S(1)}, bf16[4,8,256]{2,1,0:T(8,128)(2,1)S(1)}, u32[]{:S(2)}, u32[]{:S(2)}) collective-permute-start(bf16[4,8,256]{2,1,0:T(8,128)(2,1)S(1)} %get-tuple-element.50.x_ref), channel_id=1, source_target_pairs={{0,6},{1,7},{2,4},{3,5},{4,2},{5,3},{6,0},{7,1},{8,14},{9,15},{10,... | collective-permute-start | bytes 49160 | tf_op jit(solution)/shard_map/ppermute | solution.py:283
  16.3 4.4 %collective-permute-start.6 = (bf16[4,8,256]{2,1,0:T(8,128)(2,1)S(1)}, bf16[4,8,256]{2,1,0:T(8,128)(2,1)S(1)}, u32[]{:S(2)}, u32[]{:S(2)}) collective-permute-start(bf16[4,8,256]{2,1,0:T(8,128)(2,1)S(1)} %get-tuple-element.50.x_ref), channel_id=1, source_target_pairs={{0,2},{1,3},{2,0},{3,1},{4,6},{5,7},{6,4},{7,5},{8,10},{9,11},{10,... | collective-permute-start | bytes 49160 | tf_op jit(solution)/shard_map/ppermute | solution.py:283
  20.7 1.8 %collective-permute-start.7 = (bf16[4,4,8,256]{3,2,1,0:T(8,128)(2,1)S(1)}, bf16[4,4,8,256]{3,2,1,0:T(8,128)(2,1)S(1)}, u32[]{:S(2)}, u32[]{:S(2)}) collective-permute-start(bf16[4,4,8,256]{3,2,1,0:T(8,128)(2,1)S(1)} %pad_maximum_fusion.1.x_ref), channel_id=1, source_target_pairs={{0,1},{1,0},{2,3},{3,2},{4,5},{5,4},{6,7},{7,6},{8,9},{9,8},{10,11... | collective-permute-start | bytes 196616 | tf_op jit(solution)/shard_map/ppermute | solution.py:278
  25.6 1.4 %collective-permute-start.8 = (bf16[4,8,512]{2,1,0:T(8,128)(2,1)S(1)}, bf16[4,8,512]{2,1,0:T(8,128)(2,1)S(1)}, u32[]{:S(2)}, u32[]{:S(2)}) collective-permute-start(bf16[4,8,512]{2,1,0:T(8,128)(2,1)S(1)} %get-tuple-element.55), channel_id=1, source_target_pairs={{0,1},{1,0},{2,3},{3,2},{4,5},{5,4},{6,7},{7,6},{8,9},{9,8},{10,11... | collective-permute-start | bytes 98312 | tf_op jit(solution)/shard_map/ppermute | solution.py:278
  27.0 6.3 %collective-permute-start.10 = (bf16[4,8,512]{2,1,0:T(8,128)(2,1)S(1)}, bf16[4,8,512]{2,1,0:T(8,128)(2,1)S(1)}, u32[]{:S(2)}, u32[]{:S(2)}) collective-permute-start(bf16[4,8,512]{2,1,0:T(8,128)(2,1)S(1)} %get-tuple-element.88), channel_id=1, source_target_pairs={{0,6},{1,7},{2,4},{3,5},{4,2},{5,3},{6,0},{7,1},{8,14},{9,15},{10,... | collective-permute-start | bytes 98312 | tf_op jit(solution)/shard_map/ppermute | solution.py:283
  29.1 4.5 %collective-permute-start.11 = (bf16[4,8,512]{2,1,0:T(8,128)(2,1)S(1)}, bf16[4,8,512]{2,1,0:T(8,128)(2,1)S(1)}, u32[]{:S(2)}, u32[]{:S(2)}) collective-permute-start(bf16[4,8,512]{2,1,0:T(8,128)(2,1)S(1)} %get-tuple-element.88), channel_id=1, source_target_pairs={{0,2},{1,3},{2,0},{3,1},{4,6},{5,7},{6,4},{7,5},{8,10},{9,11},{10,... | collective-permute-start | bytes 98312 | tf_op jit(solution)/shard_map/ppermute | solution.py:283
  29.1 4.8 %collective-permute-start.9 = (bf16[4,8,512]{2,1,0:T(8,128)(2,1)S(1)}, bf16[4,8,512]{2,1,0:T(8,128)(2,1)S(1)}, u32[]{:S(2)}, u32[]{:S(2)}) collective-permute-start(bf16[4,8,512]{2,1,0:T(8,128)(2,1)S(1)} %get-tuple-element.88), channel_id=1, source_target_pairs={{0,4},{1,5},{2,6},{3,7},{4,0},{5,1},{6,2},{7,3},{8,12},{9,13},{10,... | collective-permute-start | bytes 98312 | tf_op jit(solution)/shard_map/ppermute | solution.py:283
  34.0 1.9 %collective-permute-start.12 = (bf16[4,8,512]{2,1,0:T(8,128)(2,1)S(1)}, bf16[4,8,512]{2,1,0:T(8,128)(2,1)S(1)}, u32[]{:S(2)}, u32[]{:S(2)}) collective-permute-start(bf16[4,8,512]{2,1,0:T(8,128)(2,1)S(1)} %add_convert_fusion.1.x_ref), channel_id=1, source_target_pairs={{0,1},{1,0},{2,3},{3,2},{4,5},{5,4},{6,7},{7,6},{8,9},{9,8},{10,11... | collective-permute-start | bytes 98312 | tf_op jit(solution)/shard_map/ppermute | solution.py:278
  36.5 4.6 %collective-permute-start.13 = (bf16[8,512]{1,0:T(8,128)(2,1)S(1)}, bf16[8,512]{1,0:T(8,128)(2,1)S(1)}, u32[]{:S(2)}, u32[]{:S(2)}) collective-permute-start(bf16[8,512]{1,0:T(8,128)(2,1)S(1)} %get-tuple-element.62), channel_id=1, source_target_pairs={{0,4},{1,5},{2,6},{3,7},{4,0},{5,1},{6,2},{7,3},{8,12},{9,13},{10,... | collective-permute-start | bytes 24584 | tf_op jit(solution)/shard_map/ppermute | solution.py:283
  38.9 5.4 %collective-permute-start.14 = (bf16[8,512]{1,0:T(8,128)(2,1)S(1)}, bf16[8,512]{1,0:T(8,128)(2,1)S(1)}, u32[]{:S(2)}, u32[]{:S(2)}) collective-permute-start(bf16[8,512]{1,0:T(8,128)(2,1)S(1)} %get-tuple-element.62), channel_id=1, source_target_pairs={{0,6},{1,7},{2,4},{3,5},{4,2},{5,3},{6,0},{7,1},{8,14},{9,15},{10,... | collective-permute-start | bytes 24584 | tf_op jit(solution)/shard_map/ppermute | solution.py:283
  40.9 3.7 %collective-permute-start.15 = (bf16[8,512]{1,0:T(8,128)(2,1)S(1)}, bf16[8,512]{1,0:T(8,128)(2,1)S(1)}, u32[]{:S(2)}, u32[]{:S(2)}) collective-permute-start(bf16[8,512]{1,0:T(8,128)(2,1)S(1)} %get-tuple-element.62), channel_id=1, source_target_pairs={{0,2},{1,3},{2,0},{3,1},{4,6},{5,7},{6,4},{7,5},{8,10},{9,11},{10,... | collective-permute-start | bytes 24584 | tf_op jit(solution)/shard_map/ppermute | solution.py:283
  44.6 17.6 %copy-start.4 = (bf16[512,4096]{1,0:T(8,128)(2,1)S(1)}, bf16[512,4096]{1,0:T(8,128)(2,1)}, u32[]{:S(2)}) copy-start(bf16[512,4096]{1,0:T(8,128)(2,1)} %param.23) | copy-start | bytes 12582916
  44.6 1.3 %collective-permute-start.16 = (bf16[4,8,512]{2,1,0:T(8,128)(2,1)S(1)}, bf16[4,8,512]{2,1,0:T(8,128)(2,1)S(1)}, u32[]{:S(2)}, u32[]{:S(2)}) collective-permute-start(bf16[4,8,512]{2,1,0:T(8,128)(2,1)S(1)} %pad_maximum_fusion.2.x_ref), channel_id=1, source_target_pairs={{0,1},{1,0},{2,3},{3,2},{4,5},{5,4},{6,7},{7,6},{8,9},{9,8},{10,11... | collective-permute-start | bytes 98312 | tf_op jit(solution)/shard_map/ppermute | solution.py:278
  47.2 1.3 %collective-permute-start.17 = (bf16[4,8,512]{2,1,0:T(8,128)(2,1)S(1)}, bf16[4,8,512]{2,1,0:T(8,128)(2,1)S(1)}, u32[]{:S(2)}, u32[]{:S(2)}) collective-permute-start(bf16[4,8,512]{2,1,0:T(8,128)(2,1)S(1)} %get-tuple-element.67), channel_id=1, source_target_pairs={{0,1},{1,0},{2,3},{3,2},{4,5},{5,4},{6,7},{7,6},{8,9},{9,8},{10,11... | collective-permute-start | bytes 98312 | tf_op jit(solution)/shard_map/ppermute | solution.py:278
  48.5 4.9 %collective-permute-start.18 = (bf16[4,8,512]{2,1,0:T(8,128)(2,1)S(1)}, bf16[4,8,512]{2,1,0:T(8,128)(2,1)S(1)}, u32[]{:S(2)}, u32[]{:S(2)}) collective-permute-start(bf16[4,8,512]{2,1,0:T(8,128)(2,1)S(1)} %fusion.1), channel_id=1, source_target_pairs={{0,8},{8,16},{16,24},{24,0},{1,9},{9,17},{17,25},{25,1},{2,10},{10... | collective-permute-start | bytes 98312 | tf_op jit(solution)/shard_map/ppermute | solution.py:299
  50.1 3.9 %collective-permute-start.19 = (bf16[4,8,512]{2,1,0:T(8,128)(2,1)S(1)}, bf16[4,8,512]{2,1,0:T(8,128)(2,1)S(1)}, u32[]{:S(2)}, u32[]{:S(2)}) collective-permute-start(bf16[4,8,512]{2,1,0:T(8,128)(2,1)S(1)} %fusion.1), channel_id=1, source_target_pairs={{0,16},{8,24},{16,0},{24,8},{1,17},{9,25},{17,1},{25,9},{2,18},{10... | collective-permute-start | bytes 98312 | tf_op jit(solution)/shard_map/ppermute | solution.py:299
  51.6 3.9 %collective-permute-start.20 = (bf16[4,8,512]{2,1,0:T(8,128)(2,1)S(1)}, bf16[4,8,512]{2,1,0:T(8,128)(2,1)S(1)}, u32[]{:S(2)}, u32[]{:S(2)}) collective-permute-start(bf16[4,8,512]{2,1,0:T(8,128)(2,1)S(1)} %fusion.1), channel_id=1, source_target_pairs={{0,24},{8,0},{16,8},{24,16},{1,25},{9,1},{17,9},{25,17},{2,26},{10... | collective-permute-start | bytes 98312 | tf_op jit(solution)/shard_map/ppermute | solution.py:299
  55.5 5.0 %collective-permute-start.21 = (bf16[4,8,512]{2,1,0:T(8,128)(2,1)S(1)}, bf16[4,8,512]{2,1,0:T(8,128)(2,1)S(1)}, u32[]{:S(2)}, u32[]{:S(2)}) collective-permute-start(bf16[4,8,512]{2,1,0:T(8,128)(2,1)S(1)} %fusion.27), channel_id=1, source_target_pairs={{0,4},{1,5},{2,6},{3,7},{4,0},{5,1},{6,2},{7,3},{8,12},{9,13},{10,... | collective-permute-start | bytes 98312 | tf_op jit(solution)/shard_map/ppermute | solution.py:283
  56.0 5.7 %collective-permute-start.22 = (bf16[4,8,512]{2,1,0:T(8,128)(2,1)S(1)}, bf16[4,8,512]{2,1,0:T(8,128)(2,1)S(1)}, u32[]{:S(2)}, u32[]{:S(2)}) collective-permute-start(bf16[4,8,512]{2,1,0:T(8,128)(2,1)S(1)} %fusion.27), channel_id=1, source_target_pairs={{0,6},{1,7},{2,4},{3,5},{4,2},{5,3},{6,0},{7,1},{8,14},{9,15},{10,... | collective-permute-start | bytes 98312 | tf_op jit(solution)/shard_map/ppermute | solution.py:283
  58.0 4.1 %collective-permute-start.23 = (bf16[4,8,512]{2,1,0:T(8,128)(2,1)S(1)}, bf16[4,8,512]{2,1,0:T(8,128)(2,1)S(1)}, u32[]{:S(2)}, u32[]{:S(2)}) collective-permute-start(bf16[4,8,512]{2,1,0:T(8,128)(2,1)S(1)} %fusion.27), channel_id=1, source_target_pairs={{0,2},{1,3},{2,0},{3,1},{4,6},{5,7},{6,4},{7,5},{8,10},{9,11},{10,... | collective-permute-start | bytes 98312 | tf_op jit(solution)/shard_map/ppermute | solution.py:283
  62.1 1.3 %collective-permute-start.24 = (bf16[4,8,512]{2,1,0:T(8,128)(2,1)S(1)}, bf16[4,8,512]{2,1,0:T(8,128)(2,1)S(1)}, u32[]{:S(2)}, u32[]{:S(2)}) collective-permute-start(bf16[4,8,512]{2,1,0:T(8,128)(2,1)S(1)} %add_convert_fusion.x_ref), channel_id=1, source_target_pairs={{0,1},{1,0},{2,3},{3,2},{4,5},{5,4},{6,7},{7,6},{8,9},{9,8},{10,11... | collective-permute-start | bytes 98312 | tf_op jit(solution)/shard_map/ppermute | solution.py:278
  64.4 1.2 %collective-permute-start.25 = (bf16[4,1,8,512]{3,2,0,1:T(8,128)(2,1)S(1)}, bf16[4,1,8,512]{3,2,0,1:T(8,128)(2,1)S(1)}, u32[]{:S(2)}, u32[]{:S(2)}) collective-permute-start(bf16[4,1,8,512]{3,2,0,1:T(8,128)(2,1)S(1)} %bitcast.81), channel_id=1, source_target_pairs={{0,1},{1,0},{2,3},{3,2},{4,5},{5,4},{6,7},{7,6},{8,9},{9,8},{10,11... | collective-permute-start | bytes 98312 | tf_op jit(solution)/shard_map/ppermute | solution.py:278
  65.6 5.6 %collective-permute-start.26 = (bf16[4,8,512]{2,1,0:T(8,128)(2,1)S(1)}, bf16[4,8,512]{2,1,0:T(8,128)(2,1)S(1)}, u32[]{:S(2)}, u32[]{:S(2)}) collective-permute-start(bf16[4,8,512]{2,1,0:T(8,128)(2,1)S(1)} %bitcast_convert_fusion.1), channel_id=1, source_target_pairs={{0,4},{1,5},{2,6},{3,7},{4,0},{5,1},{6,2},{7,3},{8,12},{9,13},{10,... | collective-permute-start | bytes 98312 | tf_op jit(solution)/shard_map/ppermute | solution.py:283
  67.0 5.7 %collective-permute-start.27 = (bf16[4,8,512]{2,1,0:T(8,128)(2,1)S(1)}, bf16[4,8,512]{2,1,0:T(8,128)(2,1)S(1)}, u32[]{:S(2)}, u32[]{:S(2)}) collective-permute-start(bf16[4,8,512]{2,1,0:T(8,128)(2,1)S(1)} %bitcast_convert_fusion.1), channel_id=1, source_target_pairs={{0,6},{1,7},{2,4},{3,5},{4,2},{5,3},{6,0},{7,1},{8,14},{9,15},{10,... | collective-permute-start | bytes 98312 | tf_op jit(solution)/shard_map/ppermute | solution.py:283
  68.9 4.1 %collective-permute-start.28 = (bf16[4,8,512]{2,1,0:T(8,128)(2,1)S(1)}, bf16[4,8,512]{2,1,0:T(8,128)(2,1)S(1)}, u32[]{:S(2)}, u32[]{:S(2)}) collective-permute-start(bf16[4,8,512]{2,1,0:T(8,128)(2,1)S(1)} %bitcast_convert_fusion.1), channel_id=1, source_target_pairs={{0,2},{1,3},{2,0},{3,1},{4,6},{5,7},{6,4},{7,5},{8,10},{9,11},{10,... | collective-permute-start | bytes 98312 | tf_op jit(solution)/shard_map/ppermute | solution.py:283
  73.1 1.3 %collective-permute-start.29 = (bf16[4,8,512]{2,1,0:T(8,128)(2,1)S(1)}, bf16[4,8,512]{2,1,0:T(8,128)(2,1)S(1)}, u32[]{:S(2)}, u32[]{:S(2)}) collective-permute-start(bf16[4,8,512]{2,1,0:T(8,128)(2,1)S(1)} %fusion.own_ref), channel_id=1, source_target_pairs={{0,1},{1,0},{2,3},{3,2},{4,5},{5,4},{6,7},{7,6},{8,9},{9,8},{10,11... | collective-permute-start | bytes 98312 | tf_op jit(solution)/shard_map/ppermute | solution.py:278
  75.7 1.2 %collective-permute-start.30 = (bf16[4,1,8,512]{3,2,1,0:T(8,128)(2,1)S(1)}, bf16[4,1,8,512]{3,2,1,0:T(8,128)(2,1)S(1)}, u32[]{:S(2)}, u32[]{:S(2)}) collective-permute-start(bf16[4,1,8,512]{3,2,1,0:T(8,128)(2,1)S(1)} %get-tuple-element.71), channel_id=1, source_target_pairs={{0,1},{1,0},{2,3},{3,2},{4,5},{5,4},{6,7},{7,6},{8,9},{9,8},{10,11... | collective-permute-start | bytes 98312 | tf_op jit(solution)/shard_map/ppermute | solution.py:278
  76.9 4.7 %collective-permute-start.31 = (bf16[1,8,512]{2,1,0:T(8,128)(2,1)S(1)}, bf16[1,8,512]{2,1,0:T(8,128)(2,1)S(1)}, u32[]{:S(2)}, u32[]{:S(2)}) collective-permute-start(bf16[1,8,512]{2,1,0:T(8,128)(2,1)S(1)} %get-tuple-element.99), channel_id=1, source_target_pairs={{0,4},{1,5},{2,6},{3,7},{4,0},{5,1},{6,2},{7,3},{8,12},{9,13},{10,... | collective-permute-start | bytes 24584 | tf_op jit(solution)/shard_map/ppermute | solution.py:283
  77.6 5.4 %collective-permute-start.32 = (bf16[1,8,512]{2,1,0:T(8,128)(2,1)S(1)}, bf16[1,8,512]{2,1,0:T(8,128)(2,1)S(1)}, u32[]{:S(2)}, u32[]{:S(2)}) collective-permute-start(bf16[1,8,512]{2,1,0:T(8,128)(2,1)S(1)} %get-tuple-element.98), channel_id=1, source_target_pairs={{0,6},{1,7},{2,4},{3,5},{4,2},{5,3},{6,0},{7,1},{8,14},{9,15},{10,... | collective-permute-start | bytes 24584 | tf_op jit(solution)/shard_map/ppermute | solution.py:283
  79.5 3.7 %collective-permute-start.33 = (bf16[1,8,512]{2,1,0:T(8,128)(2,1)S(1)}, bf16[1,8,512]{2,1,0:T(8,128)(2,1)S(1)}, u32[]{:S(2)}, u32[]{:S(2)}) collective-permute-start(bf16[1,8,512]{2,1,0:T(8,128)(2,1)S(1)} %get-tuple-element.97), channel_id=1, source_target_pairs={{0,2},{1,3},{2,0},{3,1},{4,6},{5,7},{6,4},{7,5},{8,10},{9,11},{10,... | collective-permute-start | bytes 24584 | tf_op jit(solution)/shard_map/ppermute | solution.py:283
  83.5 1.2 %collective-permute-start.34 = (bf16[4,1,8,512]{3,2,0,1:T(8,128)(2,1)S(1)}, bf16[4,1,8,512]{3,2,0,1:T(8,128)(2,1)S(1)}, u32[]{:S(2)}, u32[]{:S(2)}) collective-permute-start(bf16[4,1,8,512]{3,2,0,1:T(8,128)(2,1)S(1)} %bitcast.80), channel_id=1, source_target_pairs={{0,1},{1,0},{2,3},{3,2},{4,5},{5,4},{6,7},{7,6},{8,9},{9,8},{10,11... | collective-permute-start | bytes 98312 | tf_op jit(solution)/shard_map/ppermute | solution.py:278
  84.8 5.6 %collective-permute-start.35 = (bf16[4,8,512]{2,1,0:T(8,128)(2,1)S(1)}, bf16[4,8,512]{2,1,0:T(8,128)(2,1)S(1)}, u32[]{:S(2)}, u32[]{:S(2)}) collective-permute-start(bf16[4,8,512]{2,1,0:T(8,128)(2,1)S(1)} %bitcast_convert_fusion), channel_id=1, source_target_pairs={{0,4},{1,5},{2,6},{3,7},{4,0},{5,1},{6,2},{7,3},{8,12},{9,13},{10,... | collective-permute-start | bytes 98312 | tf_op jit(solution)/shard_map/ppermute | solution.py:283
  86.3 5.7 %collective-permute-start.36 = (bf16[4,8,512]{2,1,0:T(8,128)(2,1)S(1)}, bf16[4,8,512]{2,1,0:T(8,128)(2,1)S(1)}, u32[]{:S(2)}, u32[]{:S(2)}) collective-permute-start(bf16[4,8,512]{2,1,0:T(8,128)(2,1)S(1)} %bitcast_convert_fusion), channel_id=1, source_target_pairs={{0,6},{1,7},{2,4},{3,5},{4,2},{5,3},{6,0},{7,1},{8,14},{9,15},{10,... | collective-permute-start | bytes 98312 | tf_op jit(solution)/shard_map/ppermute | solution.py:283
  88.2 4.2 %collective-permute-start.37 = (bf16[4,8,512]{2,1,0:T(8,128)(2,1)S(1)}, bf16[4,8,512]{2,1,0:T(8,128)(2,1)S(1)}, u32[]{:S(2)}, u32[]{:S(2)}) collective-permute-start(bf16[4,8,512]{2,1,0:T(8,128)(2,1)S(1)} %bitcast_convert_fusion), channel_id=1, source_target_pairs={{0,2},{1,3},{2,0},{3,1},{4,6},{5,7},{6,4},{7,5},{8,10},{9,11},{10,... | collective-permute-start | bytes 98312 | tf_op jit(solution)/shard_map/ppermute | solution.py:283
  92.4 1.3 %collective-permute-start.38 = (bf16[4,8,512]{2,1,0:T(8,128)(2,1)S(1)}, bf16[4,8,512]{2,1,0:T(8,128)(2,1)S(1)}, u32[]{:S(2)}, u32[]{:S(2)}) collective-permute-start(bf16[4,8,512]{2,1,0:T(8,128)(2,1)S(1)} %get-tuple-element.86.refs_2_), channel_id=1, source_target_pairs={{0,1},{1,0},{2,3},{3,2},{4,5},{5,4},{6,7},{7,6},{8,9},{9,8},{10,11... | collective-permute-start | bytes 98312 | tf_op jit(solution)/shard_map/ppermute | solution.py:278
  96.2 1.4 %collective-permute-start.39 = (bf16[4,4,8,256]{3,2,1,0:T(8,128)(2,1)S(1)}, bf16[4,4,8,256]{3,2,1,0:T(8,128)(2,1)S(1)}, u32[]{:S(2)}, u32[]{:S(2)}) collective-permute-start(bf16[4,4,8,256]{3,2,1,0:T(8,128)(2,1)S(1)} %get-tuple-element.77), channel_id=1, source_target_pairs={{0,1},{1,0},{2,3},{3,2},{4,5},{5,4},{6,7},{7,6},{8,9},{9,8},{10,11... | collective-permute-start | bytes 196616 | tf_op jit(solution)/shard_map/ppermute | solution.py:278
  97.6 4.8 %collective-permute-start.40 = (bf16[4,8,256]{2,1,0:T(8,128)(2,1)S(1)}, bf16[4,8,256]{2,1,0:T(8,128)(2,1)S(1)}, u32[]{:S(2)}, u32[]{:S(2)}) collective-permute-start(bf16[4,8,256]{2,1,0:T(8,128)(2,1)S(1)} %get-tuple-element.95), channel_id=1, source_target_pairs={{0,4},{1,5},{2,6},{3,7},{4,0},{5,1},{6,2},{7,3},{8,12},{9,13},{10,... | collective-permute-start | bytes 49160 | tf_op jit(solution)/shard_map/ppermute | solution.py:283
  98.3 5.5 %collective-permute-start.41 = (bf16[4,8,256]{2,1,0:T(8,128)(2,1)S(1)}, bf16[4,8,256]{2,1,0:T(8,128)(2,1)S(1)}, u32[]{:S(2)}, u32[]{:S(2)}) collective-permute-start(bf16[4,8,256]{2,1,0:T(8,128)(2,1)S(1)} %get-tuple-element.94), channel_id=1, source_target_pairs={{0,6},{1,7},{2,4},{3,5},{4,2},{5,3},{6,0},{7,1},{8,14},{9,15},{10,... | collective-permute-start | bytes 49160 | tf_op jit(solution)/shard_map/ppermute | solution.py:283
  100.2 3.8 %collective-permute-start.42 = (bf16[4,8,256]{2,1,0:T(8,128)(2,1)S(1)}, bf16[4,8,256]{2,1,0:T(8,128)(2,1)S(1)}, u32[]{:S(2)}, u32[]{:S(2)}) collective-permute-start(bf16[4,8,256]{2,1,0:T(8,128)(2,1)S(1)} %get-tuple-element.93), channel_id=1, source_target_pairs={{0,2},{1,3},{2,0},{3,1},{4,6},{5,7},{6,4},{7,5},{8,10},{9,11},{10,... | collective-permute-start | bytes 49160 | tf_op jit(solution)/shard_map/ppermute | solution.py:283
  104.4 1.3 %collective-permute-start.43 = (bf16[4,4,8,256]{3,2,1,0:T(8,128)(2,1)S(1)}, bf16[4,4,8,256]{3,2,1,0:T(8,128)(2,1)S(1)}, u32[]{:S(2)}, u32[]{:S(2)}) collective-permute-start(bf16[4,4,8,256]{3,2,1,0:T(8,128)(2,1)S(1)} %get-tuple-element.80), channel_id=1, source_target_pairs={{0,1},{1,0},{2,3},{3,2},{4,5},{5,4},{6,7},{7,6},{8,9},{9,8},{10,11... | collective-permute-start | bytes 196616 | tf_op jit(solution)/shard_map/ppermute | solution.py:278
  105.7 4.8 %collective-permute-start.44 = (bf16[4,8,256]{2,1,0:T(8,128)(2,1)S(1)}, bf16[4,8,256]{2,1,0:T(8,128)(2,1)S(1)}, u32[]{:S(2)}, u32[]{:S(2)}) collective-permute-start(bf16[4,8,256]{2,1,0:T(8,128)(2,1)S(1)} %get-tuple-element.90), channel_id=1, source_target_pairs={{0,4},{1,5},{2,6},{3,7},{4,0},{5,1},{6,2},{7,3},{8,12},{9,13},{10,... | collective-permute-start | bytes 49160 | tf_op jit(solution)/shard_map/ppermute | solution.py:283
  107.1 5.5 %collective-permute-start.45 = (bf16[4,8,256]{2,1,0:T(8,128)(2,1)S(1)}, bf16[4,8,256]{2,1,0:T(8,128)(2,1)S(1)}, u32[]{:S(2)}, u32[]{:S(2)}) collective-permute-start(bf16[4,8,256]{2,1,0:T(8,128)(2,1)S(1)} %get-tuple-element.92), channel_id=1, source_target_pairs={{0,6},{1,7},{2,4},{3,5},{4,2},{5,3},{6,0},{7,1},{8,14},{9,15},{10,... | collective-permute-start | bytes 49160 | tf_op jit(solution)/shard_map/ppermute | solution.py:283
  109.1 3.8 %collective-permute-start.46 = (bf16[4,8,256]{2,1,0:T(8,128)(2,1)S(1)}, bf16[4,8,256]{2,1,0:T(8,128)(2,1)S(1)}, u32[]{:S(2)}, u32[]{:S(2)}) collective-permute-start(bf16[4,8,256]{2,1,0:T(8,128)(2,1)S(1)} %get-tuple-element.91), channel_id=1, source_target_pairs={{0,2},{1,3},{2,0},{3,1},{4,6},{5,7},{6,4},{7,5},{8,10},{9,11},{10,... | collective-permute-start | bytes 49160 | tf_op jit(solution)/shard_map/ppermute | solution.py:283
  (10 other events, 81.8 us)

commit v11 on v10

--- a/solution.py
+++ b/solution.py
@@ -142,31 +142,9 @@
     return jnp.where(along(line, below) == target, below, -1)
 
 
-def find(plan, targets, width):
-    sets, length = targets.shape
-
-    def body(plan_ref, list_ref, out_ref):
-        tiles = length // LANES
-        for tile in range(tiles):
-            for s in range(sets):
-                line = list_ref[s : s + 1, tile * LANES : (tile + 1) * LANES]
-                lo = plan_ref[s * tiles + tile]
-                out_ref[s, tile] = position(jnp.broadcast_to(line, (BLOCKS, LANES)), lo)
-
-    return call(
-        body,
-        [((sets, length // LANES, BLOCKS, LANES), I32)],
-        [plan, targets],
-        [SMEM, VMEM],
-        moved=2 << 20,
-        name="find",
-    )[0]
-
-
-def scatter_walk(plan_ref, list_ref, at_ref, update_ref, acc_ref):
+def scatter_walk(plan_ref, list_ref, update_ref, acc_ref):
     def visit(s, lanes, line, lo, first):
-        x = update_ref[s, :, lanes]
-        at = at_ref[s, lanes.start // LANES] if first else position(line, lo)
+        x, at = update_ref[s, :, lanes], position(line, lo)
         parts = [pick(x, jnp.broadcast_to(at[u : u + 1], x.shape)) for u in range(BLOCKS)]
         acc_ref[pl.ds(lo, BLOCKS)] += jnp.stack(parts)
 
@@ -371,7 +349,6 @@
     lb, prepared, rhs = lax.optimization_barrier((lb, prepared, rhs))
     leaf_list, leaf_plan = prepared
     lb = leaf_halves(lb, leaf_inv, "leaf_solve_own") if leaf_aligned else (lb,)
-    lb, leaf_at = lax.optimization_barrier((lb, find(leaf_plan, leaf_list, tall)))
 
     def leaf_solve(*refs):
         x_refs, (w_ref, y_ref, send_ref) = refs[: len(lb)], refs[len(lb) :]
@@ -396,12 +373,12 @@
 
     def leaf_update(*refs):
         x_refs, refs = refs[: len(lyb)], refs[len(lyb) :]
-        plan_ref, w_ref, list_ref, at_ref, rhs_ref, own_ref, other_ref, root_ref, *refs = refs
+        plan_ref, w_ref, list_ref, rhs_ref, own_ref, other_ref, root_ref, *refs = refs
         update_ref, acc_ref, sum_ref = refs
         acc_ref[...] = jnp.zeros(acc_ref.shape, F32)
         for s in range(leaves):
             update_ref[s] = leaf_product(x_refs, w_ref, s)
-        scatter_walk(plan_ref, list_ref, at_ref, update_ref, acc_ref)
+        scatter_walk(plan_ref, list_ref, update_ref, acc_ref)
         for b in range(parent_width // LANES):
             sum_ref[:, b * LANES : (b + 1) * LANES] = -acc_ref[b]
         sum_ref[:, spot(lax.axis_index("rows"), parent_cols)] += rhs_ref[:, 0, :]
@@ -416,8 +393,8 @@
             ((chips, rcount, parent_cols), BF16),
             ((root_width // LANES, rcount, LANES), F32),
         ],
-        [*lyb, leaf_plan, pinned(leaf_panel), leaf_list, leaf_at, parent_rhs],
-        [VMEM] * len(lyb) + [SMEM] + [VMEM] * 4,
+        [*lyb, leaf_plan, pinned(leaf_panel), leaf_list, parent_rhs],
+        [VMEM] * len(lyb) + [SMEM] + [VMEM] * 3,
         scratch=[
             pltpu.VMEM((leaves, rcount, leaf_local), F32),
             pltpu.VMEM((tall // LANES + BLOCKS, rcount, LANES), F32),
@@ -429,9 +406,6 @@
     prepared = prepare(own, [(parent_rows, parent_local, parent_height)])
     prb, prepared = lax.optimization_barrier((chips_sum(own).astype(BF16), prepared))
     parent_list, parent_plan = prepared
-    parent_at = find(parent_plan, parent_list, root_width)
-
-    prb_other, parent_at = lax.optimization_barrier((swap(prb), parent_at))
 
     def parent_solve(part_ref, x_ref, w_ref, y_ref, send_ref):
         y = both_halves(part_ref, x_ref, w_ref, 0)
@@ -441,20 +415,20 @@
     py, pyb = call(
         parent_solve,
         [((rcount, parent_cols), F32), ((rcount, parent_cols), BF16)],
-        [own_half(prb, parent_inv, "parent_solve_own"), prb_other, pinned(parent_inv)],
+        [own_half(prb, parent_inv, "parent_solve_own"), swap(prb), pinned(parent_inv)],
         [VMEM] * 3,
         name="parent_solve",
     )
     pyb = far_gather(pyb)
 
     def parent_update(
-        plan_ref, part_ref, x_ref, w_ref, list_ref, at_ref, root_ref, rhs_ref, own_ref, other_ref,
+        plan_ref, part_ref, x_ref, w_ref, list_ref, root_ref, rhs_ref, own_ref, other_ref,
         update_ref, acc_ref, sum_ref,
     ):
         for b in range(root_width // LANES):
             acc_ref[b] = root_ref[b]
         update_ref[0] = both_halves(part_ref, x_ref, w_ref, 0, xor=True)
-        scatter_walk(plan_ref, list_ref, at_ref, update_ref, acc_ref)
+        scatter_walk(plan_ref, list_ref, update_ref, acc_ref)
         for b in range(root_width // LANES):
             sum_ref[:, b * LANES : (b + 1) * LANES] = -acc_ref[b]
         if root_aligned:
@@ -472,11 +446,10 @@
             swap(pyb),
             pinned(parent_panel),
             parent_list,
-            parent_at,
             root_acc,
             rhs,
         ],
-        [SMEM] + [VMEM] * 7,
+        [SMEM] + [VMEM] * 6,
         scratch=[
             pltpu.VMEM((1, rcount, parent_local), F32),
             pltpu.VMEM((root_width // LANES + BLOCKS, rcount, LANES), F32),

time: 114 us -> 117 us (1.026)
  waiting for transfers between devices: 38.9 us -> 46.3 us
  Pallas kernels: 25.1 us -> 22.6 us
  starting transfers between devices: 45.6 us -> 43.9 us
    ppermute x30, waiting for transfers between devices: 28 us -> 32.6 us  [far(): return lax.ppermute(x, 'rows', [(i, i ^ 2 * k) for i in range(n)])]
    pallas_call x25 -> x23, Pallas kernels: 25.1 us -> 22.6 us  [call(): pl.pallas_call(body, out_shape=[jax.ShapeDtypeStruct(*o) if isinstance(o,...]
    ppermute x3, waiting for transfers between devices: 2.47 us -> 4.22 us  [leaf_sum(): lax.ppermute(b, 'leaf', [(i, (i + k) % n) for i in range(n)]).astype(F32)]
  transfers between devices with their start and end apart: 47 -> 47, of which waited for: 39 -> 40; matrix products, arithmetic and copies ran while one was open for 1% -> 1% of each run, Pallas kernels for 12% -> 10%
where the time goes in v11:
time: 117 us
  waiting for transfers between devices  46.3 us (40%)
  starting transfers between devices  43.9 us (38%)
  Pallas kernels  22.6 us (19%)
  local copies, waits for them, and re-layouts  2.04 us (2%)
  between operations  1.59 us (1%)
    ppermute x30, starting transfers between devices, far(): return lax.ppermute(x, 'rows', [(i, i ^ 2 * k) for i in range(n)])  38.5 us
    ppermute x30, waiting for transfers between devices, far(): return lax.ppermute(x, 'rows', [(i, i ^ 2 * k) for i in range(n)])  32.6 us
    pallas_call x23, Pallas kernels, call(): pl.pallas_call(body, out_shape=[jax.ShapeDtypeStruct(*o) if isinstance(o,...  22.6 us
    ppermute x14, waiting for transfers between devices, swap(): return lax.ppermute(x, 'rows', [(i, i ^ 1) for i in range(n)])  9.47 us
    ppermute x3, waiting for transfers between devices, leaf_sum(): lax.ppermute(b, 'leaf', [(i, (i + k) % n) for i in range(n)]).astype(F32)  4.22 us
    ppermute x3, starting transfers between devices, leaf_sum(): lax.ppermute(b, 'leaf', [(i, (i + k) % n) for i in range(n)]).astype(F32)  3.6 us
  transfers between devices with their start and end apart: 47, of which 40 were waited for; matrix products, arithmetic and copies ran while one was open for 1% of the time, Pallas kernels for 10%

profile of v11, /device:TPU:0, one launch (start us, length us, event | category | flops | bytes accessed | tf_op | source)
XLA Modules:
  0.0 116.7 jit_solution(18112962193541200421)
XLA Ops:
  1.4 3.1 %collective-permute-start.2 = (bf16[4,8,256]{2,1,0:T(8,128)(2,1)S(1)}, bf16[4,8,256]{2,1,0:T(8,128)(2,1)S(1)}, u32[]{:S(2)}, u32[]{:S(2)}) collective-permute-start(bf16[4,8,256]{2,1,0:T(8,128)(2,1)S(1)} %round_rhs.1.refs_0_), channel_id=1, source_target_pairs={{0,2},{1,3},{2,0},{3,1},{4,6},{5,7},{6,4},{7,5},{8,10},{9,11},{10,... | collective-permute-start | bytes 49160 | tf_op jit(solution)/shard_map/ppermute | solution.py:261
  4.5 2.5 %collective-permute-start.1 = (bf16[4,8,256]{2,1,0:T(8,128)(2,1)S(1)}, bf16[4,8,256]{2,1,0:T(8,128)(2,1)S(1)}, u32[]{:S(2)}, u32[]{:S(2)}) collective-permute-start(bf16[4,8,256]{2,1,0:T(8,128)(2,1)S(1)} %round_rhs.1.refs_0_), channel_id=1, source_target_pairs={{0,6},{1,7},{2,4},{3,5},{4,2},{5,3},{6,0},{7,1},{8,14},{9,15},{10,... | collective-permute-start | bytes 49160 | tf_op jit(solution)/shard_map/ppermute | solution.py:261
  7.1 2.2 %prepare.2 = (s32[4,1024]{1,0:T(4,128)S(1)}, s32[33]{0:T(128)S(1)}) custom-call(bf16[4,8,256]{2,1,0:T(8,128)(2,1)S(1)} %round_rhs.1.refs_0_, s32[4,1024]{1,0:T(4,128)S(1)} %copy-done.5, s32[4]{0:T(128)S(1)} %copy-done.10), custom_call_target="tpu_custom_call" | custom-call | bytes 4194304 | tf_op jit(solution)/shard_map/prepare/pallas_call | solution.py:30
  9.3 1.0 collective-permute-done.1
  10.3 1.4 %collective-permute-done = bf16[4,8,256]{2,1,0:T(8,128)(2,1)S(1)} collective-permute-done((bf16[4,8,256]{2,1,0:T(8,128)(2,1)S(1)}, bf16[4,8,256]{2,1,0:T(8,128)(2,1)S(1)}, u32[]{:S(2)}, u32[]{:S(2)}) %collective-permute-start) | collective-permute-done | bytes 16416 | tf_op jit(solution)/shard_map/ppermute | solution.py:261
  14.4 1.2 %collective-permute-start.5 = (bf16[4,8,256]{2,1,0:T(8,128)(2,1)S(1)}, bf16[4,8,256]{2,1,0:T(8,128)(2,1)S(1)}, u32[]{:S(2)}, u32[]{:S(2)}) collective-permute-start(bf16[4,8,256]{2,1,0:T(8,128)(2,1)S(1)} %get-tuple-element.42.x_ref), channel_id=1, source_target_pairs={{0,6},{1,7},{2,4},{3,5},{4,2},{5,3},{6,0},{7,1},{8,14},{9,15},{10,... | collective-permute-start | bytes 49160 | tf_op jit(solution)/shard_map/ppermute | solution.py:261
  15.6 1.5 %collective-permute-start.4 = (bf16[4,8,256]{2,1,0:T(8,128)(2,1)S(1)}, bf16[4,8,256]{2,1,0:T(8,128)(2,1)S(1)}, u32[]{:S(2)}, u32[]{:S(2)}) collective-permute-start(bf16[4,8,256]{2,1,0:T(8,128)(2,1)S(1)} %get-tuple-element.42.x_ref), channel_id=1, source_target_pairs={{0,4},{1,5},{2,6},{3,7},{4,0},{5,1},{6,2},{7,3},{8,12},{9,13},{10,... | collective-permute-start | bytes 49160 | tf_op jit(solution)/shard_map/ppermute | solution.py:261
  17.8 2.1 %collective-permute-done.5 = bf16[4,8,256]{2,1,0:T(8,128)(2,1)S(1)} collective-permute-done((bf16[4,8,256]{2,1,0:T(8,128)(2,1)S(1)}, bf16[4,8,256]{2,1,0:T(8,128)(2,1)S(1)}, u32[]{:S(2)}, u32[]{:S(2)}) %collective-permute-start.5) | collective-permute-done | bytes 16416 | tf_op jit(solution)/shard_map/ppermute | solution.py:261
  20.5 1.7 %leaf_update_own.1.refs_0_ = f32[4,8,1024]{2,1,0:T(8,128)S(1)} custom-call(bf16[4,4,8,256]{3,2,1,0:T(8,128)(2,1)S(1)} %pad_maximum_fusion.1.x_ref, bf16[4,1024,2048]{2,1,0:T(8,128)(2,1)S(1)} %copy-done, f32[4,8,1024]{2,1,0:T(8,128)S(1)} %leaf_update_first.1.refs_0_), custom_call_target="tpu_custom_call" | custom-call | bytes 12582912 | tf_op jit(solution)/shard_map/leaf_update_own/pallas_call | solution.py:30
  22.3 3.1 %leaf_update.1 = (f32[4,8,512]{2,1,0:T(8,128)S(1)}, bf16[4,8,512]{2,1,0:T(8,128)(2,1)S(1)}, f32[32,8,128]{2,1,0:T(8,128)S(1)}) custom-call(f32[4,8,1024]{2,1,0:T(8,128)S(1)} %leaf_update_own.1.refs_0_, bf16[4,4,8,256]{3,2,1,0:T(8,128)(2,1)S(1)} %collective-permute-done.7.refs_1_, s32[33]{0:T(128)S(1)} %get-tuple-element.40.refs_2_.refs_0_, ...), custom_call_target="tpu_custom_call" | custom-call | tf_op jit(solution)/shard_map/leaf_update/pallas_call | solution.py:30
  27.3 2.5 %collective-permute-start.10 = (bf16[4,8,512]{2,1,0:T(8,128)(2,1)S(1)}, bf16[4,8,512]{2,1,0:T(8,128)(2,1)S(1)}, u32[]{:S(2)}, u32[]{:S(2)}) collective-permute-start(bf16[4,8,512]{2,1,0:T(8,128)(2,1)S(1)} %get-tuple-element.78), channel_id=1, source_target_pairs={{0,6},{1,7},{2,4},{3,5},{4,2},{5,3},{6,0},{7,1},{8,14},{9,15},{10,... | collective-permute-start | bytes 98312 | tf_op jit(solution)/shard_map/ppermute | solution.py:261
  31.0 1.2 %prepare.3 = (s32[1,512]{1,0:T(1,128)S(1)}, s32[5]{0:T(128)S(1)}) custom-call(f32[4,8,512]{2,1,0:T(8,128)S(1)} %get-tuple-element.79.refs_0_, s32[1,512]{1,0:T(1,128)S(1)} %copy-done.8, s32[1]{0:T(128)S(6)} %copy.21.refs_2_), custom_call_target="tpu_custom_call" | custom-call | bytes 4194304 | tf_op jit(solution)/shard_map/prepare/pallas_call | solution.py:30
  33.0 1.9 %collective-permute-done.9 = bf16[4,8,512]{2,1,0:T(8,128)(2,1)S(1)} collective-permute-done((bf16[4,8,512]{2,1,0:T(8,128)(2,1)S(1)}, bf16[4,8,512]{2,1,0:T(8,128)(2,1)S(1)}, u32[]{:S(2)}, u32[]{:S(2)}) %collective-permute-start.9) | collective-permute-done | bytes 32800 | tf_op jit(solution)/shard_map/ppermute | solution.py:261
  37.4 1.5 %collective-permute-start.14 = (bf16[8,512]{1,0:T(8,128)(2,1)S(1)}, bf16[8,512]{1,0:T(8,128)(2,1)S(1)}, u32[]{:S(2)}, u32[]{:S(2)}) collective-permute-start(bf16[8,512]{1,0:T(8,128)(2,1)S(1)} %get-tuple-element.52), channel_id=1, source_target_pairs={{0,6},{1,7},{2,4},{3,5},{4,2},{5,3},{6,0},{7,1},{8,14},{9,15},{10,... | collective-permute-start | bytes 24584 | tf_op jit(solution)/shard_map/ppermute | solution.py:261
  38.9 1.5 %collective-permute-start.13 = (bf16[8,512]{1,0:T(8,128)(2,1)S(1)}, bf16[8,512]{1,0:T(8,128)(2,1)S(1)}, u32[]{:S(2)}, u32[]{:S(2)}) collective-permute-start(bf16[8,512]{1,0:T(8,128)(2,1)S(1)} %get-tuple-element.52), channel_id=1, source_target_pairs={{0,4},{1,5},{2,6},{3,7},{4,0},{5,1},{6,2},{7,3},{8,12},{9,13},{10,... | collective-permute-start | bytes 24584 | tf_op jit(solution)/shard_map/ppermute | solution.py:261
  40.6 2.3 %collective-permute-done.14 = bf16[8,512]{1,0:T(8,128)(2,1)S(1)} collective-permute-done((bf16[8,512]{1,0:T(8,128)(2,1)S(1)}, bf16[8,512]{1,0:T(8,128)(2,1)S(1)}, u32[]{:S(2)}, u32[]{:S(2)}) %collective-permute-start.14) | collective-permute-done | bytes 8224 | tf_op jit(solution)/shard_map/ppermute | solution.py:261
  44.7 1.4 %parent_update.1 = (f32[4,8,512]{2,1,0:T(8,128)S(1)}, bf16[4,8,512]{2,1,0:T(8,128)(2,1)S(1)}) custom-call(s32[5]{0:T(128)S(1)} %get-tuple-element.50.plan_ref, f32[1,8,512]{2,1,0:T(8,128)S(1)} %parent_update_own.1.part_ref, bf16[4,8,512]{2,1,0:T(8,128)(2,1)S(1)} %collective-permute-done.16.x_ref, bf16[1,512,4096]{2,1,0:T(8,128)(2,1)S(1)} %copy-done.1, ...), custom_call_target="tpu_custom_call" | custom-call | tf_op jit(solution)/shard_map/parent_update/pallas_call | solution.py:30
  46.3 1.0 collective-permute-done.17
  47.4 2.5 %collective-permute-start.20 = (bf16[4,8,512]{2,1,0:T(8,128)(2,1)S(1)}, bf16[4,8,512]{2,1,0:T(8,128)(2,1)S(1)}, u32[]{:S(2)}, u32[]{:S(2)}) collective-permute-start(bf16[4,8,512]{2,1,0:T(8,128)(2,1)S(1)} %fusion.1), channel_id=1, source_target_pairs={{0,24},{8,0},{16,8},{24,16},{1,25},{9,1},{17,9},{25,17},{2,26},{10... | collective-permute-start | bytes 98312 | tf_op jit(solution)/shard_map/ppermute | solution.py:277
  51.5 2.7 %collective-permute-done.19 = bf16[4,8,512]{2,1,0:T(8,128)(2,1)S(1)} collective-permute-done((bf16[4,8,512]{2,1,0:T(8,128)(2,1)S(1)}, bf16[4,8,512]{2,1,0:T(8,128)(2,1)S(1)}, u32[]{:S(2)}, u32[]{:S(2)}) %collective-permute-start.19) | collective-permute-done | bytes 32800 | tf_op jit(solution)/shard_map/ppermute | solution.py:277
  54.1 1.1 collective-permute-done.18
  55.2 1.0 collective-permute-start.23
  56.2 2.1 %collective-permute-start.22 = (bf16[4,8,512]{2,1,0:T(8,128)(2,1)S(1)}, bf16[4,8,512]{2,1,0:T(8,128)(2,1)S(1)}, u32[]{:S(2)}, u32[]{:S(2)}) collective-permute-start(bf16[4,8,512]{2,1,0:T(8,128)(2,1)S(1)} %fusion.27), channel_id=1, source_target_pairs={{0,6},{1,7},{2,4},{3,5},{4,2},{5,3},{6,0},{7,1},{8,14},{9,15},{10,... | collective-permute-start | bytes 98312 | tf_op jit(solution)/shard_map/ppermute | solution.py:261
  59.5 2.4 %collective-permute-done.22 = bf16[4,8,512]{2,1,0:T(8,128)(2,1)S(1)} collective-permute-done((bf16[4,8,512]{2,1,0:T(8,128)(2,1)S(1)}, bf16[4,8,512]{2,1,0:T(8,128)(2,1)S(1)}, u32[]{:S(2)}, u32[]{:S(2)}) %collective-permute-start.22) | collective-permute-done | bytes 32800 | tf_op jit(solution)/shard_map/ppermute | solution.py:261
  61.9 1.5 %collective-permute-done.21 = bf16[4,8,512]{2,1,0:T(8,128)(2,1)S(1)} collective-permute-done((bf16[4,8,512]{2,1,0:T(8,128)(2,1)S(1)}, bf16[4,8,512]{2,1,0:T(8,128)(2,1)S(1)}, u32[]{:S(2)}, u32[]{:S(2)}) %collective-permute-start.21) | collective-permute-done | bytes 32800 | tf_op jit(solution)/shard_map/ppermute | solution.py:261
  67.2 1.4 %collective-permute-start.27 = (bf16[4,8,512]{2,1,0:T(8,128)(2,1)S(1)}, bf16[4,8,512]{2,1,0:T(8,128)(2,1)S(1)}, u32[]{:S(2)}, u32[]{:S(2)}) collective-permute-start(bf16[4,8,512]{2,1,0:T(8,128)(2,1)S(1)} %bitcast_convert_fusion.1), channel_id=1, source_target_pairs={{0,6},{1,7},{2,4},{3,5},{4,2},{5,3},{6,0},{7,1},{8,14},{9,15},{10,... | collective-permute-start | bytes 98312 | tf_op jit(solution)/shard_map/ppermute | solution.py:261
  68.6 1.8 %collective-permute-start.26 = (bf16[4,8,512]{2,1,0:T(8,128)(2,1)S(1)}, bf16[4,8,512]{2,1,0:T(8,128)(2,1)S(1)}, u32[]{:S(2)}, u32[]{:S(2)}) collective-permute-start(bf16[4,8,512]{2,1,0:T(8,128)(2,1)S(1)} %bitcast_convert_fusion.1), channel_id=1, source_target_pairs={{0,4},{1,5},{2,6},{3,7},{4,0},{5,1},{6,2},{7,3},{8,12},{9,13},{10,... | collective-permute-start | bytes 98312 | tf_op jit(solution)/shard_map/ppermute | solution.py:261
  70.9 2.0 %collective-permute-done.27 = bf16[4,8,512]{2,1,0:T(8,128)(2,1)S(1)} collective-permute-done((bf16[4,8,512]{2,1,0:T(8,128)(2,1)S(1)}, bf16[4,8,512]{2,1,0:T(8,128)(2,1)S(1)}, u32[]{:S(2)}, u32[]{:S(2)}) %collective-permute-start.27) | collective-permute-done | bytes 32800 | tf_op jit(solution)/shard_map/ppermute | solution.py:261
  72.9 1.1 collective-permute-done.26
  74.2 1.2 %collective-permute-done.29.other_ref = bf16[4,8,512]{2,1,0:T(8,128)(2,1)S(1)} collective-permute-done((bf16[4,8,512]{2,1,0:T(8,128)(2,1)S(1)}, bf16[4,8,512]{2,1,0:T(8,128)(2,1)S(1)}, u32[]{:S(2)}, u32[]{:S(2)}) %collective-permute-start.29) | collective-permute-done | bytes 32800 | tf_op jit(solution)/shard_map/ppermute | solution.py:256
  75.4 1.3 %parent_back.1 = (bf16[4,1,8,512]{3,2,1,0:T(8,128)(2,1)S(1)}, f32[40,8,128]{2,1,0:T(8,128)S(1)}, f32[8,128]{1,0:T(8,128)}, bf16[1,8,512]{2,1,0:T(8,128)(2,1)S(1)}) custom-call(s32[5]{0:T(128)S(1)} %get-tuple-element.50.plan_ref, bf16[4,8,512]{2,1,0:T(8,128)(2,1)S(1)} %fusion.own_ref, bf16[4,8,512]{2,1,0:T(8,128)(2,1)S(1)} %collective-permute-done.29.other_ref, ...), custom_call_target="tpu_custom_call" | custom-call | tf_op jit(solution)/shard_map/parent_back/pallas_call | solution.py:30
  78.4 2.3 %collective-permute-start.32 = (bf16[1,8,512]{2,1,0:T(8,128)(2,1)S(1)}, bf16[1,8,512]{2,1,0:T(8,128)(2,1)S(1)}, u32[]{:S(2)}, u32[]{:S(2)}) collective-permute-start(bf16[1,8,512]{2,1,0:T(8,128)(2,1)S(1)} %get-tuple-element.88), channel_id=1, source_target_pairs={{0,6},{1,7},{2,4},{3,5},{4,2},{5,3},{6,0},{7,1},{8,14},{9,15},{10,... | collective-permute-start | bytes 24584 | tf_op jit(solution)/shard_map/ppermute | solution.py:261
  81.6 2.2 %collective-permute-done.32.refs_2_ = bf16[1,8,512]{2,1,0:T(8,128)(2,1)S(1)} collective-permute-done((bf16[1,8,512]{2,1,0:T(8,128)(2,1)S(1)}, bf16[1,8,512]{2,1,0:T(8,128)(2,1)S(1)}, u32[]{:S(2)}, u32[]{:S(2)}) %collective-permute-start.32) | collective-permute-done | bytes 8224 | tf_op jit(solution)/shard_map/ppermute | solution.py:261
  83.8 1.4 %collective-permute-done.31.refs_1_ = bf16[1,8,512]{2,1,0:T(8,128)(2,1)S(1)} collective-permute-done((bf16[1,8,512]{2,1,0:T(8,128)(2,1)S(1)}, bf16[1,8,512]{2,1,0:T(8,128)(2,1)S(1)}, u32[]{:S(2)}, u32[]{:S(2)}) %collective-permute-start.31) | collective-permute-done | bytes 8224 | tf_op jit(solution)/shard_map/ppermute | solution.py:261
  87.1 2.0 %collective-permute-start.36 = (bf16[4,8,512]{2,1,0:T(8,128)(2,1)S(1)}, bf16[4,8,512]{2,1,0:T(8,128)(2,1)S(1)}, u32[]{:S(2)}, u32[]{:S(2)}) collective-permute-start(bf16[4,8,512]{2,1,0:T(8,128)(2,1)S(1)} %bitcast_convert_fusion), channel_id=1, source_target_pairs={{0,6},{1,7},{2,4},{3,5},{4,2},{5,3},{6,0},{7,1},{8,14},{9,15},{10,... | collective-permute-start | bytes 98312 | tf_op jit(solution)/shard_map/ppermute | solution.py:261
  89.2 1.2 %collective-permute-start.35 = (bf16[4,8,512]{2,1,0:T(8,128)(2,1)S(1)}, bf16[4,8,512]{2,1,0:T(8,128)(2,1)S(1)}, u32[]{:S(2)}, u32[]{:S(2)}) collective-permute-start(bf16[4,8,512]{2,1,0:T(8,128)(2,1)S(1)} %bitcast_convert_fusion), channel_id=1, source_target_pairs={{0,4},{1,5},{2,6},{3,7},{4,0},{5,1},{6,2},{7,3},{8,12},{9,13},{10,... | collective-permute-start | bytes 98312 | tf_op jit(solution)/shard_map/ppermute | solution.py:261
  90.8 2.1 %collective-permute-done.36 = bf16[4,8,512]{2,1,0:T(8,128)(2,1)S(1)} collective-permute-done((bf16[4,8,512]{2,1,0:T(8,128)(2,1)S(1)}, bf16[4,8,512]{2,1,0:T(8,128)(2,1)S(1)}, u32[]{:S(2)}, u32[]{:S(2)}) %collective-permute-start.36) | collective-permute-done | bytes 32800 | tf_op jit(solution)/shard_map/ppermute | solution.py:261
  92.9 1.3 %collective-permute-done.35 = bf16[4,8,512]{2,1,0:T(8,128)(2,1)S(1)} collective-permute-done((bf16[4,8,512]{2,1,0:T(8,128)(2,1)S(1)}, bf16[4,8,512]{2,1,0:T(8,128)(2,1)S(1)}, u32[]{:S(2)}, u32[]{:S(2)}) %collective-permute-start.35) | collective-permute-done | bytes 32800 | tf_op jit(solution)/shard_map/ppermute | solution.py:261
  94.3 1.2 %collective-permute-done.38.refs_3_ = bf16[4,8,512]{2,1,0:T(8,128)(2,1)S(1)} collective-permute-done((bf16[4,8,512]{2,1,0:T(8,128)(2,1)S(1)}, bf16[4,8,512]{2,1,0:T(8,128)(2,1)S(1)}, u32[]{:S(2)}, u32[]{:S(2)}) %collective-permute-start.38) | collective-permute-done | bytes 32800 | tf_op jit(solution)/shard_map/ppermute | solution.py:256
  95.5 2.6 %leaf_back.1 = (bf16[4,4,8,256]{3,2,1,0:T(8,128)(2,1)S(1)}, f32[8,512]{1,0:T(8,128)S(1)}, bf16[4,8,1024]{2,1,0:T(8,128)(2,1)S(1)}) custom-call(s32[33]{0:T(128)S(1)} %get-tuple-element.40.refs_2_.refs_0_, f32[4,8,512]{2,1,0:T(8,128)S(1)} %get-tuple-element.77.refs_1_, bf16[4,8,512]{2,1,0:T(8,128)(2,1)S(1)} %get-tuple-element.76.refs_2_, ...), custom_call_target="tpu_custom_call" | custom-call | tf_op jit(solution)/shard_map/leaf_back/pallas_call | solution.py:30
  98.2 1.2 %leaf_back_own.1 = f32[4,4,8,256]{3,2,1,0:T(8,128)S(1)} custom-call(bf16[4,8,1024]{2,1,0:T(8,128)(2,1)S(1)} %get-tuple-element.66.x_ref, bf16[4,1024,2048]{2,1,0:T(8,128)(2,1)S(1)} %copy-done), custom_call_target="tpu_custom_call" | custom-call | bytes 12582912 | tf_op jit(solution)/shard_map/leaf_back_own/pallas_call | solution.py:30
  99.8 2.3 %collective-permute-start.41 = (bf16[4,8,256]{2,1,0:T(8,128)(2,1)S(1)}, bf16[4,8,256]{2,1,0:T(8,128)(2,1)S(1)}, u32[]{:S(2)}, u32[]{:S(2)}) collective-permute-start(bf16[4,8,256]{2,1,0:T(8,128)(2,1)S(1)} %get-tuple-element.84), channel_id=1, source_target_pairs={{0,6},{1,7},{2,4},{3,5},{4,2},{5,3},{6,0},{7,1},{8,14},{9,15},{10,... | collective-permute-start | bytes 49160 | tf_op jit(solution)/shard_map/ppermute | solution.py:261
  103.3 2.1 %collective-permute-done.41.refs_2_ = bf16[4,8,256]{2,1,0:T(8,128)(2,1)S(1)} collective-permute-done((bf16[4,8,256]{2,1,0:T(8,128)(2,1)S(1)}, bf16[4,8,256]{2,1,0:T(8,128)(2,1)S(1)}, u32[]{:S(2)}, u32[]{:S(2)}) %collective-permute-start.41) | collective-permute-done | bytes 16416 | tf_op jit(solution)/shard_map/ppermute | solution.py:261
  105.3 1.3 %collective-permute-done.40.refs_1_ = bf16[4,8,256]{2,1,0:T(8,128)(2,1)S(1)} collective-permute-done((bf16[4,8,256]{2,1,0:T(8,128)(2,1)S(1)}, bf16[4,8,256]{2,1,0:T(8,128)(2,1)S(1)}, u32[]{:S(2)}, u32[]{:S(2)}) %collective-permute-start.40) | collective-permute-done | bytes 16416 | tf_op jit(solution)/shard_map/ppermute | solution.py:261
  108.4 1.0 collective-permute-start.44
  109.4 1.1 collective-permute-start.46
  110.5 2.3 %collective-permute-start.45 = (bf16[4,8,256]{2,1,0:T(8,128)(2,1)S(1)}, bf16[4,8,256]{2,1,0:T(8,128)(2,1)S(1)}, u32[]{:S(2)}, u32[]{:S(2)}) collective-permute-start(bf16[4,8,256]{2,1,0:T(8,128)(2,1)S(1)} %get-tuple-element.82), channel_id=1, source_target_pairs={{0,6},{1,7},{2,4},{3,5},{4,2},{5,3},{6,0},{7,1},{8,14},{9,15},{10,... | collective-permute-start | bytes 49160 | tf_op jit(solution)/shard_map/ppermute | solution.py:261
  113.5 2.6 %collective-permute-done.45 = bf16[4,8,256]{2,1,0:T(8,128)(2,1)S(1)} collective-permute-done((bf16[4,8,256]{2,1,0:T(8,128)(2,1)S(1)}, bf16[4,8,256]{2,1,0:T(8,128)(2,1)S(1)}, u32[]{:S(2)}, u32[]{:S(2)}) %collective-permute-start.45) | collective-permute-done | bytes 16416 | tf_op jit(solution)/shard_map/ppermute | solution.py:261
  (109 shorter events, 29.7 us)
Async XLA Ops:
  1.4 7.9 %collective-permute-start.2 = (bf16[4,8,256]{2,1,0:T(8,128)(2,1)S(1)}, bf16[4,8,256]{2,1,0:T(8,128)(2,1)S(1)}, u32[]{:S(2)}, u32[]{:S(2)}) collective-permute-start(bf16[4,8,256]{2,1,0:T(8,128)(2,1)S(1)} %round_rhs.1.refs_0_), channel_id=1, source_target_pairs={{0,2},{1,3},{2,0},{3,1},{4,6},{5,7},{6,4},{7,5},{8,10},{9,11},{10,... | collective-permute-start | bytes 49160 | tf_op jit(solution)/shard_map/ppermute | solution.py:261
  4.5 5.8 %collective-permute-start.1 = (bf16[4,8,256]{2,1,0:T(8,128)(2,1)S(1)}, bf16[4,8,256]{2,1,0:T(8,128)(2,1)S(1)}, u32[]{:S(2)}, u32[]{:S(2)}) collective-permute-start(bf16[4,8,256]{2,1,0:T(8,128)(2,1)S(1)} %round_rhs.1.refs_0_), channel_id=1, source_target_pairs={{0,6},{1,7},{2,4},{3,5},{4,2},{5,3},{6,0},{7,1},{8,14},{9,15},{10,... | collective-permute-start | bytes 49160 | tf_op jit(solution)/shard_map/ppermute | solution.py:261
  7.0 4.6 %collective-permute-start = (bf16[4,8,256]{2,1,0:T(8,128)(2,1)S(1)}, bf16[4,8,256]{2,1,0:T(8,128)(2,1)S(1)}, u32[]{:S(2)}, u32[]{:S(2)}) collective-permute-start(bf16[4,8,256]{2,1,0:T(8,128)(2,1)S(1)} %round_rhs.1.refs_0_), channel_id=1, source_target_pairs={{0,4},{1,5},{2,6},{3,7},{4,0},{5,1},{6,2},{7,3},{8,12},{9,13},{10,... | collective-permute-start | bytes 49160 | tf_op jit(solution)/shard_map/ppermute | solution.py:261
  11.7 1.3 %collective-permute-start.3 = (bf16[4,4,8,256]{3,2,1,0:T(8,128)(2,1)S(1)}, bf16[4,4,8,256]{3,2,1,0:T(8,128)(2,1)S(1)}, u32[]{:S(2)}, u32[]{:S(2)}) collective-permute-start(bf16[4,4,8,256]{3,2,1,0:T(8,128)(2,1)S(1)} %pad_maximum_fusion.x_ref), channel_id=1, source_target_pairs={{0,1},{1,0},{2,3},{3,2},{4,5},{5,4},{6,7},{7,6},{8,9},{9,8},{10,11... | collective-permute-start | bytes 196616 | tf_op jit(solution)/shard_map/ppermute | solution.py:256
  13.6 4.2 %collective-permute-start.6 = (bf16[4,8,256]{2,1,0:T(8,128)(2,1)S(1)}, bf16[4,8,256]{2,1,0:T(8,128)(2,1)S(1)}, u32[]{:S(2)}, u32[]{:S(2)}) collective-permute-start(bf16[4,8,256]{2,1,0:T(8,128)(2,1)S(1)} %get-tuple-element.42.x_ref), channel_id=1, source_target_pairs={{0,2},{1,3},{2,0},{3,1},{4,6},{5,7},{6,4},{7,5},{8,10},{9,11},{10,... | collective-permute-start | bytes 49160 | tf_op jit(solution)/shard_map/ppermute | solution.py:261
  14.4 5.5 %collective-permute-start.5 = (bf16[4,8,256]{2,1,0:T(8,128)(2,1)S(1)}, bf16[4,8,256]{2,1,0:T(8,128)(2,1)S(1)}, u32[]{:S(2)}, u32[]{:S(2)}) collective-permute-start(bf16[4,8,256]{2,1,0:T(8,128)(2,1)S(1)} %get-tuple-element.42.x_ref), channel_id=1, source_target_pairs={{0,6},{1,7},{2,4},{3,5},{4,2},{5,3},{6,0},{7,1},{8,14},{9,15},{10,... | collective-permute-start | bytes 49160 | tf_op jit(solution)/shard_map/ppermute | solution.py:261
  15.6 4.8 %collective-permute-start.4 = (bf16[4,8,256]{2,1,0:T(8,128)(2,1)S(1)}, bf16[4,8,256]{2,1,0:T(8,128)(2,1)S(1)}, u32[]{:S(2)}, u32[]{:S(2)}) collective-permute-start(bf16[4,8,256]{2,1,0:T(8,128)(2,1)S(1)} %get-tuple-element.42.x_ref), channel_id=1, source_target_pairs={{0,4},{1,5},{2,6},{3,7},{4,0},{5,1},{6,2},{7,3},{8,12},{9,13},{10,... | collective-permute-start | bytes 49160 | tf_op jit(solution)/shard_map/ppermute | solution.py:261
  20.4 1.8 %collective-permute-start.7 = (bf16[4,4,8,256]{3,2,1,0:T(8,128)(2,1)S(1)}, bf16[4,4,8,256]{3,2,1,0:T(8,128)(2,1)S(1)}, u32[]{:S(2)}, u32[]{:S(2)}) collective-permute-start(bf16[4,4,8,256]{3,2,1,0:T(8,128)(2,1)S(1)} %pad_maximum_fusion.1.x_ref), channel_id=1, source_target_pairs={{0,1},{1,0},{2,3},{3,2},{4,5},{5,4},{6,7},{7,6},{8,9},{9,8},{10,11... | collective-permute-start | bytes 196616 | tf_op jit(solution)/shard_map/ppermute | solution.py:256
  25.4 1.4 %collective-permute-start.8 = (bf16[4,8,512]{2,1,0:T(8,128)(2,1)S(1)}, bf16[4,8,512]{2,1,0:T(8,128)(2,1)S(1)}, u32[]{:S(2)}, u32[]{:S(2)}) collective-permute-start(bf16[4,8,512]{2,1,0:T(8,128)(2,1)S(1)} %get-tuple-element.47), channel_id=1, source_target_pairs={{0,1},{1,0},{2,3},{3,2},{4,5},{5,4},{6,7},{7,6},{8,9},{9,8},{10,11... | collective-permute-start | bytes 98312 | tf_op jit(solution)/shard_map/ppermute | solution.py:256
  26.8 5.4 %collective-permute-start.11 = (bf16[4,8,512]{2,1,0:T(8,128)(2,1)S(1)}, bf16[4,8,512]{2,1,0:T(8,128)(2,1)S(1)}, u32[]{:S(2)}, u32[]{:S(2)}) collective-permute-start(bf16[4,8,512]{2,1,0:T(8,128)(2,1)S(1)} %get-tuple-element.78), channel_id=1, source_target_pairs={{0,2},{1,3},{2,0},{3,1},{4,6},{5,7},{6,4},{7,5},{8,10},{9,11},{10,... | collective-permute-start | bytes 98312 | tf_op jit(solution)/shard_map/ppermute | solution.py:261
  27.3 5.7 %collective-permute-start.10 = (bf16[4,8,512]{2,1,0:T(8,128)(2,1)S(1)}, bf16[4,8,512]{2,1,0:T(8,128)(2,1)S(1)}, u32[]{:S(2)}, u32[]{:S(2)}) collective-permute-start(bf16[4,8,512]{2,1,0:T(8,128)(2,1)S(1)} %get-tuple-element.78), channel_id=1, source_target_pairs={{0,6},{1,7},{2,4},{3,5},{4,2},{5,3},{6,0},{7,1},{8,14},{9,15},{10,... | collective-permute-start | bytes 98312 | tf_op jit(solution)/shard_map/ppermute | solution.py:261
  29.8 5.2 %collective-permute-start.9 = (bf16[4,8,512]{2,1,0:T(8,128)(2,1)S(1)}, bf16[4,8,512]{2,1,0:T(8,128)(2,1)S(1)}, u32[]{:S(2)}, u32[]{:S(2)}) collective-permute-start(bf16[4,8,512]{2,1,0:T(8,128)(2,1)S(1)} %get-tuple-element.78), channel_id=1, source_target_pairs={{0,4},{1,5},{2,6},{3,7},{4,0},{5,1},{6,2},{7,3},{8,12},{9,13},{10,... | collective-permute-start | bytes 98312 | tf_op jit(solution)/shard_map/ppermute | solution.py:261
  35.0 1.3 %collective-permute-start.12 = (bf16[4,8,512]{2,1,0:T(8,128)(2,1)S(1)}, bf16[4,8,512]{2,1,0:T(8,128)(2,1)S(1)}, u32[]{:S(2)}, u32[]{:S(2)}) collective-permute-start(bf16[4,8,512]{2,1,0:T(8,128)(2,1)S(1)} %add_convert_fusion.1.x_ref), channel_id=1, source_target_pairs={{0,1},{1,0},{2,3},{3,2},{4,5},{5,4},{6,7},{7,6},{8,9},{9,8},{10,11... | collective-permute-start | bytes 98312 | tf_op jit(solution)/shard_map/ppermute | solution.py:256
  36.9 3.7 %collective-permute-start.15 = (bf16[8,512]{1,0:T(8,128)(2,1)S(1)}, bf16[8,512]{1,0:T(8,128)(2,1)S(1)}, u32[]{:S(2)}, u32[]{:S(2)}) collective-permute-start(bf16[8,512]{1,0:T(8,128)(2,1)S(1)} %get-tuple-element.52), channel_id=1, source_target_pairs={{0,2},{1,3},{2,0},{3,1},{4,6},{5,7},{6,4},{7,5},{8,10},{9,11},{10,... | collective-permute-start | bytes 24584 | tf_op jit(solution)/shard_map/ppermute | solution.py:261
  37.4 5.4 %collective-permute-start.14 = (bf16[8,512]{1,0:T(8,128)(2,1)S(1)}, bf16[8,512]{1,0:T(8,128)(2,1)S(1)}, u32[]{:S(2)}, u32[]{:S(2)}) collective-permute-start(bf16[8,512]{1,0:T(8,128)(2,1)S(1)} %get-tuple-element.52), channel_id=1, source_target_pairs={{0,6},{1,7},{2,4},{3,5},{4,2},{5,3},{6,0},{7,1},{8,14},{9,15},{10,... | collective-permute-start | bytes 24584 | tf_op jit(solution)/shard_map/ppermute | solution.py:261
  38.9 4.5 %collective-permute-start.13 = (bf16[8,512]{1,0:T(8,128)(2,1)S(1)}, bf16[8,512]{1,0:T(8,128)(2,1)S(1)}, u32[]{:S(2)}, u32[]{:S(2)}) collective-permute-start(bf16[8,512]{1,0:T(8,128)(2,1)S(1)} %get-tuple-element.52), channel_id=1, source_target_pairs={{0,4},{1,5},{2,6},{3,7},{4,0},{5,1},{6,2},{7,3},{8,12},{9,13},{10,... | collective-permute-start | bytes 24584 | tf_op jit(solution)/shard_map/ppermute | solution.py:261
  43.4 20.1 %copy-start.4 = (bf16[512,4096]{1,0:T(8,128)(2,1)S(1)}, bf16[512,4096]{1,0:T(8,128)(2,1)}, u32[]{:S(2)}) copy-start(bf16[512,4096]{1,0:T(8,128)(2,1)} %param.23) | copy-start | bytes 12582916
  43.4 1.3 %collective-permute-start.16 = (bf16[4,8,512]{2,1,0:T(8,128)(2,1)S(1)}, bf16[4,8,512]{2,1,0:T(8,128)(2,1)S(1)}, u32[]{:S(2)}, u32[]{:S(2)}) collective-permute-start(bf16[4,8,512]{2,1,0:T(8,128)(2,1)S(1)} %pad_maximum_fusion.2.x_ref), channel_id=1, source_target_pairs={{0,1},{1,0},{2,3},{3,2},{4,5},{5,4},{6,7},{7,6},{8,9},{9,8},{10,11... | collective-permute-start | bytes 98312 | tf_op jit(solution)/shard_map/ppermute | solution.py:256
  46.1 1.3 %collective-permute-start.17 = (bf16[4,8,512]{2,1,0:T(8,128)(2,1)S(1)}, bf16[4,8,512]{2,1,0:T(8,128)(2,1)S(1)}, u32[]{:S(2)}, u32[]{:S(2)}) collective-permute-start(bf16[4,8,512]{2,1,0:T(8,128)(2,1)S(1)} %get-tuple-element.57), channel_id=1, source_target_pairs={{0,1},{1,0},{2,3},{3,2},{4,5},{5,4},{6,7},{7,6},{8,9},{9,8},{10,11... | collective-permute-start | bytes 98312 | tf_op jit(solution)/shard_map/ppermute | solution.py:256
  47.4 4.1 %collective-permute-start.20 = (bf16[4,8,512]{2,1,0:T(8,128)(2,1)S(1)}, bf16[4,8,512]{2,1,0:T(8,128)(2,1)S(1)}, u32[]{:S(2)}, u32[]{:S(2)}) collective-permute-start(bf16[4,8,512]{2,1,0:T(8,128)(2,1)S(1)} %fusion.1), channel_id=1, source_target_pairs={{0,24},{8,0},{16,8},{24,16},{1,25},{9,1},{17,9},{25,17},{2,26},{10... | collective-permute-start | bytes 98312 | tf_op jit(solution)/shard_map/ppermute | solution.py:277
  49.9 4.3 %collective-permute-start.19 = (bf16[4,8,512]{2,1,0:T(8,128)(2,1)S(1)}, bf16[4,8,512]{2,1,0:T(8,128)(2,1)S(1)}, u32[]{:S(2)}, u32[]{:S(2)}) collective-permute-start(bf16[4,8,512]{2,1,0:T(8,128)(2,1)S(1)} %fusion.1), channel_id=1, source_target_pairs={{0,16},{8,24},{16,0},{24,8},{1,17},{9,25},{17,1},{25,9},{2,18},{10... | collective-permute-start | bytes 98312 | tf_op jit(solution)/shard_map/ppermute | solution.py:277
  50.4 4.8 %collective-permute-start.18 = (bf16[4,8,512]{2,1,0:T(8,128)(2,1)S(1)}, bf16[4,8,512]{2,1,0:T(8,128)(2,1)S(1)}, u32[]{:S(2)}, u32[]{:S(2)}) collective-permute-start(bf16[4,8,512]{2,1,0:T(8,128)(2,1)S(1)} %fusion.1), channel_id=1, source_target_pairs={{0,8},{8,16},{16,24},{24,0},{1,9},{9,17},{17,25},{25,1},{2,10},{10... | collective-permute-start | bytes 98312 | tf_op jit(solution)/shard_map/ppermute | solution.py:277
  55.2 4.3 %collective-permute-start.23 = (bf16[4,8,512]{2,1,0:T(8,128)(2,1)S(1)}, bf16[4,8,512]{2,1,0:T(8,128)(2,1)S(1)}, u32[]{:S(2)}, u32[]{:S(2)}) collective-permute-start(bf16[4,8,512]{2,1,0:T(8,128)(2,1)S(1)} %fusion.27), channel_id=1, source_target_pairs={{0,2},{1,3},{2,0},{3,1},{4,6},{5,7},{6,4},{7,5},{8,10},{9,11},{10,... | collective-permute-start | bytes 98312 | tf_op jit(solution)/shard_map/ppermute | solution.py:261
  56.2 5.7 %collective-permute-start.22 = (bf16[4,8,512]{2,1,0:T(8,128)(2,1)S(1)}, bf16[4,8,512]{2,1,0:T(8,128)(2,1)S(1)}, u32[]{:S(2)}, u32[]{:S(2)}) collective-permute-start(bf16[4,8,512]{2,1,0:T(8,128)(2,1)S(1)} %fusion.27), channel_id=1, source_target_pairs={{0,6},{1,7},{2,4},{3,5},{4,2},{5,3},{6,0},{7,1},{8,14},{9,15},{10,... | collective-permute-start | bytes 98312 | tf_op jit(solution)/shard_map/ppermute | solution.py:261
  58.3 5.1 %collective-permute-start.21 = (bf16[4,8,512]{2,1,0:T(8,128)(2,1)S(1)}, bf16[4,8,512]{2,1,0:T(8,128)(2,1)S(1)}, u32[]{:S(2)}, u32[]{:S(2)}) collective-permute-start(bf16[4,8,512]{2,1,0:T(8,128)(2,1)S(1)} %fusion.27), channel_id=1, source_target_pairs={{0,4},{1,5},{2,6},{3,7},{4,0},{5,1},{6,2},{7,3},{8,12},{9,13},{10,... | collective-permute-start | bytes 98312 | tf_op jit(solution)/shard_map/ppermute | solution.py:261
  63.4 1.3 %collective-permute-start.24 = (bf16[4,8,512]{2,1,0:T(8,128)(2,1)S(1)}, bf16[4,8,512]{2,1,0:T(8,128)(2,1)S(1)}, u32[]{:S(2)}, u32[]{:S(2)}) collective-permute-start(bf16[4,8,512]{2,1,0:T(8,128)(2,1)S(1)} %add_convert_fusion.x_ref), channel_id=1, source_target_pairs={{0,1},{1,0},{2,3},{3,2},{4,5},{5,4},{6,7},{7,6},{8,9},{9,8},{10,11... | collective-permute-start | bytes 98312 | tf_op jit(solution)/shard_map/ppermute | solution.py:256
  65.7 1.2 %collective-permute-start.25 = (bf16[4,1,8,512]{3,2,0,1:T(8,128)(2,1)S(1)}, bf16[4,1,8,512]{3,2,0,1:T(8,128)(2,1)S(1)}, u32[]{:S(2)}, u32[]{:S(2)}) collective-permute-start(bf16[4,1,8,512]{3,2,0,1:T(8,128)(2,1)S(1)} %bitcast.81), channel_id=1, source_target_pairs={{0,1},{1,0},{2,3},{3,2},{4,5},{5,4},{6,7},{7,6},{8,9},{9,8},{10,11... | collective-permute-start | bytes 98312 | tf_op jit(solution)/shard_map/ppermute | solution.py:256
  66.9 4.0 %collective-permute-start.28 = (bf16[4,8,512]{2,1,0:T(8,128)(2,1)S(1)}, bf16[4,8,512]{2,1,0:T(8,128)(2,1)S(1)}, u32[]{:S(2)}, u32[]{:S(2)}) collective-permute-start(bf16[4,8,512]{2,1,0:T(8,128)(2,1)S(1)} %bitcast_convert_fusion.1), channel_id=1, source_target_pairs={{0,2},{1,3},{2,0},{3,1},{4,6},{5,7},{6,4},{7,5},{8,10},{9,11},{10,... | collective-permute-start | bytes 98312 | tf_op jit(solution)/shard_map/ppermute | solution.py:261
  67.2 5.7 %collective-permute-start.27 = (bf16[4,8,512]{2,1,0:T(8,128)(2,1)S(1)}, bf16[4,8,512]{2,1,0:T(8,128)(2,1)S(1)}, u32[]{:S(2)}, u32[]{:S(2)}) collective-permute-start(bf16[4,8,512]{2,1,0:T(8,128)(2,1)S(1)} %bitcast_convert_fusion.1), channel_id=1, source_target_pairs={{0,6},{1,7},{2,4},{3,5},{4,2},{5,3},{6,0},{7,1},{8,14},{9,15},{10,... | collective-permute-start | bytes 98312 | tf_op jit(solution)/shard_map/ppermute | solution.py:261
  68.6 5.4 %collective-permute-start.26 = (bf16[4,8,512]{2,1,0:T(8,128)(2,1)S(1)}, bf16[4,8,512]{2,1,0:T(8,128)(2,1)S(1)}, u32[]{:S(2)}, u32[]{:S(2)}) collective-permute-start(bf16[4,8,512]{2,1,0:T(8,128)(2,1)S(1)} %bitcast_convert_fusion.1), channel_id=1, source_target_pairs={{0,4},{1,5},{2,6},{3,7},{4,0},{5,1},{6,2},{7,3},{8,12},{9,13},{10,... | collective-permute-start | bytes 98312 | tf_op jit(solution)/shard_map/ppermute | solution.py:261
  74.1 1.3 %collective-permute-start.29 = (bf16[4,8,512]{2,1,0:T(8,128)(2,1)S(1)}, bf16[4,8,512]{2,1,0:T(8,128)(2,1)S(1)}, u32[]{:S(2)}, u32[]{:S(2)}) collective-permute-start(bf16[4,8,512]{2,1,0:T(8,128)(2,1)S(1)} %fusion.own_ref), channel_id=1, source_target_pairs={{0,1},{1,0},{2,3},{3,2},{4,5},{5,4},{6,7},{7,6},{8,9},{9,8},{10,11... | collective-permute-start | bytes 98312 | tf_op jit(solution)/shard_map/ppermute | solution.py:256
  76.7 1.2 %collective-permute-start.30 = (bf16[4,1,8,512]{3,2,1,0:T(8,128)(2,1)S(1)}, bf16[4,1,8,512]{3,2,1,0:T(8,128)(2,1)S(1)}, u32[]{:S(2)}, u32[]{:S(2)}) collective-permute-start(bf16[4,1,8,512]{3,2,1,0:T(8,128)(2,1)S(1)} %get-tuple-element.61), channel_id=1, source_target_pairs={{0,1},{1,0},{2,3},{3,2},{4,5},{5,4},{6,7},{7,6},{8,9},{9,8},{10,11... | collective-permute-start | bytes 98312 | tf_op jit(solution)/shard_map/ppermute | solution.py:256
  77.9 3.7 %collective-permute-start.33 = (bf16[1,8,512]{2,1,0:T(8,128)(2,1)S(1)}, bf16[1,8,512]{2,1,0:T(8,128)(2,1)S(1)}, u32[]{:S(2)}, u32[]{:S(2)}) collective-permute-start(bf16[1,8,512]{2,1,0:T(8,128)(2,1)S(1)} %get-tuple-element.87), channel_id=1, source_target_pairs={{0,2},{1,3},{2,0},{3,1},{4,6},{5,7},{6,4},{7,5},{8,10},{9,11},{10,... | collective-permute-start | bytes 24584 | tf_op jit(solution)/shard_map/ppermute | solution.py:261
  78.4 5.5 %collective-permute-start.32 = (bf16[1,8,512]{2,1,0:T(8,128)(2,1)S(1)}, bf16[1,8,512]{2,1,0:T(8,128)(2,1)S(1)}, u32[]{:S(2)}, u32[]{:S(2)}) collective-permute-start(bf16[1,8,512]{2,1,0:T(8,128)(2,1)S(1)} %get-tuple-element.88), channel_id=1, source_target_pairs={{0,6},{1,7},{2,4},{3,5},{4,2},{5,3},{6,0},{7,1},{8,14},{9,15},{10,... | collective-permute-start | bytes 24584 | tf_op jit(solution)/shard_map/ppermute | solution.py:261
  80.7 4.5 %collective-permute-start.31 = (bf16[1,8,512]{2,1,0:T(8,128)(2,1)S(1)}, bf16[1,8,512]{2,1,0:T(8,128)(2,1)S(1)}, u32[]{:S(2)}, u32[]{:S(2)}) collective-permute-start(bf16[1,8,512]{2,1,0:T(8,128)(2,1)S(1)} %get-tuple-element.89), channel_id=1, source_target_pairs={{0,4},{1,5},{2,6},{3,7},{4,0},{5,1},{6,2},{7,3},{8,12},{9,13},{10,... | collective-permute-start | bytes 24584 | tf_op jit(solution)/shard_map/ppermute | solution.py:261
  85.6 1.2 %collective-permute-start.34 = (bf16[4,1,8,512]{3,2,0,1:T(8,128)(2,1)S(1)}, bf16[4,1,8,512]{3,2,0,1:T(8,128)(2,1)S(1)}, u32[]{:S(2)}, u32[]{:S(2)}) collective-permute-start(bf16[4,1,8,512]{3,2,0,1:T(8,128)(2,1)S(1)} %bitcast.80), channel_id=1, source_target_pairs={{0,1},{1,0},{2,3},{3,2},{4,5},{5,4},{6,7},{7,6},{8,9},{9,8},{10,11... | collective-permute-start | bytes 98312 | tf_op jit(solution)/shard_map/ppermute | solution.py:256
  86.9 4.0 %collective-permute-start.37 = (bf16[4,8,512]{2,1,0:T(8,128)(2,1)S(1)}, bf16[4,8,512]{2,1,0:T(8,128)(2,1)S(1)}, u32[]{:S(2)}, u32[]{:S(2)}) collective-permute-start(bf16[4,8,512]{2,1,0:T(8,128)(2,1)S(1)} %bitcast_convert_fusion), channel_id=1, source_target_pairs={{0,2},{1,3},{2,0},{3,1},{4,6},{5,7},{6,4},{7,5},{8,10},{9,11},{10,... | collective-permute-start | bytes 98312 | tf_op jit(solution)/shard_map/ppermute | solution.py:261
  87.1 5.8 %collective-permute-start.36 = (bf16[4,8,512]{2,1,0:T(8,128)(2,1)S(1)}, bf16[4,8,512]{2,1,0:T(8,128)(2,1)S(1)}, u32[]{:S(2)}, u32[]{:S(2)}) collective-permute-start(bf16[4,8,512]{2,1,0:T(8,128)(2,1)S(1)} %bitcast_convert_fusion), channel_id=1, source_target_pairs={{0,6},{1,7},{2,4},{3,5},{4,2},{5,3},{6,0},{7,1},{8,14},{9,15},{10,... | collective-permute-start | bytes 98312 | tf_op jit(solution)/shard_map/ppermute | solution.py:261
  89.2 5.0 %collective-permute-start.35 = (bf16[4,8,512]{2,1,0:T(8,128)(2,1)S(1)}, bf16[4,8,512]{2,1,0:T(8,128)(2,1)S(1)}, u32[]{:S(2)}, u32[]{:S(2)}) collective-permute-start(bf16[4,8,512]{2,1,0:T(8,128)(2,1)S(1)} %bitcast_convert_fusion), channel_id=1, source_target_pairs={{0,4},{1,5},{2,6},{3,7},{4,0},{5,1},{6,2},{7,3},{8,12},{9,13},{10,... | collective-permute-start | bytes 98312 | tf_op jit(solution)/shard_map/ppermute | solution.py:261
  94.2 1.3 %collective-permute-start.38 = (bf16[4,8,512]{2,1,0:T(8,128)(2,1)S(1)}, bf16[4,8,512]{2,1,0:T(8,128)(2,1)S(1)}, u32[]{:S(2)}, u32[]{:S(2)}) collective-permute-start(bf16[4,8,512]{2,1,0:T(8,128)(2,1)S(1)} %get-tuple-element.76.refs_2_), channel_id=1, source_target_pairs={{0,1},{1,0},{2,3},{3,2},{4,5},{5,4},{6,7},{7,6},{8,9},{9,8},{10,11... | collective-permute-start | bytes 98312 | tf_op jit(solution)/shard_map/ppermute | solution.py:256
  98.1 1.4 %collective-permute-start.39 = (bf16[4,4,8,256]{3,2,1,0:T(8,128)(2,1)S(1)}, bf16[4,4,8,256]{3,2,1,0:T(8,128)(2,1)S(1)}, u32[]{:S(2)}, u32[]{:S(2)}) collective-permute-start(bf16[4,4,8,256]{3,2,1,0:T(8,128)(2,1)S(1)} %get-tuple-element.67), channel_id=1, source_target_pairs={{0,1},{1,0},{2,3},{3,2},{4,5},{5,4},{6,7},{7,6},{8,9},{9,8},{10,11... | collective-permute-start | bytes 196616 | tf_op jit(solution)/shard_map/ppermute | solution.py:256
  99.5 3.8 %collective-permute-start.42 = (bf16[4,8,256]{2,1,0:T(8,128)(2,1)S(1)}, bf16[4,8,256]{2,1,0:T(8,128)(2,1)S(1)}, u32[]{:S(2)}, u32[]{:S(2)}) collective-permute-start(bf16[4,8,256]{2,1,0:T(8,128)(2,1)S(1)} %get-tuple-element.83), channel_id=1, source_target_pairs={{0,2},{1,3},{2,0},{3,1},{4,6},{5,7},{6,4},{7,5},{8,10},{9,11},{10,... | collective-permute-start | bytes 49160 | tf_op jit(solution)/shard_map/ppermute | solution.py:261
  99.8 5.6 %collective-permute-start.41 = (bf16[4,8,256]{2,1,0:T(8,128)(2,1)S(1)}, bf16[4,8,256]{2,1,0:T(8,128)(2,1)S(1)}, u32[]{:S(2)}, u32[]{:S(2)}) collective-permute-start(bf16[4,8,256]{2,1,0:T(8,128)(2,1)S(1)} %get-tuple-element.84), channel_id=1, source_target_pairs={{0,6},{1,7},{2,4},{3,5},{4,2},{5,3},{6,0},{7,1},{8,14},{9,15},{10,... | collective-permute-start | bytes 49160 | tf_op jit(solution)/shard_map/ppermute | solution.py:261
  102.0 4.6 %collective-permute-start.40 = (bf16[4,8,256]{2,1,0:T(8,128)(2,1)S(1)}, bf16[4,8,256]{2,1,0:T(8,128)(2,1)S(1)}, u32[]{:S(2)}, u32[]{:S(2)}) collective-permute-start(bf16[4,8,256]{2,1,0:T(8,128)(2,1)S(1)} %get-tuple-element.85), channel_id=1, source_target_pairs={{0,4},{1,5},{2,6},{3,7},{4,0},{5,1},{6,2},{7,3},{8,12},{9,13},{10,... | collective-permute-start | bytes 49160 | tf_op jit(solution)/shard_map/ppermute | solution.py:261
  107.1 1.3 %collective-permute-start.43 = (bf16[4,4,8,256]{3,2,1,0:T(8,128)(2,1)S(1)}, bf16[4,4,8,256]{3,2,1,0:T(8,128)(2,1)S(1)}, u32[]{:S(2)}, u32[]{:S(2)}) collective-permute-start(bf16[4,4,8,256]{3,2,1,0:T(8,128)(2,1)S(1)} %get-tuple-element.70), channel_id=1, source_target_pairs={{0,1},{1,0},{2,3},{3,2},{4,5},{5,4},{6,7},{7,6},{8,9},{9,8},{10,11... | collective-permute-start | bytes 196616 | tf_op jit(solution)/shard_map/ppermute | solution.py:256
  108.4 5.1 %collective-permute-start.44 = (bf16[4,8,256]{2,1,0:T(8,128)(2,1)S(1)}, bf16[4,8,256]{2,1,0:T(8,128)(2,1)S(1)}, u32[]{:S(2)}, u32[]{:S(2)}) collective-permute-start(bf16[4,8,256]{2,1,0:T(8,128)(2,1)S(1)} %get-tuple-element.80), channel_id=1, source_target_pairs={{0,4},{1,5},{2,6},{3,7},{4,0},{5,1},{6,2},{7,3},{8,12},{9,13},{10,... | collective-permute-start | bytes 49160 | tf_op jit(solution)/shard_map/ppermute | solution.py:261
  109.4 4.0 %collective-permute-start.46 = (bf16[4,8,256]{2,1,0:T(8,128)(2,1)S(1)}, bf16[4,8,256]{2,1,0:T(8,128)(2,1)S(1)}, u32[]{:S(2)}, u32[]{:S(2)}) collective-permute-start(bf16[4,8,256]{2,1,0:T(8,128)(2,1)S(1)} %get-tuple-element.81), channel_id=1, source_target_pairs={{0,2},{1,3},{2,0},{3,1},{4,6},{5,7},{6,4},{7,5},{8,10},{9,11},{10,... | collective-permute-start | bytes 49160 | tf_op jit(solution)/shard_map/ppermute | solution.py:261
  110.5 5.5 %collective-permute-start.45 = (bf16[4,8,256]{2,1,0:T(8,128)(2,1)S(1)}, bf16[4,8,256]{2,1,0:T(8,128)(2,1)S(1)}, u32[]{:S(2)}, u32[]{:S(2)}) collective-permute-start(bf16[4,8,256]{2,1,0:T(8,128)(2,1)S(1)} %get-tuple-element.82), channel_id=1, source_target_pairs={{0,6},{1,7},{2,4},{3,5},{4,2},{5,3},{6,0},{7,1},{8,14},{9,15},{10,... | collective-permute-start | bytes 49160 | tf_op jit(solution)/shard_map/ppermute | solution.py:261
  (10 other events, 79.4 us)
